TPU v7x, 32 devices: a whole 2x2x4 slice. The times are simulated.
32 devices in a mesh: seq: 8 (over z, x), tp: 4 (over y, core).
Axes of the slice: x: 2, y: 2, z: 4, core: 2. Of those that a mesh axis runs over, the one named last changes fastest.
Arguments:
- tokens: bfloat16 [2048, 4096], P('seq', 'tp'), may hold values from -6 to 6
- w_qkv: bfloat16 [3, 4096, 4096], P(None, None, 'tp'), may hold values from -0.09375 to 0.09375
- forget: float32 [2048, 32], P('seq', 'tp'), as said below
- out_grad: bfloat16 [2048, 4096], P('seq', 'tp'), may hold values from -6 to 6
- doc_lengths: int32 [16], replicated, may hold values from 1 to 1024, 2048 in all
Outputs:
- attn_out: float32 [2048, 4096], P('seq', 'tp')
- input_grad: float32 [2048, 4096], P('seq', 'tp')
Inputs may be any that keep to these rules, and one draw needn't show every extreme that they name: `doc_lengths`: the documents' lengths in stream order; they sum to 2048, and the longest has exactly 1024 tokens. `forget`: log decay factors, all negative.
All inputs are finite; a program needn't handle non-finite values.
Results may differ from a plain program's by a relative error of at most 0.0046.
Values may be sent and summed in bfloat16 or wider, within the bound.
No kernel may reach another device: no remote copies, remote signals or barrier semaphores. Data moves between devices by JAX's collectives and lax.ppermute only.
A program may use at most 128 MiB of HBM per device.

v0:
```python
import jax
import jax.numpy as jnp
from jax import lax
from jax.sharding import PartitionSpec as P

DH = 128
BLOCK = 256


HIGHEST = lax.Precision.HIGHEST


def entering(part, axis, combine, identity, reverse):
    count = lax.axis_size(axis)
    place = lax.axis_index(axis)
    ahead = count - 1 - place if reverse else place
    gathered = jax.tree.map(lambda a: lax.all_gather(a, axis), part)
    state = jax.tree.map(lambda a, e: jnp.zeros_like(a) + jnp.asarray(e, a.dtype), part, identity)

    def one(step, state):
        source = count - 1 - step if reverse else step
        return combine(
            state, jax.tree.map(lambda a: lax.dynamic_index_in_dim(a, source, 0, False), gathered)
        )

    return lax.fori_loop(0, ahead, one, state)


def document_ids(doc_lengths, positions):
    doc_ends = jnp.cumsum(doc_lengths)
    return jnp.sum((positions[:, None] >= doc_ends[None, :]).astype(jnp.int32), axis=1)


def join_forward(earlier, later):
    return (earlier[0] * later[0], later[0][:, None, None] * earlier[1] + later[1])


def join_backward(earlier, later):
    return (earlier[0] * later[0], later[1] + later[0][:, None, None] * earlier[1])


def block_masks(decay_blk, docs_blk, prior_doc):
    cumulative = jnp.cumsum(decay_blk, axis=0)
    carried = docs_blk == prior_doc
    length = docs_blk.shape[0]
    lower = jnp.tril(jnp.ones((length, length), jnp.bool_))
    same_doc = (docs_blk[:, None] == docs_blk[None, :]) & lower
    cum_heads = cumulative.T
    log_gap = jnp.where(same_doc[None], cum_heads[:, :, None] - cum_heads[:, None, :], 0.0)
    weights = jnp.where(same_doc[None], jnp.exp(log_gap), 0.0)
    lead_weight = jnp.where(carried[:, None], jnp.exp(cumulative), 0.0)
    tail_weight = jnp.where(
        (docs_blk == docs_blk[-1])[:, None], jnp.exp(cumulative[-1][None, :] - cumulative), 0.0
    )
    keep_state = jnp.where(carried[-1], jnp.exp(cumulative[-1]), 0.0)
    return (weights, lead_weight, tail_weight, keep_state)


def forward_block(state_in, block_items):
    query_blk, key_blk, value_blk, decay_blk, docs_blk, prior_doc = block_items
    weights, lead_weight, tail_weight, keep_state = block_masks(decay_blk, docs_blk, prior_doc)
    value_exact = value_blk.astype(jnp.float32)
    scores = (
        jnp.einsum("thd,shd->hts", query_blk, key_blk, preferred_element_type=jnp.float32) * weights
    )
    intra_out = jnp.einsum("hts,she->the", scores, value_exact, precision=HIGHEST)
    inter_out = (
        jnp.einsum("thd,hde->the", query_blk.astype(jnp.float32), state_in, precision=HIGHEST)
        * lead_weight[:, :, None]
    )
    state_out = keep_state[:, None, None] * state_in + jnp.einsum(
        "thd,the->hde",
        key_blk.astype(jnp.float32) * tail_weight[:, :, None],
        value_exact,
        precision=HIGHEST,
    )
    return (state_out, ((intra_out + inter_out) / DH, state_in))


def backward_block(grad_state, block_items):
    query_blk, key_blk, value_blk, decay_blk, grad_blk, docs_blk, prior_doc, state_in = block_items
    weights, lead_weight, tail_weight, keep_state = block_masks(decay_blk, docs_blk, prior_doc)
    query_exact = query_blk.astype(jnp.float32)
    key_exact = key_blk.astype(jnp.float32)
    value_exact = value_blk.astype(jnp.float32)
    grad_exact = grad_blk.astype(jnp.float32)
    dot_grads = (
        jnp.einsum("the,she->hts", grad_blk, value_blk, preferred_element_type=jnp.float32)
        * weights
    )
    pair_scores = (
        jnp.einsum("thd,shd->hts", query_blk, key_blk, preferred_element_type=jnp.float32) * weights
    )
    grad_query = (
        jnp.einsum("hts,shd->thd", dot_grads, key_exact, precision=HIGHEST)
        + jnp.einsum("hde,the->thd", state_in, grad_exact, precision=HIGHEST)
        * lead_weight[:, :, None]
    ) / DH
    grad_key = (
        jnp.einsum("hts,thd->shd", dot_grads, query_exact, precision=HIGHEST) / DH
        + jnp.einsum("hde,she->shd", grad_state, value_exact, precision=HIGHEST)
        * tail_weight[:, :, None]
    )
    grad_value = (
        jnp.einsum("hts,the->she", pair_scores, grad_exact, precision=HIGHEST) / DH
        + jnp.einsum("hde,shd->she", grad_state, key_exact, precision=HIGHEST)
        * tail_weight[:, :, None]
    )
    grad_prev = (
        jnp.einsum(
            "thd,the->hde", query_exact * lead_weight[:, :, None], grad_exact, precision=HIGHEST
        )
        / DH
        + keep_state[:, None, None] * grad_state
    )
    return (grad_prev, jnp.stack([grad_query, grad_key, grad_value]).astype(jnp.bfloat16))


def local(tokens, w_qkv, forget, out_grad, doc_lengths):
    row_count = tokens.shape[0]
    col_width = w_qkv.shape[2]
    head_count = col_width // DH
    block_count = row_count // BLOCK
    offset = lax.axis_index("seq") * row_count
    positions = offset + jnp.arange(row_count, dtype=jnp.int32)
    doc_ids = document_ids(doc_lengths, positions)
    prior_dev = jnp.where(
        offset > 0, document_ids(doc_lengths, jnp.reshape(offset - 1, (1,)))[0], -1
    )
    gathered = lax.all_gather(tokens, "tp", axis=1, tiled=True)
    projected = jnp.einsum("td,mdc->mtc", gathered, w_qkv, preferred_element_type=jnp.float32)
    projections = projected.astype(jnp.bfloat16)
    query_rows = projections[0].reshape(row_count, head_count, DH)
    key_rows = projections[1].reshape(row_count, head_count, DH)
    value_rows = projections[2].reshape(row_count, head_count, DH)
    grad_rows = out_grad.reshape(row_count, head_count, DH)
    device_decay = jnp.cumsum(forget, axis=0)
    device_carried = doc_ids == prior_dev
    device_lead = jnp.where(device_carried[:, None], jnp.exp(device_decay), 0.0)
    device_tail = jnp.where(
        (doc_ids == doc_ids[-1])[:, None], jnp.exp(device_decay[-1][None, :] - device_decay), 0.0
    )
    through = jnp.where(device_carried[-1], jnp.exp(device_decay[-1]), 0.0)
    own_state = jnp.einsum(
        "thd,the->hde",
        key_rows.astype(jnp.float32) * device_tail[:, :, None],
        value_rows.astype(jnp.float32),
        precision=HIGHEST,
    )
    grad_own = (
        jnp.einsum(
            "thd,the->hde",
            query_rows.astype(jnp.float32) * device_lead[:, :, None],
            grad_rows.astype(jnp.float32),
            precision=HIGHEST,
        )
        / DH
    )
    identity = (jnp.ones((head_count,), jnp.float32), jnp.zeros((head_count, DH, DH), jnp.float32))

    def blocked(matrix):
        return matrix.reshape((block_count, BLOCK) + matrix.shape[1:])

    docs_blocks = blocked(doc_ids)
    prior_blocks = jnp.concatenate([jnp.reshape(prior_dev, (1,)), docs_blocks[:-1, -1]])
    state_start = entering((through, own_state), "seq", join_forward, identity, False)[1]
    outputs, states_in = lax.scan(
        forward_block,
        state_start,
        (
            blocked(query_rows),
            blocked(key_rows),
            blocked(value_rows),
            blocked(forget),
            docs_blocks,
            prior_blocks,
        ),
    )[1]
    grad_end = entering((through, grad_own), "seq", join_backward, identity, True)[1]
    attn_out = outputs.reshape(row_count, col_width).astype(jnp.float32)
    grad_blocks = lax.scan(
        backward_block,
        grad_end,
        (
            blocked(query_rows),
            blocked(key_rows),
            blocked(value_rows),
            blocked(forget),
            blocked(grad_rows),
            docs_blocks,
            prior_blocks,
            states_in,
        ),
        reverse=True,
    )[1]
    grad_stack = grad_blocks.transpose(1, 0, 2, 3, 4).reshape(3, row_count, col_width)
    grad_terms = jnp.einsum("mtc,mdc->td", grad_stack, w_qkv, preferred_element_type=jnp.float32)
    input_grad = lax.psum_scatter(grad_terms, "tp", scatter_dimension=1, tiled=True)
    return (attn_out, input_grad)


def solution(mesh):
    placed = (P("seq", "tp"), P(None, None, "tp"), P("seq", "tp"), P("seq", "tp"), P())
    return jax.shard_map(
        local,
        mesh=mesh,
        in_specs=placed,
        out_specs=(P("seq", "tp"), P("seq", "tp")),
        check_vma=False,
    )
```

profile of v0, /device:TPU:0, one launch (start us, length us, event | category | flops | bytes accessed | tf_op | source)
XLA Modules:
  0.0 275.4 jit_solution(8305470277707579623)
XLA Ops:
  7.2 0.7 all-gather.7.cloned.1.call-update
  7.9 1.3 reduce-window.20
  9.2 0.2 slice_reduce_fusion
  9.4 0.7 copy.94
  10.2 0.6 convert_reduce_fusion.1
  10.8 0.1 convert_reduce_fusion
  10.9 0.6 slice.50
  12.1 0.7 broadcast_compare_fusion
  12.8 0.6 slice.48
  13.4 0.1 exponential_select_fusion.1
  13.5 0.8 slice_reduce_fusion.1
  14.4 20.5 %all-gather.7.cloned.1.call-done = bf16[256,4096]{1,0:T(8,128)(2,1)} async-done(((bf16[256,1024]{1,0:T(8,128)(2,1)}), bf16[256,4096]{1,0:T(8,128)(2,1)}) %all-gather.7.cloned.1.call-update) | async-done | bytes 2097168 | tf_op jit(solution)/shard_map/all_gather | solution.py:130
  34.9 12.3 %fusion.11 = bf16[3,256,1024]{1,2,0:T(8,128)(2,1)S(1)} fusion(bf16[3,4096,1024]{2,1,0:T(8,128)(2,1)} %param.10, bf16[256,4096]{1,0:T(8,128)(2,1)} %all-gather.7.cloned.1.call-done), kind=kOutput, calls=%fused_computation.16 | convolution fusion | flops 6443237376 | bytes 28835840 | tf_op jit(solution)/shard_map/td,mdc->mtc/dot_general | solution.py:131
  47.2 0.1 fusion.38
  47.3 1.5 fusion.31
  48.9 0.2 copy.122
  49.1 1.5 convolution_multiply_fusion.2
  50.7 20.6 %all-gather.2 = f32[8,1,8]{2,1,0:T(1,128)S(1)} all-gather(f32[1,1,8]{2,1,0:T(1,128)S(1)} %bitcast.143), channel_id=1, replica_groups=mesh['seq'=8,'tp'=4] {'seq'}, dimensions={0}, use_global_device_ids=true | all-gather | bytes 288 | tf_op jit(solution)/shard_map/all_gather | solution.py:17
  71.3 0.1 fusion.36
  71.4 0.7 fusion.2
  72.2 0.7 bitcast_multiply_fusion
  72.9 1.9 fusion.25
  74.7 2.3 convolution_bitcast_fusion.1
  77.0 1.9 fusion.24
  78.9 43.5 %all-gather.9.cloned.1.call-done = f32[64,128,128]{2,1,0:T(8,128)} async-done(((f32[8,128,128]{2,1,0:T(8,128)}), f32[64,128,128]{2,1,0:T(8,128)}) %all-gather.9.cloned.1.call-update) | async-done | bytes 4194320 | tf_op jit(solution)/shard_map/all_gather | solution.py:17
  122.5 73.8 %all-gather.11.cloned.1.call-done = f32[64,128,128]{2,1,0:T(8,128)} async-done(((f32[8,128,128]{2,1,0:T(8,128)}), f32[64,128,128]{2,1,0:T(8,128)}) %all-gather.11.cloned.1.call-update) | async-done | bytes 4194320 | tf_op jit(solution)/shard_map/all_gather | solution.py:17
  196.3 8.8 %while.17 = (s32[]{:T(128)}, f32[8,128,128]{2,1,0:T(8,128)S(1)}, s32[]{:T(128)}, f32[8,8,128,128]{3,2,1,0:T(8,128)}, f32[8,8]{1,0:T(8,128)S(1)}, /*index=5*/s32[]{:T(128)}, s32[]{:T(128)}, s32[]{:T(128)}, s32[]{:T(128)}) while((s32[]{:T(128)}, f32[8,128,128]{2,1,0:T(8,128)S(1)}, s32[]{:T(128)}, f32[8,8,128,128]{3,2,1,0:T(8,128)}, ...), condition=%wide.region_8.9_spmd, body=%wide.region_7.8_spmd.sunk | while | flops 262150 | bytes 1573115 | solution.py:26
  196.3 1.2 bitcast_add_fusion.5
  197.6 1.2 bitcast_add_fusion.5
  198.8 1.2 bitcast_add_fusion.5
  200.0 1.2 bitcast_add_fusion.5
  201.3 1.2 bitcast_add_fusion.5
  202.5 1.2 bitcast_add_fusion.5
  203.7 1.2 bitcast_add_fusion.5
  205.1 1.9 fusion.27
  207.0 1.0 copy.109
  208.0 2.7 fusion.26
  210.7 2.0 copy.108
  212.7 0.6 fusion.28
  213.3 0.2 copy.107
  213.5 0.2 copy-done.8
  213.8 13.1 %convolution_bitcast_fusion = f32[256,4096]{1,0:T(8,128)} fusion(bf16[3,4096,1024]{2,1,0:T(8,128)(2,1)} %param.10, bf16[1,256,1024]{2,1,0:T(8,128)(2,1)S(1)} %copy-done.8, bf16[1,256,1024]{2,1,0:T(8,128)(2,1)} %copy.108, bf16[1,256,1024]{2,1,0:T(8,128)(2,1)S(1)} %copy.107), kind=kOutput, calls=%fused_computation.4 | convolution fusion | flops 6444023808 | bytes 30932992 | tf_op jit(solution)/shard_map/mtc,mdc->td/dot_general | solution.py:197
  226.9 1.6 copy-done.1
  228.5 0.1 copy-done.3
  228.6 1.3 convolution_bitcast_fusion.2
  229.9 0.7 fusion.23
  230.6 1.3 copy.110
  231.9 36.9 %reduce-scatter.2.cloned.1.call-done = f32[256,1024]{1,0:T(8,128)} async-done(((f32[256,4096]{1,0:T(8,128)}), f32[256,1024]{1,0:T(8,128)}) %reduce-scatter.2.cloned.1.call-update) | async-done | bytes 1048592 | tf_op jit(solution)/shard_map/reduce_scatter | solution.py:198
  (38 shorter events, 0.6 us)
Async XLA Ops:
  7.2 27.7 %all-gather.7.cloned.1.call-start = ((), (), s32[]{:S(2)}) async-start(), calls=%async_computation.1 | async-start | bytes 2621440 | tf_op jit(solution)/shard_map/all_gather | solution.py:130
  7.9 114.5 %all-gather.9.cloned.1.call-start = ((), (), s32[]{:S(2)}) async-start(), calls=%async_computation.3 | async-start | bytes 4718592 | tf_op jit(solution)/shard_map/all_gather | solution.py:17
  47.2 1.7 copy-start.7
  47.3 25.6 %copy-start.4 = (bf16[1,256,1024]{1,2,0:T(8,128)(2,1)}, bf16[1,256,1024]{1,2,0:T(8,128)(2,1)S(1)}, u32[]{:S(2)}) copy-start(bf16[1,256,1024]{1,2,0:T(8,128)(2,1)S(1)} %get-tuple-element.232) | copy-start | bytes 1572868
  47.3 160.7 %copy-start.2 = (bf16[1,256,1024]{1,2,0:T(8,128)(2,1)}, bf16[1,256,1024]{1,2,0:T(8,128)(2,1)S(1)}, u32[]{:S(2)}) copy-start(bf16[1,256,1024]{1,2,0:T(8,128)(2,1)S(1)} %get-tuple-element.233) | copy-start | bytes 1572868
  48.8 147.4 %all-gather.11.cloned.1.call-start = ((), (), s32[]{:S(2)}) async-start(), calls=%async_computation.4 | async-start | bytes 4718592 | tf_op jit(solution)/shard_map/all_gather | solution.py:17
  50.6 218.2 %reduce-scatter.2.cloned.1.call-start = ((), (), s32[]{:S(2)}) async-start(), calls=%async_computation.2 | async-start | bytes 5242880 | tf_op jit(solution)/shard_map/reduce_scatter | solution.py:198
  72.1 4.9 %copy-start = (f32[8,256,256]{2,1,0:T(8,128)}, f32[8,256,256]{2,1,0:T(8,128)S(1)}, u32[]{:S(2)}) copy-start(f32[8,256,256]{2,1,0:T(8,128)S(1)} %fusion.2) | copy-start | bytes 6291460
  208.0 4.7 %copy-start.6 = (f32[256,8,128]{0,2,1:T(8,128)S(1)}, f32[256,8,128]{0,2,1:T(8,128)}, u32[]{:S(2)}) copy-start(f32[256,8,128]{0,2,1:T(8,128)} %convolution_bitcast_fusion.1) | copy-start | bytes 3145732
  212.7 1.0 copy-start.8
  226.9 1.6 copy-start.1
  226.9 1.7 copy-start.3
  228.6 1.3 copy-start.5
Sparse Core Ops, SparseCore 0:
  9.6 25.2 all-gather.6
  49.0 73.4 all-gather.8
  124.5 71.6 all-gather.10
  227.0 41.7 reduce-scatter.1
where the time goes:
time: 276 us; the launch traced here: 275 us
  waiting for transfers between devices  175 us (63%)
  matrix products  43 us (16%)
  blocking collectives  20.6 us (7%)
  between operations  14.6 us (5%)
  other arithmetic  12.2 us (4%)
  local copies, waits for them, and re-layouts  8.94 us (3%)
    all_gather x2, waiting for transfers between devices, entering(): gathered = jax.tree.map(lambda a: lax.all_gather(a, axis), part)  117 us
    reduce_scatter x1, waiting for transfers between devices, local(): lax.psum_scatter(grad_terms, 'tp', scatter_dimension=1, tiled=True)  36.9 us
    all_gather x1, blocking collectives, entering(): gathered = jax.tree.map(lambda a: lax.all_gather(a, axis), part)  20.6 us
    all_gather x1, waiting for transfers between devices, local(): gathered = lax.all_gather(tokens, 'tp', axis=1, tiled=True)  20.5 us
    dot_general x1, matrix products, local(): jnp.einsum('mtc,mdc->td', grad_stack, w_qkv, preferred_element_type=jnp.f...  13.1 us
    dot_general x1, matrix products, local(): jnp.einsum('td,mdc->mtc', gathered, w_qkv, preferred_element_type=jnp.flo...  12.3 us
    add x7, other arithmetic, join_backward(): later[1] + later[0][:, None, None] * earlier[1]  8.33 us
  transfers between devices with their start and end apart: 4, of which 4 were waited for; matrix products, arithmetic and copies ran while one was open for 7% of the time, Pallas kernels for 0%

commit v1 on v0

v1 whole, which is shorter than its diff:
```python
import functools

import jax
import jax.numpy as jnp
from jax import lax
from jax.experimental import pallas as pl
from jax.experimental.pallas import tpu as pltpu
from jax.sharding import PartitionSpec as P

DH = 128
F32 = jnp.float32
BF16 = jnp.bfloat16
MIB = 1 << 20


def dot(a, b, ca, cb):
    return lax.dot_general(a, b, (((ca,), (cb,)), ((), ())), preferred_element_type=F32)


def split(a):
    high = a.astype(BF16)
    return high, (a - high.astype(F32)).astype(BF16)


def dot_split(a, b, ca, cb):
    high, low = split(a)
    return dot(high, b, ca, cb) + dot(low, b, ca, cb)


def call(kernel, name, outs, args, spaces=None, flops=0, nbytes=0, limit=16, scratch=()):
    spaces = spaces or ["v"] * len(args)
    kinds = {"v": pltpu.VMEM, "s": pltpu.SMEM, "a": pl.ANY}
    placed = [
        pltpu.with_memory_space_constraint(a, pltpu.VMEM) if s == "v" else a
        for a, s in zip(args, spaces)
    ]
    return pl.pallas_call(
        kernel,
        name=name,
        out_shape=[pltpu.VMEM(shape, dtype) for shape, dtype in outs],
        in_specs=[pl.BlockSpec(memory_space=kinds[s]) for s in spaces],
        out_specs=[pl.BlockSpec(memory_space=pltpu.VMEM)] * len(outs),
        scratch_shapes=scratch,
        compiler_params=pltpu.CompilerParams(vmem_limit_bytes=limit * MIB),
        cost_estimate=pl.CostEstimate(flops=flops, bytes_accessed=nbytes, transcendentals=0),
    )(*placed)


def tile_of(width):
    return 256 if width % 256 == 0 else 128


def load_and_project(starts, own, other, w, w_vm, acc, sems):
    part, count = own.shape[1], w.shape[1] // own.shape[1]
    width = w.shape[2]
    tile = tile_of(width)
    copies = []
    for j in range(count):
        rows = pl.ds(pl.multiple_of(starts[j] * part, part), part)
        copies.append(pltpu.make_async_copy(w.at[:, rows, :], w_vm.at[:, rows, :], sems.at[j]))
        copies[-1].start()
    for j, x in enumerate((own, other)):
        copies[j].wait()
        rows = pl.ds(pl.multiple_of(starts[j] * part, part), part)

        @pl.loop(0, 3 * (width // tile))
        def _(n):
            m, cols = n // (width // tile), pl.ds(pl.multiple_of(n % (width // tile) * tile, tile), tile)
            term = dot(x[...], w_vm[m, rows, cols], 1, 0)
            if j:
                acc[m, :, cols] += term
            else:
                acc[m, :, cols] = term

    for j in range(2, count):
        copies[j].wait()


def project_more(starts, x, w_vm, acc_in, acc):
    part, width = x.shape[1], w_vm.shape[2]
    tile = tile_of(width)
    rows = pl.ds(pl.multiple_of(starts[2] * part, part), part)

    @pl.loop(0, 3 * (width // tile))
    def _(n):
        m, cols = n // (width // tile), pl.ds(pl.multiple_of(n % (width // tile) * tile, tile), tile)
        acc[m, :, cols] = acc_in[m, :, cols] + dot(x[...], w_vm[m, rows, cols], 1, 0)


def project_last(starts, x, w_vm, acc_in, grads, cols_h, qkv, states):
    part, width = x.shape[1], w_vm.shape[2]
    tile = tile_of(width)
    rows = pl.ds(pl.multiple_of(starts[3] * part, part), part)

    @pl.loop(0, 3 * (width // tile))
    def _(n):
        m, cols = n // (width // tile), pl.ds(pl.multiple_of(n % (width // tile) * tile, tile), tile)
        qkv[m, :, cols] = (acc_in[m, :, cols] + dot(x[...], w_vm[m, rows, cols], 1, 0)).astype(BF16)

    own_states(qkv, grads, cols_h, states)


def own_states(qkv, grads, cols_h, states):
    @pl.loop(0, states.shape[1])
    def _(h):
        cols = pl.ds(pl.multiple_of(h * DH, DH), DH)
        col = cols_h[h]
        lead, tail = col[:, 1:2], col[:, 2:3]
        states[0, h] = dot_split(qkv[1, :, cols].astype(F32) * tail, qkv[2, :, cols], 0, 0)
        states[1, h] = dot_split(qkv[0, :, cols].astype(F32) * lead, grads[:, cols], 0, 0) * (1.0 / DH)


def project_whole(x, w, qkv):
    qkv[0] = dot(x[...], w[0], 1, 0).astype(BF16)


def intra(qkv, grads, cols_h, rows_h, first, out, gq, gk, gv):
    length = first.shape[0]
    t = lax.broadcasted_iota(jnp.int32, (length, length), 0)
    s = lax.broadcasted_iota(jnp.int32, (length, length), 1)
    mask = (s <= t) & (s >= first[...])

    @pl.loop(0, cols_h.shape[0])
    def _(h):
        cols = pl.ds(pl.multiple_of(h * DH, DH), DH)
        gap = jnp.where(mask, cols_h[h][:, 0:1] - rows_h[h], 0.0)
        weight = jnp.where(mask, jnp.exp(gap), 0.0)
        q, k, v, g = qkv[0, :, cols], qkv[1, :, cols], qkv[2, :, cols], grads[:, cols]
        scores = split(dot(q, k, 1, 1) * weight)
        dots = split(dot(g, v, 1, 1) * weight)
        out[:, cols] = dot(scores[0], v, 1, 0) + dot(scores[1], v, 1, 0)
        gq[:, cols] = dot(dots[0], k, 1, 0) + dot(dots[1], k, 1, 0)
        gk[:, cols] = dot(dots[0], q, 0, 0) + dot(dots[1], q, 0, 0)
        gv[:, cols] = dot(scores[0], g, 0, 0) + dot(scores[1], g, 0, 0)


def finish(qkv, grads, cols_h, out, gq, gk, gv, states, ends, attn, gstack):
    @pl.loop(0, cols_h.shape[0])
    def _(h):
        cols = pl.ds(pl.multiple_of(h * DH, DH), DH)
        col = cols_h[h]
        lead, tail = col[:, 1:2], col[:, 2:3]
        q, k, v, g = qkv[0, :, cols], qkv[1, :, cols], qkv[2, :, cols], grads[:, cols]
        state, end = states[h], ends[h]
        attn[:, cols] = (out[:, cols] + dot(q, state, 1, 0) * lead) * (1.0 / DH)
        gstack[0, :, cols] = ((gq[:, cols] + dot(g, state, 1, 1) * lead) * (1.0 / DH)).astype(BF16)
        gstack[1, :, cols] = (gk[:, cols] * (1.0 / DH) + dot(v, end, 1, 1) * tail).astype(BF16)
        gstack[2, :, cols] = (gv[:, cols] * (1.0 / DH) + dot(k, end, 1, 0) * tail).astype(BF16)


def back(starts, which, gstack, w_vm, out):
    part = out.shape[1]
    base = starts[which] * part
    tile = tile_of(part)

    @pl.loop(0, part // tile)
    def _(n):
        rows = pl.ds(pl.multiple_of(base + n * tile, tile), tile)
        total = dot(gstack[0], w_vm[0, rows, :], 1, 1)
        total += dot(gstack[1], w_vm[1, rows, :], 1, 1)
        total += dot(gstack[2], w_vm[2, rows, :], 1, 1)
        out[:, pl.ds(pl.multiple_of(n * tile, tile), tile)] = total.astype(out.dtype)


def back_first(starts, qkv, grads, cols_h, out, gq, gk, gv, states, ends, w_vm, attn, gstack, chunk):
    finish(qkv, grads, cols_h, out, gq, gk, gv, states, ends, attn, gstack)
    back(starts, 3, gstack, w_vm, chunk)


def back_second(starts, gstack, w_vm, chunk):
    back(starts, 2, gstack, w_vm, chunk)


def back_rest(starts, gstack, w_vm, chunk_other, chunk_own):
    back(starts, 1, gstack, w_vm, chunk_other)
    back(starts, 0, gstack, w_vm, chunk_own)


def per_head(scale, matrix):
    return scale[..., None, None] * matrix


def states_direct(own, through):
    heads = own.shape[1]
    half = heads // 2
    place = lax.axis_index("seq")
    x, z = place % 2, place // 2
    upper = x == 1
    mate = [(i, i ^ 1) for i in range(8)]
    near = [(i, i ^ 2) for i in range(8)]
    middle = [(2, 4), (4, 2), (3, 5), (5, 3)]
    far = [(i, i ^ 4) for i in range(8)]

    def shift(a, pairs):
        return lax.ppermute(a, "seq", pairs)

    mine = lax.dynamic_slice_in_dim(own, x * half, half, 1)
    theirs = lax.dynamic_slice_in_dim(own, (1 - x) * half, half, 1)
    mate_through = shift(through, mate)
    pair_through = through * mate_through
    near_through = shift(pair_through, near)
    middle_through = shift(pair_through, middle)
    next_through = jnp.where((z == 0) | (z == 3), near_through, middle_through)
    low_through = lax.dynamic_slice_in_dim(jnp.where(upper, mate_through, through), x * half, half, 0)
    high_through = lax.dynamic_slice_in_dim(jnp.where(upper, through, mate_through), x * half, half, 0)
    next_through = lax.dynamic_slice_in_dim(next_through, x * half, half, 0)

    got = shift(theirs.astype(BF16), mate).astype(F32)
    low, high = jnp.where(upper, got, mine), jnp.where(upper, mine, got)
    pair_state = high[0] + per_head(high_through, low[0])
    pair_grad = low[1] + per_head(low_through, high[1])
    to_near = jnp.where(z % 2 == 0, pair_state, pair_grad).astype(BF16)
    to_middle = jnp.where(z == 1, pair_state, pair_grad).astype(BF16)
    to_far = jnp.where(z < 2, pair_state, pair_grad).astype(BF16)
    from_near = shift(to_near, near).astype(F32)
    from_middle = shift(to_middle, middle).astype(F32)
    from_far = shift(to_far, far).astype(F32)
    from_far = per_head(next_through, from_far)
    zero = jnp.zeros_like(from_near)
    inner_far = from_middle + from_far
    state = jnp.where(z == 0, zero, jnp.where(z == 1, from_near, jnp.where(z == 2, inner_far, from_near + from_far)))
    grad = jnp.where(z == 3, zero, jnp.where(z == 2, from_near, jnp.where(z == 1, inner_far, from_near + from_far)))
    low_pair = jnp.stack([state, high[1] + per_head(high_through, grad)]).astype(BF16)
    high_pair = jnp.stack([low[0] + per_head(low_through, state), grad]).astype(BF16)
    kept = jnp.where(upper, high_pair, low_pair)
    passed = shift(jnp.where(upper, low_pair, high_pair), mate)
    both = jnp.where(
        upper, jnp.concatenate([passed, kept], axis=1), jnp.concatenate([kept, passed], axis=1)
    )
    return both[0], both[1]


def states_gathered(own, through):
    count = lax.axis_size("seq")
    place = lax.axis_index("seq")
    all_own = lax.all_gather(own, "seq")
    all_through = lax.all_gather(through, "seq")

    def pick(a, i):
        return lax.dynamic_index_in_dim(a, i, 0, False)

    def ahead(step, state):
        return per_head(pick(all_through, step), state) + pick(all_own, step)[0]

    def behind(step, state):
        source = count - 1 - step
        return per_head(pick(all_through, source), state) + pick(all_own, source)[1]

    zero = jnp.zeros_like(own[0])
    state = lax.fori_loop(0, place, ahead, zero)
    grad = lax.fori_loop(0, count - 1 - place, behind, zero)
    return state.astype(BF16), grad.astype(BF16)


def local(tokens, w_qkv, forget, out_grad, doc_lengths):
    length, part = tokens.shape
    width = w_qkv.shape[2]
    heads = width // DH
    depth = w_qkv.shape[1]
    tps = lax.axis_size("tp")
    tp = lax.axis_index("tp")
    seqs = lax.axis_size("seq")
    offset = lax.axis_index("seq") * length
    by_hand = tps == 4

    positions = offset + jnp.arange(length, dtype=jnp.int32)
    doc_ends = jnp.cumsum(doc_lengths)
    past = positions[:, None] >= doc_ends[None, :]
    first = jnp.max(jnp.where(past, doc_ends[None, :], 0), axis=1) - offset
    carried = first < 0
    total = jnp.cumsum(forget, axis=0)
    lead = jnp.where(carried[:, None], jnp.exp(total), 0.0)
    tail = jnp.where((first == first[-1])[:, None], jnp.exp(total[-1][None, :] - total), 0.0)
    through = jnp.where(carried[-1], jnp.exp(total[-1]), 0.0)
    cols_h = jnp.stack([total.T, lead.T, tail.T], axis=-1)
    rows_h = total.T[:, None, :]
    first = first[:, None]

    qkv_shape = ((3, length, width), BF16)
    states_shape = ((2, heads, DH, DH), F32)
    if by_hand:
        starts = jnp.stack([tp, tp ^ 1, tp ^ 2, tp ^ 3]).astype(jnp.int32)
        core = [(i, i ^ 1) for i in range(4)]
        chip = [(i, i ^ 2) for i in range(4)]
        step_flops = 2 * 3 * length * part * width
        across = lax.ppermute(tokens, "tp", chip)
        beside = lax.ppermute(tokens, "tp", core)
        across_beside = lax.ppermute(across, "tp", core)
        w_vm, acc = call(
            load_and_project,
            "load_and_project",
            [(w_qkv.shape, BF16), ((3, length, width), F32)],
            [starts, tokens, beside, w_qkv],
            ["s", "v", "v", "a"],
            flops=2 * step_flops,
            nbytes=w_qkv.size * 2,
            scratch=[pltpu.SemaphoreType.DMA((4,))],
        )
        (acc,) = call(
            project_more, "project_more", [(acc.shape, F32)], [starts, across, w_vm, acc],
            ["s", "v", "v", "v"], flops=step_flops,
        )
        qkv, own = call(
            project_last,
            "project_last",
            [qkv_shape, states_shape],
            [starts, across_beside, w_vm, acc, out_grad, cols_h],
            ["s", "v", "v", "v", "v", "v"],
            flops=step_flops,
        )
    else:
        gathered = lax.all_gather(tokens, "tp", axis=1, tiled=True)
        qkv = jnp.einsum("td,mdc->mtc", gathered, w_qkv, preferred_element_type=F32).astype(BF16)
        (own,) = call(own_states, "own_states", [states_shape], [qkv, out_grad, cols_h])

    out, gq, gk, gv = call(
        intra,
        "intra",
        [((length, width), F32)] * 4,
        [qkv, out_grad, cols_h, rows_h, first],
        flops=16 * length * length * width,
    )
    states, ends = states_direct(own, through) if seqs == 8 and heads % 2 == 0 else states_gathered(own, through)

    attn_shape = ((length, width), F32)
    finish_args = [qkv, out_grad, cols_h, out, gq, gk, gv, states, ends]
    if by_hand:
        attn, gstack, chunk = call(
            back_first,
            "back_first",
            [attn_shape, qkv_shape, ((length, part), BF16)],
            [starts] + finish_args + [w_vm],
            ["s"] + ["v"] * 10,
            flops=step_flops,
        )
        beside = lax.ppermute(chunk, "tp", core)
        (chunk,) = call(
            back_second, "back_second", [((length, part), F32)], [starts, gstack, w_vm], ["s", "v", "v"], flops=step_flops
        )
        across = lax.ppermute((chunk + beside.astype(F32)).astype(BF16), "tp", chip)
        chunk_other, chunk_own = call(
            back_rest,
            "back_rest",
            [((length, part), BF16), ((length, part), F32)],
            [starts, gstack, w_vm],
            ["s", "v", "v"],
            flops=2 * step_flops,
        )
        beside = lax.ppermute(chunk_other, "tp", core)
        input_grad = chunk_own + beside.astype(F32) + across.astype(F32)
    else:
        attn, gstack = call(finish, "finish", [attn_shape, qkv_shape], finish_args)
        grad_terms = jnp.einsum("mtc,mdc->td", gstack, w_qkv, preferred_element_type=F32)
        input_grad = lax.psum_scatter(grad_terms, "tp", scatter_dimension=1, tiled=True)
    return (attn, input_grad)


def solution(mesh):
    placed = (P("seq", "tp"), P(None, None, "tp"), P("seq", "tp"), P("seq", "tp"), P())
    return jax.shard_map(
        local,
        mesh=mesh,
        in_specs=placed,
        out_specs=(P("seq", "tp"), P("seq", "tp")),
        check_vma=False,
    )
```

time: 276 us -> 135 us (0.49)
  waiting for transfers between devices: 175 us -> 33.1 us
  matrix products: 43 us -> 0 us
  Pallas kernels: 0 us -> 40.8 us
  local copies, waits for them, and re-layouts: 8.94 us -> 31.3 us
  blocking collectives: 20.6 us -> 0 us
  starting transfers between devices: 0.16 us -> 19.8 us
  between operations: 14.6 us -> 0.89 us
  other arithmetic: 12.2 us -> 8.36 us
    all_gather x3 -> x0, waiting for transfers between devices: 138 us -> none  [the longest x2 117 us: entering(): gathered = jax.tree.map(lambda a: lax.all_gather(a, axis), part)]
    dot_general x14 -> x0, matrix products: 43 us -> none  [the longest x1 13.1 us: local(): jnp.einsum('mtc,mdc->td', grad_stack, w_qkv, preferred_element_type=jnp.f...]
    pallas_call x0 -> x7, Pallas kernels: none -> 40.8 us  [call(): pl.pallas_call(kernel, name=name, out_shape=[pltpu.VMEM(shape, dtype) for...]
    reduce_scatter x1 -> x0, waiting for transfers between devices: 36.9 us -> none  [local(): lax.psum_scatter(grad_terms, 'tp', scatter_dimension=1, tiled=True)]
    ppermute x0 -> x14, waiting for transfers between devices: none -> 33.1 us  [the longest x8 14.6 us: shift(): return lax.ppermute(a, 'seq', pairs)]
    unnamed x19 -> x17, local copies, waits for them, and re-layouts: 3.2 us -> 27.6 us
    all_gather x1 -> x0, blocking collectives: 20.6 us -> none  [entering(): gathered = jax.tree.map(lambda a: lax.all_gather(a, axis), part)]
    ppermute x0 -> x14, starting transfers between devices: none -> 19.8 us  [the longest x8 14.5 us: shift(): return lax.ppermute(a, 'seq', pairs)]
  transfers between devices with their start and end apart: 4 -> 14, of which waited for: 4 -> 5; matrix products, arithmetic and copies ran while one was open for 7% -> 7% of each run, Pallas kernels for 0% -> 21%
where the time goes in v1:
time: 135 us; the launch traced here: 134 us
  Pallas kernels  40.8 us (30%)
  waiting for transfers between devices  33.1 us (25%)
  local copies, waits for them, and re-layouts  31.3 us (23%)
  starting transfers between devices  19.8 us (15%)
  other arithmetic  8.36 us (6%)
    pallas_call x7, Pallas kernels, call(): pl.pallas_call(kernel, name=name, out_shape=[pltpu.VMEM(shape, dtype) for...  40.8 us
    unnamed x17, local copies, waits for them, and re-layouts  27.6 us
    ppermute x8, waiting for transfers between devices, shift(): return lax.ppermute(a, 'seq', pairs)  14.6 us
    ppermute x8, starting transfers between devices, shift(): return lax.ppermute(a, 'seq', pairs)  14.5 us
    ppermute x1, waiting for transfers between devices, local(): across = lax.ppermute((chunk + beside.astype(F32)).astype(BF16), 'tp', chip)  11.3 us
    ppermute x1, waiting for transfers between devices, local(): across = lax.ppermute(tokens, 'tp', chip)  7.12 us
    ppermute x1, starting transfers between devices, local(): across = lax.ppermute(tokens, 'tp', chip)  3.03 us
  transfers between devices with their start and end apart: 14, of which 5 were waited for; matrix products, arithmetic and copies ran while one was open for 7% of the time, Pallas kernels for 21%

profile of v1, /device:TPU:0, one launch (start us, length us, event | category | flops | bytes accessed | tf_op | source)
XLA Modules:
  0.0 134.3 jit_solution(10664578680079915343)
XLA Ops:
  0.6 3.0 %collective-permute-start = (bf16[256,1024]{1,0:T(8,128)(2,1)}, bf16[256,1024]{1,0:T(8,128)(2,1)S(1)}, u32[]{:S(2)}, u32[]{:S(2)}) collective-permute-start(bf16[256,1024]{1,0:T(8,128)(2,1)} %own.1), channel_id=1, source_target_pairs={{0,2},{1,3},{2,0},{3,1},{4,6},{5,7},{6,4},{7,5},{8,10},{9,11},{10,... | collective-permute-start | bytes 1572872 | tf_op jit(solution)/shard_map/ppermute | solution.py:286
  3.7 1.2 reduce-window.18
  4.9 0.2 slice_reduce_fusion
  5.1 0.7 copy.28
  5.9 0.1 reduce.1
  6.1 0.6 slice.38
  6.8 0.7 broadcast_compare_fusion
  7.4 0.6 slice.41
  8.0 0.2 slice_reduce_fusion.1
  8.3 0.4 copy.29.cols_h
  8.7 7.1 %collective-permute-done.x = bf16[256,1024]{1,0:T(8,128)(2,1)S(1)} collective-permute-done((bf16[256,1024]{1,0:T(8,128)(2,1)}, bf16[256,1024]{1,0:T(8,128)(2,1)S(1)}, u32[]{:S(2)}, u32[]{:S(2)}) %collective-permute-start) | collective-permute-done | bytes 524320 | tf_op jit(solution)/shard_map/ppermute | solution.py:286
  15.9 1.0 copy-done.5
  16.9 11.0 %load_and_project.1 = (bf16[3,4096,1024]{2,1,0:T(8,128)(2,1)S(1)}, f32[3,256,1024]{2,1,0:T(8,128)S(1)}) custom-call(s32[4]{0:T(128)S(1)} %pad_add_fusion.starts, bf16[256,1024]{1,0:T(8,128)(2,1)S(1)} %copy-done.5, bf16[256,1024]{1,0:T(8,128)(2,1)S(1)} %collective-permute-done.2.other, bf16[3,4096,1024]{2,1,0:T(8,128)(2,1)} %w.1), custom_call_target="tpu_custom_call" | custom-call | flops 3221225472 | bytes 25165824 | tf_op jit(solution)/shard_map/load_and_project/pallas_call | solution.py:37
  27.9 8.3 %copy-done = bf16[3,4096,1024]{2,1,0:T(8,128)(2,1)} copy-done((bf16[3,4096,1024]{2,1,0:T(8,128)(2,1)}, bf16[3,4096,1024]{2,1,0:T(8,128)(2,1)S(1)}, u32[]{:S(2)}) %copy-start) | copy-done | bytes 25165848
  36.2 8.2 %copy-done.1 = bf16[3,4096,1024]{2,1,0:T(8,128)(2,1)S(1)} copy-done((bf16[3,4096,1024]{2,1,0:T(8,128)(2,1)S(1)}, bf16[3,4096,1024]{2,1,0:T(8,128)(2,1)}, u32[]{:S(2)}) %copy-start.1) | copy-done | bytes 25165848
  44.4 4.4 %project_more.1.acc_in = f32[3,256,1024]{2,1,0:T(8,128)S(1)} custom-call(s32[4]{0:T(128)S(1)} %pad_add_fusion.starts, bf16[256,1024]{1,0:T(8,128)(2,1)S(1)} %collective-permute-done.x, bf16[3,4096,1024]{2,1,0:T(8,128)(2,1)S(1)} %copy-done.1, f32[3,256,1024]{2,1,0:T(8,128)S(1)} %get-tuple-element.16.acc_in), custom_call_target="tpu_custom_call" | custom-call | flops 1610612736 | tf_op jit(solution)/shard_map/project_more/pallas_call | solution.py:37
  48.8 7.3 %project_last.1 = (bf16[3,256,1024]{2,1,0:T(8,128)(2,1)S(1)}, f32[2,8,128,128]{3,2,1,0:T(8,128)S(1)}) custom-call(s32[4]{0:T(128)S(1)} %pad_add_fusion.starts, bf16[256,1024]{1,0:T(8,128)(2,1)S(1)} %collective-permute-done.1.x, bf16[3,4096,1024]{2,1,0:T(8,128)(2,1)S(1)} %copy-done.1, f32[3,256,1024]{2,1,0:T(8,128)S(1)} %project_more.1.acc_in, ...), custom_call_target="tpu_custom_call" | custom-call | flops 1610612736 | tf_op jit(solution)/shard_map/project_last/pallas_call | solution.py:37
  56.1 1.0 copy-done.4
  57.1 0.7 dynamic-slice_convert_fusion
  57.8 1.7 %collective-permute-start.3 = (bf16[2,4,128,128]{3,2,1,0:T(8,128)(2,1)}, bf16[2,4,128,128]{3,2,1,0:T(8,128)(2,1)S(1)}, u32[]{:S(2)}, u32[]{:S(2)}) collective-permute-start(bf16[2,4,128,128]{3,2,1,0:T(8,128)(2,1)} %dynamic-slice_convert_fusion), channel_id=1, source_target_pairs={{0,4},{4,0},{8,12},{12,8},{16,20},{20,16},{24,28},{28,24},{1,5},{5... | collective-permute-start | bytes 786440 | tf_op jit(solution)/shard_map/ppermute | solution.py:195
  59.5 0.6 broadcast_select_fusion.3
  60.1 0.4 collective-permute-start.4
  60.5 6.3 %collective-permute-done.4 = f32[8]{0:T(128)S(1)} collective-permute-done((f32[8]{0:T(128)S(1)}, f32[8]{0:T(128)S(1)}, u32[]{:S(2)}, u32[]{:S(2)}) %collective-permute-start.4) | collective-permute-done | bytes 64 | tf_op jit(solution)/shard_map/ppermute | solution.py:195
  66.8 0.6 fusion.9
  67.4 0.7 collective-permute-start.8
  68.1 4.7 %collective-permute-start.7 = (f32[8]{0:T(128)S(1)}, f32[8]{0:T(128)S(1)}, u32[]{:S(2)}, u32[]{:S(2)}) collective-permute-start(f32[8]{0:T(128)S(1)} %get-tuple-element.47), channel_id=1, source_target_pairs={{0,8},{4,12},{8,0},{12,4},{16,24},{20,28},{24,16},{28,20},{1,9},{5... | collective-permute-start | bytes 104 | tf_op jit(solution)/shard_map/ppermute | solution.py:195
  72.9 1.2 convert_select_fusion
  74.1 0.2 select_convert_fusion.2
  74.3 0.7 collective-permute-start.6
  75.0 4.8 %collective-permute-start.9 = (bf16[4,128,128]{2,1,0:T(8,128)(2,1)S(1)}, bf16[4,128,128]{2,1,0:T(8,128)(2,1)S(1)}, u32[]{:S(2)}, u32[]{:S(2)}) collective-permute-start(bf16[4,128,128]{2,1,0:T(8,128)(2,1)S(1)} %get-tuple-element.46), channel_id=1, source_target_pairs={{0,16},{4,20},{8,24},{12,28},{16,0},{20,4},{24,8},{28,12},{1,17},{... | collective-permute-start | bytes 393224 | tf_op jit(solution)/shard_map/ppermute | solution.py:195
  79.9 7.6 %collective-permute-done.9 = bf16[4,128,128]{2,1,0:T(8,128)(2,1)S(1)} collective-permute-done((bf16[4,128,128]{2,1,0:T(8,128)(2,1)S(1)}, bf16[4,128,128]{2,1,0:T(8,128)(2,1)S(1)}, u32[]{:S(2)}, u32[]{:S(2)}) %collective-permute-start.9) | collective-permute-done | bytes 131104 | tf_op jit(solution)/shard_map/ppermute | solution.py:195
  87.5 0.2 convert_bitcast_fusion.1
  87.7 0.8 broadcast_select_fusion.1
  88.5 1.5 %collective-permute-start.10 = (bf16[2,4,128,128]{3,2,1,0:T(8,128)(2,1)}, bf16[2,4,128,128]{3,2,1,0:T(8,128)(2,1)}, u32[]{:S(2)}, u32[]{:S(2)}) collective-permute-start(bf16[2,4,128,128]{3,2,1,0:T(8,128)(2,1)} %get-tuple-element.39), channel_id=1, source_target_pairs={{0,4},{4,0},{8,12},{12,8},{16,20},{20,16},{24,28},{28,24},{1,5},{5... | collective-permute-start | bytes 786440 | tf_op jit(solution)/shard_map/ppermute | solution.py:195
  90.0 0.1 copy.32.first
  90.1 5.0 %intra.1 = (f32[256,1024]{1,0:T(8,128)S(1)}, f32[256,1024]{1,0:T(8,128)S(1)}, f32[256,1024]{1,0:T(8,128)S(1)}, f32[256,1024]{1,0:T(8,128)S(1)}) custom-call(bf16[3,256,1024]{2,1,0:T(8,128)(2,1)S(1)} %get-tuple-element.17.qkv, bf16[256,1024]{1,0:T(8,128)(2,1)S(1)} %copy-done.3, f32[8,256,3]{2,1,0:T(8,128)S(1)} %copy.29.cols_h, f32[8,1,256]{2,1,0:T(1,128)S(1)} %bitcast.58, ...), custom_call_target="tpu_custom_call" | custom-call | flops 1073741824 | tf_op jit(solution)/shard_map/intra/pallas_call | solution.py:37
  95.1 0.7 collective-permute-done.10
  95.8 1.1 maximum_select_fusion
  96.9 8.1 %copy-done.2 = bf16[3,4096,1024]{2,1,0:T(8,128)(2,1)S(1)} copy-done((bf16[3,4096,1024]{2,1,0:T(8,128)(2,1)S(1)}, bf16[3,4096,1024]{2,1,0:T(8,128)(2,1)}, u32[]{:S(2)}) %copy-start.2) | copy-done | bytes 25165848
  105.1 4.9 %back_first.1 = (f32[256,1024]{1,0:T(8,128)S(1)}, bf16[3,256,1024]{2,1,0:T(8,128)(2,1)S(1)}, bf16[256,1024]{1,0:T(8,128)(2,1)S(1)}) custom-call(s32[4]{0:T(128)S(1)} %pad_add_fusion.starts, bf16[3,256,1024]{2,1,0:T(8,128)(2,1)S(1)} %get-tuple-element.17.qkv, bf16[256,1024]{1,0:T(8,128)(2,1)S(1)} %copy-done.3, f32[8,256,3]{2,1,0:T(8,128)S(1)} %copy.29.cols_h, ...), custom_call_target="tpu_custom_call" | custom-call | flops 1610612736 | tf_op jit(solution)/shard_map/back_first/pallas_call | solution.py:37
  110.1 5.4 %back_rest.1 = (bf16[256,1024]{1,0:T(8,128)(2,1)S(1)}, f32[256,1024]{1,0:T(8,128)S(1)}) custom-call(s32[4]{0:T(128)S(1)} %pad_add_fusion.starts, bf16[3,256,1024]{2,1,0:T(8,128)(2,1)S(1)} %get-tuple-element.24.gstack, bf16[3,4096,1024]{2,1,0:T(8,128)(2,1)S(1)} %copy-done.2), custom_call_target="tpu_custom_call" | custom-call | flops 3221225472 | tf_op jit(solution)/shard_map/back_rest/pallas_call | solution.py:37
  115.5 0.6 collective-permute-start.11
  116.0 3.0 %back_second.1 = f32[256,1024]{1,0:T(8,128)S(1)} custom-call(s32[4]{0:T(128)S(1)} %pad_add_fusion.starts, bf16[3,256,1024]{2,1,0:T(8,128)(2,1)S(1)} %get-tuple-element.24.gstack, bf16[3,4096,1024]{2,1,0:T(8,128)(2,1)S(1)} %copy-done.2), custom_call_target="tpu_custom_call" | custom-call | flops 1610612736 | tf_op jit(solution)/shard_map/back_second/pallas_call | solution.py:37
  119.0 0.1 add_convert_fusion
  119.1 1.6 %collective-permute-start.13 = (bf16[256,1024]{1,0:T(8,128)(2,1)S(1)}, bf16[256,1024]{1,0:T(8,128)(2,1)S(1)}, u32[]{:S(2)}, u32[]{:S(2)}) collective-permute-start(bf16[256,1024]{1,0:T(8,128)(2,1)S(1)} %add_convert_fusion), channel_id=1, source_target_pairs={{0,2},{1,3},{2,0},{3,1},{4,6},{5,7},{6,4},{7,5},{8,10},{9,11},{10,... | collective-permute-start | bytes 1572872 | tf_op jit(solution)/shard_map/ppermute | solution.py:340
  120.8 1.0 copy.34
  121.8 11.3 %collective-permute-done.13 = bf16[256,1024]{1,0:T(8,128)(2,1)S(1)} collective-permute-done((bf16[256,1024]{1,0:T(8,128)(2,1)S(1)}, bf16[256,1024]{1,0:T(8,128)(2,1)S(1)}, u32[]{:S(2)}, u32[]{:S(2)}) %collective-permute-start.13) | collective-permute-done | bytes 524320 | tf_op jit(solution)/shard_map/ppermute | solution.py:340
  133.1 1.2 convert_add_fusion
  (41 shorter events, 0.9 us)
Async XLA Ops:
  0.6 15.2 %collective-permute-start = (bf16[256,1024]{1,0:T(8,128)(2,1)}, bf16[256,1024]{1,0:T(8,128)(2,1)S(1)}, u32[]{:S(2)}, u32[]{:S(2)}) collective-permute-start(bf16[256,1024]{1,0:T(8,128)(2,1)} %own.1), channel_id=1, source_target_pairs={{0,2},{1,3},{2,0},{3,1},{4,6},{5,7},{6,4},{7,5},{8,10},{9,11},{10,... | collective-permute-start | bytes 1572872 | tf_op jit(solution)/shard_map/ppermute | solution.py:286
  3.7 12.2 %collective-permute-start.2 = (bf16[256,1024]{1,0:T(8,128)(2,1)}, bf16[256,1024]{1,0:T(8,128)(2,1)S(1)}, u32[]{:S(2)}, u32[]{:S(2)}) collective-permute-start(bf16[256,1024]{1,0:T(8,128)(2,1)} %own.1), channel_id=1, source_target_pairs={{0,1},{1,0},{2,3},{3,2},{4,5},{5,4},{6,7},{7,6},{8,9},{9,8},{10,11... | collective-permute-start | bytes 1572872 | tf_op jit(solution)/shard_map/ppermute | solution.py:287
  6.8 1.5 %copy-start.6 = (f32[8,2,128]{2,0,1:T(8,128)}, f32[8,2,128]{2,0,1:T(8,128)S(1)}, u32[]{:S(2)}) copy-start(f32[8,2,128]{2,0,1:T(8,128)S(1)} %get-tuple-element.32) | copy-start | bytes 24580
  15.8 33.0 %collective-permute-start.1 = (bf16[256,1024]{1,0:T(8,128)(2,1)S(1)}, bf16[256,1024]{1,0:T(8,128)(2,1)S(1)}, u32[]{:S(2)}, u32[]{:S(2)}) collective-permute-start(bf16[256,1024]{1,0:T(8,128)(2,1)S(1)} %collective-permute-done.x), channel_id=1, source_target_pairs={{0,1},{1,0},{2,3},{3,2},{4,5},{5,4},{6,7},{7,6},{8,9},{9,8},{10,11... | collective-permute-start | bytes 1572872 | tf_op jit(solution)/shard_map/ppermute | solution.py:288
  15.9 1.0 copy-start.5
  27.9 8.3 %copy-start = (bf16[3,4096,1024]{2,1,0:T(8,128)(2,1)}, bf16[3,4096,1024]{2,1,0:T(8,128)(2,1)S(1)}, u32[]{:S(2)}) copy-start(bf16[3,4096,1024]{2,1,0:T(8,128)(2,1)S(1)} %get-tuple-element.15.w_vm) | copy-start | bytes 75497472
  36.2 8.2 %copy-start.1 = (bf16[3,4096,1024]{2,1,0:T(8,128)(2,1)S(1)}, bf16[3,4096,1024]{2,1,0:T(8,128)(2,1)}, u32[]{:S(2)}) copy-start(bf16[3,4096,1024]{2,1,0:T(8,128)(2,1)} %copy-done) | copy-start | bytes 75497472
  44.4 4.4 %copy-start.3 = (bf16[256,1024]{1,0:T(8,128)(2,1)S(1)}, bf16[256,1024]{1,0:T(8,128)(2,1)}, u32[]{:S(2)}) copy-start(bf16[256,1024]{1,0:T(8,128)(2,1)} %grads.5) | copy-start | bytes 1572868
  56.1 1.0 copy-start.4
  57.8 15.1 %collective-permute-start.3 = (bf16[2,4,128,128]{3,2,1,0:T(8,128)(2,1)}, bf16[2,4,128,128]{3,2,1,0:T(8,128)(2,1)S(1)}, u32[]{:S(2)}, u32[]{:S(2)}) collective-permute-start(bf16[2,4,128,128]{3,2,1,0:T(8,128)(2,1)} %dynamic-slice_convert_fusion), channel_id=1, source_target_pairs={{0,4},{4,0},{8,12},{12,8},{16,20},{20,16},{24,28},{28,24},{1,5},{5... | collective-permute-start | bytes 786440 | tf_op jit(solution)/shard_map/ppermute | solution.py:195
  60.1 6.7 %collective-permute-start.4 = (f32[8]{0:T(128)S(1)}, f32[8]{0:T(128)S(1)}, u32[]{:S(2)}, u32[]{:S(2)}) collective-permute-start(f32[8]{0:T(128)S(1)} %broadcast_select_fusion.3), channel_id=1, source_target_pairs={{0,4},{4,0},{8,12},{12,8},{16,20},{20,16},{24,28},{28,24},{1,5},{5... | collective-permute-start | bytes 104 | tf_op jit(solution)/shard_map/ppermute | solution.py:195
  67.4 12.4 %collective-permute-start.8 = (f32[8]{0:T(128)S(1)}, f32[8]{0:T(128)S(1)}, u32[]{:S(2)}, u32[]{:S(2)}) collective-permute-start(f32[8]{0:T(128)S(1)} %get-tuple-element.47), channel_id=1, source_target_pairs={{8,16},{16,8},{12,20},{20,12},{9,17},{17,9},{13,21},{21,13},{10,18... | collective-permute-start | bytes 104 | tf_op jit(solution)/shard_map/ppermute | solution.py:195
  68.1 11.7 %collective-permute-start.7 = (f32[8]{0:T(128)S(1)}, f32[8]{0:T(128)S(1)}, u32[]{:S(2)}, u32[]{:S(2)}) collective-permute-start(f32[8]{0:T(128)S(1)} %get-tuple-element.47), channel_id=1, source_target_pairs={{0,8},{4,12},{8,0},{12,4},{16,24},{20,28},{24,16},{28,20},{1,9},{5... | collective-permute-start | bytes 104 | tf_op jit(solution)/shard_map/ppermute | solution.py:195
  72.9 17.1 %copy-start.7 = (f32[8,2,128]{2,0,1:T(8,128)S(1)}, f32[8,2,128]{2,0,1:T(8,128)}, u32[]{:S(2)}) copy-start(f32[8,2,128]{2,0,1:T(8,128)} %copy-done.6) | copy-start | bytes 24580
  74.2 5.7 %collective-permute-start.5 = (bf16[4,128,128]{2,1,0:T(8,128)(2,1)S(1)}, bf16[4,128,128]{2,1,0:T(8,128)(2,1)S(1)}, u32[]{:S(2)}, u32[]{:S(2)}) collective-permute-start(bf16[4,128,128]{2,1,0:T(8,128)(2,1)S(1)} %get-tuple-element.28), channel_id=1, source_target_pairs={{0,8},{4,12},{8,0},{12,4},{16,24},{20,28},{24,16},{28,20},{1,9},{5... | collective-permute-start | bytes 393224 | tf_op jit(solution)/shard_map/ppermute | solution.py:195
  74.3 5.5 %collective-permute-start.6 = (bf16[4,128,128]{2,1,0:T(8,128)(2,1)S(1)}, bf16[4,128,128]{2,1,0:T(8,128)(2,1)S(1)}, u32[]{:S(2)}, u32[]{:S(2)}) collective-permute-start(bf16[4,128,128]{2,1,0:T(8,128)(2,1)S(1)} %get-tuple-element.45), channel_id=1, source_target_pairs={{8,16},{16,8},{12,20},{20,12},{9,17},{17,9},{13,21},{21,13},{10,18... | collective-permute-start | bytes 393224 | tf_op jit(solution)/shard_map/ppermute | solution.py:195
  75.0 12.5 %collective-permute-start.9 = (bf16[4,128,128]{2,1,0:T(8,128)(2,1)S(1)}, bf16[4,128,128]{2,1,0:T(8,128)(2,1)S(1)}, u32[]{:S(2)}, u32[]{:S(2)}) collective-permute-start(bf16[4,128,128]{2,1,0:T(8,128)(2,1)S(1)} %get-tuple-element.46), channel_id=1, source_target_pairs={{0,16},{4,20},{8,24},{12,28},{16,0},{20,4},{24,8},{28,12},{1,17},{... | collective-permute-start | bytes 393224 | tf_op jit(solution)/shard_map/ppermute | solution.py:195
  88.5 7.3 %collective-permute-start.10 = (bf16[2,4,128,128]{3,2,1,0:T(8,128)(2,1)}, bf16[2,4,128,128]{3,2,1,0:T(8,128)(2,1)}, u32[]{:S(2)}, u32[]{:S(2)}) collective-permute-start(bf16[2,4,128,128]{3,2,1,0:T(8,128)(2,1)} %get-tuple-element.39), channel_id=1, source_target_pairs={{0,4},{4,0},{8,12},{12,8},{16,20},{20,16},{24,28},{28,24},{1,5},{5... | collective-permute-start | bytes 786440 | tf_op jit(solution)/shard_map/ppermute | solution.py:195
  96.9 8.2 %copy-start.2 = (bf16[3,4096,1024]{2,1,0:T(8,128)(2,1)S(1)}, bf16[3,4096,1024]{2,1,0:T(8,128)(2,1)}, u32[]{:S(2)}) copy-start(bf16[3,4096,1024]{2,1,0:T(8,128)(2,1)} %copy-done) | copy-start | bytes 75497472
  110.0 9.0 %collective-permute-start.12 = (bf16[256,1024]{1,0:T(8,128)(2,1)S(1)}, bf16[256,1024]{1,0:T(8,128)(2,1)S(1)}, u32[]{:S(2)}, u32[]{:S(2)}) collective-permute-start(bf16[256,1024]{1,0:T(8,128)(2,1)S(1)} %get-tuple-element.27), channel_id=1, source_target_pairs={{0,1},{1,0},{2,3},{3,2},{4,5},{5,4},{6,7},{7,6},{8,9},{9,8},{10,11... | collective-permute-start | bytes 1572872 | tf_op jit(solution)/shard_map/ppermute | solution.py:336
  115.5 6.3 %collective-permute-start.11 = (bf16[256,1024]{1,0:T(8,128)(2,1)S(1)}, bf16[256,1024]{1,0:T(8,128)(2,1)S(1)}, u32[]{:S(2)}, u32[]{:S(2)}) collective-permute-start(bf16[256,1024]{1,0:T(8,128)(2,1)S(1)} %get-tuple-element.26), channel_id=1, source_target_pairs={{0,1},{1,0},{2,3},{3,2},{4,5},{5,4},{6,7},{7,6},{8,9},{9,8},{10,11... | collective-permute-start | bytes 1572872 | tf_op jit(solution)/shard_map/ppermute | solution.py:349
  119.1 13.9 %collective-permute-start.13 = (bf16[256,1024]{1,0:T(8,128)(2,1)S(1)}, bf16[256,1024]{1,0:T(8,128)(2,1)S(1)}, u32[]{:S(2)}, u32[]{:S(2)}) collective-permute-start(bf16[256,1024]{1,0:T(8,128)(2,1)S(1)} %add_convert_fusion), channel_id=1, source_target_pairs={{0,2},{1,3},{2,0},{3,1},{4,6},{5,7},{6,4},{7,5},{8,10},{9,11},{10,... | collective-permute-start | bytes 1572872 | tf_op jit(solution)/shard_map/ppermute | solution.py:340

commit v2 on v1

v2 whole, which is shorter than its diff:
```python
import jax
import jax.numpy as jnp
from jax import lax
from jax.experimental import pallas as pl
from jax.experimental.pallas import tpu as pltpu
from jax.sharding import PartitionSpec as P

DH = 128
F32 = jnp.float32
BF16 = jnp.bfloat16
MIB = 1 << 20


def dot(a, b, ca, cb):
    return lax.dot_general(a, b, (((ca,), (cb,)), ((), ())), preferred_element_type=F32)


def split(a):
    high = a.astype(BF16)
    return high, (a - high.astype(F32)).astype(BF16)


def dot_split(a, b, ca, cb):
    high, low = split(a)
    return dot(high, b, ca, cb) + dot(low, b, ca, cb)


def call(kernel, name, outs, args, spaces=None, flops=0, limit=4, aliases=None, scratch=()):
    spaces = spaces or ["v"] * len(args)
    kinds = {"v": pltpu.VMEM, "s": pltpu.SMEM, "a": pl.ANY}
    placed = [
        pltpu.with_memory_space_constraint(a, pltpu.VMEM) if s == "v" else a
        for a, s in zip(args, spaces)
    ]
    return pl.pallas_call(
        kernel,
        name=name,
        out_shape=[pltpu.VMEM(shape, dtype) for shape, dtype in outs],
        in_specs=[pl.BlockSpec(memory_space=kinds[s]) for s in spaces],
        out_specs=[pl.BlockSpec(memory_space=pltpu.VMEM)] * len(outs),
        input_output_aliases=aliases or {},
        scratch_shapes=scratch,
        compiler_params=pltpu.CompilerParams(vmem_limit_bytes=limit * MIB),
        cost_estimate=pl.CostEstimate(flops=flops, bytes_accessed=0, transcendentals=0),
    )(*placed)


def tiles(width):
    tile = 256 if width % 256 == 0 else 128
    return [slice(i, i + tile) for i in range(0, width, tile)]


def rows_of(starts, which, part):
    return pl.ds(pl.multiple_of(starts[which] * part, part), part)


def prepare(starts, lengths, forget, cols_h, rows_h, through):
    count, heads = forget.shape
    offset = starts[6]
    t = lax.broadcasted_iota(jnp.int32, (count, count), 0)
    s = lax.broadcasted_iota(jnp.int32, (count, count), 1)
    lower = jnp.where(s <= t, 1.0, 0.0).astype(BF16)
    high, rest = split(forget[...])
    rest = forget[...] - high.astype(F32)
    middle, low = split(rest)
    total = dot(lower, high, 1, 0) + (dot(lower, middle, 1, 0) + dot(lower, low, 1, 0))
    rows = dot(high, lower, 0, 1) + (dot(middle, lower, 0, 1) + dot(low, lower, 0, 1))
    position = offset + lax.broadcasted_iota(jnp.int32, (count, 1), 0)
    first, end = jnp.zeros((count, 1), jnp.int32), jnp.int32(0)
    for j in range(lengths.shape[0]):
        end = end + lengths[j]
        first = jnp.where(position >= end, end, first)
    first = first - offset
    last = first[count - 1 :, :]
    final = total[count - 1 :, :]
    rows_h[...] = rows
    cols_h[:, :heads] = total
    cols_h[:, heads : 2 * heads] = jnp.where(first < 0, jnp.exp(total), 0.0)
    cols_h[:, 2 * heads : 3 * heads] = jnp.where(first == last, jnp.exp(jnp.where(first == last, final - total, 0.0)), 0.0)
    cols_h[:, 3 * heads : 3 * heads + 1] = first.astype(F32)
    factor = jnp.where(last < 0, jnp.exp(rows[:, count - 1 :]), 0.0)
    factor = jnp.broadcast_to(factor, (heads, DH))
    through[...] = jnp.concatenate(split(factor), axis=0)


def load_and_project(starts, lengths, forget, own, other, w, w_vm, acc, cols_h, rows_h, through, sems):
    part = own.shape[1]
    copies = []
    for j in range(w.shape[1] // part):
        rows = rows_of(starts, j, part)
        copies.append(pltpu.make_async_copy(w.at[:, rows, :], w_vm.at[:, rows, :], sems.at[j]))
        copies[-1].start()
    prepare(starts, lengths, forget, cols_h, rows_h, through)
    for j, x in enumerate((own, other)):
        copies[j].wait()
        for m in range(3):
            for cols in tiles(w.shape[2]):
                term = dot(x[...], w_vm[m, rows_of(starts, j, part), cols], 1, 0)
                acc[m, :, cols] = acc[m, :, cols] + term if j else term
    for copy in copies[2:]:
        copy.wait()


def project_more(starts, x, w, acc_in, acc):
    part = x.shape[1]
    for m in range(3):
        for cols in tiles(w.shape[2]):
            acc[m, :, cols] = acc_in[m, :, cols] + dot(x[...], w[m, rows_of(starts, 2, part), cols], 1, 0)


def project_last(starts, x, w, acc_in, grads, cols_h, own_through, qkv, mine, message):
    part = x.shape[1]
    for m in range(3):
        for cols in tiles(w.shape[2]):
            term = dot(x[...], w[m, rows_of(starts, 3, part), cols], 1, 0)
            qkv[m, :, cols] = (acc_in[m, :, cols] + term).astype(BF16)
    half = mine.shape[1]
    upper = starts[4]
    for h in range(2 * half):
        state = own_state(qkv, grads, cols_h, h)
        kept = (h >= half) == (upper == 1)

        @pl.when(kept)
        def _():
            mine[0, h % half], mine[1, h % half] = state

        @pl.when(jnp.logical_not(kept))
        def _():
            for i in range(2):
                message[(i * half + h % half) * DH : (i * half + h % half + 1) * DH, :] = state[i].astype(BF16)

    message[2 * half * DH :, :] = own_through[...]


def columns(cols_h, h):
    heads = cols_h.shape[1] // 3
    return [cols_h[:, i * heads + h : i * heads + h + 1] for i in range(3)]


def own_state(qkv, grads, cols_h, h):
    cols = slice(h * DH, (h + 1) * DH)
    lead, tail = columns(cols_h, h)[1:]
    state = dot_split(qkv[1, :, cols].astype(F32) * tail, qkv[2, :, cols], 0, 0)
    grad = dot_split(qkv[0, :, cols].astype(F32) * lead, grads[:, cols], 0, 0) * (1.0 / DH)
    return state, grad


def own_states(qkv, grads, cols_h, states):
    for h in range(states.shape[1]):
        states[0, h], states[1, h] = own_state(qkv, grads, cols_h, h)


def intra(qkv, grads, cols_h, rows_h, out, gq, gk, gv):
    length, heads = qkv.shape[1], rows_h.shape[0]
    t = lax.broadcasted_iota(jnp.int32, (length, length), 0)
    s = lax.broadcasted_iota(jnp.int32, (length, length), 1)
    mask = (s <= t) & (s.astype(F32) >= cols_h[:, 3 * heads : 3 * heads + 1])
    for h in range(heads):
        cols = slice(h * DH, (h + 1) * DH)
        gap = jnp.where(mask, columns(cols_h, h)[0] - rows_h[h : h + 1, :], 0.0)
        weight = jnp.where(mask, jnp.exp(gap), 0.0)
        q, k, v, g = qkv[0, :, cols], qkv[1, :, cols], qkv[2, :, cols], grads[:, cols]
        scores = split(dot(q, k, 1, 1) * weight)
        dots = split(dot(g, v, 1, 1) * weight)
        out[:, cols] = dot(scores[0], v, 1, 0) + dot(scores[1], v, 1, 0)
        gq[:, cols] = dot(dots[0], k, 1, 0) + dot(dots[1], k, 1, 0)
        gk[:, cols] = dot(dots[0], q, 0, 0) + dot(dots[1], q, 0, 0)
        gv[:, cols] = dot(scores[0], g, 0, 0) + dot(scores[1], g, 0, 0)


def finish(qkv, grads, cols_h, out, gq, gk, gv, state_of, attn, gstack):
    for h in range(qkv.shape[2] // DH):
        cols = slice(h * DH, (h + 1) * DH)
        lead, tail = columns(cols_h, h)[1:]
        q, k, v, g = qkv[0, :, cols], qkv[1, :, cols], qkv[2, :, cols], grads[:, cols]
        state, end = state_of(0, h), state_of(1, h)
        attn[:, cols] = (out[:, cols] + dot(q, state, 1, 0) * lead) * (1.0 / DH)
        gstack[0, :, cols] = ((gq[:, cols] + dot(g, state, 1, 1) * lead) * (1.0 / DH)).astype(BF16)
        gstack[1, :, cols] = (gk[:, cols] * (1.0 / DH) + dot(v, end, 1, 1) * tail).astype(BF16)
        gstack[2, :, cols] = (gv[:, cols] * (1.0 / DH) + dot(k, end, 1, 0) * tail).astype(BF16)


def finish_whole(qkv, grads, cols_h, out, gq, gk, gv, both, attn, gstack):
    finish(qkv, grads, cols_h, out, gq, gk, gv, lambda i, h: both[i, h], attn, gstack)


def back(starts, which, gstack, w, out):
    part = out.shape[1]
    for cols in tiles(part):
        rows = pl.ds(pl.multiple_of(starts[which] * part + cols.start, cols.stop - cols.start), cols.stop - cols.start)
        total = dot(gstack[0], w[0, rows, :], 1, 1)
        total += dot(gstack[1], w[1, rows, :], 1, 1)
        total += dot(gstack[2], w[2, rows, :], 1, 1)
        out[:, cols] = total.astype(out.dtype)


def back_first(starts, qkv, grads, cols_h, out, gq, gk, gv, kept, passed, w, attn, gstack, chunk):
    half = kept.shape[1]
    upper = starts[4] == 1

    def state_of(i, h):
        mine = (h >= half) == upper
        return jnp.where(mine, kept[i, h % half], passed[i, h % half])

    finish(qkv, grads, cols_h, out, gq, gk, gv, state_of, attn, gstack)
    back(starts, 3, gstack, w, chunk)


def back_second(starts, gstack, w, chunk):
    back(starts, 2, gstack, w, chunk)


def back_rest(starts, gstack, w, chunk_other, chunk_own):
    back(starts, 1, gstack, w, chunk_other)
    back(starts, 0, gstack, w, chunk_own)


def per_head(scale, matrix):
    return scale[..., None, None] * matrix


def head_factors(rows):
    half = rows.shape[0] // 2
    return rows[:half].astype(F32) + rows[half:].astype(F32)


def pair_kernel(starts, own_through, mine, got, to_near, to_middle, to_far, mate_through):
    half = mine.shape[1]
    upper, z = starts[4] == 1, starts[5]
    own, mate = head_factors(own_through[...]), head_factors(got[2 * half * DH :, :])
    mate_through[...] = mate
    low, high = jnp.where(upper, mate, own), jnp.where(upper, own, mate)
    first = jnp.where(upper, half, 0)
    joint = split(own * mate)
    ends = jnp.concatenate(joint, axis=0)
    for to in (to_near, to_middle, to_far):
        to[half * DH :, :] = ends
    for j in range(half):
        rows = slice(j * DH, (j + 1) * DH)
        got_state = got[j * DH : (j + 1) * DH, :].astype(F32)
        got_grad = got[(half + j) * DH : (half + j + 1) * DH, :].astype(F32)
        low_j = jnp.where(upper, low[half + j : half + j + 1], low[j : j + 1])
        high_j = jnp.where(upper, high[half + j : half + j + 1], high[j : j + 1])
        state = jnp.where(upper, mine[0, j] + high_j * got_state, got_state + high_j * mine[0, j]).astype(BF16)
        grad = jnp.where(upper, got_grad + low_j * mine[1, j], mine[1, j] + low_j * got_grad).astype(BF16)
        to_near[rows, :] = jnp.where(z % 2 == 0, state, grad)
        to_middle[rows, :] = jnp.where(z == 1, state, grad)
        to_far[rows, :] = jnp.where(z < 2, state, grad)


def spread_kernel(starts, own_through, mate_through, mine, got, near, middle, far, kept, passed):
    half = mine.shape[1]
    upper, z = starts[4] == 1, starts[5]
    own, mate = head_factors(own_through[...]), mate_through[...]
    low, high = jnp.where(upper, mate, own), jnp.where(upper, own, mate)
    inner = (z == 1) | (z == 2)
    step = head_factors(jnp.where(inner, middle[half * DH :, :], near[half * DH :, :]))
    for j in range(half):
        rows = slice(j * DH, (j + 1) * DH)

        def factor(a):
            return jnp.where(upper, a[half + j : half + j + 1], a[j : j + 1])

        close = near[rows, :].astype(F32)
        beyond = jnp.where(inner, middle[rows, :], near[rows, :]).astype(F32) + factor(step) * far[rows, :].astype(F32)
        state = jnp.where(z == 0, 0.0, jnp.where(z == 1, close, beyond))
        grad = jnp.where(z == 3, 0.0, jnp.where(z == 2, close, beyond))
        got_state = got[j * DH : (j + 1) * DH, :].astype(F32)
        got_grad = got[(half + j) * DH : (half + j + 1) * DH, :].astype(F32)
        low_state, high_grad = jnp.where(upper, got_state, mine[0, j]), jnp.where(upper, mine[1, j], got_grad)
        high_in = (low_state + factor(low) * state).astype(BF16)
        low_in = (high_grad + factor(high) * grad).astype(BF16)
        state, grad = state.astype(BF16), grad.astype(BF16)
        kept[0, j], passed[0, j] = jnp.where(upper, high_in, state), jnp.where(upper, state, high_in)
        kept[1, j], passed[1, j] = jnp.where(upper, grad, low_in), jnp.where(upper, low_in, grad)


def states_direct(starts, own_through, mine, message, inside):
    half = mine.shape[1]
    mate = [(i, i ^ 1) for i in range(8)]
    near = [(i, i ^ 2) for i in range(8)]
    middle = [(2, 4), (4, 2), (3, 5), (5, 3)]
    far = [(i, i ^ 4) for i in range(8)]
    got = lax.ppermute(message, "seq", mate)
    to = ((half * DH + own_through.shape[0], DH), BF16)
    to_near, to_middle, to_far, mate_through = call(
        pair_kernel,
        "pair",
        [to, to, to, ((2 * half, DH), F32)],
        [starts, own_through, mine, got],
        ["s", "v", "v", "v"],
    )
    from_far = lax.ppermute(to_far, "seq", far)
    from_middle = lax.ppermute(to_middle, "seq", middle)
    from_near = lax.ppermute(to_near, "seq", near)
    inside, mine = lax.optimization_barrier((inside, mine))
    kept, passed = call(
        spread_kernel,
        "spread",
        [(mine.shape, BF16), (mine.shape, BF16)],
        [starts, own_through, mate_through, mine, got, from_near, from_middle, from_far],
        ["s"] + ["v"] * 7,
    )
    return kept, lax.ppermute(passed, "seq", mate), inside


def states_gathered(own, through):
    count = lax.axis_size("seq")
    place = lax.axis_index("seq")
    all_own = lax.all_gather(own, "seq")
    all_through = lax.all_gather(through, "seq")

    def pick(a, i):
        return lax.dynamic_index_in_dim(a, i, 0, False)

    def ahead(step, state):
        return per_head(pick(all_through, step), state) + pick(all_own, step)[0]

    def behind(step, state):
        source = count - 1 - step
        return per_head(pick(all_through, source), state) + pick(all_own, source)[1]

    zero = jnp.zeros_like(own[0])
    state = lax.fori_loop(0, place, ahead, zero)
    grad = lax.fori_loop(0, count - 1 - place, behind, zero)
    return jnp.stack([state, grad]).astype(BF16)


def local(tokens, w_qkv, forget, out_grad, doc_lengths):
    length, part = tokens.shape
    width = w_qkv.shape[2]
    heads = width // DH
    tps = lax.axis_size("tp")
    tp = lax.axis_index("tp")
    seqs = lax.axis_size("seq")
    place = lax.axis_index("seq")
    starts = jnp.stack([tp, tp ^ 1, tp ^ 2, tp ^ 3, place % 2, place // 2, place * length]).astype(jnp.int32)
    decays = [((length, 3 * heads + 1), F32), ((heads, length), F32), ((2 * heads, DH), BF16)]
    qkv_shape = ((3, length, width), BF16)
    sum_shape = ((length, width), F32)
    by_hand = tps == 4 and seqs == 8 and heads % 8 == 0
    if by_hand:
        half = heads // 2
        core = [(i, i ^ 1) for i in range(4)]
        chip = [(i, i ^ 2) for i in range(4)]
        step_flops = 2 * 3 * length * part * width
        across = lax.ppermute(tokens, "tp", chip)
        beside = lax.ppermute(tokens, "tp", core)
        w_vm, acc, cols_h, rows_h, own_through = call(
            load_and_project,
            "load_and_project",
            [(w_qkv.shape, BF16), ((3, length, width), F32)] + decays,
            [starts, doc_lengths, forget, tokens, beside, w_qkv],
            ["s", "s", "v", "v", "v", "a"],
            flops=2 * step_flops,
            scratch=[pltpu.SemaphoreType.DMA((tps,))],
        )
        across, acc = lax.optimization_barrier((across, acc))
        across_beside = lax.ppermute(across, "tp", core)
        (acc,) = call(
            project_more, "project_more", [(acc.shape, F32)], [starts, across, w_vm, acc],
            ["s", "v", "v", "v"], flops=step_flops, aliases={3: 0},
        )
        qkv, mine, message = call(
            project_last,
            "project_last",
            [qkv_shape, ((2, half, DH, DH), F32), ((heads * DH + own_through.shape[0], DH), BF16)],
            [starts, across_beside, w_vm, acc, out_grad, cols_h, own_through],
            ["s"] + ["v"] * 6,
            flops=step_flops,
        )
        inside = call(
            intra,
            "intra",
            [sum_shape] * 4,
            [qkv, out_grad, cols_h, rows_h],
            flops=16 * length * length * width,
        )
        kept, passed, inside = states_direct(starts, own_through, mine, message, inside)
    else:
        gathered = lax.all_gather(tokens, "tp", axis=1, tiled=True)
        qkv = jnp.einsum("td,mdc->mtc", gathered, w_qkv, preferred_element_type=F32).astype(BF16)
        cols_h, rows_h, own_through = call(
            prepare, "prepare", decays, [starts, doc_lengths, forget], ["s", "s", "v"]
        )
        through = jnp.sum(own_through.astype(F32).reshape(2, heads, DH), axis=0)[:, 0]
        (own,) = call(own_states, "own_states", [((2, heads, DH, DH), F32)], [qkv, out_grad, cols_h])
        both = states_gathered(own, through)
        inside = call(
            intra,
            "intra",
            [sum_shape] * 4,
            [qkv, out_grad, cols_h, rows_h],
            flops=16 * length * length * width,
        )

    if by_hand:
        attn, gstack, chunk = call(
            back_first,
            "back_first",
            [sum_shape, qkv_shape, ((length, part), BF16)],
            [starts, qkv, out_grad, cols_h] + list(inside) + [kept, passed, w_vm],
            ["s"] + ["v"] * 10,
            flops=step_flops,
        )
        beside = lax.ppermute(chunk, "tp", core)
        (chunk,) = call(
            back_second, "back_second", [((length, part), F32)], [starts, gstack, w_vm], ["s", "v", "v"], flops=step_flops
        )
        chunk = (chunk + beside.astype(F32)).astype(BF16)
        chunk, gstack = lax.optimization_barrier((chunk, gstack))
        across = lax.ppermute(chunk, "tp", chip)
        chunk_other, chunk_own = call(
            back_rest,
            "back_rest",
            [((length, part), BF16), ((length, part), F32)],
            [starts, gstack, w_vm],
            ["s", "v", "v"],
            flops=2 * step_flops,
        )
        beside = [lax.ppermute(c, "tp", core) for c in jnp.split(chunk_other, 2)]
        input_grad = chunk_own + jnp.concatenate(beside).astype(F32) + across.astype(F32)
    else:
        attn, gstack = call(
            finish_whole, "finish", [sum_shape, qkv_shape], [qkv, out_grad, cols_h] + list(inside) + [both]
        )
        grad_terms = jnp.einsum("mtc,mdc->td", gstack, w_qkv, preferred_element_type=F32)
        input_grad = lax.psum_scatter(grad_terms, "tp", scatter_dimension=1, tiled=True)
    return (attn, input_grad)


def solution(mesh):
    placed = (P("seq", "tp"), P(None, None, "tp"), P("seq", "tp"), P("seq", "tp"), P())
    return jax.shard_map(
        local,
        mesh=mesh,
        in_specs=placed,
        out_specs=(P("seq", "tp"), P("seq", "tp")),
        check_vma=False,
    )
```

time: 135 us -> 79.2 us (0.59)
  local copies, waits for them, and re-layouts: 31.3 us -> 3.61 us
  Pallas kernels: 40.8 us -> 32 us
  waiting for transfers between devices: 33.1 us -> 25.9 us
  other arithmetic: 8.36 us -> 1.34 us
  starting transfers between devices: 19.8 us -> 15.3 us
    unnamed x17 -> x8, local copies, waits for them, and re-layouts: 27.6 us -> 3.49 us
    pallas_call x7 -> x9, Pallas kernels: 40.8 us -> 32 us  [call(): pl.pallas_call(kernel, name=name, out_shape=[pltpu.VMEM(shape, dtype) for...]
    ppermute x1, waiting for transfers between devices: 7.12 us -> 0.92 us  [local(): across = lax.ppermute(tokens, 'tp', chip)]
    ppermute x10 -> x8, starting transfers between devices: 16.7 us -> 12.1 us  [the longest x1 3.91 us: states_direct(): from_far = lax.ppermute(to_far, 'seq', far)]
    select_n x7 -> x0, other arithmetic: 3.75 us -> none  [the longest x1 1.15 us: states_direct(): low, high = (jnp.where(upper, got, mine), jnp.where(upper, mine, got))]
    another operation x7 -> x0, other arithmetic: 1.76 us -> none
    slice x4 -> x0, local copies, waits for them, and re-layouts: 1.5 us -> none  [the longest x1 0.58 us: local(): first[-1]]
    ppermute x10 -> x8, waiting for transfers between devices: 25.9 us -> 24.9 us  [the longest x1 7.07 us: states_direct(): got = lax.ppermute(message, 'seq', mate)]
  transfers between devices with their start and end apart: 14 -> 12, of which waited for: 5 -> 7; matrix products, arithmetic and copies ran while one was open for 7% -> 2% of each run, Pallas kernels for 21% -> 28%
where the time goes in v2:
time: 79.2 us; the launch traced here: 79 us
  Pallas kernels  32 us (40%)
  waiting for transfers between devices  25.9 us (33%)
  starting transfers between devices  15.3 us (19%)
  local copies, waits for them, and re-layouts  3.61 us (5%)
  other arithmetic  1.34 us (2%)
  between operations  0.8 us (1%)
    pallas_call x9, Pallas kernels, call(): pl.pallas_call(kernel, name=name, out_shape=[pltpu.VMEM(shape, dtype) for...  32 us
    ppermute x1, waiting for transfers between devices, states_direct(): got = lax.ppermute(message, 'seq', mate)  7.07 us
    ppermute x1, waiting for transfers between devices, local(): across = lax.ppermute(chunk, 'tp', chip)  6.79 us
    ppermute x1, waiting for transfers between devices, states_direct(): return (kept, lax.ppermute(passed, 'seq', mate), inside)  5.56 us
    ppermute x1, waiting for transfers between devices, states_direct(): from_far = lax.ppermute(to_far, 'seq', far)  5.08 us
    ppermute x1, starting transfers between devices, states_direct(): from_far = lax.ppermute(to_far, 'seq', far)  3.91 us
    unnamed x8, local copies, waits for them, and re-layouts  3.49 us
    ppermute x1, starting transfers between devices, local(): across = lax.ppermute(tokens, 'tp', chip)  2.59 us
  transfers between devices with their start and end apart: 12, of which 7 were waited for; matrix products, arithmetic and copies ran while one was open for 2% of the time, Pallas kernels for 28%

profile of v2, /device:TPU:0, one launch (start us, length us, event | category | flops | bytes accessed | tf_op | source)
XLA Modules:
  0.0 79.0 jit_solution(10426102664712204003)
XLA Ops:
  0.6 0.5 collective-permute-start.1
  1.1 2.6 %collective-permute-start = (bf16[256,1024]{1,0:T(8,128)(2,1)}, bf16[256,1024]{1,0:T(8,128)(2,1)S(1)}, u32[]{:S(2)}, u32[]{:S(2)}) collective-permute-start(bf16[256,1024]{1,0:T(8,128)(2,1)} %own.1), channel_id=1, source_target_pairs={{0,2},{1,3},{2,0},{3,1},{4,6},{5,7},{6,4},{7,5},{8,10},{9,11},{10,... | collective-permute-start | bytes 1572872 | tf_op jit(solution)/shard_map/ppermute | solution.py:347
  3.7 0.8 %copy.8.forget = f32[256,8]{1,0:T(8,128)S(1)} copy(f32[256,8]{0,1:T(8,128)} %param.7) | data formatting | bytes 16384 | tf_op args[2]
  4.6 0.1 stack.31.starts
  4.7 0.0 collective-permute-done.1.other
  4.7 0.0 copy-start.1
  4.7 1.0 %copy-done.1 = bf16[256,1024]{1,0:T(8,128)(2,1)S(1)} copy-done((bf16[256,1024]{1,0:T(8,128)(2,1)S(1)}, bf16[256,1024]{1,0:T(8,128)(2,1)}, u32[]{:S(2)}) %copy-start.1) | copy-done | bytes 524312
  5.7 0.0 copy-start.2
  5.7 0.7 copy-done.2
  6.4 9.2 %load_and_project.1 = (bf16[3,4096,1024]{2,1,0:T(8,128)(2,1)S(1)}, f32[3,256,1024]{2,1,0:T(8,128)S(1)}, f32[256,25]{1,0:T(8,128)S(1)}, f32[8,256]{1,0:T(8,128)S(1)}, bf16[16,128]{1,0:T(8,128)(2,1)S(1)}) custom-call(s32[7]{0:T(128)S(1)} %stack.31.starts, s32[16]{0:T(128)S(1)} %copy-done.2, f32[256,8]{1,0:T(8,128)S(1)} %copy.8.forget, ...), custom_call_target="tpu_custom_call" | custom-call | flops 3221225472 | tf_op jit(solution)/shard_map/load_and_project/pallas_call | solution.py:35
  15.5 0.9 %collective-permute-done.x = bf16[256,1024]{1,0:T(8,128)(2,1)S(1)} collective-permute-done((bf16[256,1024]{1,0:T(8,128)(2,1)}, bf16[256,1024]{1,0:T(8,128)(2,1)S(1)}, u32[]{:S(2)}, u32[]{:S(2)}) %collective-permute-start) | collective-permute-done | bytes 524320 | tf_op jit(solution)/shard_map/ppermute | solution.py:347
  16.5 0.0 collective-permute-start.2
  16.5 0.0 copy-start
  16.5 2.7 %project_more.1.acc_in = f32[3,256,1024]{2,1,0:T(8,128)S(1)} custom-call(s32[7]{0:T(128)S(1)} %stack.31.starts, bf16[256,1024]{1,0:T(8,128)(2,1)S(1)} %collective-permute-done.x, bf16[3,4096,1024]{2,1,0:T(8,128)(2,1)S(1)} %get-tuple-element.36.w, f32[3,256,1024]{2,1,0:T(8,128)S(1)} %get-tuple-element.37.acc_in), custom_call_target="tpu_custom_call", output_to_operand_aliasing={{}: (3, {})} | custom-call | flops 1610612736 | tf_op jit(solution)/shard_map/project_more/pallas_call | solution.py:35
  19.2 0.0 collective-permute-done.2.x
  19.2 0.0 copy-done
  19.2 5.1 %project_last.1 = (bf16[3,256,1024]{2,1,0:T(8,128)(2,1)S(1)}, f32[2,4,128,128]{3,2,1,0:T(8,128)S(1)}, bf16[1040,128]{1,0:T(8,128)(2,1)S(1)}) custom-call(s32[7]{0:T(128)S(1)} %stack.31.starts, bf16[256,1024]{1,0:T(8,128)(2,1)S(1)} %collective-permute-done.2.x, bf16[3,4096,1024]{2,1,0:T(8,128)(2,1)S(1)} %get-tuple-element.36.w, ...), custom_call_target="tpu_custom_call" | custom-call | flops 1610612736 | tf_op jit(solution)/shard_map/project_last/pallas_call | solution.py:35
  24.3 1.8 %collective-permute-start.3 = (bf16[1040,128]{1,0:T(8,128)(2,1)S(1)}, bf16[1040,128]{1,0:T(8,128)(2,1)S(1)}, u32[]{:S(2)}, u32[]{:S(2)}) collective-permute-start(bf16[1040,128]{1,0:T(8,128)(2,1)S(1)} %get-tuple-element.51), channel_id=1, source_target_pairs={{0,4},{4,0},{8,12},{12,8},{16,20},{20,16},{24,28},{28,24},{1,5},{5... | collective-permute-start | bytes 798728 | tf_op jit(solution)/shard_map/ppermute | solution.py:284
  26.1 7.1 %collective-permute-done.3.got = bf16[1040,128]{1,0:T(8,128)(2,1)S(1)} collective-permute-done((bf16[1040,128]{1,0:T(8,128)(2,1)S(1)}, bf16[1040,128]{1,0:T(8,128)(2,1)S(1)}, u32[]{:S(2)}, u32[]{:S(2)}) %collective-permute-start.3) | collective-permute-done | bytes 266272 | tf_op jit(solution)/shard_map/ppermute | solution.py:284
  33.1 0.7 pair.1
  33.9 1.9 %collective-permute-start.4 = (bf16[528,128]{1,0:T(8,128)(2,1)S(1)}, bf16[528,128]{1,0:T(8,128)(2,1)S(1)}, u32[]{:S(2)}, u32[]{:S(2)}) collective-permute-start(bf16[528,128]{1,0:T(8,128)(2,1)S(1)} %get-tuple-element.54), channel_id=1, source_target_pairs={{0,8},{4,12},{8,0},{12,4},{16,24},{20,28},{24,16},{28,20},{1,9},{5... | collective-permute-start | bytes 405512 | tf_op jit(solution)/shard_map/ppermute | solution.py:295
  35.7 0.8 %collective-permute-start.5 = (bf16[528,128]{1,0:T(8,128)(2,1)S(1)}, bf16[528,128]{1,0:T(8,128)(2,1)S(1)}, u32[]{:S(2)}, u32[]{:S(2)}) collective-permute-start(bf16[528,128]{1,0:T(8,128)(2,1)S(1)} %get-tuple-element.55), channel_id=1, source_target_pairs={{8,16},{16,8},{12,20},{20,12},{9,17},{17,9},{13,21},{21,13},{10,18... | collective-permute-start | bytes 405512 | tf_op jit(solution)/shard_map/ppermute | solution.py:294
  36.6 3.9 %collective-permute-start.6 = (bf16[528,128]{1,0:T(8,128)(2,1)S(1)}, bf16[528,128]{1,0:T(8,128)(2,1)S(1)}, u32[]{:S(2)}, u32[]{:S(2)}) collective-permute-start(bf16[528,128]{1,0:T(8,128)(2,1)S(1)} %get-tuple-element.56), channel_id=1, source_target_pairs={{0,16},{4,20},{8,24},{12,28},{16,0},{20,4},{24,8},{28,12},{1,17},{... | collective-permute-start | bytes 405512 | tf_op jit(solution)/shard_map/ppermute | solution.py:293
  40.5 3.6 %intra.1 = (f32[256,1024]{1,0:T(8,128)S(1)}, f32[256,1024]{1,0:T(8,128)S(1)}, f32[256,1024]{1,0:T(8,128)S(1)}, f32[256,1024]{1,0:T(8,128)S(1)}) custom-call(bf16[3,256,1024]{2,1,0:T(8,128)(2,1)S(1)} %get-tuple-element.40.qkv, bf16[256,1024]{1,0:T(8,128)(2,1)S(1)} %copy-done, f32[256,25]{1,0:T(8,128)S(1)} %get-tuple-element.38.cols_h, ...), custom_call_target="tpu_custom_call" | custom-call | flops 1073741824 | tf_op jit(solution)/shard_map/intra/pallas_call | solution.py:35
  44.1 0.0 collective-permute-done.4.near
  44.1 0.0 collective-permute-done.5.middle
  44.1 5.1 %collective-permute-done.6.far = bf16[528,128]{1,0:T(8,128)(2,1)S(1)} collective-permute-done((bf16[528,128]{1,0:T(8,128)(2,1)S(1)}, bf16[528,128]{1,0:T(8,128)(2,1)S(1)}, u32[]{:S(2)}, u32[]{:S(2)}) %collective-permute-start.6) | collective-permute-done | bytes 135200 | tf_op jit(solution)/shard_map/ppermute | solution.py:293
  49.2 0.8 spread.1
  50.0 1.6 %collective-permute-start.7 = (bf16[2,4,128,128]{3,2,1,0:T(8,128)(2,1)S(1)}, bf16[2,4,128,128]{3,2,1,0:T(8,128)(2,1)S(1)}, u32[]{:S(2)}, u32[]{:S(2)}) collective-permute-start(bf16[2,4,128,128]{3,2,1,0:T(8,128)(2,1)S(1)} %get-tuple-element.58), channel_id=1, source_target_pairs={{0,4},{4,0},{8,12},{12,8},{16,20},{20,16},{24,28},{28,24},{1,5},{5... | collective-permute-start | bytes 786440 | tf_op jit(solution)/shard_map/ppermute | solution.py:304
  51.6 5.6 %collective-permute-done.7.passed = bf16[2,4,128,128]{3,2,1,0:T(8,128)(2,1)S(1)} collective-permute-done((bf16[2,4,128,128]{3,2,1,0:T(8,128)(2,1)S(1)}, bf16[2,4,128,128]{3,2,1,0:T(8,128)(2,1)S(1)}, u32[]{:S(2)}, u32[]{:S(2)}) %collective-permute-start.7) | collective-permute-done | bytes 262176 | tf_op jit(solution)/shard_map/ppermute | solution.py:304
  57.1 3.7 %back_first.1 = (f32[256,1024]{1,0:T(8,128)S(1)}, bf16[3,256,1024]{2,1,0:T(8,128)(2,1)S(1)}, bf16[256,1024]{1,0:T(8,128)(2,1)S(1)}) custom-call(s32[7]{0:T(128)S(1)} %stack.31.starts, bf16[3,256,1024]{2,1,0:T(8,128)(2,1)S(1)} %get-tuple-element.40.qkv, bf16[256,1024]{1,0:T(8,128)(2,1)S(1)} %copy-done, f32[256,25]{1,0:T(8,128)S(1)} %get-tuple-element.38.cols_h, ...), custom_call_target="tpu_custom_call" | custom-call | flops 1610612736 | tf_op jit(solution)/shard_map/back_first/pallas_call | solution.py:35
  60.8 0.1 collective-permute-start.8
  60.9 2.4 %back_second.1 = f32[256,1024]{1,0:T(8,128)S(1)} custom-call(s32[7]{0:T(128)S(1)} %stack.31.starts, bf16[3,256,1024]{2,1,0:T(8,128)(2,1)S(1)} %get-tuple-element.62.gstack, bf16[3,4096,1024]{2,1,0:T(8,128)(2,1)S(1)} %get-tuple-element.36.w), custom_call_target="tpu_custom_call" | custom-call | flops 1610612736 | tf_op jit(solution)/shard_map/back_second/pallas_call | solution.py:35
  63.2 0.0 collective-permute-done.8
  63.3 0.2 add_convert_fusion
  63.4 1.6 %collective-permute-start.11 = (bf16[256,1024]{1,0:T(8,128)(2,1)S(1)}, bf16[256,1024]{1,0:T(8,128)(2,1)S(1)}, u32[]{:S(2)}, u32[]{:S(2)}) collective-permute-start(bf16[256,1024]{1,0:T(8,128)(2,1)S(1)} %add_convert_fusion), channel_id=1, source_target_pairs={{0,2},{1,3},{2,0},{3,1},{4,6},{5,7},{6,4},{7,5},{8,10},{9,11},{10,... | collective-permute-start | bytes 1572872 | tf_op jit(solution)/shard_map/ppermute | solution.py:412
  65.0 4.0 %back_rest.1 = (bf16[256,1024]{1,0:T(8,128)(2,1)S(1)}, f32[256,1024]{1,0:T(8,128)S(1)}) custom-call(s32[7]{0:T(128)S(1)} %stack.31.starts, bf16[3,256,1024]{2,1,0:T(8,128)(2,1)S(1)} %get-tuple-element.62.gstack, bf16[3,4096,1024]{2,1,0:T(8,128)(2,1)S(1)} %get-tuple-element.36.w), custom_call_target="tpu_custom_call" | custom-call | flops 3221225472 | tf_op jit(solution)/shard_map/back_rest/pallas_call | solution.py:35
  69.0 0.3 collective-permute-start.9
  69.3 0.3 collective-permute-start.10
  69.6 1.0 %copy.10 = f32[256,1024]{1,0:T(8,128)} copy(f32[256,1024]{1,0:T(8,128)S(1)} %get-tuple-element.68) | data formatting | bytes 2097152
  70.6 0.1 collective-permute-done.9
  70.6 0.4 collective-permute-done.10
  71.0 6.8 %collective-permute-done.11 = bf16[256,1024]{1,0:T(8,128)(2,1)S(1)} collective-permute-done((bf16[256,1024]{1,0:T(8,128)(2,1)S(1)}, bf16[256,1024]{1,0:T(8,128)(2,1)S(1)}, u32[]{:S(2)}, u32[]{:S(2)}) %collective-permute-start.11) | collective-permute-done | bytes 524320 | tf_op jit(solution)/shard_map/ppermute | solution.py:412
  77.8 1.2 %convert_add_fusion = f32[256,1024]{1,0:T(8,128)} fusion(bf16[256,1024]{1,0:T(8,128)(2,1)S(1)} %collective-permute-done.11, f32[256,1024]{1,0:T(8,128)S(1)} %get-tuple-element.63, bf16[128,1024]{1,0:T(8,128)(2,1)S(1)} %collective-permute-done.10, bf16[128,1024]{1,0:T(8,128)(2,1)S(1)} %collective-permute-done.9), kind=kLoop, calls=%fused_computation | loop fusion | flops 1835008 | bytes 3145728 | tf_op jit(solution)/shard_map/add | solution.py:422
  (1 shorter events, 0.0 us)
Async XLA Ops:
  0.6 4.0 %collective-permute-start.1 = (bf16[256,1024]{1,0:T(8,128)(2,1)}, bf16[256,1024]{1,0:T(8,128)(2,1)S(1)}, u32[]{:S(2)}, u32[]{:S(2)}) collective-permute-start(bf16[256,1024]{1,0:T(8,128)(2,1)} %own.1), channel_id=1, source_target_pairs={{0,1},{1,0},{2,3},{3,2},{4,5},{5,4},{6,7},{7,6},{8,9},{9,8},{10,11... | collective-permute-start | bytes 1572872 | tf_op jit(solution)/shard_map/ppermute | solution.py:348
  1.1 15.3 %collective-permute-start = (bf16[256,1024]{1,0:T(8,128)(2,1)}, bf16[256,1024]{1,0:T(8,128)(2,1)S(1)}, u32[]{:S(2)}, u32[]{:S(2)}) collective-permute-start(bf16[256,1024]{1,0:T(8,128)(2,1)} %own.1), channel_id=1, source_target_pairs={{0,2},{1,3},{2,0},{3,1},{4,6},{5,7},{6,4},{7,5},{8,10},{9,11},{10,... | collective-permute-start | bytes 1572872 | tf_op jit(solution)/shard_map/ppermute | solution.py:347
  4.7 1.0 %copy-start.1 = (bf16[256,1024]{1,0:T(8,128)(2,1)S(1)}, bf16[256,1024]{1,0:T(8,128)(2,1)}, u32[]{:S(2)}) copy-start(bf16[256,1024]{1,0:T(8,128)(2,1)} %own.1) | copy-start | bytes 1572868
  5.7 0.7 copy-start.2
  16.5 2.7 %collective-permute-start.2 = (bf16[256,1024]{1,0:T(8,128)(2,1)S(1)}, bf16[256,1024]{1,0:T(8,128)(2,1)S(1)}, u32[]{:S(2)}, u32[]{:S(2)}) collective-permute-start(bf16[256,1024]{1,0:T(8,128)(2,1)S(1)} %collective-permute-done.x), channel_id=1, source_target_pairs={{0,1},{1,0},{2,3},{3,2},{4,5},{5,4},{6,7},{7,6},{8,9},{9,8},{10,11... | collective-permute-start | bytes 1572872 | tf_op jit(solution)/shard_map/ppermute | solution.py:359
  16.5 2.7 %copy-start = (bf16[256,1024]{1,0:T(8,128)(2,1)S(1)}, bf16[256,1024]{1,0:T(8,128)(2,1)}, u32[]{:S(2)}) copy-start(bf16[256,1024]{1,0:T(8,128)(2,1)} %grads.5) | copy-start | bytes 1572868
  24.3 8.9 %collective-permute-start.3 = (bf16[1040,128]{1,0:T(8,128)(2,1)S(1)}, bf16[1040,128]{1,0:T(8,128)(2,1)S(1)}, u32[]{:S(2)}, u32[]{:S(2)}) collective-permute-start(bf16[1040,128]{1,0:T(8,128)(2,1)S(1)} %get-tuple-element.51), channel_id=1, source_target_pairs={{0,4},{4,0},{8,12},{12,8},{16,20},{20,16},{24,28},{28,24},{1,5},{5... | collective-permute-start | bytes 798728 | tf_op jit(solution)/shard_map/ppermute | solution.py:284
  33.9 10.3 %collective-permute-start.4 = (bf16[528,128]{1,0:T(8,128)(2,1)S(1)}, bf16[528,128]{1,0:T(8,128)(2,1)S(1)}, u32[]{:S(2)}, u32[]{:S(2)}) collective-permute-start(bf16[528,128]{1,0:T(8,128)(2,1)S(1)} %get-tuple-element.54), channel_id=1, source_target_pairs={{0,8},{4,12},{8,0},{12,4},{16,24},{20,28},{24,16},{28,20},{1,9},{5... | collective-permute-start | bytes 405512 | tf_op jit(solution)/shard_map/ppermute | solution.py:295
  35.7 8.4 %collective-permute-start.5 = (bf16[528,128]{1,0:T(8,128)(2,1)S(1)}, bf16[528,128]{1,0:T(8,128)(2,1)S(1)}, u32[]{:S(2)}, u32[]{:S(2)}) collective-permute-start(bf16[528,128]{1,0:T(8,128)(2,1)S(1)} %get-tuple-element.55), channel_id=1, source_target_pairs={{8,16},{16,8},{12,20},{20,12},{9,17},{17,9},{13,21},{21,13},{10,18... | collective-permute-start | bytes 405512 | tf_op jit(solution)/shard_map/ppermute | solution.py:294
  36.6 12.6 %collective-permute-start.6 = (bf16[528,128]{1,0:T(8,128)(2,1)S(1)}, bf16[528,128]{1,0:T(8,128)(2,1)S(1)}, u32[]{:S(2)}, u32[]{:S(2)}) collective-permute-start(bf16[528,128]{1,0:T(8,128)(2,1)S(1)} %get-tuple-element.56), channel_id=1, source_target_pairs={{0,16},{4,20},{8,24},{12,28},{16,0},{20,4},{24,8},{28,12},{1,17},{... | collective-permute-start | bytes 405512 | tf_op jit(solution)/shard_map/ppermute | solution.py:293
  50.0 7.1 %collective-permute-start.7 = (bf16[2,4,128,128]{3,2,1,0:T(8,128)(2,1)S(1)}, bf16[2,4,128,128]{3,2,1,0:T(8,128)(2,1)S(1)}, u32[]{:S(2)}, u32[]{:S(2)}) collective-permute-start(bf16[2,4,128,128]{3,2,1,0:T(8,128)(2,1)S(1)} %get-tuple-element.58), channel_id=1, source_target_pairs={{0,4},{4,0},{8,12},{12,8},{16,20},{20,16},{24,28},{28,24},{1,5},{5... | collective-permute-start | bytes 786440 | tf_op jit(solution)/shard_map/ppermute | solution.py:304
  60.8 2.5 %collective-permute-start.8 = (bf16[256,1024]{1,0:T(8,128)(2,1)S(1)}, bf16[256,1024]{1,0:T(8,128)(2,1)S(1)}, u32[]{:S(2)}, u32[]{:S(2)}) collective-permute-start(bf16[256,1024]{1,0:T(8,128)(2,1)S(1)} %get-tuple-element.61), channel_id=1, source_target_pairs={{0,1},{1,0},{2,3},{3,2},{4,5},{5,4},{6,7},{7,6},{8,9},{9,8},{10,11... | collective-permute-start | bytes 1572872 | tf_op jit(solution)/shard_map/ppermute | solution.py:406
  63.4 14.4 %collective-permute-start.11 = (bf16[256,1024]{1,0:T(8,128)(2,1)S(1)}, bf16[256,1024]{1,0:T(8,128)(2,1)S(1)}, u32[]{:S(2)}, u32[]{:S(2)}) collective-permute-start(bf16[256,1024]{1,0:T(8,128)(2,1)S(1)} %add_convert_fusion), channel_id=1, source_target_pairs={{0,2},{1,3},{2,0},{3,1},{4,6},{5,7},{6,4},{7,5},{8,10},{9,11},{10,... | collective-permute-start | bytes 1572872 | tf_op jit(solution)/shard_map/ppermute | solution.py:412
  69.0 1.6 %collective-permute-start.9 = (bf16[128,1024]{1,0:T(8,128)(2,1)S(1)}, bf16[128,1024]{1,0:T(8,128)(2,1)S(1)}, u32[]{:S(2)}, u32[]{:S(2)}) collective-permute-start(bf16[128,1024]{1,0:T(8,128)(2,1)S(1)} %get-tuple-element.66), channel_id=1, source_target_pairs={{0,1},{1,0},{2,3},{3,2},{4,5},{5,4},{6,7},{7,6},{8,9},{9,8},{10,11... | collective-permute-start | bytes 786440 | tf_op jit(solution)/shard_map/ppermute | solution.py:421
  69.3 1.7 %collective-permute-start.10 = (bf16[128,1024]{1,0:T(8,128)(2,1)S(1)}, bf16[128,1024]{1,0:T(8,128)(2,1)S(1)}, u32[]{:S(2)}, u32[]{:S(2)}) collective-permute-start(bf16[128,1024]{1,0:T(8,128)(2,1)S(1)} %get-tuple-element.67), channel_id=1, source_target_pairs={{0,1},{1,0},{2,3},{3,2},{4,5},{5,4},{6,7},{7,6},{8,9},{9,8},{10,11... | collective-permute-start | bytes 786440 | tf_op jit(solution)/shard_map/ppermute | solution.py:421

commit v3 on v2

--- a/solution.py
+++ b/solution.py
@@ -27,9 +27,9 @@
 
 def call(kernel, name, outs, args, spaces=None, flops=0, limit=4, aliases=None, scratch=()):
     spaces = spaces or ["v"] * len(args)
-    kinds = {"v": pltpu.VMEM, "s": pltpu.SMEM, "a": pl.ANY}
+    kinds = {"v": pltpu.VMEM, "s": pltpu.SMEM, "h": pltpu.HBM}
     placed = [
-        pltpu.with_memory_space_constraint(a, pltpu.VMEM) if s == "v" else a
+        a if s == "s" else pltpu.with_memory_space_constraint(a, kinds[s])
         for a, s in zip(args, spaces)
     ]
     return pl.pallas_call(
@@ -54,8 +54,8 @@
     return pl.ds(pl.multiple_of(starts[which] * part, part), part)
 
 
-def prepare(starts, lengths, forget, cols_h, rows_h, through):
-    count, heads = forget.shape
+def prepare(starts, forget, cols_h, rows_h, through):
+    heads, count = forget.shape
     offset = starts[6]
     t = lax.broadcasted_iota(jnp.int32, (count, count), 0)
     s = lax.broadcasted_iota(jnp.int32, (count, count), 1)
@@ -63,34 +63,49 @@
     high, rest = split(forget[...])
     rest = forget[...] - high.astype(F32)
     middle, low = split(rest)
-    total = dot(lower, high, 1, 0) + (dot(lower, middle, 1, 0) + dot(lower, low, 1, 0))
-    rows = dot(high, lower, 0, 1) + (dot(middle, lower, 0, 1) + dot(low, lower, 0, 1))
-    position = offset + lax.broadcasted_iota(jnp.int32, (count, 1), 0)
-    first, end = jnp.zeros((count, 1), jnp.int32), jnp.int32(0)
-    for j in range(lengths.shape[0]):
-        end = end + lengths[j]
-        first = jnp.where(position >= end, end, first)
-    first = first - offset
-    last = first[count - 1 :, :]
-    final = total[count - 1 :, :]
-    rows_h[...] = rows
+
+    def weights(axis):
+        if axis:
+            total = dot(high, lower, 1, 1) + (dot(middle, lower, 1, 1) + dot(low, lower, 1, 1))
+        else:
+            total = dot(lower, high, 1, 1) + (dot(lower, middle, 1, 1) + dot(lower, low, 1, 1))
+        shape = (1, count) if axis else (count, 1)
+        position = offset + lax.broadcasted_iota(jnp.int32, shape, axis)
+        first, end = jnp.zeros(shape, jnp.int32), jnp.int32(0)
+        for j in range(7, starts.shape[0]):
+            end = end + starts[j]
+            first = jnp.where(position >= end, end, first)
+        first = first - offset
+        last = lax.slice_in_dim(first, count - 1, count, axis=axis)
+        final = lax.slice_in_dim(total, count - 1, count, axis=axis)
+        lead = jnp.where(first < 0, jnp.exp(total), 0.0)
+        tail = jnp.where(first == last, jnp.exp(jnp.where(first == last, final - total, 0.0)), 0.0)
+        return total, lead, tail, first
+
+    total, lead, tail, first = weights(0)
     cols_h[:, :heads] = total
-    cols_h[:, heads : 2 * heads] = jnp.where(first < 0, jnp.exp(total), 0.0)
-    cols_h[:, 2 * heads : 3 * heads] = jnp.where(first == last, jnp.exp(jnp.where(first == last, final - total, 0.0)), 0.0)
+    cols_h[:, heads : 2 * heads] = lead
+    cols_h[:, 2 * heads : 3 * heads] = tail
     cols_h[:, 3 * heads : 3 * heads + 1] = first.astype(F32)
-    factor = jnp.where(last < 0, jnp.exp(rows[:, count - 1 :]), 0.0)
-    factor = jnp.broadcast_to(factor, (heads, DH))
+    total, lead, tail, first = weights(1)
+    rows_h[:heads, :] = total
+    rows_h[heads : 2 * heads, :] = lead
+    rows_h[2 * heads :, :] = tail
+    factor = jnp.broadcast_to(lead[:, count - 1 :], (heads, DH))
     through[...] = jnp.concatenate(split(factor), axis=0)
 
 
-def load_and_project(starts, lengths, forget, own, other, w, w_vm, acc, cols_h, rows_h, through, sems):
-    part = own.shape[1]
+def load_and_project(starts, forget, tokens, other, w, own, w_vm, acc, cols_h, rows_h, through, sems):
+    part = tokens.shape[1]
+    own_copy = pltpu.make_async_copy(tokens, own, sems.at[w.shape[1] // part])
+    own_copy.start()
     copies = []
     for j in range(w.shape[1] // part):
         rows = rows_of(starts, j, part)
         copies.append(pltpu.make_async_copy(w.at[:, rows, :], w_vm.at[:, rows, :], sems.at[j]))
         copies[-1].start()
-    prepare(starts, lengths, forget, cols_h, rows_h, through)
+    prepare(starts, forget, cols_h, rows_h, through)
+    own_copy.wait()
     for j, x in enumerate((own, other)):
         copies[j].wait()
         for m in range(3):
@@ -108,7 +123,7 @@
             acc[m, :, cols] = acc_in[m, :, cols] + dot(x[...], w[m, rows_of(starts, 2, part), cols], 1, 0)
 
 
-def project_last(starts, x, w, acc_in, grads, cols_h, own_through, qkv, mine, message):
+def project_last(starts, x, w, acc_in, grads, rows_h, own_through, qkv, mine, message):
     part = x.shape[1]
     for m in range(3):
         for cols in tiles(w.shape[2]):
@@ -117,7 +132,7 @@
     half = mine.shape[1]
     upper = starts[4]
     for h in range(2 * half):
-        state = own_state(qkv, grads, cols_h, h)
+        state = own_state(qkv, grads, rows_h, h)
         kept = (h >= half) == (upper == 1)
 
         @pl.when(kept)
@@ -137,21 +152,22 @@
     return [cols_h[:, i * heads + h : i * heads + h + 1] for i in range(3)]
 
 
-def own_state(qkv, grads, cols_h, h):
+def own_state(qkv, grads, rows_h, h):
     cols = slice(h * DH, (h + 1) * DH)
-    lead, tail = columns(cols_h, h)[1:]
-    state = dot_split(qkv[1, :, cols].astype(F32) * tail, qkv[2, :, cols], 0, 0)
-    grad = dot_split(qkv[0, :, cols].astype(F32) * lead, grads[:, cols], 0, 0) * (1.0 / DH)
+    heads = rows_h.shape[0] // 3
+    lead, tail = rows_h[heads + h : heads + h + 1, :], rows_h[2 * heads + h : 2 * heads + h + 1, :]
+    state = dot_split(qkv[1, :, cols].T.astype(F32) * tail, qkv[2, :, cols], 1, 0)
+    grad = dot_split(qkv[0, :, cols].T.astype(F32) * (lead * (1.0 / DH)), grads[:, cols], 1, 0)
     return state, grad
 
 
-def own_states(qkv, grads, cols_h, states):
+def own_states(qkv, grads, rows_h, states):
     for h in range(states.shape[1]):
-        states[0, h], states[1, h] = own_state(qkv, grads, cols_h, h)
+        states[0, h], states[1, h] = own_state(qkv, grads, rows_h, h)
 
 
 def intra(qkv, grads, cols_h, rows_h, out, gq, gk, gv):
-    length, heads = qkv.shape[1], rows_h.shape[0]
+    length, heads = qkv.shape[1], rows_h.shape[0] // 3
     t = lax.broadcasted_iota(jnp.int32, (length, length), 0)
     s = lax.broadcasted_iota(jnp.int32, (length, length), 1)
     mask = (s <= t) & (s.astype(F32) >= cols_h[:, 3 * heads : 3 * heads + 1])
@@ -168,51 +184,67 @@
         gv[:, cols] = dot(scores[0], g, 0, 0) + dot(scores[1], g, 0, 0)
 
 
-def finish(qkv, grads, cols_h, out, gq, gk, gv, state_of, attn, gstack):
+def finish_grads(qkv, grads, cols_h, gq, gk, gv, state_of, gstack):
     for h in range(qkv.shape[2] // DH):
         cols = slice(h * DH, (h + 1) * DH)
         lead, tail = columns(cols_h, h)[1:]
-        q, k, v, g = qkv[0, :, cols], qkv[1, :, cols], qkv[2, :, cols], grads[:, cols]
         state, end = state_of(0, h), state_of(1, h)
-        attn[:, cols] = (out[:, cols] + dot(q, state, 1, 0) * lead) * (1.0 / DH)
-        gstack[0, :, cols] = ((gq[:, cols] + dot(g, state, 1, 1) * lead) * (1.0 / DH)).astype(BF16)
-        gstack[1, :, cols] = (gk[:, cols] * (1.0 / DH) + dot(v, end, 1, 1) * tail).astype(BF16)
-        gstack[2, :, cols] = (gv[:, cols] * (1.0 / DH) + dot(k, end, 1, 0) * tail).astype(BF16)
+        gstack[0, :, cols] = ((gq[:, cols] + dot(grads[:, cols], state, 1, 1) * lead) * (1.0 / DH)).astype(BF16)
+        gstack[1, :, cols] = (gk[:, cols] * (1.0 / DH) + dot(qkv[2, :, cols], end, 1, 1) * tail).astype(BF16)
+        gstack[2, :, cols] = (gv[:, cols] * (1.0 / DH) + dot(qkv[1, :, cols], end, 1, 0) * tail).astype(BF16)
+
+
+def finish_out(qkv, cols_h, out, state_of, attn):
+    for h in range(qkv.shape[2] // DH):
+        cols = slice(h * DH, (h + 1) * DH)
+        lead = columns(cols_h, h)[1]
+        attn[:, cols] = (out[:, cols] + dot(qkv[0, :, cols], state_of(0, h), 1, 0) * lead) * (1.0 / DH)
 
 
 def finish_whole(qkv, grads, cols_h, out, gq, gk, gv, both, attn, gstack):
-    finish(qkv, grads, cols_h, out, gq, gk, gv, lambda i, h: both[i, h], attn, gstack)
-
-
-def back(starts, which, gstack, w, out):
-    part = out.shape[1]
-    for cols in tiles(part):
-        rows = pl.ds(pl.multiple_of(starts[which] * part + cols.start, cols.stop - cols.start), cols.stop - cols.start)
+    finish_grads(qkv, grads, cols_h, gq, gk, gv, lambda i, h: both[i, h], gstack)
+    finish_out(qkv, cols_h, out, lambda i, h: both[i, h], attn)
+
+
+def states_of(starts, kept, passed):
+    half = kept.shape[1]
+    upper = starts[4] == 1
+    return lambda i, h: jnp.where((h >= half) == upper, kept[i, h % half], passed[i, h % half])
+
+
+def back(starts, which, gstack, w, out, offset=0):
+    part = w.shape[1] // 4
+    for cols in tiles(out.shape[1]):
+        size = cols.stop - cols.start
+        rows = pl.ds(pl.multiple_of(starts[which] * part + offset + cols.start, size), size)
         total = dot(gstack[0], w[0, rows, :], 1, 1)
         total += dot(gstack[1], w[1, rows, :], 1, 1)
         total += dot(gstack[2], w[2, rows, :], 1, 1)
         out[:, cols] = total.astype(out.dtype)
 
 
-def back_first(starts, qkv, grads, cols_h, out, gq, gk, gv, kept, passed, w, attn, gstack, chunk):
-    half = kept.shape[1]
-    upper = starts[4] == 1
-
-    def state_of(i, h):
-        mine = (h >= half) == upper
-        return jnp.where(mine, kept[i, h % half], passed[i, h % half])
-
-    finish(qkv, grads, cols_h, out, gq, gk, gv, state_of, attn, gstack)
-    back(starts, 3, gstack, w, chunk)
-
-
-def back_second(starts, gstack, w, chunk):
+def back_first(starts, qkv, grads, cols_h, gq, gk, gv, kept, passed, w, gstack, chunk_a, chunk_b):
+    finish_grads(qkv, grads, cols_h, gq, gk, gv, states_of(starts, kept, passed), gstack)
+    back(starts, 3, gstack, w, chunk_a)
+    back(starts, 3, gstack, w, chunk_b, chunk_a.shape[1])
+
+
+def back_second_a(starts, gstack, w, chunk):
     back(starts, 2, gstack, w, chunk)
 
 
-def back_rest(starts, gstack, w, chunk_other, chunk_own):
+def back_second_b(starts, gstack, w, chunk):
+    back(starts, 2, gstack, w, chunk, w.shape[1] // 4 - chunk.shape[1])
+
+
+def hand_on(a, b, a_out, b_out):
+    pass
+
+
+def back_rest(starts, gstack, w, qkv, cols_h, out, kept, passed, attn, chunk_other, chunk_own):
     back(starts, 1, gstack, w, chunk_other)
     back(starts, 0, gstack, w, chunk_own)
+    finish_out(qkv, cols_h, out, states_of(starts, kept, passed), attn)
 
 
 def per_head(scale, matrix):
@@ -248,7 +280,7 @@
         to_far[rows, :] = jnp.where(z < 2, state, grad)
 
 
-def spread_kernel(starts, own_through, mate_through, mine, got, near, middle, far, kept, passed):
+def spread_kernel(starts, own_through, mate_through, mine, got, far, middle, near, kept, passed):
     half = mine.shape[1]
     upper, z = starts[4] == 1, starts[5]
     own, mate = head_factors(own_through[...]), mate_through[...]
@@ -298,7 +330,7 @@
         spread_kernel,
         "spread",
         [(mine.shape, BF16), (mine.shape, BF16)],
-        [starts, own_through, mate_through, mine, got, from_near, from_middle, from_far],
+        [starts, own_through, mate_through, mine, got, from_far, from_middle, from_near],
         ["s"] + ["v"] * 7,
     )
     return kept, lax.ppermute(passed, "seq", mate), inside
@@ -335,7 +367,8 @@
     seqs = lax.axis_size("seq")
     place = lax.axis_index("seq")
     starts = jnp.stack([tp, tp ^ 1, tp ^ 2, tp ^ 3, place % 2, place // 2, place * length]).astype(jnp.int32)
-    decays = [((length, 3 * heads + 1), F32), ((heads, length), F32), ((2 * heads, DH), BF16)]
+    starts = jnp.concatenate([starts, doc_lengths])
+    decays = [((length, 3 * heads + 1), F32), ((3 * heads, length), F32), ((2 * heads, DH), BF16)]
     qkv_shape = ((3, length, width), BF16)
     sum_shape = ((length, width), F32)
     by_hand = tps == 4 and seqs == 8 and heads % 8 == 0
@@ -346,14 +379,14 @@
         step_flops = 2 * 3 * length * part * width
         across = lax.ppermute(tokens, "tp", chip)
         beside = lax.ppermute(tokens, "tp", core)
-        w_vm, acc, cols_h, rows_h, own_through = call(
+        _, w_vm, acc, cols_h, rows_h, own_through = call(
             load_and_project,
             "load_and_project",
-            [(w_qkv.shape, BF16), ((3, length, width), F32)] + decays,
-            [starts, doc_lengths, forget, tokens, beside, w_qkv],
-            ["s", "s", "v", "v", "v", "a"],
+            [(tokens.shape, BF16), (w_qkv.shape, BF16), ((3, length, width), F32)] + decays,
+            [starts, forget.T, tokens, beside, w_qkv],
+            ["s", "v", "h", "v", "h"],
             flops=2 * step_flops,
-            scratch=[pltpu.SemaphoreType.DMA((tps,))],
+            scratch=[pltpu.SemaphoreType.DMA((tps + 1,))],
         )
         across, acc = lax.optimization_barrier((across, acc))
         across_beside = lax.ppermute(across, "tp", core)
@@ -365,7 +398,7 @@
             project_last,
             "project_last",
             [qkv_shape, ((2, half, DH, DH), F32), ((heads * DH + own_through.shape[0], DH), BF16)],
-            [starts, across_beside, w_vm, acc, out_grad, cols_h, own_through],
+            [starts, across_beside, w_vm, acc, out_grad, rows_h, own_through],
             ["s"] + ["v"] * 6,
             flops=step_flops,
         )
@@ -381,10 +414,10 @@
         gathered = lax.all_gather(tokens, "tp", axis=1, tiled=True)
         qkv = jnp.einsum("td,mdc->mtc", gathered, w_qkv, preferred_element_type=F32).astype(BF16)
         cols_h, rows_h, own_through = call(
-            prepare, "prepare", decays, [starts, doc_lengths, forget], ["s", "s", "v"]
+            prepare, "prepare", decays, [starts, forget.T], ["s", "v"]
         )
         through = jnp.sum(own_through.astype(F32).reshape(2, heads, DH), axis=0)[:, 0]
-        (own,) = call(own_states, "own_states", [((2, heads, DH, DH), F32)], [qkv, out_grad, cols_h])
+        (own,) = call(own_states, "own_states", [((2, heads, DH, DH), F32)], [qkv, out_grad, rows_h])
         both = states_gathered(own, through)
         inside = call(
             intra,
@@ -395,31 +428,47 @@
         )
 
     if by_hand:
-        attn, gstack, chunk = call(
+        part_a = part // 2
+        part_b = part - part_a
+        gstack, chunk_a, chunk_b = call(
             back_first,
             "back_first",
-            [sum_shape, qkv_shape, ((length, part), BF16)],
-            [starts, qkv, out_grad, cols_h] + list(inside) + [kept, passed, w_vm],
-            ["s"] + ["v"] * 10,
-            flops=step_flops,
-        )
-        beside = lax.ppermute(chunk, "tp", core)
-        (chunk,) = call(
-            back_second, "back_second", [((length, part), F32)], [starts, gstack, w_vm], ["s", "v", "v"], flops=step_flops
-        )
-        chunk = (chunk + beside.astype(F32)).astype(BF16)
-        chunk, gstack = lax.optimization_barrier((chunk, gstack))
-        across = lax.ppermute(chunk, "tp", chip)
-        chunk_other, chunk_own = call(
+            [qkv_shape, ((length, part_a), BF16), ((length, part_b), BF16)],
+            [starts, qkv, out_grad, cols_h] + list(inside[1:]) + [kept, passed, w_vm],
+            ["s"] + ["v"] * 9,
+        )
+        beside_a = lax.ppermute(chunk_a, "tp", core)
+        beside_b = lax.ppermute(chunk_b, "tp", core)
+        (chunk_a,) = call(
+            back_second_a, "back_second_a", [((length, part_a), F32)], [starts, gstack, w_vm], ["s", "v", "v"]
+        )
+        chunk_a = (chunk_a + beside_a.astype(F32)).astype(BF16)
+        chunk_a, gstack = lax.optimization_barrier((chunk_a, gstack))
+        across_a = lax.ppermute(chunk_a, "tp", chip)
+        (chunk_b,) = call(
+            back_second_b, "back_second_b", [((length, part_b), F32)], [starts, gstack, w_vm], ["s", "v", "v"]
+        )
+        chunk_b = (chunk_b + beside_b.astype(F32)).astype(BF16)
+        chunk_b, gstack = lax.optimization_barrier((chunk_b, gstack))
+        across_b = lax.ppermute(chunk_b, "tp", chip)
+        attn, chunk_other, chunk_own = call(
             back_rest,
             "back_rest",
-            [((length, part), BF16), ((length, part), F32)],
-            [starts, gstack, w_vm],
-            ["s", "v", "v"],
-            flops=2 * step_flops,
-        )
-        beside = [lax.ppermute(c, "tp", core) for c in jnp.split(chunk_other, 2)]
-        input_grad = chunk_own + jnp.concatenate(beside).astype(F32) + across.astype(F32)
+            [sum_shape, ((length, part), BF16), ((length, part), F32)],
+            [starts, gstack, w_vm, qkv, cols_h, inside[0], kept, passed],
+            ["s"] + ["v"] * 7,
+        )
+        beside = [lax.ppermute(c, "tp", core) for c in jnp.split(chunk_other, 4)]
+        across = call(
+            hand_on,
+            "hand_on",
+            [(across_a.shape, BF16), (across_b.shape, BF16)],
+            [across_a, across_b],
+            flops=8 * step_flops,
+            aliases={0: 0, 1: 1},
+        )
+        across = jnp.concatenate(across, axis=1)
+        input_grad = (across.astype(F32) + chunk_own) + jnp.concatenate(beside).astype(F32)
     else:
         attn, gstack = call(
             finish_whole, "finish", [sum_shape, qkv_shape], [qkv, out_grad, cols_h] + list(inside) + [both]

time: 79.2 us -> 74.1 us (0.936)
  waiting for transfers between devices: 25.9 us -> 19.7 us
  starting transfers between devices: 15.3 us -> 17 us
  local copies, waits for them, and re-layouts: 3.61 us -> 2.44 us
    ppermute x1, waiting for transfers between devices: 5.08 us -> 0.07 us  [states_direct(): from_far = lax.ppermute(to_far, 'seq', far)]
    ppermute x4 -> x8, waiting for transfers between devices: 7.22 us -> 3.93 us  [the longest x1 3.91 us: local(): across_b = lax.ppermute(chunk_b, 'tp', chip)]
    unnamed x8 -> x5, local copies, waits for them, and re-layouts: 3.49 us -> 1.67 us
    ppermute x4 -> x8, starting transfers between devices: 2.23 us -> 3.8 us  [the longest x1 1.63 us: local(): across_a = lax.ppermute(chunk_a, 'tp', chip)]
    ppermute x1, waiting for transfers between devices: 0.01 us -> 1.24 us  [states_direct(): from_near = lax.ppermute(to_near, 'seq', near)]
    ppermute x1, starting transfers between devices: 3.91 us -> 2.89 us  [states_direct(): from_far = lax.ppermute(to_far, 'seq', far)]
    ppermute x1, starting transfers between devices: 1.88 us -> 2.89 us  [states_direct(): from_near = lax.ppermute(to_near, 'seq', near)]
    pallas_call x9 -> x11, Pallas kernels: 32 us -> 32.7 us  [call(): pl.pallas_call(kernel, name=name, out_shape=[pltpu.VMEM(shape, dtype) for...]
  transfers between devices with their start and end apart: 12 -> 16, of which waited for: 7 -> 6; matrix products, arithmetic and copies ran while one was open for 2% -> 3% of each run, Pallas kernels for 28% -> 32%
where the time goes in v3:
time: 74.1 us; the launch traced here: 73.9 us
  Pallas kernels  32.7 us (44%)
  waiting for transfers between devices  19.7 us (27%)
  starting transfers between devices  17 us (23%)
  local copies, waits for them, and re-layouts  2.44 us (3%)
  other arithmetic  1.31 us (2%)
  between operations  0.81 us (1%)
    pallas_call x11, Pallas kernels, call(): pl.pallas_call(kernel, name=name, out_shape=[pltpu.VMEM(shape, dtype) for...  32.7 us
    ppermute x1, waiting for transfers between devices, states_direct(): got = lax.ppermute(message, 'seq', mate)  7.07 us
    ppermute x1, waiting for transfers between devices, states_direct(): return (kept, lax.ppermute(passed, 'seq', mate), inside)  6.04 us
    ppermute x1, waiting for transfers between devices, local(): across_b = lax.ppermute(chunk_b, 'tp', chip)  3.91 us
    ppermute x1, starting transfers between devices, states_direct(): from_near = lax.ppermute(to_near, 'seq', near)  2.89 us
    ppermute x1, starting transfers between devices, states_direct(): from_far = lax.ppermute(to_far, 'seq', far)  2.89 us
    ppermute x1, starting transfers between devices, local(): across = lax.ppermute(tokens, 'tp', chip)  2.59 us
    ppermute x1, starting transfers between devices, states_direct(): got = lax.ppermute(message, 'seq', mate)  1.8 us
  transfers between devices with their start and end apart: 16, of which 6 were waited for; matrix products, arithmetic and copies ran while one was open for 3% of the time, Pallas kernels for 32%

profile of v3, /device:TPU:0, one launch (start us, length us, event | category | flops | bytes accessed | tf_op | source)
XLA Modules:
  0.0 73.9 jit_solution(11632710277855532480)
XLA Ops:
  0.6 0.5 collective-permute-start.1
  1.1 2.6 %collective-permute-start = (bf16[256,1024]{1,0:T(8,128)(2,1)}, bf16[256,1024]{1,0:T(8,128)(2,1)S(1)}, u32[]{:S(2)}, u32[]{:S(2)}) collective-permute-start(bf16[256,1024]{1,0:T(8,128)(2,1)} %tokens.1), channel_id=1, source_target_pairs={{0,2},{1,3},{2,0},{3,1},{4,6},{5,7},{6,4},{7,5},{8,10},{9,11},{10,... | collective-permute-start | bytes 1572872 | tf_op jit(solution)/shard_map/ppermute | solution.py:380
  3.7 0.7 concatenate.9.starts
  4.5 0.0 collective-permute-done.1.other
  4.5 0.0 copy-start.1
  4.5 0.7 copy-done.1
  5.2 9.9 %load_and_project.1 = (bf16[256,1024]{1,0:T(8,128)(2,1)}, bf16[3,4096,1024]{2,1,0:T(8,128)(2,1)S(1)}, f32[3,256,1024]{2,1,0:T(8,128)S(1)}, f32[256,25]{1,0:T(8,1...) custom-call(s32[23]{0:T(128)S(1)} %concatenate.9.starts, f32[8,256]{1,0:T(8,128)S(1)} %bitcast.8, ...), custom_call_target="tpu_custom_call" | custom-call | flops 3221225472 | tf_op jit(solution)/shard_map/load_and_project/pallas_call | solution.py:35
  15.1 1.4 %collective-permute-done.x = bf16[256,1024]{1,0:T(8,128)(2,1)S(1)} collective-permute-done((bf16[256,1024]{1,0:T(8,128)(2,1)}, bf16[256,1024]{1,0:T(8,128)(2,1)S(1)}, u32[]{:S(2)}, u32[]{:S(2)}) %collective-permute-start) | collective-permute-done | bytes 524320 | tf_op jit(solution)/shard_map/ppermute | solution.py:380
  16.5 0.0 collective-permute-start.2
  16.5 2.7 %project_more.1.acc_in = f32[3,256,1024]{2,1,0:T(8,128)S(1)} custom-call(s32[23]{0:T(128)S(1)} %concatenate.9.starts, bf16[256,1024]{1,0:T(8,128)(2,1)S(1)} %collective-permute-done.x, bf16[3,4096,1024]{2,1,0:T(8,128)(2,1)S(1)} %get-tuple-element.41.w, f32[3,256,1024]{2,1,0:T(8,128)S(1)} %get-tuple-element.42.acc_in), custom_call_target="tpu_custom_call", output_to_operand_aliasing={{}: (3, {})} | custom-call | flops 1610612736 | tf_op jit(solution)/shard_map/project_more/pallas_call | solution.py:35
  19.2 0.0 collective-permute-done.2.x
  19.2 4.4 %project_last.1 = (bf16[3,256,1024]{2,1,0:T(8,128)(2,1)S(1)}, f32[2,4,128,128]{3,2,1,0:T(8,128)S(1)}, bf16[1040,128]{1,0:T(8,128)(2,1)S(1)}) custom-call(s32[23]{0:T(128)S(1)} %concatenate.9.starts, bf16[256,1024]{1,0:T(8,128)(2,1)S(1)} %collective-permute-done.2.x, bf16[3,4096,1024]{2,1,0:T(8,128)(2,1)S(1)} %get-tuple-element.41.w, ...), custom_call_target="tpu_custom_call" | custom-call | flops 1610612736 | tf_op jit(solution)/shard_map/project_last/pallas_call | solution.py:35
  23.7 1.8 %collective-permute-start.3 = (bf16[1040,128]{1,0:T(8,128)(2,1)S(1)}, bf16[1040,128]{1,0:T(8,128)(2,1)S(1)}, u32[]{:S(2)}, u32[]{:S(2)}) collective-permute-start(bf16[1040,128]{1,0:T(8,128)(2,1)S(1)} %get-tuple-element.55), channel_id=1, source_target_pairs={{0,4},{4,0},{8,12},{12,8},{16,20},{20,16},{24,28},{28,24},{1,5},{5... | collective-permute-start | bytes 798728 | tf_op jit(solution)/shard_map/ppermute | solution.py:316
  25.5 7.1 %collective-permute-done.3.got = bf16[1040,128]{1,0:T(8,128)(2,1)S(1)} collective-permute-done((bf16[1040,128]{1,0:T(8,128)(2,1)S(1)}, bf16[1040,128]{1,0:T(8,128)(2,1)S(1)}, u32[]{:S(2)}, u32[]{:S(2)}) %collective-permute-start.3) | collective-permute-done | bytes 266272 | tf_op jit(solution)/shard_map/ppermute | solution.py:316
  32.5 0.7 pair.1
  33.2 2.9 %collective-permute-start.4 = (bf16[528,128]{1,0:T(8,128)(2,1)S(1)}, bf16[528,128]{1,0:T(8,128)(2,1)S(1)}, u32[]{:S(2)}, u32[]{:S(2)}) collective-permute-start(bf16[528,128]{1,0:T(8,128)(2,1)S(1)} %get-tuple-element.58), channel_id=1, source_target_pairs={{0,16},{4,20},{8,24},{12,28},{16,0},{20,4},{24,8},{28,12},{1,17},{... | collective-permute-start | bytes 405512 | tf_op jit(solution)/shard_map/ppermute | solution.py:325
  36.1 0.8 %collective-permute-start.5 = (bf16[528,128]{1,0:T(8,128)(2,1)S(1)}, bf16[528,128]{1,0:T(8,128)(2,1)S(1)}, u32[]{:S(2)}, u32[]{:S(2)}) collective-permute-start(bf16[528,128]{1,0:T(8,128)(2,1)S(1)} %get-tuple-element.59), channel_id=1, source_target_pairs={{8,16},{16,8},{12,20},{20,12},{9,17},{17,9},{13,21},{21,13},{10,18... | collective-permute-start | bytes 405512 | tf_op jit(solution)/shard_map/ppermute | solution.py:326
  37.0 2.9 %collective-permute-start.6 = (bf16[528,128]{1,0:T(8,128)(2,1)S(1)}, bf16[528,128]{1,0:T(8,128)(2,1)S(1)}, u32[]{:S(2)}, u32[]{:S(2)}) collective-permute-start(bf16[528,128]{1,0:T(8,128)(2,1)S(1)} %get-tuple-element.60), channel_id=1, source_target_pairs={{0,8},{4,12},{8,0},{12,4},{16,24},{20,28},{24,16},{28,20},{1,9},{5... | collective-permute-start | bytes 405512 | tf_op jit(solution)/shard_map/ppermute | solution.py:327
  39.9 3.6 %intra.1 = (f32[256,1024]{1,0:T(8,128)S(1)}, f32[256,1024]{1,0:T(8,128)S(1)}, f32[256,1024]{1,0:T(8,128)S(1)}, f32[256,1024]{1,0:T(8,128)S(1)}) custom-call(bf16[3,256,1024]{2,1,0:T(8,128)(2,1)S(1)} %get-tuple-element.45.qkv, bf16[256,1024]{1,0:T(8,128)(2,1)S(1)} %copy-done, f32[256,25]{1,0:T(8,128)S(1)} %get-tuple-element.46.cols_h, ...), custom_call_target="tpu_custom_call" | custom-call | flops 1073741824 | tf_op jit(solution)/shard_map/intra/pallas_call | solution.py:35
  43.5 0.1 collective-permute-done.4.far
  43.6 0.0 collective-permute-done.5.middle
  43.6 1.2 %collective-permute-done.6.near = bf16[528,128]{1,0:T(8,128)(2,1)S(1)} collective-permute-done((bf16[528,128]{1,0:T(8,128)(2,1)S(1)}, bf16[528,128]{1,0:T(8,128)(2,1)S(1)}, u32[]{:S(2)}, u32[]{:S(2)}) %collective-permute-start.6) | collective-permute-done | bytes 135200 | tf_op jit(solution)/shard_map/ppermute | solution.py:327
  44.8 0.8 %spread.1 = (bf16[2,4,128,128]{3,2,1,0:T(8,128)(2,1)S(1)}, bf16[2,4,128,128]{3,2,1,0:T(8,128)(2,1)S(1)}) custom-call(s32[23]{0:T(128)S(1)} %concatenate.9.starts, bf16[16,128]{1,0:T(8,128)(2,1)S(1)} %get-tuple-element.44.own_through, f32[8,128]{1,0:T(8,128)S(1)} %get-tuple-element.56.mate_through, f32[2,4,128,128]{3,2,1,0:T(8,128)S(1)} %get-tuple-element.57.mine, ...), custom_call_target="tpu_custom_call" | custom-call | tf_op jit(solution)/shard_map/spread/pallas_call | solution.py:35
  45.6 1.6 %collective-permute-start.7 = (bf16[2,4,128,128]{3,2,1,0:T(8,128)(2,1)S(1)}, bf16[2,4,128,128]{3,2,1,0:T(8,128)(2,1)S(1)}, u32[]{:S(2)}, u32[]{:S(2)}) collective-permute-start(bf16[2,4,128,128]{3,2,1,0:T(8,128)(2,1)S(1)} %get-tuple-element.62), channel_id=1, source_target_pairs={{0,4},{4,0},{8,12},{12,8},{16,20},{20,16},{24,28},{28,24},{1,5},{5... | collective-permute-start | bytes 786440 | tf_op jit(solution)/shard_map/ppermute | solution.py:336
  47.2 6.0 %collective-permute-done.7.passed = bf16[2,4,128,128]{3,2,1,0:T(8,128)(2,1)S(1)} collective-permute-done((bf16[2,4,128,128]{3,2,1,0:T(8,128)(2,1)S(1)}, bf16[2,4,128,128]{3,2,1,0:T(8,128)(2,1)S(1)}, u32[]{:S(2)}, u32[]{:S(2)}) %collective-permute-start.7) | collective-permute-done | bytes 262176 | tf_op jit(solution)/shard_map/ppermute | solution.py:336
  53.3 3.3 %back_first.1 = (bf16[3,256,1024]{2,1,0:T(8,128)(2,1)S(1)}, bf16[256,512]{1,0:T(8,128)(2,1)S(1)}, bf16[256,512]{1,0:T(8,128)(2,1)S(1)}) custom-call(s32[23]{0:T(128)S(1)} %concatenate.9.starts, bf16[3,256,1024]{2,1,0:T(8,128)(2,1)S(1)} %get-tuple-element.45.qkv, bf16[256,1024]{1,0:T(8,128)(2,1)S(1)} %copy-done, f32[256,25]{1,0:T(8,128)S(1)} %get-tuple-element.46.cols_h, ...), custom_call_target="tpu_custom_call" | custom-call | tf_op jit(solution)/shard_map/back_first/pallas_call | solution.py:35
  56.5 0.1 collective-permute-start.8
  56.6 0.5 collective-permute-start.9
  57.1 1.6 %back_second_a.1 = f32[256,512]{1,0:T(8,128)S(1)} custom-call(s32[23]{0:T(128)S(1)} %concatenate.9.starts, bf16[3,256,1024]{2,1,0:T(8,128)(2,1)S(1)} %get-tuple-element.67.gstack, bf16[3,4096,1024]{2,1,0:T(8,128)(2,1)S(1)} %get-tuple-element.41.w), custom_call_target="tpu_custom_call" | custom-call | tf_op jit(solution)/shard_map/back_second_a/pallas_call | solution.py:35
  58.7 0.0 collective-permute-done.8
  58.7 0.1 add_convert_fusion.1
  58.8 1.6 %collective-permute-start.10 = (bf16[256,512]{1,0:T(8,128)(2,1)S(1)}, bf16[256,512]{1,0:T(8,128)(2,1)S(1)}, u32[]{:S(2)}, u32[]{:S(2)}) collective-permute-start(bf16[256,512]{1,0:T(8,128)(2,1)S(1)} %add_convert_fusion.1), channel_id=1, source_target_pairs={{0,2},{1,3},{2,0},{3,1},{4,6},{5,7},{6,4},{7,5},{8,10},{9,11},{10,... | collective-permute-start | bytes 786440 | tf_op jit(solution)/shard_map/ppermute | solution.py:447
  60.4 1.5 %back_second_b.1 = f32[256,512]{1,0:T(8,128)S(1)} custom-call(s32[23]{0:T(128)S(1)} %concatenate.9.starts, bf16[3,256,1024]{2,1,0:T(8,128)(2,1)S(1)} %get-tuple-element.67.gstack, bf16[3,4096,1024]{2,1,0:T(8,128)(2,1)S(1)} %get-tuple-element.41.w), custom_call_target="tpu_custom_call" | custom-call | tf_op jit(solution)/shard_map/back_second_b/pallas_call | solution.py:35
  61.9 0.0 collective-permute-done.9
  61.9 0.1 add_convert_fusion
  62.0 0.5 collective-permute-start.11
  62.6 4.2 %back_rest.1 = (f32[256,1024]{1,0:T(8,128)S(1)}, bf16[256,1024]{1,0:T(8,128)(2,1)S(1)}, f32[256,1024]{1,0:T(8,128)S(1)}) custom-call(s32[23]{0:T(128)S(1)} %concatenate.9.starts, bf16[3,256,1024]{2,1,0:T(8,128)(2,1)S(1)} %get-tuple-element.67.gstack, bf16[3,4096,1024]{2,1,0:T(8,128)(2,1)S(1)} %get-tuple-element.41.w, ...), custom_call_target="tpu_custom_call" | custom-call | tf_op jit(solution)/shard_map/back_rest/pallas_call | solution.py:35
  66.7 1.0 %copy.13 = f32[256,1024]{1,0:T(8,128)} copy(f32[256,1024]{1,0:T(8,128)S(1)} %get-tuple-element.80) | data formatting | bytes 2097152
  67.7 0.1 collective-permute-start.12
  67.8 0.5 collective-permute-start.15
  68.3 0.1 collective-permute-start.14
  68.4 0.0 collective-permute-done.10.a
  68.4 0.4 collective-permute-start.13
  68.8 3.9 %collective-permute-done.11.b = bf16[256,512]{1,0:T(8,128)(2,1)S(1)} collective-permute-done((bf16[256,512]{1,0:T(8,128)(2,1)S(1)}, bf16[256,512]{1,0:T(8,128)(2,1)S(1)}, u32[]{:S(2)}, u32[]{:S(2)}) %collective-permute-start.11) | collective-permute-done | bytes 262176 | tf_op jit(solution)/shard_map/ppermute | solution.py:453
  72.7 0.0 collective-permute-done.12
  72.7 0.0 collective-permute-done.15
  72.7 0.0 collective-permute-done.13
  72.8 1.2 %convert_add_fusion = f32[256,1024]{1,0:T(8,128)} fusion(f32[256,1024]{1,0:T(8,128)S(1)} %get-tuple-element.74, bf16[256,512]{1,0:T(8,128)(2,1)S(1)} %get-tuple-element.73, bf16[256,512]{1,0:T(8,128)(2,1)S(1)} %get-tuple-element.72, bf16[64,1024]{1,0:T(8,128)(2,1)S(1)} %collective-permute-done.15, bf16[64,1024]{1,0:T(8,128)(2,1)S(1)} %collective-permute-done.14, ...), kind=kLoop, calls=%fused_computation | loop fusion | flops 3670016 | bytes 3145728 | tf_op jit(solution)/shard_map/add | solution.py:471
  (5 shorter events, 0.0 us)
Async XLA Ops:
  0.6 3.9 %collective-permute-start.1 = (bf16[256,1024]{1,0:T(8,128)(2,1)}, bf16[256,1024]{1,0:T(8,128)(2,1)S(1)}, u32[]{:S(2)}, u32[]{:S(2)}) collective-permute-start(bf16[256,1024]{1,0:T(8,128)(2,1)} %tokens.1), channel_id=1, source_target_pairs={{0,1},{1,0},{2,3},{3,2},{4,5},{5,4},{6,7},{7,6},{8,9},{9,8},{10,11... | collective-permute-start | bytes 1572872 | tf_op jit(solution)/shard_map/ppermute | solution.py:381
  1.1 15.3 %collective-permute-start = (bf16[256,1024]{1,0:T(8,128)(2,1)}, bf16[256,1024]{1,0:T(8,128)(2,1)S(1)}, u32[]{:S(2)}, u32[]{:S(2)}) collective-permute-start(bf16[256,1024]{1,0:T(8,128)(2,1)} %tokens.1), channel_id=1, source_target_pairs={{0,2},{1,3},{2,0},{3,1},{4,6},{5,7},{6,4},{7,5},{8,10},{9,11},{10,... | collective-permute-start | bytes 1572872 | tf_op jit(solution)/shard_map/ppermute | solution.py:380
  4.5 0.7 copy-start.1
  16.5 2.7 %collective-permute-start.2 = (bf16[256,1024]{1,0:T(8,128)(2,1)S(1)}, bf16[256,1024]{1,0:T(8,128)(2,1)S(1)}, u32[]{:S(2)}, u32[]{:S(2)}) collective-permute-start(bf16[256,1024]{1,0:T(8,128)(2,1)S(1)} %collective-permute-done.x), channel_id=1, source_target_pairs={{0,1},{1,0},{2,3},{3,2},{4,5},{5,4},{6,7},{7,6},{8,9},{9,8},{10,11... | collective-permute-start | bytes 1572872 | tf_op jit(solution)/shard_map/ppermute | solution.py:392
  16.5 2.7 %copy-start = (bf16[256,1024]{1,0:T(8,128)(2,1)S(1)}, bf16[256,1024]{1,0:T(8,128)(2,1)}, u32[]{:S(2)}) copy-start(bf16[256,1024]{1,0:T(8,128)(2,1)} %grads.5) | copy-start | bytes 1572868
  23.7 8.9 %collective-permute-start.3 = (bf16[1040,128]{1,0:T(8,128)(2,1)S(1)}, bf16[1040,128]{1,0:T(8,128)(2,1)S(1)}, u32[]{:S(2)}, u32[]{:S(2)}) collective-permute-start(bf16[1040,128]{1,0:T(8,128)(2,1)S(1)} %get-tuple-element.55), channel_id=1, source_target_pairs={{0,4},{4,0},{8,12},{12,8},{16,20},{20,16},{24,28},{28,24},{1,5},{5... | collective-permute-start | bytes 798728 | tf_op jit(solution)/shard_map/ppermute | solution.py:316
  33.2 10.3 %collective-permute-start.4 = (bf16[528,128]{1,0:T(8,128)(2,1)S(1)}, bf16[528,128]{1,0:T(8,128)(2,1)S(1)}, u32[]{:S(2)}, u32[]{:S(2)}) collective-permute-start(bf16[528,128]{1,0:T(8,128)(2,1)S(1)} %get-tuple-element.58), channel_id=1, source_target_pairs={{0,16},{4,20},{8,24},{12,28},{16,0},{20,4},{24,8},{28,12},{1,17},{... | collective-permute-start | bytes 405512 | tf_op jit(solution)/shard_map/ppermute | solution.py:325
  36.1 7.4 %collective-permute-start.5 = (bf16[528,128]{1,0:T(8,128)(2,1)S(1)}, bf16[528,128]{1,0:T(8,128)(2,1)S(1)}, u32[]{:S(2)}, u32[]{:S(2)}) collective-permute-start(bf16[528,128]{1,0:T(8,128)(2,1)S(1)} %get-tuple-element.59), channel_id=1, source_target_pairs={{8,16},{16,8},{12,20},{20,12},{9,17},{17,9},{13,21},{21,13},{10,18... | collective-permute-start | bytes 405512 | tf_op jit(solution)/shard_map/ppermute | solution.py:326
  37.0 7.8 %collective-permute-start.6 = (bf16[528,128]{1,0:T(8,128)(2,1)S(1)}, bf16[528,128]{1,0:T(8,128)(2,1)S(1)}, u32[]{:S(2)}, u32[]{:S(2)}) collective-permute-start(bf16[528,128]{1,0:T(8,128)(2,1)S(1)} %get-tuple-element.60), channel_id=1, source_target_pairs={{0,8},{4,12},{8,0},{12,4},{16,24},{20,28},{24,16},{28,20},{1,9},{5... | collective-permute-start | bytes 405512 | tf_op jit(solution)/shard_map/ppermute | solution.py:327
  45.6 7.7 %collective-permute-start.7 = (bf16[2,4,128,128]{3,2,1,0:T(8,128)(2,1)S(1)}, bf16[2,4,128,128]{3,2,1,0:T(8,128)(2,1)S(1)}, u32[]{:S(2)}, u32[]{:S(2)}) collective-permute-start(bf16[2,4,128,128]{3,2,1,0:T(8,128)(2,1)S(1)} %get-tuple-element.62), channel_id=1, source_target_pairs={{0,4},{4,0},{8,12},{12,8},{16,20},{20,16},{24,28},{28,24},{1,5},{5... | collective-permute-start | bytes 786440 | tf_op jit(solution)/shard_map/ppermute | solution.py:336
  56.5 2.1 %collective-permute-start.8 = (bf16[256,512]{1,0:T(8,128)(2,1)S(1)}, bf16[256,512]{1,0:T(8,128)(2,1)S(1)}, u32[]{:S(2)}, u32[]{:S(2)}) collective-permute-start(bf16[256,512]{1,0:T(8,128)(2,1)S(1)} %get-tuple-element.64), channel_id=1, source_target_pairs={{0,1},{1,0},{2,3},{3,2},{4,5},{5,4},{6,7},{7,6},{8,9},{9,8},{10,11... | collective-permute-start | bytes 786440 | tf_op jit(solution)/shard_map/ppermute | solution.py:440
  56.6 5.3 %collective-permute-start.9 = (bf16[256,512]{1,0:T(8,128)(2,1)S(1)}, bf16[256,512]{1,0:T(8,128)(2,1)S(1)}, u32[]{:S(2)}, u32[]{:S(2)}) collective-permute-start(bf16[256,512]{1,0:T(8,128)(2,1)S(1)} %get-tuple-element.66), channel_id=1, source_target_pairs={{0,1},{1,0},{2,3},{3,2},{4,5},{5,4},{6,7},{7,6},{8,9},{9,8},{10,11... | collective-permute-start | bytes 786440 | tf_op jit(solution)/shard_map/ppermute | solution.py:441
  58.8 9.6 %collective-permute-start.10 = (bf16[256,512]{1,0:T(8,128)(2,1)S(1)}, bf16[256,512]{1,0:T(8,128)(2,1)S(1)}, u32[]{:S(2)}, u32[]{:S(2)}) collective-permute-start(bf16[256,512]{1,0:T(8,128)(2,1)S(1)} %add_convert_fusion.1), channel_id=1, source_target_pairs={{0,2},{1,3},{2,0},{3,1},{4,6},{5,7},{6,4},{7,5},{8,10},{9,11},{10,... | collective-permute-start | bytes 786440 | tf_op jit(solution)/shard_map/ppermute | solution.py:447
  62.0 10.7 %collective-permute-start.11 = (bf16[256,512]{1,0:T(8,128)(2,1)S(1)}, bf16[256,512]{1,0:T(8,128)(2,1)S(1)}, u32[]{:S(2)}, u32[]{:S(2)}) collective-permute-start(bf16[256,512]{1,0:T(8,128)(2,1)S(1)} %add_convert_fusion), channel_id=1, source_target_pairs={{0,2},{1,3},{2,0},{3,1},{4,6},{5,7},{6,4},{7,5},{8,10},{9,11},{10,... | collective-permute-start | bytes 786440 | tf_op jit(solution)/shard_map/ppermute | solution.py:453
  67.7 5.0 %collective-permute-start.12 = (bf16[64,1024]{1,0:T(8,128)(2,1)S(1)}, bf16[64,1024]{1,0:T(8,128)(2,1)S(1)}, u32[]{:S(2)}, u32[]{:S(2)}) collective-permute-start(bf16[64,1024]{1,0:T(8,128)(2,1)S(1)} %get-tuple-element.76), channel_id=1, source_target_pairs={{0,1},{1,0},{2,3},{3,2},{4,5},{5,4},{6,7},{7,6},{8,9},{9,8},{10,11... | collective-permute-start | bytes 393224 | tf_op jit(solution)/shard_map/ppermute | solution.py:461
  67.8 4.9 %collective-permute-start.15 = (bf16[64,1024]{1,0:T(8,128)(2,1)S(1)}, bf16[64,1024]{1,0:T(8,128)(2,1)S(1)}, u32[]{:S(2)}, u32[]{:S(2)}) collective-permute-start(bf16[64,1024]{1,0:T(8,128)(2,1)S(1)} %get-tuple-element.77), channel_id=1, source_target_pairs={{0,1},{1,0},{2,3},{3,2},{4,5},{5,4},{6,7},{7,6},{8,9},{9,8},{10,11... | collective-permute-start | bytes 393224 | tf_op jit(solution)/shard_map/ppermute | solution.py:461
  68.3 4.4 %collective-permute-start.14 = (bf16[64,1024]{1,0:T(8,128)(2,1)S(1)}, bf16[64,1024]{1,0:T(8,128)(2,1)S(1)}, u32[]{:S(2)}, u32[]{:S(2)}) collective-permute-start(bf16[64,1024]{1,0:T(8,128)(2,1)S(1)} %get-tuple-element.78), channel_id=1, source_target_pairs={{0,1},{1,0},{2,3},{3,2},{4,5},{5,4},{6,7},{7,6},{8,9},{9,8},{10,11... | collective-permute-start | bytes 393224 | tf_op jit(solution)/shard_map/ppermute | solution.py:461
  68.4 4.4 %collective-permute-start.13 = (bf16[64,1024]{1,0:T(8,128)(2,1)S(1)}, bf16[64,1024]{1,0:T(8,128)(2,1)S(1)}, u32[]{:S(2)}, u32[]{:S(2)}) collective-permute-start(bf16[64,1024]{1,0:T(8,128)(2,1)S(1)} %get-tuple-element.79), channel_id=1, source_target_pairs={{0,1},{1,0},{2,3},{3,2},{4,5},{5,4},{6,7},{7,6},{8,9},{9,8},{10,11... | collective-permute-start | bytes 393224 | tf_op jit(solution)/shard_map/ppermute | solution.py:461

commit v4 on v3

v4 whole, which is shorter than its diff:
```python
import functools

import jax
import jax.numpy as jnp
from jax import lax
from jax.experimental import pallas as pl
from jax.experimental.pallas import tpu as pltpu
from jax.sharding import PartitionSpec as P

DH = 128
F32 = jnp.float32
BF16 = jnp.bfloat16
MIB = 1 << 20


def dot(a, b, ca, cb):
    return lax.dot_general(a, b, (((ca,), (cb,)), ((), ())), preferred_element_type=F32)


def split(a):
    high = a.astype(BF16)
    return high, (a - high.astype(F32)).astype(BF16)


def dot_split(a, b, ca, cb):
    high, low = split(a)
    return dot(high, b, ca, cb) + dot(low, b, ca, cb)


def call(kernel, name, outs, args, spaces=None, flops=0, limit=4, aliases=None, scratch=()):
    spaces = spaces or "v" * len(args)
    kinds = {"v": pltpu.VMEM, "s": pltpu.SMEM, "h": pltpu.HBM}
    placed = [
        a if s == "s" else pltpu.with_memory_space_constraint(a, kinds[s])
        for a, s in zip(args, spaces)
    ]
    return pl.pallas_call(
        kernel,
        name=name,
        out_shape=[pltpu.VMEM(shape, dtype) for shape, dtype in outs],
        in_specs=[pl.BlockSpec(memory_space=kinds[s]) for s in spaces],
        out_specs=[pl.BlockSpec(memory_space=pltpu.VMEM)] * len(outs),
        input_output_aliases=aliases or {},
        scratch_shapes=scratch,
        compiler_params=pltpu.CompilerParams(vmem_limit_bytes=limit * MIB),
        cost_estimate=pl.CostEstimate(flops=flops, bytes_accessed=0, transcendentals=0),
    )(*placed)


def tiles(width):
    tile = 256 if width % 256 == 0 else 128
    return [slice(i, i + tile) for i in range(0, width, tile)]


def rows_of(which, part, offset=0, size=None):
    size = size or part
    return pl.ds(pl.multiple_of((lax.axis_index("tp") ^ which) * part + offset, size), size)


def pair_place():
    place = lax.axis_index("seq")
    return place % 2 == 1, place // 2


def prepare(lengths, forget, cols_h, rows_h, through):
    heads, count = forget.shape
    offset = lax.axis_index("seq") * count
    t = lax.broadcasted_iota(jnp.int32, (count, count), 0)
    s = lax.broadcasted_iota(jnp.int32, (count, count), 1)
    lower = jnp.where(s <= t, 1.0, 0.0).astype(BF16)
    high, rest = split(forget[...])
    rest = forget[...] - high.astype(F32)
    middle, low = split(rest)

    def weights(axis):
        if axis:
            total = dot(high, lower, 1, 1) + (dot(middle, lower, 1, 1) + dot(low, lower, 1, 1))
        else:
            total = dot(lower, high, 1, 1) + (dot(lower, middle, 1, 1) + dot(lower, low, 1, 1))
        shape = (1, count) if axis else (count, 1)
        position = offset + lax.broadcasted_iota(jnp.int32, shape, axis)
        first, end = jnp.zeros(shape, jnp.int32), jnp.int32(0)
        for j in range(lengths.shape[0]):
            end = end + lengths[j]
            first = jnp.where(position >= end, end, first)
        first = first - offset
        last = lax.slice_in_dim(first, count - 1, count, axis=axis)
        final = lax.slice_in_dim(total, count - 1, count, axis=axis)
        lead = jnp.where(first < 0, jnp.exp(total), 0.0)
        tail = jnp.where(first == last, jnp.exp(jnp.where(first == last, final - total, 0.0)), 0.0)
        return total, lead, tail, first

    total, lead, tail, first = weights(0)
    cols_h[:, :heads] = total
    cols_h[:, heads : 2 * heads] = lead
    cols_h[:, 2 * heads : 3 * heads] = tail
    cols_h[:, 3 * heads : 3 * heads + 1] = first.astype(F32)
    total, lead, tail, first = weights(1)
    rows_h[:heads, :] = total
    rows_h[heads : 2 * heads, :] = lead
    rows_h[2 * heads :, :] = tail
    factor = jnp.broadcast_to(lead[:, count - 1 :], (heads, DH))
    through[...] = jnp.concatenate(split(factor), axis=0)


def load_and_project(lengths, forget, tokens, w, w_vm, acc, cols_h, rows_h, through, lengths_sm, forget_vm, own, sems):
    part = tokens.shape[1]
    count = w.shape[1] // part
    small = [
        pltpu.make_async_copy(lengths, lengths_sm, sems.at[count]),
        pltpu.make_async_copy(forget, forget_vm, sems.at[count + 1]),
        pltpu.make_async_copy(tokens, own, sems.at[count + 2]),
    ]
    copies = []
    for j in range(count):
        rows = rows_of(j, part)
        copies.append(pltpu.make_async_copy(w.at[:, rows, :], w_vm.at[:, rows, :], sems.at[j]))
    for copy in small + copies:
        copy.start()
    for copy in small:
        copy.wait()
    prepare(lengths_sm, forget_vm, cols_h, rows_h, through)
    copies[0].wait()
    for m in range(3):
        for cols in tiles(w.shape[2]):
            acc[m, :, cols] = dot(own[...], w_vm[m, rows_of(0, part), cols], 1, 0)
    for copy in copies[1:]:
        copy.wait()


def project_more(which, x, w, acc_in, acc):
    part = x.shape[1]
    for m in range(3):
        for cols in tiles(w.shape[2]):
            acc[m, :, cols] = acc_in[m, :, cols] + dot(x[...], w[m, rows_of(which, part), cols], 1, 0)


def project_last(m, x, w, acc_in, out):
    part = x.shape[1]
    for cols in tiles(w.shape[2]):
        out[:, cols] = (acc_in[m, :, cols] + dot(x[...], w[m, rows_of(3, part), cols], 1, 0)).astype(BF16)


def project_key_value(x, w, acc_in, rows_h, through, key, value, mine, message, states):
    project_last(1, x, w, acc_in, key)
    project_last(2, x, w, acc_in, value)
    hand_out(lambda h: state_end(key, value, rows_h, h), states, mine, message)
    message[mine.shape[0] * DH :, :] = through[...]


def project_query(x, w, acc_in, rows_h, grads, query, mine, message, states):
    project_last(0, x, w, acc_in, query)
    hand_out(lambda h: grad_start(query, grads, rows_h, h), states, mine, message)


def hand_out(state_of, states, mine, message):
    half = mine.shape[0]
    for h in range(2 * half):
        states[h] = state_of(h)
    upper = jnp.where(pair_place()[0], half, 0)
    for j in range(half):
        mine[j] = states[upper + j]
        message[j * DH : (j + 1) * DH, :] = states[half - upper + j].astype(BF16)


def columns(cols_h, h):
    heads = cols_h.shape[1] // 3
    return [cols_h[:, i * heads + h : i * heads + h + 1] for i in range(3)]


def state_end(key, value, rows_h, h):
    cols = slice(h * DH, (h + 1) * DH)
    heads = rows_h.shape[0] // 3
    return dot_split(key[:, cols].T.astype(F32) * rows_h[2 * heads + h : 2 * heads + h + 1, :], value[:, cols], 1, 0)


def grad_start(query, grads, rows_h, h):
    cols = slice(h * DH, (h + 1) * DH)
    heads = rows_h.shape[0] // 3
    weight = rows_h[heads + h : heads + h + 1, :] * (1.0 / DH)
    return dot_split(query[:, cols].T.astype(F32) * weight, grads[:, cols], 1, 0)


def own_states(query, key, value, grads, rows_h, states):
    for h in range(states.shape[1]):
        states[0, h] = state_end(key, value, rows_h, h)
        states[1, h] = grad_start(query, grads, rows_h, h)


def intra(query, key, value, grads, cols_h, rows_h, out, gq, gk, gv):
    length, heads = query.shape[0], rows_h.shape[0] // 3
    t = lax.broadcasted_iota(jnp.int32, (length, length), 0)
    s = lax.broadcasted_iota(jnp.int32, (length, length), 1)
    mask = (s <= t) & (s.astype(F32) >= cols_h[:, 3 * heads : 3 * heads + 1])
    for h in range(heads):
        cols = slice(h * DH, (h + 1) * DH)
        gap = jnp.where(mask, columns(cols_h, h)[0] - rows_h[h : h + 1, :], 0.0)
        weight = jnp.where(mask, jnp.exp(gap), 0.0)
        q, k, v, g = query[:, cols], key[:, cols], value[:, cols], grads[:, cols]
        scores = split(dot(q, k, 1, 1) * weight)
        dots = split(dot(g, v, 1, 1) * weight)
        out[:, cols] = dot(scores[0], v, 1, 0) + dot(scores[1], v, 1, 0)
        gq[:, cols] = dot(dots[0], k, 1, 0) + dot(dots[1], k, 1, 0)
        gk[:, cols] = dot(dots[0], q, 0, 0) + dot(dots[1], q, 0, 0)
        gv[:, cols] = dot(scores[0], g, 0, 0) + dot(scores[1], g, 0, 0)


def finish_grads(key, value, grads, gq, gk, gv, cols, lead, tail, state, end, gstack, at):
    gstack[0, :, at] = ((gq[:, cols] + dot(grads[:, cols], state, 1, 1) * lead) * (1.0 / DH)).astype(BF16)
    gstack[1, :, at] = (gk[:, cols] * (1.0 / DH) + dot(value[:, cols], end, 1, 1) * tail).astype(BF16)
    gstack[2, :, at] = (gv[:, cols] * (1.0 / DH) + dot(key[:, cols], end, 1, 0) * tail).astype(BF16)


def finish_out(query, cols_h, out, state_of, attn):
    for h in range(query.shape[1] // DH):
        cols = slice(h * DH, (h + 1) * DH)
        lead = columns(cols_h, h)[1]
        attn[:, cols] = (out[:, cols] + dot(query[:, cols], state_of(h), 1, 0) * lead) * (1.0 / DH)


def finish_whole(query, key, value, grads, cols_h, out, gq, gk, gv, both, attn, gstack):
    for h in range(query.shape[1] // DH):
        cols = slice(h * DH, (h + 1) * DH)
        lead, tail = columns(cols_h, h)[1:]
        finish_grads(key, value, grads, gq, gk, gv, cols, lead, tail, both[0, h], both[1, h], gstack, cols)
    finish_out(query, cols_h, out, lambda h: both[0, h], attn)


def finish_half(kept, key, value, grads, cols_h, gq, gk, gv, states, gstack):
    half = states.shape[1]
    second = pair_place()[0] == kept
    base = jnp.where(second, half * DH, 0)
    for j in range(half):
        cols = pl.ds(pl.multiple_of(base + j * DH, DH), DH)
        lead, tail = [
            jnp.where(second, b, a) for a, b in zip(columns(cols_h, j)[1:], columns(cols_h, half + j)[1:])
        ]
        at = slice(j * DH, (j + 1) * DH)
        finish_grads(key, value, grads, gq, gk, gv, cols, lead, tail, states[0, j], states[1, j], gstack, at)
    return pl.ds(pl.multiple_of(base, half * DH), half * DH)


def back(which, stacks, w, out, offset=0, start=None):
    part = w.shape[1] // 4
    for cols in tiles(out.shape[1]):
        rows = rows_of(which, part, offset + cols.start, cols.stop - cols.start)
        total = None if start is None else start[:, slice(offset + cols.start, offset + cols.stop)]
        for gstack, heads in stacks:
            for m in range(3):
                term = dot(gstack[m], w[m, rows, heads], 1, 1)
                total = term if total is None else total + term
        out[:, cols] = total.astype(out.dtype)


def half_columns(kept, w):
    width = w.shape[2] // 2
    return pl.ds(pl.multiple_of(jnp.where(pair_place()[0] == kept, width, 0), width), width)


def back_kept(key, value, grads, cols_h, gq, gk, gv, kept, w, stack, start3, start2):
    heads = finish_half(True, key, value, grads, cols_h, gq, gk, gv, kept, stack)
    back(3, [(stack, heads)], w, start3)
    back(2, [(stack, heads)], w, start2)


def back_first(key, value, grads, cols_h, gq, gk, gv, passed, w, start3, stack, chunk_a, chunk_b):
    heads = finish_half(False, key, value, grads, cols_h, gq, gk, gv, passed, stack)
    back(3, [(stack, heads)], w, chunk_a, 0, start3)
    back(3, [(stack, heads)], w, chunk_b, chunk_a.shape[1], start3)


def back_second_a(stack, w, start2, chunk):
    back(2, [(stack, half_columns(False, w))], w, chunk, 0, start2)


def back_second_b(stack, w, start2, chunk):
    back(2, [(stack, half_columns(False, w))], w, chunk, w.shape[1] // 4 - chunk.shape[1], start2)


def hand_on(*refs):
    pass


def back_rest(kept_stack, stack, w, query, cols_h, out, kept, passed, attn, chunk_other, chunk_own):
    stacks = [(kept_stack, half_columns(True, w)), (stack, half_columns(False, w))]
    back(1, stacks, w, chunk_other)
    back(0, stacks, w, chunk_own)
    half = kept.shape[1]
    upper = pair_place()[0]

    def state_of(h):
        return jnp.where((h >= half) == upper, kept[0, h % half], passed[0, h % half])

    finish_out(query, cols_h, out, state_of, attn)


def per_head(scale, matrix):
    return scale[..., None, None] * matrix


def head_factors(rows):
    half = rows.shape[0] // 2
    return rows[:half].astype(F32) + rows[half:].astype(F32)


def pair_kernel(own_through, my_state, my_grad, got_state, got_grad, to_far, to_middle, to_near, mate_through):
    half = my_state.shape[0]
    upper, z = pair_place()
    own, mate = head_factors(own_through[...]), head_factors(got_state[half * DH :, :])
    mate_through[...] = mate
    low, high = jnp.where(upper, mate, own), jnp.where(upper, own, mate)
    ends = jnp.concatenate(split(own * mate), axis=0)
    for to in (to_near, to_middle, to_far):
        to[half * DH :, :] = ends
    for j in range(half):
        rows = slice(j * DH, (j + 1) * DH)
        theirs, theirs_grad = got_state[rows, :].astype(F32), got_grad[rows, :].astype(F32)
        low_j, high_j = half_factor(upper, low, j), half_factor(upper, high, j)
        mine, mine_grad = my_state[j], my_grad[j]
        state = jnp.where(upper, mine + high_j * theirs, theirs + high_j * mine).astype(BF16)
        grad = jnp.where(upper, theirs_grad + low_j * mine_grad, mine_grad + low_j * theirs_grad).astype(BF16)
        to_near[rows, :] = jnp.where(z % 2 == 0, state, grad)
        to_middle[rows, :] = jnp.where(z == 1, state, grad)
        to_far[rows, :] = jnp.where(z < 2, state, grad)


def half_factor(upper, factors, j):
    half = factors.shape[0] // 2
    return jnp.where(upper, factors[half + j : half + j + 1], factors[j : j + 1])


def spread_kernel(own_through, mate_through, my_state, my_grad, got_state, got_grad, far, middle, near, kept, passed):
    half = my_state.shape[0]
    upper, z = pair_place()
    own, mate = head_factors(own_through[...]), mate_through[...]
    low, high = jnp.where(upper, mate, own), jnp.where(upper, own, mate)
    inner = (z == 1) | (z == 2)
    step = head_factors(jnp.where(inner, middle[half * DH :, :], near[half * DH :, :]))
    for j in range(half):
        rows = slice(j * DH, (j + 1) * DH)
        close = near[rows, :].astype(F32)
        beyond = jnp.where(inner, middle[rows, :], near[rows, :]).astype(F32)
        beyond = beyond + half_factor(upper, step, j) * far[rows, :].astype(F32)
        state = jnp.where(z == 0, 0.0, jnp.where(z == 1, close, beyond))
        grad = jnp.where(z == 3, 0.0, jnp.where(z == 2, close, beyond))
        low_state = jnp.where(upper, got_state[rows, :].astype(F32), my_state[j])
        high_grad = jnp.where(upper, my_grad[j], got_grad[rows, :].astype(F32))
        high_in = (low_state + half_factor(upper, low, j) * state).astype(BF16)
        low_in = (high_grad + half_factor(upper, high, j) * grad).astype(BF16)
        state, grad = state.astype(BF16), grad.astype(BF16)
        kept[0, j], passed[0, j] = jnp.where(upper, high_in, state), jnp.where(upper, state, high_in)
        kept[1, j], passed[1, j] = jnp.where(upper, grad, low_in), jnp.where(upper, low_in, grad)


MATE = [(i, i ^ 1) for i in range(8)]
NEAR = [(i, i ^ 2) for i in range(8)]
MIDDLE = [(2, 4), (4, 2), (3, 5), (5, 3)]
FAR = [(i, i ^ 4) for i in range(8)]


def states_direct(own_through, my_state, my_grad, got_state, got_grad, inside):
    half = my_state.shape[0]
    to = ((half * DH + own_through.shape[0], DH), BF16)
    known = [my_state, my_grad, got_state, got_grad]
    to_far, to_middle, to_near, mate_through = call(
        pair_kernel, "pair", [to, to, to, ((2 * half, DH), F32)], [own_through] + known
    )
    from_far = lax.ppermute(to_far, "seq", FAR)
    from_middle = lax.ppermute(to_middle, "seq", MIDDLE)
    from_near = lax.ppermute(to_near, "seq", NEAR)
    inside, mate_through = lax.optimization_barrier((inside, mate_through))
    both = ((2, half, DH, DH), BF16)
    kept, passed = call(
        spread_kernel, "spread", [both, both], [own_through, mate_through] + known + [from_far, from_middle, from_near]
    )
    return kept, lax.ppermute(passed, "seq", MATE), inside


def states_gathered(own, through):
    count = lax.axis_size("seq")
    place = lax.axis_index("seq")
    all_own = lax.all_gather(own, "seq")
    all_through = lax.all_gather(through, "seq")

    def pick(a, i):
        return lax.dynamic_index_in_dim(a, i, 0, False)

    def ahead(step, state):
        return per_head(pick(all_through, step), state) + pick(all_own, step)[0]

    def behind(step, state):
        source = count - 1 - step
        return per_head(pick(all_through, source), state) + pick(all_own, source)[1]

    zero = jnp.zeros_like(own[0])
    state = lax.fori_loop(0, place, ahead, zero)
    grad = lax.fori_loop(0, count - 1 - place, behind, zero)
    return jnp.stack([state, grad]).astype(BF16)


def local(tokens, w_qkv, forget, out_grad, doc_lengths):
    length, part = tokens.shape
    width = w_qkv.shape[2]
    heads = width // DH
    tps = lax.axis_size("tp")
    seqs = lax.axis_size("seq")
    by_hand = tps == 4 and seqs == 8 and heads % 8 == 0
    decays = [((length, 3 * heads + 1), F32), ((3 * heads, length), F32), ((2 * heads, DH), BF16)]
    rows_shape = ((length, width), BF16)
    sum_shape = ((length, width), F32)
    intra_flops = 16 * length * length * width
    forget = forget.T
    if not by_hand:
        gathered = lax.all_gather(tokens, "tp", axis=1, tiled=True)
        projected = jnp.einsum("td,mdc->mtc", gathered, w_qkv, preferred_element_type=F32).astype(BF16)
        qkv = [projected[m] for m in range(3)]
        cols_h, rows_h, through = call(prepare, "prepare", decays, [doc_lengths, forget], "sv")
        through = jnp.sum(through.astype(F32).reshape(2, heads, DH), axis=0)[:, 0]
        (own,) = call(own_states, "own_states", [((2, heads, DH, DH), F32)], qkv + [out_grad, rows_h])
        both = states_gathered(own, through)
        inside = call(intra, "intra", [sum_shape] * 4, qkv + [out_grad, cols_h, rows_h], flops=intra_flops)
        attn, gstack = call(
            finish_whole,
            "finish",
            [sum_shape, ((3, length, width), BF16)],
            qkv + [out_grad, cols_h] + list(inside) + [both],
        )
        grad_terms = jnp.einsum("mtc,mdc->td", gstack, w_qkv, preferred_element_type=F32)
        return attn, lax.psum_scatter(grad_terms, "tp", scatter_dimension=1, tiled=True)

    half = heads // 2
    core = [(i, i ^ 1) for i in range(4)]
    chip = [(i, i ^ 2) for i in range(4)]
    step_flops = 2 * 3 * length * part * width
    across = lax.ppermute(tokens, "tp", chip)
    beside = lax.ppermute(tokens, "tp", core)
    w_vm, acc, cols_h, rows_h, through = call(
        load_and_project,
        "load_and_project",
        [(w_qkv.shape, BF16), ((3, length, width), F32)] + decays,
        [doc_lengths, forget, tokens, w_qkv],
        "hhhh",
        scratch=[
            pltpu.SMEM(doc_lengths.shape, jnp.int32),
            pltpu.VMEM(forget.shape, F32),
            pltpu.VMEM(tokens.shape, BF16),
            pltpu.SemaphoreType.DMA((tps + 3,)),
        ],
    )
    (acc,) = call(
        functools.partial(project_more, 1),
        "project_beside",
        [(acc.shape, F32)],
        [beside, w_vm, acc],
        aliases={2: 0},
    )
    across, acc = lax.optimization_barrier((across, acc))
    across_beside = lax.ppermute(across, "tp", core)
    (acc,) = call(
        functools.partial(project_more, 2),
        "project_across",
        [(acc.shape, F32)],
        [across, w_vm, acc],
        aliases={2: 0},
    )
    states_scratch = [pltpu.VMEM((heads, DH, DH), F32)]
    mine_shape = ((half, DH, DH), F32)
    key, value, my_state, message = call(
        project_key_value,
        "project_key_value",
        [rows_shape, rows_shape, mine_shape, ((half * DH + through.shape[0], DH), BF16)],
        [across_beside, w_vm, acc, rows_h, through],
        scratch=states_scratch,
    )
    got_state = lax.ppermute(message, "seq", MATE)
    acc, my_state = lax.optimization_barrier((acc, my_state))
    query, my_grad, message = call(
        project_query,
        "project_query",
        [rows_shape, mine_shape, ((half * DH, DH), BF16)],
        [across_beside, w_vm, acc, rows_h, out_grad],
        scratch=states_scratch,
    )
    got_grad = lax.ppermute(message, "seq", MATE)
    inside = call(
        intra, "intra", [sum_shape] * 4, [query, key, value, out_grad, cols_h, rows_h], flops=intra_flops
    )
    kept, passed, inside = states_direct(through, my_state, my_grad, got_state, got_grad, inside)

    part_a = part // 2
    part_b = part - part_a
    stack_shape = ((3, length, width // 2), BF16)
    chunk_shape = ((length, part), F32)
    common = [key, value, out_grad, cols_h] + list(inside[1:])
    kept_stack, start3, start2 = call(
        back_kept, "back_kept", [stack_shape, chunk_shape, chunk_shape], common + [kept, w_vm]
    )
    stack, chunk_a, chunk_b = call(
        back_first,
        "back_first",
        [stack_shape, ((length, part_a), BF16), ((length, part_b), BF16)],
        common + [passed, w_vm, start3],
    )
    beside_a = lax.ppermute(chunk_a, "tp", core)
    beside_b = lax.ppermute(chunk_b, "tp", core)
    (chunk_a,) = call(back_second_a, "back_second_a", [((length, part_a), F32)], [stack, w_vm, start2])
    chunk_a = (chunk_a + beside_a.astype(F32)).astype(BF16)
    chunk_a, stack = lax.optimization_barrier((chunk_a, stack))
    across_a = lax.ppermute(chunk_a, "tp", chip)
    (chunk_b,) = call(back_second_b, "back_second_b", [((length, part_b), F32)], [stack, w_vm, start2])
    chunk_b = (chunk_b + beside_b.astype(F32)).astype(BF16)
    chunk_b, stack = lax.optimization_barrier((chunk_b, stack))
    across_b = lax.ppermute(chunk_b, "tp", chip)
    attn, chunk_other, chunk_own = call(
        back_rest,
        "back_rest",
        [sum_shape, ((length, part), BF16), chunk_shape],
        [kept_stack, stack, w_vm, query, cols_h, inside[0], kept, passed],
    )
    beside = [lax.ppermute(c, "tp", core) for c in jnp.split(chunk_other, 4)]
    across = [across_a]
    for more in ([], [across_b]):
        across = list(across) + more
        across = call(
            hand_on,
            "hand_on",
            [(a.shape, BF16) for a in across],
            across,
            flops=8 * step_flops if more else 0,
            aliases={i: i for i in range(len(across))},
        )
    across = jnp.concatenate(across, axis=1)
    input_grad = (across.astype(F32) + chunk_own) + jnp.concatenate(beside).astype(F32)
    return attn, input_grad


def solution(mesh):
    placed = (P("seq", "tp"), P(None, None, "tp"), P("seq", "tp"), P("seq", "tp"), P())
    return jax.shard_map(
        local,
        mesh=mesh,
        in_specs=placed,
        out_specs=(P("seq", "tp"), P("seq", "tp")),
        check_vma=False,
    )
```

time: 74.1 us -> 68.2 us (0.920)
  Pallas kernels: 32.7 us -> 28.4 us
  local copies, waits for them, and re-layouts: 2.44 us -> 1.01 us
    pallas_call x11 -> x15, Pallas kernels: 32.7 us -> 28.4 us  [call(): pl.pallas_call(kernel, name=name, out_shape=[pltpu.VMEM(shape, dtype) for...]
    ppermute x5 -> x6, waiting for transfers between devices: 14.4 us -> 10.5 us  [the longest x1 5.54 us: local(): got_grad = lax.ppermute(message, 'seq', MATE)]
    ppermute x1, waiting for transfers between devices: 0.01 us -> 1.7 us  [local(): across_a = lax.ppermute(chunk_a, 'tp', chip)]
    ppermute x1, waiting for transfers between devices: 3.91 us -> 4.81 us  [local(): across_b = lax.ppermute(chunk_b, 'tp', chip)]
    ppermute x1, waiting for transfers between devices: 1.36 us -> 2.14 us  [local(): across = lax.ppermute(tokens, 'tp', chip)]
    unnamed x5 -> x3, local copies, waits for them, and re-layouts: 1.67 us -> 0.98 us
    ppermute x5 -> x6, starting transfers between devices: 10 us -> 10.4 us  [the longest x1 2.89 us: states_direct(): from_near = lax.ppermute(to_near, 'seq', NEAR)]
  transfers between devices with their start and end apart: 16 -> 17, of which waited for: 6 -> 8; matrix products, arithmetic and copies ran while one was open for 3% -> 2% of each run, Pallas kernels for 32% -> 36%
where the time goes in v4:
time: 68.2 us; the launch traced here: 68 us
  Pallas kernels  28.4 us (42%)
  waiting for transfers between devices  19.6 us (29%)
  starting transfers between devices  16.9 us (25%)
  other arithmetic  1.34 us (2%)
  local copies, waits for them, and re-layouts  1.01 us (1%)
  between operations  0.8 us (1%)
    pallas_call x15, Pallas kernels, call(): pl.pallas_call(kernel, name=name, out_shape=[pltpu.VMEM(shape, dtype) for...  28.4 us
    ppermute x1, waiting for transfers between devices, local(): got_grad = lax.ppermute(message, 'seq', MATE)  5.54 us
    ppermute x1, waiting for transfers between devices, local(): across_b = lax.ppermute(chunk_b, 'tp', chip)  4.81 us
    ppermute x1, waiting for transfers between devices, states_direct(): return (kept, lax.ppermute(passed, 'seq', MATE), inside)  3.65 us
    ppermute x1, starting transfers between devices, states_direct(): from_near = lax.ppermute(to_near, 'seq', NEAR)  2.89 us
    ppermute x1, starting transfers between devices, states_direct(): from_far = lax.ppermute(to_far, 'seq', FAR)  2.89 us
    ppermute x1, starting transfers between devices, local(): across = lax.ppermute(tokens, 'tp', chip)  2.59 us
    ppermute x1, waiting for transfers between devices, local(): across = lax.ppermute(tokens, 'tp', chip)  2.14 us
  transfers between devices with their start and end apart: 17, of which 8 were waited for; matrix products, arithmetic and copies ran while one was open for 2% of the time, Pallas kernels for 36%

profile of v4, /device:TPU:0, one launch (start us, length us, event | category | flops | bytes accessed | tf_op | source)
XLA Modules:
  0.0 68.0 jit_solution(2202900687298528281)
XLA Ops:
  0.6 0.5 collective-permute-start.1
  1.1 2.6 %collective-permute-start = (bf16[256,1024]{1,0:T(8,128)(2,1)}, bf16[256,1024]{1,0:T(8,128)(2,1)S(1)}, u32[]{:S(2)}, u32[]{:S(2)}) collective-permute-start(bf16[256,1024]{1,0:T(8,128)(2,1)} %tokens.1), channel_id=1, source_target_pairs={{0,2},{1,3},{2,0},{3,1},{4,6},{5,7},{6,4},{7,5},{8,10},{9,11},{10,... | collective-permute-start | bytes 1572872 | tf_op jit(solution)/shard_map/ppermute | solution.py:435
  3.7 8.4 %load_and_project.1 = (bf16[3,4096,1024]{2,1,0:T(8,128)(2,1)S(1)}, f32[3,256,1024]{2,1,0:T(8,128)S(1)}, f32[256,25]{1,0:T(8,128)S(1)}, f32[24,256]{1,0:T(8,128)S(1)}, bf16[16,128]{1,0:T(8,128)(2,1)S(1)}) custom-call(s32[16]{0:T(128)} %lengths.1, f32[8,256]{1,0:T(8,128)} %bitcast.1, bf16[256,1024]{1,0:T(8,128)(2,1)} %tokens.1, bf16[3,4096,1024]{2,1,0:T(8,128)(2,1)} %w.1), custom_call_target="tpu_custom_call" | custom-call | tf_op jit(solution)/shard_map/load_and_project/pallas_call | solution.py:37
  12.2 0.0 collective-permute-done.1.x
  12.2 2.2 %project_beside.1.acc_in = f32[3,256,1024]{2,1,0:T(8,128)S(1)} custom-call(bf16[256,1024]{1,0:T(8,128)(2,1)S(1)} %collective-permute-done.1.x, bf16[3,4096,1024]{2,1,0:T(8,128)(2,1)S(1)} %get-tuple-element.48.w, f32[3,256,1024]{2,1,0:T(8,128)S(1)} %get-tuple-element.49.acc_in), custom_call_target="tpu_custom_call", output_to_operand_aliasing={{}: (2, {})} | custom-call | tf_op jit(solution)/shard_map/project_beside/pallas_call | solution.py:37
  14.3 2.1 %collective-permute-done.x = bf16[256,1024]{1,0:T(8,128)(2,1)S(1)} collective-permute-done((bf16[256,1024]{1,0:T(8,128)(2,1)}, bf16[256,1024]{1,0:T(8,128)(2,1)S(1)}, u32[]{:S(2)}, u32[]{:S(2)}) %collective-permute-start) | collective-permute-done | bytes 524320 | tf_op jit(solution)/shard_map/ppermute | solution.py:435
  16.5 0.0 collective-permute-start.2
  16.5 2.1 %project_across.1.acc_in = f32[3,256,1024]{2,1,0:T(8,128)S(1)} custom-call(bf16[256,1024]{1,0:T(8,128)(2,1)S(1)} %collective-permute-done.x, bf16[3,4096,1024]{2,1,0:T(8,128)(2,1)S(1)} %get-tuple-element.48.w, f32[3,256,1024]{2,1,0:T(8,128)S(1)} %project_beside.1.acc_in), custom_call_target="tpu_custom_call", output_to_operand_aliasing={{}: (2, {})} | custom-call | tf_op jit(solution)/shard_map/project_across/pallas_call | solution.py:37
  18.6 0.0 collective-permute-done.2.x
  18.6 0.0 copy-start
  18.7 1.7 %project_key_value.1 = (bf16[256,1024]{1,0:T(8,128)(2,1)S(1)}, bf16[256,1024]{1,0:T(8,128)(2,1)S(1)}, f32[4,128,128]{2,1,0:T(8,128)S(1)}, bf16[528,128]{1,0:T(8,128)(2,1)S(1)}) custom-call(bf16[256,1024]{1,0:T(8,128)(2,1)S(1)} %collective-permute-done.2.x, bf16[3,4096,1024]{2,1,0:T(8,128)(2,1)S(1)} %get-tuple-element.48.w, ...), custom_call_target="tpu_custom_call" | custom-call | tf_op jit(solution)/shard_map/project_key_value/pallas_call | solution.py:37
  20.3 1.8 %collective-permute-start.3 = (bf16[528,128]{1,0:T(8,128)(2,1)S(1)}, bf16[528,128]{1,0:T(8,128)(2,1)S(1)}, u32[]{:S(2)}, u32[]{:S(2)}) collective-permute-start(bf16[528,128]{1,0:T(8,128)(2,1)S(1)} %get-tuple-element.66), channel_id=1, source_target_pairs={{0,4},{4,0},{8,12},{12,8},{16,20},{20,16},{24,28},{28,24},{1,5},{5... | collective-permute-start | bytes 405512 | tf_op jit(solution)/shard_map/ppermute | solution.py:475
  22.1 1.2 %project_query.1 = (bf16[256,1024]{1,0:T(8,128)(2,1)S(1)}, f32[4,128,128]{2,1,0:T(8,128)S(1)}, bf16[512,128]{1,0:T(8,128)(2,1)S(1)}) custom-call(bf16[256,1024]{1,0:T(8,128)(2,1)S(1)} %collective-permute-done.2.x, bf16[3,4096,1024]{2,1,0:T(8,128)(2,1)S(1)} %get-tuple-element.48.w, f32[3,256,1024]{2,1,0:T(8,128)S(1)} %project_across.1.acc_in, ...), custom_call_target="tpu_custom_call" | custom-call | tf_op jit(solution)/shard_map/project_query/pallas_call | solution.py:37
  23.3 0.4 collective-permute-start.4
  23.6 5.5 %collective-permute-done.4.got_grad = bf16[512,128]{1,0:T(8,128)(2,1)S(1)} collective-permute-done((bf16[512,128]{1,0:T(8,128)(2,1)S(1)}, bf16[512,128]{1,0:T(8,128)(2,1)S(1)}, u32[]{:S(2)}, u32[]{:S(2)}) %collective-permute-start.4) | collective-permute-done | bytes 131104 | tf_op jit(solution)/shard_map/ppermute | solution.py:484
  29.2 0.2 pair.1
  29.4 2.9 %collective-permute-start.5 = (bf16[528,128]{1,0:T(8,128)(2,1)S(1)}, bf16[528,128]{1,0:T(8,128)(2,1)S(1)}, u32[]{:S(2)}, u32[]{:S(2)}) collective-permute-start(bf16[528,128]{1,0:T(8,128)(2,1)S(1)} %get-tuple-element.73), channel_id=1, source_target_pairs={{0,16},{4,20},{8,24},{12,28},{16,0},{20,4},{24,8},{28,12},{1,17},{... | collective-permute-start | bytes 405512 | tf_op jit(solution)/shard_map/ppermute | solution.py:368
  32.3 0.8 %collective-permute-start.6 = (bf16[528,128]{1,0:T(8,128)(2,1)S(1)}, bf16[528,128]{1,0:T(8,128)(2,1)S(1)}, u32[]{:S(2)}, u32[]{:S(2)}) collective-permute-start(bf16[528,128]{1,0:T(8,128)(2,1)S(1)} %get-tuple-element.74), channel_id=1, source_target_pairs={{8,16},{16,8},{12,20},{20,12},{9,17},{17,9},{13,21},{21,13},{10,18... | collective-permute-start | bytes 405512 | tf_op jit(solution)/shard_map/ppermute | solution.py:369
  33.1 2.9 %collective-permute-start.7 = (bf16[528,128]{1,0:T(8,128)(2,1)S(1)}, bf16[528,128]{1,0:T(8,128)(2,1)S(1)}, u32[]{:S(2)}, u32[]{:S(2)}) collective-permute-start(bf16[528,128]{1,0:T(8,128)(2,1)S(1)} %get-tuple-element.75), channel_id=1, source_target_pairs={{0,8},{4,12},{8,0},{12,4},{16,24},{20,28},{24,16},{28,20},{1,9},{5... | collective-permute-start | bytes 405512 | tf_op jit(solution)/shard_map/ppermute | solution.py:370
  36.0 3.6 %intra.1 = (f32[256,1024]{1,0:T(8,128)S(1)}, f32[256,1024]{1,0:T(8,128)S(1)}, f32[256,1024]{1,0:T(8,128)S(1)}, f32[256,1024]{1,0:T(8,128)S(1)}) custom-call(bf16[256,1024]{1,0:T(8,128)(2,1)S(1)} %get-tuple-element.59.query, bf16[256,1024]{1,0:T(8,128)(2,1)S(1)} %get-tuple-element.54.key, bf16[256,1024]{1,0:T(8,128)(2,1)S(1)} %get-tuple-element.55.value, ...), custom_call_target="tpu_custom_call" | custom-call | flops 1073741824 | tf_op jit(solution)/shard_map/intra/pallas_call | solution.py:37
  39.6 0.1 collective-permute-done.5.far
  39.7 0.0 collective-permute-done.6.middle
  39.7 1.2 %collective-permute-done.7.near = bf16[528,128]{1,0:T(8,128)(2,1)S(1)} collective-permute-done((bf16[528,128]{1,0:T(8,128)(2,1)S(1)}, bf16[528,128]{1,0:T(8,128)(2,1)S(1)}, u32[]{:S(2)}, u32[]{:S(2)}) %collective-permute-start.7) | collective-permute-done | bytes 135200 | tf_op jit(solution)/shard_map/ppermute | solution.py:370
  40.9 0.3 spread.1
  41.2 1.6 %collective-permute-start.8 = (bf16[2,4,128,128]{3,2,1,0:T(8,128)(2,1)S(1)}, bf16[2,4,128,128]{3,2,1,0:T(8,128)(2,1)S(1)}, u32[]{:S(2)}, u32[]{:S(2)}) collective-permute-start(bf16[2,4,128,128]{3,2,1,0:T(8,128)(2,1)S(1)} %get-tuple-element.78), channel_id=1, source_target_pairs={{0,4},{4,0},{8,12},{12,8},{16,20},{20,16},{24,28},{28,24},{1,5},{5... | collective-permute-start | bytes 786440 | tf_op jit(solution)/shard_map/ppermute | solution.py:376
  42.8 2.4 %back_kept.1 = (bf16[3,256,512]{2,1,0:T(8,128)(2,1)S(1)}, f32[256,1024]{1,0:T(8,128)S(1)}, f32[256,1024]{1,0:T(8,128)S(1)}) custom-call(bf16[256,1024]{1,0:T(8,128)(2,1)S(1)} %get-tuple-element.54.key, bf16[256,1024]{1,0:T(8,128)(2,1)S(1)} %get-tuple-element.55.value, bf16[256,1024]{1,0:T(8,128)(2,1)S(1)} %copy-done, ...), custom_call_target="tpu_custom_call" | custom-call | tf_op jit(solution)/shard_map/back_kept/pallas_call | solution.py:37
  45.2 3.6 %collective-permute-done.8.passed = bf16[2,4,128,128]{3,2,1,0:T(8,128)(2,1)S(1)} collective-permute-done((bf16[2,4,128,128]{3,2,1,0:T(8,128)(2,1)S(1)}, bf16[2,4,128,128]{3,2,1,0:T(8,128)(2,1)S(1)}, u32[]{:S(2)}, u32[]{:S(2)}) %collective-permute-start.8) | collective-permute-done | bytes 262176 | tf_op jit(solution)/shard_map/ppermute | solution.py:376
  48.9 1.6 %back_first.1 = (bf16[3,256,512]{2,1,0:T(8,128)(2,1)S(1)}, bf16[256,512]{1,0:T(8,128)(2,1)S(1)}, bf16[256,512]{1,0:T(8,128)(2,1)S(1)}) custom-call(bf16[256,1024]{1,0:T(8,128)(2,1)S(1)} %get-tuple-element.54.key, bf16[256,1024]{1,0:T(8,128)(2,1)S(1)} %get-tuple-element.55.value, bf16[256,1024]{1,0:T(8,128)(2,1)S(1)} %copy-done, ...), custom_call_target="tpu_custom_call" | custom-call | tf_op jit(solution)/shard_map/back_first/pallas_call | solution.py:37
  50.5 0.1 collective-permute-start.9
  50.6 0.5 collective-permute-start.10
  51.1 0.6 back_second_a.1
  51.7 0.4 collective-permute-done.9
  52.1 0.1 add_convert_fusion.1
  52.2 0.6 back_second_b.1
  52.8 1.6 %collective-permute-start.11 = (bf16[256,512]{1,0:T(8,128)(2,1)S(1)}, bf16[256,512]{1,0:T(8,128)(2,1)S(1)}, u32[]{:S(2)}, u32[]{:S(2)}) collective-permute-start(bf16[256,512]{1,0:T(8,128)(2,1)S(1)} %add_convert_fusion.1), channel_id=1, source_target_pairs={{0,2},{1,3},{2,0},{3,1},{4,6},{5,7},{6,4},{7,5},{8,10},{9,11},{10,... | collective-permute-start | bytes 786440 | tf_op jit(solution)/shard_map/ppermute | solution.py:509
  54.4 0.1 add_convert_fusion
  54.5 0.5 collective-permute-start.12
  55.0 3.6 %back_rest.1 = (f32[256,1024]{1,0:T(8,128)S(1)}, bf16[256,1024]{1,0:T(8,128)(2,1)S(1)}, f32[256,1024]{1,0:T(8,128)S(1)}) custom-call(bf16[3,256,512]{2,1,0:T(8,128)(2,1)S(1)} %get-tuple-element.77.kept_stack, bf16[3,256,512]{2,1,0:T(8,128)(2,1)S(1)} %get-tuple-element.85.stack, bf16[3,4096,1024]{2,1,0:T(8,128)(2,1)S(1)} %get-tuple-element.48.w, ...), custom_call_target="tpu_custom_call" | custom-call | tf_op jit(solution)/shard_map/back_rest/pallas_call | solution.py:37
  58.6 1.0 %copy.17 = f32[256,1024]{1,0:T(8,128)} copy(f32[256,1024]{1,0:T(8,128)S(1)} %get-tuple-element.98) | data formatting | bytes 2097152
  59.6 0.1 collective-permute-start.13
  59.7 0.5 collective-permute-start.16
  60.2 0.1 collective-permute-start.15
  60.3 1.7 %collective-permute-done.11.refs_0_ = bf16[256,512]{1,0:T(8,128)(2,1)S(1)} collective-permute-done((bf16[256,512]{1,0:T(8,128)(2,1)S(1)}, bf16[256,512]{1,0:T(8,128)(2,1)S(1)}, u32[]{:S(2)}, u32[]{:S(2)}) %collective-permute-start.11) | collective-permute-done | bytes 262176 | tf_op jit(solution)/shard_map/ppermute | solution.py:509
  62.0 4.8 %collective-permute-done.12.refs_1_ = bf16[256,512]{1,0:T(8,128)(2,1)S(1)} collective-permute-done((bf16[256,512]{1,0:T(8,128)(2,1)S(1)}, bf16[256,512]{1,0:T(8,128)(2,1)S(1)}, u32[]{:S(2)}, u32[]{:S(2)}) %collective-permute-start.12) | collective-permute-done | bytes 262176 | tf_op jit(solution)/shard_map/ppermute | solution.py:513
  66.8 0.0 collective-permute-done.13
  66.8 0.0 collective-permute-done.16
  66.8 0.0 collective-permute-done.15
  66.8 1.2 %convert_add_fusion = f32[256,1024]{1,0:T(8,128)} fusion(f32[256,1024]{1,0:T(8,128)S(1)} %get-tuple-element.92, bf16[256,512]{1,0:T(8,128)(2,1)S(1)} %get-tuple-element.91, bf16[256,512]{1,0:T(8,128)(2,1)S(1)} %get-tuple-element.90, bf16[64,1024]{1,0:T(8,128)(2,1)S(1)} %collective-permute-done.16, bf16[64,1024]{1,0:T(8,128)(2,1)S(1)} %collective-permute-done.15, ...), kind=kLoop, calls=%fused_computation | loop fusion | flops 3670016 | bytes 3145728 | tf_op jit(solution)/shard_map/add | solution.py:533
  (8 shorter events, 0.0 us)
Async XLA Ops:
  0.6 11.5 %collective-permute-start.1 = (bf16[256,1024]{1,0:T(8,128)(2,1)}, bf16[256,1024]{1,0:T(8,128)(2,1)S(1)}, u32[]{:S(2)}, u32[]{:S(2)}) collective-permute-start(bf16[256,1024]{1,0:T(8,128)(2,1)} %tokens.1), channel_id=1, source_target_pairs={{0,1},{1,0},{2,3},{3,2},{4,5},{5,4},{6,7},{7,6},{8,9},{9,8},{10,11... | collective-permute-start | bytes 1572872 | tf_op jit(solution)/shard_map/ppermute | solution.py:436
  1.1 15.3 %collective-permute-start = (bf16[256,1024]{1,0:T(8,128)(2,1)}, bf16[256,1024]{1,0:T(8,128)(2,1)S(1)}, u32[]{:S(2)}, u32[]{:S(2)}) collective-permute-start(bf16[256,1024]{1,0:T(8,128)(2,1)} %tokens.1), channel_id=1, source_target_pairs={{0,2},{1,3},{2,0},{3,1},{4,6},{5,7},{6,4},{7,5},{8,10},{9,11},{10,... | collective-permute-start | bytes 1572872 | tf_op jit(solution)/shard_map/ppermute | solution.py:435
  16.5 2.2 %collective-permute-start.2 = (bf16[256,1024]{1,0:T(8,128)(2,1)S(1)}, bf16[256,1024]{1,0:T(8,128)(2,1)S(1)}, u32[]{:S(2)}, u32[]{:S(2)}) collective-permute-start(bf16[256,1024]{1,0:T(8,128)(2,1)S(1)} %collective-permute-done.x), channel_id=1, source_target_pairs={{0,1},{1,0},{2,3},{3,2},{4,5},{5,4},{6,7},{7,6},{8,9},{9,8},{10,11... | collective-permute-start | bytes 1572872 | tf_op jit(solution)/shard_map/ppermute | solution.py:458
  18.6 3.5 %copy-start = (bf16[256,1024]{1,0:T(8,128)(2,1)S(1)}, bf16[256,1024]{1,0:T(8,128)(2,1)}, u32[]{:S(2)}) copy-start(bf16[256,1024]{1,0:T(8,128)(2,1)} %grads.7) | copy-start | bytes 1572868
  20.3 8.9 %collective-permute-start.3 = (bf16[528,128]{1,0:T(8,128)(2,1)S(1)}, bf16[528,128]{1,0:T(8,128)(2,1)S(1)}, u32[]{:S(2)}, u32[]{:S(2)}) collective-permute-start(bf16[528,128]{1,0:T(8,128)(2,1)S(1)} %get-tuple-element.66), channel_id=1, source_target_pairs={{0,4},{4,0},{8,12},{12,8},{16,20},{20,16},{24,28},{28,24},{1,5},{5... | collective-permute-start | bytes 405512 | tf_op jit(solution)/shard_map/ppermute | solution.py:475
  23.3 5.9 %collective-permute-start.4 = (bf16[512,128]{1,0:T(8,128)(2,1)S(1)}, bf16[512,128]{1,0:T(8,128)(2,1)S(1)}, u32[]{:S(2)}, u32[]{:S(2)}) collective-permute-start(bf16[512,128]{1,0:T(8,128)(2,1)S(1)} %get-tuple-element.67), channel_id=1, source_target_pairs={{0,4},{4,0},{8,12},{12,8},{16,20},{20,16},{24,28},{28,24},{1,5},{5... | collective-permute-start | bytes 393224 | tf_op jit(solution)/shard_map/ppermute | solution.py:484
  29.4 10.3 %collective-permute-start.5 = (bf16[528,128]{1,0:T(8,128)(2,1)S(1)}, bf16[528,128]{1,0:T(8,128)(2,1)S(1)}, u32[]{:S(2)}, u32[]{:S(2)}) collective-permute-start(bf16[528,128]{1,0:T(8,128)(2,1)S(1)} %get-tuple-element.73), channel_id=1, source_target_pairs={{0,16},{4,20},{8,24},{12,28},{16,0},{20,4},{24,8},{28,12},{1,17},{... | collective-permute-start | bytes 405512 | tf_op jit(solution)/shard_map/ppermute | solution.py:368
  32.3 7.4 %collective-permute-start.6 = (bf16[528,128]{1,0:T(8,128)(2,1)S(1)}, bf16[528,128]{1,0:T(8,128)(2,1)S(1)}, u32[]{:S(2)}, u32[]{:S(2)}) collective-permute-start(bf16[528,128]{1,0:T(8,128)(2,1)S(1)} %get-tuple-element.74), channel_id=1, source_target_pairs={{8,16},{16,8},{12,20},{20,12},{9,17},{17,9},{13,21},{21,13},{10,18... | collective-permute-start | bytes 405512 | tf_op jit(solution)/shard_map/ppermute | solution.py:369
  33.1 7.8 %collective-permute-start.7 = (bf16[528,128]{1,0:T(8,128)(2,1)S(1)}, bf16[528,128]{1,0:T(8,128)(2,1)S(1)}, u32[]{:S(2)}, u32[]{:S(2)}) collective-permute-start(bf16[528,128]{1,0:T(8,128)(2,1)S(1)} %get-tuple-element.75), channel_id=1, source_target_pairs={{0,8},{4,12},{8,0},{12,4},{16,24},{20,28},{24,16},{28,20},{1,9},{5... | collective-permute-start | bytes 405512 | tf_op jit(solution)/shard_map/ppermute | solution.py:370
  41.2 7.7 %collective-permute-start.8 = (bf16[2,4,128,128]{3,2,1,0:T(8,128)(2,1)S(1)}, bf16[2,4,128,128]{3,2,1,0:T(8,128)(2,1)S(1)}, u32[]{:S(2)}, u32[]{:S(2)}) collective-permute-start(bf16[2,4,128,128]{3,2,1,0:T(8,128)(2,1)S(1)} %get-tuple-element.78), channel_id=1, source_target_pairs={{0,4},{4,0},{8,12},{12,8},{16,20},{20,16},{24,28},{28,24},{1,5},{5... | collective-permute-start | bytes 786440 | tf_op jit(solution)/shard_map/ppermute | solution.py:376
  50.5 1.6 %collective-permute-start.9 = (bf16[256,512]{1,0:T(8,128)(2,1)S(1)}, bf16[256,512]{1,0:T(8,128)(2,1)S(1)}, u32[]{:S(2)}, u32[]{:S(2)}) collective-permute-start(bf16[256,512]{1,0:T(8,128)(2,1)S(1)} %get-tuple-element.82), channel_id=1, source_target_pairs={{0,1},{1,0},{2,3},{3,2},{4,5},{5,4},{6,7},{7,6},{8,9},{9,8},{10,11... | collective-permute-start | bytes 786440 | tf_op jit(solution)/shard_map/ppermute | solution.py:504
  50.6 3.9 %collective-permute-start.10 = (bf16[256,512]{1,0:T(8,128)(2,1)S(1)}, bf16[256,512]{1,0:T(8,128)(2,1)S(1)}, u32[]{:S(2)}, u32[]{:S(2)}) collective-permute-start(bf16[256,512]{1,0:T(8,128)(2,1)S(1)} %get-tuple-element.84), channel_id=1, source_target_pairs={{0,1},{1,0},{2,3},{3,2},{4,5},{5,4},{6,7},{7,6},{8,9},{9,8},{10,11... | collective-permute-start | bytes 786440 | tf_op jit(solution)/shard_map/ppermute | solution.py:505
  52.8 9.2 %collective-permute-start.11 = (bf16[256,512]{1,0:T(8,128)(2,1)S(1)}, bf16[256,512]{1,0:T(8,128)(2,1)S(1)}, u32[]{:S(2)}, u32[]{:S(2)}) collective-permute-start(bf16[256,512]{1,0:T(8,128)(2,1)S(1)} %add_convert_fusion.1), channel_id=1, source_target_pairs={{0,2},{1,3},{2,0},{3,1},{4,6},{5,7},{6,4},{7,5},{8,10},{9,11},{10,... | collective-permute-start | bytes 786440 | tf_op jit(solution)/shard_map/ppermute | solution.py:509
  54.5 12.3 %collective-permute-start.12 = (bf16[256,512]{1,0:T(8,128)(2,1)S(1)}, bf16[256,512]{1,0:T(8,128)(2,1)S(1)}, u32[]{:S(2)}, u32[]{:S(2)}) collective-permute-start(bf16[256,512]{1,0:T(8,128)(2,1)S(1)} %add_convert_fusion), channel_id=1, source_target_pairs={{0,2},{1,3},{2,0},{3,1},{4,6},{5,7},{6,4},{7,5},{8,10},{9,11},{10,... | collective-permute-start | bytes 786440 | tf_op jit(solution)/shard_map/ppermute | solution.py:513
  59.6 7.2 %collective-permute-start.13 = (bf16[64,1024]{1,0:T(8,128)(2,1)S(1)}, bf16[64,1024]{1,0:T(8,128)(2,1)S(1)}, u32[]{:S(2)}, u32[]{:S(2)}) collective-permute-start(bf16[64,1024]{1,0:T(8,128)(2,1)S(1)} %get-tuple-element.94), channel_id=1, source_target_pairs={{0,1},{1,0},{2,3},{3,2},{4,5},{5,4},{6,7},{7,6},{8,9},{9,8},{10,11... | collective-permute-start | bytes 393224 | tf_op jit(solution)/shard_map/ppermute | solution.py:520
  59.7 7.1 %collective-permute-start.16 = (bf16[64,1024]{1,0:T(8,128)(2,1)S(1)}, bf16[64,1024]{1,0:T(8,128)(2,1)S(1)}, u32[]{:S(2)}, u32[]{:S(2)}) collective-permute-start(bf16[64,1024]{1,0:T(8,128)(2,1)S(1)} %get-tuple-element.95), channel_id=1, source_target_pairs={{0,1},{1,0},{2,3},{3,2},{4,5},{5,4},{6,7},{7,6},{8,9},{9,8},{10,11... | collective-permute-start | bytes 393224 | tf_op jit(solution)/shard_map/ppermute | solution.py:520
  60.2 6.6 %collective-permute-start.15 = (bf16[64,1024]{1,0:T(8,128)(2,1)S(1)}, bf16[64,1024]{1,0:T(8,128)(2,1)S(1)}, u32[]{:S(2)}, u32[]{:S(2)}) collective-permute-start(bf16[64,1024]{1,0:T(8,128)(2,1)S(1)} %get-tuple-element.96), channel_id=1, source_target_pairs={{0,1},{1,0},{2,3},{3,2},{4,5},{5,4},{6,7},{7,6},{8,9},{9,8},{10,11... | collective-permute-start | bytes 393224 | tf_op jit(solution)/shard_map/ppermute | solution.py:520
  62.0 4.8 %collective-permute-start.14 = (bf16[64,1024]{1,0:T(8,128)(2,1)S(1)}, bf16[64,1024]{1,0:T(8,128)(2,1)S(1)}, u32[]{:S(2)}, u32[]{:S(2)}) collective-permute-start(bf16[64,1024]{1,0:T(8,128)(2,1)S(1)} %get-tuple-element.97), channel_id=1, source_target_pairs={{0,1},{1,0},{2,3},{3,2},{4,5},{5,4},{6,7},{7,6},{8,9},{9,8},{10,11... | collective-permute-start | bytes 393224 | tf_op jit(solution)/shard_map/ppermute | solution.py:520

commit v5 on v4

--- a/solution.py
+++ b/solution.py
@@ -27,7 +27,7 @@
     return dot(high, b, ca, cb) + dot(low, b, ca, cb)
 
 
-def call(kernel, name, outs, args, spaces=None, flops=0, limit=4, aliases=None, scratch=()):
+def call(kernel, name, outs, args, spaces=None, flops=0, limit=4, aliases=None, scratch=(), out_space=pltpu.VMEM):
     spaces = spaces or "v" * len(args)
     kinds = {"v": pltpu.VMEM, "s": pltpu.SMEM, "h": pltpu.HBM}
     placed = [
@@ -37,9 +37,9 @@
     return pl.pallas_call(
         kernel,
         name=name,
-        out_shape=[pltpu.VMEM(shape, dtype) for shape, dtype in outs],
+        out_shape=[out_space(shape, dtype) for shape, dtype in outs],
         in_specs=[pl.BlockSpec(memory_space=kinds[s]) for s in spaces],
-        out_specs=[pl.BlockSpec(memory_space=pltpu.VMEM)] * len(outs),
+        out_specs=[pl.BlockSpec(memory_space=out_space)] * len(outs),
         input_output_aliases=aliases or {},
         scratch_shapes=scratch,
         compiler_params=pltpu.CompilerParams(vmem_limit_bytes=limit * MIB),
@@ -128,28 +128,36 @@
         copy.wait()
 
 
-def project_more(which, x, w, acc_in, acc):
-    part = x.shape[1]
+def project_chunks(pieces, *refs):
+    xs, (w, acc_in, acc) = refs[: len(pieces)], refs[len(pieces) :]
     for m in range(3):
         for cols in tiles(w.shape[2]):
-            acc[m, :, cols] = acc_in[m, :, cols] + dot(x[...], w[m, rows_of(which, part), cols], 1, 0)
-
-
-def project_last(m, x, w, acc_in, out):
-    part = x.shape[1]
+            acc[m, :, cols] = acc_in[m, :, cols] + products(pieces, xs, w, m, cols)
+
+
+def products(pieces, xs, w, m, cols):
+    part = w.shape[1] // 4
+    total = None
+    for (which, offset), x in zip(pieces, xs):
+        term = dot(x[...], w[m, rows_of(which, part, offset, x.shape[1]), cols], 1, 0)
+        total = term if total is None else total + term
+    return total
+
+
+def project_last(piece, m, x, w, acc_in, out):
     for cols in tiles(w.shape[2]):
-        out[:, cols] = (acc_in[m, :, cols] + dot(x[...], w[m, rows_of(3, part), cols], 1, 0)).astype(BF16)
-
-
-def project_key_value(x, w, acc_in, rows_h, through, key, value, mine, message, states):
-    project_last(1, x, w, acc_in, key)
-    project_last(2, x, w, acc_in, value)
+        out[:, cols] = (acc_in[m, :, cols] + products([piece], [x], w, m, cols)).astype(BF16)
+
+
+def project_key_value(piece, x, w, acc_in, rows_h, through, key, value, mine, message, states):
+    project_last(piece, 1, x, w, acc_in, key)
+    project_last(piece, 2, x, w, acc_in, value)
     hand_out(lambda h: state_end(key, value, rows_h, h), states, mine, message)
     message[mine.shape[0] * DH :, :] = through[...]
 
 
-def project_query(x, w, acc_in, rows_h, grads, query, mine, message, states):
-    project_last(0, x, w, acc_in, query)
+def project_query(piece, x, w, acc_in, rows_h, grads, query, mine, message, states):
+    project_last(piece, 0, x, w, acc_in, query)
     hand_out(lambda h: grad_start(query, grads, rows_h, h), states, mine, message)
 
 
@@ -263,22 +271,34 @@
     back(2, [(stack, heads)], w, start2)
 
 
-def back_first(key, value, grads, cols_h, gq, gk, gv, passed, w, start3, stack, chunk_a, chunk_b):
+def back_first(key, value, grads, cols_h, gq, gk, gv, passed, w, start3, stack, chunk3_a):
     heads = finish_half(False, key, value, grads, cols_h, gq, gk, gv, passed, stack)
-    back(3, [(stack, heads)], w, chunk_a, 0, start3)
-    back(3, [(stack, heads)], w, chunk_b, chunk_a.shape[1], start3)
-
-
-def back_second_a(stack, w, start2, chunk):
-    back(2, [(stack, half_columns(False, w))], w, chunk, 0, start2)
-
-
-def back_second_b(stack, w, start2, chunk):
-    back(2, [(stack, half_columns(False, w))], w, chunk, w.shape[1] // 4 - chunk.shape[1], start2)
+    back(3, [(stack, heads)], w, chunk3_a, 0, start3)
+
+
+def back_second(stack, w, start3, start2, chunk3_b, chunk2_a, chunk2_b):
+    stacks = [(stack, half_columns(False, w))]
+    back(3, stacks, w, chunk3_b, start3.shape[1] - chunk3_b.shape[1], start3)
+    back(2, stacks, w, chunk2_a, 0, start2)
+    back(2, stacks, w, chunk2_b, chunk2_a.shape[1], start2)
 
 
 def hand_on(*refs):
     pass
+
+
+def last_sum(own, across_a, across_b, *refs):
+    besides, (out, total, sems) = refs[:-3], refs[-3:]
+    size, middle = besides[0].shape[0], across_a.shape[1]
+    copies = []
+    for i, beside in enumerate(besides):
+        rows = slice(i * size, (i + 1) * size)
+        for cols, across in ((slice(0, middle), across_a), (slice(middle, own.shape[1]), across_b)):
+            total[rows, cols] = (own[rows, cols] + beside[:, cols].astype(F32)) + across[rows, :].astype(F32)
+        copies.append(pltpu.make_async_copy(total.at[rows, :], out.at[rows, :], sems.at[i]))
+        copies[-1].start()
+    for copy in copies:
+        copy.wait()
 
 
 def back_rest(kept_stack, stack, w, query, cols_h, out, kept, passed, attn, chunk_other, chunk_own):
@@ -440,6 +460,7 @@
         [(w_qkv.shape, BF16), ((3, length, width), F32)] + decays,
         [doc_lengths, forget, tokens, w_qkv],
         "hhhh",
+        flops=8 * step_flops,
         scratch=[
             pltpu.SMEM(doc_lengths.shape, jnp.int32),
             pltpu.VMEM(forget.shape, F32),
@@ -447,26 +468,20 @@
             pltpu.SemaphoreType.DMA((tps + 3,)),
         ],
     )
-    (acc,) = call(
-        functools.partial(project_more, 1),
-        "project_beside",
-        [(acc.shape, F32)],
-        [beside, w_vm, acc],
-        aliases={2: 0},
-    )
+
+    def project(name, acc, *pieces):
+        kernel = functools.partial(project_chunks, [place for place, _ in pieces])
+        return call(kernel, name, [(acc.shape, F32)], [x for _, x in pieces] + [w_vm, acc])[0]
+
+    acc = project("project_beside", acc, ((1, 0), beside))
     across, acc = lax.optimization_barrier((across, acc))
     across_beside = lax.ppermute(across, "tp", core)
-    (acc,) = call(
-        functools.partial(project_more, 2),
-        "project_across",
-        [(acc.shape, F32)],
-        [across, w_vm, acc],
-        aliases={2: 0},
-    )
+    acc = project("project_across", acc, ((2, 0), across))
+    last = (3, 0)
     states_scratch = [pltpu.VMEM((heads, DH, DH), F32)]
     mine_shape = ((half, DH, DH), F32)
     key, value, my_state, message = call(
-        project_key_value,
+        functools.partial(project_key_value, last),
         "project_key_value",
         [rows_shape, rows_shape, mine_shape, ((half * DH + through.shape[0], DH), BF16)],
         [across_beside, w_vm, acc, rows_h, through],
@@ -475,7 +490,7 @@
     got_state = lax.ppermute(message, "seq", MATE)
     acc, my_state = lax.optimization_barrier((acc, my_state))
     query, my_grad, message = call(
-        project_query,
+        functools.partial(project_query, last),
         "project_query",
         [rows_shape, mine_shape, ((half * DH, DH), BF16)],
         [across_beside, w_vm, acc, rows_h, out_grad],
@@ -495,19 +510,20 @@
     kept_stack, start3, start2 = call(
         back_kept, "back_kept", [stack_shape, chunk_shape, chunk_shape], common + [kept, w_vm]
     )
-    stack, chunk_a, chunk_b = call(
-        back_first,
-        "back_first",
-        [stack_shape, ((length, part_a), BF16), ((length, part_b), BF16)],
-        common + [passed, w_vm, start3],
-    )
-    beside_a = lax.ppermute(chunk_a, "tp", core)
-    beside_b = lax.ppermute(chunk_b, "tp", core)
-    (chunk_a,) = call(back_second_a, "back_second_a", [((length, part_a), F32)], [stack, w_vm, start2])
+    stack, chunk3_a = call(
+        back_first, "back_first", [stack_shape, ((length, part_a), BF16)], common + [passed, w_vm, start3]
+    )
+    beside_a = lax.ppermute(chunk3_a, "tp", core)
+    chunk3_b, chunk_a, chunk_b = call(
+        back_second,
+        "back_second",
+        [((length, part_b), BF16), ((length, part_a), F32), ((length, part_b), F32)],
+        [stack, w_vm, start3, start2],
+    )
+    beside_b = lax.ppermute(chunk3_b, "tp", core)
     chunk_a = (chunk_a + beside_a.astype(F32)).astype(BF16)
-    chunk_a, stack = lax.optimization_barrier((chunk_a, stack))
+    chunk_a, chunk_b = lax.optimization_barrier((chunk_a, chunk_b))
     across_a = lax.ppermute(chunk_a, "tp", chip)
-    (chunk_b,) = call(back_second_b, "back_second_b", [((length, part_b), F32)], [stack, w_vm, start2])
     chunk_b = (chunk_b + beside_b.astype(F32)).astype(BF16)
     chunk_b, stack = lax.optimization_barrier((chunk_b, stack))
     across_b = lax.ppermute(chunk_b, "tp", chip)
@@ -529,8 +545,14 @@
             flops=8 * step_flops if more else 0,
             aliases={i: i for i in range(len(across))},
         )
-    across = jnp.concatenate(across, axis=1)
-    input_grad = (across.astype(F32) + chunk_own) + jnp.concatenate(beside).astype(F32)
+    (input_grad,) = call(
+        last_sum,
+        "last_sum",
+        [chunk_shape],
+        [chunk_own] + list(across) + beside,
+        out_space=pltpu.HBM,
+        scratch=[pltpu.VMEM(chunk_shape[0], F32), pltpu.SemaphoreType.DMA((len(beside),))],
+    )
     return attn, input_grad
 
 

time: 68.2 us -> 66.5 us (0.975)
  waiting for transfers between devices: 19.6 us -> 18.3 us
  other arithmetic: 1.34 us -> 0.14 us
    add x1 -> x0, other arithmetic: 1.21 us -> none  [local(): across.astype(F32) + chunk_own + jnp.concatenate(beside).astype(F32)]
  transfers between devices with their start and end apart: 17 -> 17, of which waited for: 8 -> 8; matrix products, arithmetic and copies ran while one was open for 2% -> 2% of each run, Pallas kernels for 36% -> 37%
where the time goes in v5:
time: 66.5 us; the launch traced here: 66.3 us
  Pallas kernels  28.6 us (43%)
  waiting for transfers between devices  18.3 us (28%)
  starting transfers between devices  17.3 us (26%)
  local copies, waits for them, and re-layouts  1.01 us (2%)
  between operations  0.93 us (1%)
    pallas_call x15, Pallas kernels, call(): pl.pallas_call(kernel, name=name, out_shape=[out_space(shape, dtype) for...  28.6 us
    ppermute x1, waiting for transfers between devices, local(): got_grad = lax.ppermute(message, 'seq', MATE)  5.47 us
    ppermute x1, waiting for transfers between devices, local(): across_b = lax.ppermute(chunk_b, 'tp', chip)  4.69 us
    ppermute x1, waiting for transfers between devices, states_direct(): return (kept, lax.ppermute(passed, 'seq', MATE), inside)  3.72 us
    ppermute x1, starting transfers between devices, local(): across = lax.ppermute(tokens, 'tp', chip)  3.03 us
    ppermute x1, starting transfers between devices, states_direct(): from_near = lax.ppermute(to_near, 'seq', NEAR)  2.89 us
    ppermute x1, starting transfers between devices, states_direct(): from_far = lax.ppermute(to_far, 'seq', FAR)  2.88 us
    ppermute x1, waiting for transfers between devices, local(): across = lax.ppermute(tokens, 'tp', chip)  1.89 us
  transfers between devices with their start and end apart: 17, of which 8 were waited for; matrix products, arithmetic and copies ran while one was open for 2% of the time, Pallas kernels for 37%

profile of v5, /device:TPU:0, one launch (start us, length us, event | category | flops | bytes accessed | tf_op | source)
XLA Modules:
  0.0 66.3 jit_solution(14296330379974870605)
XLA Ops:
  0.6 3.0 %collective-permute-start = (bf16[256,1024]{1,0:T(8,128)(2,1)}, bf16[256,1024]{1,0:T(8,128)(2,1)S(1)}, u32[]{:S(2)}, u32[]{:S(2)}) collective-permute-start(bf16[256,1024]{1,0:T(8,128)(2,1)} %tokens.1), channel_id=1, source_target_pairs={{0,2},{1,3},{2,0},{3,1},{4,6},{5,7},{6,4},{7,5},{8,10},{9,11},{10,... | collective-permute-start | bytes 1572872 | tf_op jit(solution)/shard_map/ppermute | solution.py:455
  3.7 0.0 collective-permute-start.1
  3.7 8.4 %load_and_project.1 = (bf16[3,4096,1024]{2,1,0:T(8,128)(2,1)S(1)}, f32[3,256,1024]{2,1,0:T(8,128)S(1)}, f32[256,25]{1,0:T(8,128)S(1)}, f32[24,256]{1,0:T(8,128)S(1)}, bf16[16,128]{1,0:T(8,128)(2,1)S(1)}) custom-call(s32[16]{0:T(128)} %lengths.1, f32[8,256]{1,0:T(8,128)} %bitcast.1, bf16[256,1024]{1,0:T(8,128)(2,1)} %tokens.1, bf16[3,4096,1024]{2,1,0:T(8,128)(2,1)} %w.1), custom_call_target="tpu_custom_call" | custom-call | flops 12884901888 | tf_op jit(solution)/shard_map/load_and_project/pallas_call | solution.py:37
  12.1 0.0 collective-permute-done.1.refs_0_
  12.1 1.8 %project_beside.1.refs_2_ = f32[3,256,1024]{2,1,0:T(8,128)S(1)} custom-call(bf16[256,1024]{1,0:T(8,128)(2,1)S(1)} %collective-permute-done.1.refs_0_, bf16[3,4096,1024]{2,1,0:T(8,128)(2,1)S(1)} %get-tuple-element.50.refs_1_.w, f32[3,256,1024]{2,1,0:T(8,128)S(1)} %get-tuple-element.51.refs_2_), custom_call_target="tpu_custom_call" | custom-call | tf_op jit(solution)/shard_map/project_beside/pallas_call | solution.py:37
  13.9 1.9 %collective-permute-done.refs_0_ = bf16[256,1024]{1,0:T(8,128)(2,1)S(1)} collective-permute-done((bf16[256,1024]{1,0:T(8,128)(2,1)}, bf16[256,1024]{1,0:T(8,128)(2,1)S(1)}, u32[]{:S(2)}, u32[]{:S(2)}) %collective-permute-start) | collective-permute-done | bytes 524320 | tf_op jit(solution)/shard_map/ppermute | solution.py:455
  15.8 0.0 collective-permute-start.2
  15.8 1.8 %project_across.1.acc_in = f32[3,256,1024]{2,1,0:T(8,128)S(1)} custom-call(bf16[256,1024]{1,0:T(8,128)(2,1)S(1)} %collective-permute-done.refs_0_, bf16[3,4096,1024]{2,1,0:T(8,128)(2,1)S(1)} %get-tuple-element.50.refs_1_.w, f32[3,256,1024]{2,1,0:T(8,128)S(1)} %project_beside.1.refs_2_), custom_call_target="tpu_custom_call" | custom-call | tf_op jit(solution)/shard_map/project_across/pallas_call | solution.py:37
  17.6 0.1 collective-permute-done.2.x
  17.7 1.6 %project_key_value.1 = (bf16[256,1024]{1,0:T(8,128)(2,1)S(1)}, bf16[256,1024]{1,0:T(8,128)(2,1)S(1)}, f32[4,128,128]{2,1,0:T(8,128)S(1)}, bf16[528,128]{1,0:T(8,128)(2,1)S(1)}) custom-call(bf16[256,1024]{1,0:T(8,128)(2,1)S(1)} %collective-permute-done.2.x, bf16[3,4096,1024]{2,1,0:T(8,128)(2,1)S(1)} %get-tuple-element.50.refs_1_.w, ...), custom_call_target="tpu_custom_call" | custom-call | tf_op jit(solution)/shard_map/project_key_value/pallas_call | solution.py:37
  19.4 1.8 %collective-permute-start.3 = (bf16[528,128]{1,0:T(8,128)(2,1)S(1)}, bf16[528,128]{1,0:T(8,128)(2,1)S(1)}, u32[]{:S(2)}, u32[]{:S(2)}) collective-permute-start(bf16[528,128]{1,0:T(8,128)(2,1)S(1)} %get-tuple-element.68), channel_id=1, source_target_pairs={{0,4},{4,0},{8,12},{12,8},{16,20},{20,16},{24,28},{28,24},{1,5},{5... | collective-permute-start | bytes 405512 | tf_op jit(solution)/shard_map/ppermute | solution.py:490
  21.1 1.2 %project_query.1 = (bf16[256,1024]{1,0:T(8,128)(2,1)S(1)}, f32[4,128,128]{2,1,0:T(8,128)S(1)}, bf16[512,128]{1,0:T(8,128)(2,1)S(1)}) custom-call(bf16[256,1024]{1,0:T(8,128)(2,1)S(1)} %collective-permute-done.2.x, bf16[3,4096,1024]{2,1,0:T(8,128)(2,1)S(1)} %get-tuple-element.50.refs_1_.w, f32[3,256,1024]{2,1,0:T(8,128)S(1)} %project_across.1.acc_in, ...), custom_call_target="tpu_custom_call" | custom-call | tf_op jit(solution)/shard_map/project_query/pallas_call | solution.py:37
  22.3 0.4 collective-permute-start.4
  22.7 5.5 %collective-permute-done.4.got_grad = bf16[512,128]{1,0:T(8,128)(2,1)S(1)} collective-permute-done((bf16[512,128]{1,0:T(8,128)(2,1)S(1)}, bf16[512,128]{1,0:T(8,128)(2,1)S(1)}, u32[]{:S(2)}, u32[]{:S(2)}) %collective-permute-start.4) | collective-permute-done | bytes 131104 | tf_op jit(solution)/shard_map/ppermute | solution.py:499
  28.2 0.0 collective-permute-done.3.got_state
  28.2 0.2 pair.1
  28.4 2.9 %collective-permute-start.5 = (bf16[528,128]{1,0:T(8,128)(2,1)S(1)}, bf16[528,128]{1,0:T(8,128)(2,1)S(1)}, u32[]{:S(2)}, u32[]{:S(2)}) collective-permute-start(bf16[528,128]{1,0:T(8,128)(2,1)S(1)} %get-tuple-element.75), channel_id=1, source_target_pairs={{0,16},{4,20},{8,24},{12,28},{16,0},{20,4},{24,8},{28,12},{1,17},{... | collective-permute-start | bytes 405512 | tf_op jit(solution)/shard_map/ppermute | solution.py:388
  31.2 0.8 %collective-permute-start.6 = (bf16[528,128]{1,0:T(8,128)(2,1)S(1)}, bf16[528,128]{1,0:T(8,128)(2,1)S(1)}, u32[]{:S(2)}, u32[]{:S(2)}) collective-permute-start(bf16[528,128]{1,0:T(8,128)(2,1)S(1)} %get-tuple-element.76), channel_id=1, source_target_pairs={{8,16},{16,8},{12,20},{20,12},{9,17},{17,9},{13,21},{21,13},{10,18... | collective-permute-start | bytes 405512 | tf_op jit(solution)/shard_map/ppermute | solution.py:389
  32.1 2.9 %collective-permute-start.7 = (bf16[528,128]{1,0:T(8,128)(2,1)S(1)}, bf16[528,128]{1,0:T(8,128)(2,1)S(1)}, u32[]{:S(2)}, u32[]{:S(2)}) collective-permute-start(bf16[528,128]{1,0:T(8,128)(2,1)S(1)} %get-tuple-element.77), channel_id=1, source_target_pairs={{0,8},{4,12},{8,0},{12,4},{16,24},{20,28},{24,16},{28,20},{1,9},{5... | collective-permute-start | bytes 405512 | tf_op jit(solution)/shard_map/ppermute | solution.py:390
  35.0 3.6 %intra.1 = (f32[256,1024]{1,0:T(8,128)S(1)}, f32[256,1024]{1,0:T(8,128)S(1)}, f32[256,1024]{1,0:T(8,128)S(1)}, f32[256,1024]{1,0:T(8,128)S(1)}) custom-call(bf16[256,1024]{1,0:T(8,128)(2,1)S(1)} %get-tuple-element.61.query, bf16[256,1024]{1,0:T(8,128)(2,1)S(1)} %get-tuple-element.56.key, bf16[256,1024]{1,0:T(8,128)(2,1)S(1)} %get-tuple-element.57.value, ...), custom_call_target="tpu_custom_call" | custom-call | flops 1073741824 | tf_op jit(solution)/shard_map/intra/pallas_call | solution.py:37
  38.6 0.1 collective-permute-done.5.far
  38.7 0.0 collective-permute-done.6.middle
  38.7 1.2 %collective-permute-done.7.near = bf16[528,128]{1,0:T(8,128)(2,1)S(1)} collective-permute-done((bf16[528,128]{1,0:T(8,128)(2,1)S(1)}, bf16[528,128]{1,0:T(8,128)(2,1)S(1)}, u32[]{:S(2)}, u32[]{:S(2)}) %collective-permute-start.7) | collective-permute-done | bytes 135200 | tf_op jit(solution)/shard_map/ppermute | solution.py:390
  39.9 0.3 spread.1
  40.2 1.5 %collective-permute-start.8 = (bf16[2,4,128,128]{3,2,1,0:T(8,128)(2,1)S(1)}, bf16[2,4,128,128]{3,2,1,0:T(8,128)(2,1)S(1)}, u32[]{:S(2)}, u32[]{:S(2)}) collective-permute-start(bf16[2,4,128,128]{3,2,1,0:T(8,128)(2,1)S(1)} %get-tuple-element.80), channel_id=1, source_target_pairs={{0,4},{4,0},{8,12},{12,8},{16,20},{20,16},{24,28},{28,24},{1,5},{5... | collective-permute-start | bytes 786440 | tf_op jit(solution)/shard_map/ppermute | solution.py:396
  41.7 2.4 %back_kept.1 = (bf16[3,256,512]{2,1,0:T(8,128)(2,1)S(1)}, f32[256,1024]{1,0:T(8,128)S(1)}, f32[256,1024]{1,0:T(8,128)S(1)}) custom-call(bf16[256,1024]{1,0:T(8,128)(2,1)S(1)} %get-tuple-element.56.key, bf16[256,1024]{1,0:T(8,128)(2,1)S(1)} %get-tuple-element.57.value, bf16[256,1024]{1,0:T(8,128)(2,1)S(1)} %copy-done, ...), custom_call_target="tpu_custom_call" | custom-call | tf_op jit(solution)/shard_map/back_kept/pallas_call | solution.py:37
  44.1 3.7 %collective-permute-done.8.passed = bf16[2,4,128,128]{3,2,1,0:T(8,128)(2,1)S(1)} collective-permute-done((bf16[2,4,128,128]{3,2,1,0:T(8,128)(2,1)S(1)}, bf16[2,4,128,128]{3,2,1,0:T(8,128)(2,1)S(1)}, u32[]{:S(2)}, u32[]{:S(2)}) %collective-permute-start.8) | collective-permute-done | bytes 262176 | tf_op jit(solution)/shard_map/ppermute | solution.py:396
  47.8 1.2 %back_first.1 = (bf16[3,256,512]{2,1,0:T(8,128)(2,1)S(1)}, bf16[256,512]{1,0:T(8,128)(2,1)S(1)}) custom-call(bf16[256,1024]{1,0:T(8,128)(2,1)S(1)} %get-tuple-element.56.key, bf16[256,1024]{1,0:T(8,128)(2,1)S(1)} %get-tuple-element.57.value, bf16[256,1024]{1,0:T(8,128)(2,1)S(1)} %copy-done, f32[256,25]{1,0:T(8,128)S(1)} %get-tuple-element.58.cols_h, ...), custom_call_target="tpu_custom_call" | custom-call | tf_op jit(solution)/shard_map/back_first/pallas_call | solution.py:37
  49.0 0.1 collective-permute-start.9
  49.1 1.4 %back_second.1 = (bf16[256,512]{1,0:T(8,128)(2,1)S(1)}, f32[256,512]{1,0:T(8,128)S(1)}, f32[256,512]{1,0:T(8,128)S(1)}) custom-call(bf16[3,256,512]{2,1,0:T(8,128)(2,1)S(1)} %get-tuple-element.89.stack, bf16[3,4096,1024]{2,1,0:T(8,128)(2,1)S(1)} %get-tuple-element.50.refs_1_.w, f32[256,1024]{1,0:T(8,128)S(1)} %get-tuple-element.81.start3, ...), custom_call_target="tpu_custom_call" | custom-call | tf_op jit(solution)/shard_map/back_second/pallas_call | solution.py:37
  50.6 0.5 collective-permute-start.10
  51.1 0.0 collective-permute-done.9
  51.1 0.1 add_convert_fusion.1
  51.2 1.6 %collective-permute-start.11 = (bf16[256,512]{1,0:T(8,128)(2,1)S(1)}, bf16[256,512]{1,0:T(8,128)(2,1)S(1)}, u32[]{:S(2)}, u32[]{:S(2)}) collective-permute-start(bf16[256,512]{1,0:T(8,128)(2,1)S(1)} %add_convert_fusion.1), channel_id=1, source_target_pairs={{0,2},{1,3},{2,0},{3,1},{4,6},{5,7},{6,4},{7,5},{8,10},{9,11},{10,... | collective-permute-start | bytes 786440 | tf_op jit(solution)/shard_map/ppermute | solution.py:526
  52.8 0.0 collective-permute-done.10
  52.8 0.1 add_convert_fusion
  52.9 1.1 %collective-permute-start.12 = (bf16[256,512]{1,0:T(8,128)(2,1)S(1)}, bf16[256,512]{1,0:T(8,128)(2,1)S(1)}, u32[]{:S(2)}, u32[]{:S(2)}) collective-permute-start(bf16[256,512]{1,0:T(8,128)(2,1)S(1)} %add_convert_fusion), channel_id=1, source_target_pairs={{0,2},{1,3},{2,0},{3,1},{4,6},{5,7},{6,4},{7,5},{8,10},{9,11},{10,... | collective-permute-start | bytes 786440 | tf_op jit(solution)/shard_map/ppermute | solution.py:529
  54.0 3.6 %back_rest.1 = (f32[256,1024]{1,0:T(8,128)S(1)}, bf16[256,1024]{1,0:T(8,128)(2,1)S(1)}, f32[256,1024]{1,0:T(8,128)S(1)}) custom-call(bf16[3,256,512]{2,1,0:T(8,128)(2,1)S(1)} %get-tuple-element.79.kept_stack, bf16[3,256,512]{2,1,0:T(8,128)(2,1)S(1)} %get-tuple-element.89.stack, bf16[3,4096,1024]{2,1,0:T(8,128)(2,1)S(1)} %get-tuple-element.50.refs_1_.w, ...), custom_call_target="tpu_custom_call" | custom-call | tf_op jit(solution)/shard_map/back_rest/pallas_call | solution.py:37
  57.6 1.0 %copy.13 = f32[256,1024]{1,0:T(8,128)} copy(f32[256,1024]{1,0:T(8,128)S(1)} %get-tuple-element.102) | data formatting | bytes 2097152
  58.6 0.1 collective-permute-start.16
  58.8 0.4 collective-permute-start.15
  59.2 0.1 collective-permute-start.14
  59.3 1.1 %collective-permute-done.11.refs_0_ = bf16[256,512]{1,0:T(8,128)(2,1)S(1)} collective-permute-done((bf16[256,512]{1,0:T(8,128)(2,1)S(1)}, bf16[256,512]{1,0:T(8,128)(2,1)S(1)}, u32[]{:S(2)}, u32[]{:S(2)}) %collective-permute-start.11) | collective-permute-done | bytes 262176 | tf_op jit(solution)/shard_map/ppermute | solution.py:526
  60.4 4.7 %collective-permute-done.12.refs_1_ = bf16[256,512]{1,0:T(8,128)(2,1)S(1)} collective-permute-done((bf16[256,512]{1,0:T(8,128)(2,1)S(1)}, bf16[256,512]{1,0:T(8,128)(2,1)S(1)}, u32[]{:S(2)}, u32[]{:S(2)}) %collective-permute-start.12) | collective-permute-done | bytes 262176 | tf_op jit(solution)/shard_map/ppermute | solution.py:529
  65.1 0.0 collective-permute-done.16.refs_3_
  65.1 0.0 collective-permute-done.15.refs_2_
  65.1 0.0 collective-permute-done.14.refs_1_
  65.1 1.0 %last_sum.1 = f32[256,1024]{1,0:T(8,128)} custom-call(f32[256,1024]{1,0:T(8,128)S(1)} %get-tuple-element.92.own, bf16[256,512]{1,0:T(8,128)(2,1)S(1)} %get-tuple-element.95.across_a, bf16[256,512]{1,0:T(8,128)(2,1)S(1)} %get-tuple-element.96.across_b, bf16[64,1024]{1,0:T(8,128)(2,1)S(1)} %collective-permute-done.13.refs_0_, ...), custom_call_target="tpu_custom_call" | custom-call | tf_op jit(solution)/shard_map/last_sum/pallas_call | solution.py:37
  (7 shorter events, 0.0 us)
Async XLA Ops:
  0.6 15.2 %collective-permute-start = (bf16[256,1024]{1,0:T(8,128)(2,1)}, bf16[256,1024]{1,0:T(8,128)(2,1)S(1)}, u32[]{:S(2)}, u32[]{:S(2)}) collective-permute-start(bf16[256,1024]{1,0:T(8,128)(2,1)} %tokens.1), channel_id=1, source_target_pairs={{0,2},{1,3},{2,0},{3,1},{4,6},{5,7},{6,4},{7,5},{8,10},{9,11},{10,... | collective-permute-start | bytes 1572872 | tf_op jit(solution)/shard_map/ppermute | solution.py:455
  3.7 8.4 %collective-permute-start.1 = (bf16[256,1024]{1,0:T(8,128)(2,1)}, bf16[256,1024]{1,0:T(8,128)(2,1)S(1)}, u32[]{:S(2)}, u32[]{:S(2)}) collective-permute-start(bf16[256,1024]{1,0:T(8,128)(2,1)} %tokens.1), channel_id=1, source_target_pairs={{0,1},{1,0},{2,3},{3,2},{4,5},{5,4},{6,7},{7,6},{8,9},{9,8},{10,11... | collective-permute-start | bytes 1572872 | tf_op jit(solution)/shard_map/ppermute | solution.py:456
  15.8 1.9 %collective-permute-start.2 = (bf16[256,1024]{1,0:T(8,128)(2,1)S(1)}, bf16[256,1024]{1,0:T(8,128)(2,1)S(1)}, u32[]{:S(2)}, u32[]{:S(2)}) collective-permute-start(bf16[256,1024]{1,0:T(8,128)(2,1)S(1)} %collective-permute-done.refs_0_), channel_id=1, source_target_pairs={{0,1},{1,0},{2,3},{3,2},{4,5},{5,4},{6,7},{7,6},{8,9},{9,8},{10,11... | collective-permute-start | bytes 1572872 | tf_op jit(solution)/shard_map/ppermute | solution.py:478
  17.7 3.4 %copy-start = (bf16[256,1024]{1,0:T(8,128)(2,1)S(1)}, bf16[256,1024]{1,0:T(8,128)(2,1)}, u32[]{:S(2)}) copy-start(bf16[256,1024]{1,0:T(8,128)(2,1)} %grads.7) | copy-start | bytes 1572868
  19.4 8.8 %collective-permute-start.3 = (bf16[528,128]{1,0:T(8,128)(2,1)S(1)}, bf16[528,128]{1,0:T(8,128)(2,1)S(1)}, u32[]{:S(2)}, u32[]{:S(2)}) collective-permute-start(bf16[528,128]{1,0:T(8,128)(2,1)S(1)} %get-tuple-element.68), channel_id=1, source_target_pairs={{0,4},{4,0},{8,12},{12,8},{16,20},{20,16},{24,28},{28,24},{1,5},{5... | collective-permute-start | bytes 405512 | tf_op jit(solution)/shard_map/ppermute | solution.py:490
  22.3 5.9 %collective-permute-start.4 = (bf16[512,128]{1,0:T(8,128)(2,1)S(1)}, bf16[512,128]{1,0:T(8,128)(2,1)S(1)}, u32[]{:S(2)}, u32[]{:S(2)}) collective-permute-start(bf16[512,128]{1,0:T(8,128)(2,1)S(1)} %get-tuple-element.69), channel_id=1, source_target_pairs={{0,4},{4,0},{8,12},{12,8},{16,20},{20,16},{24,28},{28,24},{1,5},{5... | collective-permute-start | bytes 393224 | tf_op jit(solution)/shard_map/ppermute | solution.py:499
  28.4 10.3 %collective-permute-start.5 = (bf16[528,128]{1,0:T(8,128)(2,1)S(1)}, bf16[528,128]{1,0:T(8,128)(2,1)S(1)}, u32[]{:S(2)}, u32[]{:S(2)}) collective-permute-start(bf16[528,128]{1,0:T(8,128)(2,1)S(1)} %get-tuple-element.75), channel_id=1, source_target_pairs={{0,16},{4,20},{8,24},{12,28},{16,0},{20,4},{24,8},{28,12},{1,17},{... | collective-permute-start | bytes 405512 | tf_op jit(solution)/shard_map/ppermute | solution.py:388
  31.2 7.4 %collective-permute-start.6 = (bf16[528,128]{1,0:T(8,128)(2,1)S(1)}, bf16[528,128]{1,0:T(8,128)(2,1)S(1)}, u32[]{:S(2)}, u32[]{:S(2)}) collective-permute-start(bf16[528,128]{1,0:T(8,128)(2,1)S(1)} %get-tuple-element.76), channel_id=1, source_target_pairs={{8,16},{16,8},{12,20},{20,12},{9,17},{17,9},{13,21},{21,13},{10,18... | collective-permute-start | bytes 405512 | tf_op jit(solution)/shard_map/ppermute | solution.py:389
  32.1 7.8 %collective-permute-start.7 = (bf16[528,128]{1,0:T(8,128)(2,1)S(1)}, bf16[528,128]{1,0:T(8,128)(2,1)S(1)}, u32[]{:S(2)}, u32[]{:S(2)}) collective-permute-start(bf16[528,128]{1,0:T(8,128)(2,1)S(1)} %get-tuple-element.77), channel_id=1, source_target_pairs={{0,8},{4,12},{8,0},{12,4},{16,24},{20,28},{24,16},{28,20},{1,9},{5... | collective-permute-start | bytes 405512 | tf_op jit(solution)/shard_map/ppermute | solution.py:390
  40.2 7.7 %collective-permute-start.8 = (bf16[2,4,128,128]{3,2,1,0:T(8,128)(2,1)S(1)}, bf16[2,4,128,128]{3,2,1,0:T(8,128)(2,1)S(1)}, u32[]{:S(2)}, u32[]{:S(2)}) collective-permute-start(bf16[2,4,128,128]{3,2,1,0:T(8,128)(2,1)S(1)} %get-tuple-element.80), channel_id=1, source_target_pairs={{0,4},{4,0},{8,12},{12,8},{16,20},{20,16},{24,28},{28,24},{1,5},{5... | collective-permute-start | bytes 786440 | tf_op jit(solution)/shard_map/ppermute | solution.py:396
  49.0 2.1 %collective-permute-start.9 = (bf16[256,512]{1,0:T(8,128)(2,1)S(1)}, bf16[256,512]{1,0:T(8,128)(2,1)S(1)}, u32[]{:S(2)}, u32[]{:S(2)}) collective-permute-start(bf16[256,512]{1,0:T(8,128)(2,1)S(1)} %get-tuple-element.85), channel_id=1, source_target_pairs={{0,1},{1,0},{2,3},{3,2},{4,5},{5,4},{6,7},{7,6},{8,9},{9,8},{10,11... | collective-permute-start | bytes 786440 | tf_op jit(solution)/shard_map/ppermute | solution.py:516
  50.6 2.3 %collective-permute-start.10 = (bf16[256,512]{1,0:T(8,128)(2,1)S(1)}, bf16[256,512]{1,0:T(8,128)(2,1)S(1)}, u32[]{:S(2)}, u32[]{:S(2)}) collective-permute-start(bf16[256,512]{1,0:T(8,128)(2,1)S(1)} %get-tuple-element.88), channel_id=1, source_target_pairs={{0,1},{1,0},{2,3},{3,2},{4,5},{5,4},{6,7},{7,6},{8,9},{9,8},{10,11... | collective-permute-start | bytes 786440 | tf_op jit(solution)/shard_map/ppermute | solution.py:523
  51.2 9.2 %collective-permute-start.11 = (bf16[256,512]{1,0:T(8,128)(2,1)S(1)}, bf16[256,512]{1,0:T(8,128)(2,1)S(1)}, u32[]{:S(2)}, u32[]{:S(2)}) collective-permute-start(bf16[256,512]{1,0:T(8,128)(2,1)S(1)} %add_convert_fusion.1), channel_id=1, source_target_pairs={{0,2},{1,3},{2,0},{3,1},{4,6},{5,7},{6,4},{7,5},{8,10},{9,11},{10,... | collective-permute-start | bytes 786440 | tf_op jit(solution)/shard_map/ppermute | solution.py:526
  52.9 12.2 %collective-permute-start.12 = (bf16[256,512]{1,0:T(8,128)(2,1)S(1)}, bf16[256,512]{1,0:T(8,128)(2,1)S(1)}, u32[]{:S(2)}, u32[]{:S(2)}) collective-permute-start(bf16[256,512]{1,0:T(8,128)(2,1)S(1)} %add_convert_fusion), channel_id=1, source_target_pairs={{0,2},{1,3},{2,0},{3,1},{4,6},{5,7},{6,4},{7,5},{8,10},{9,11},{10,... | collective-permute-start | bytes 786440 | tf_op jit(solution)/shard_map/ppermute | solution.py:529
  58.6 6.5 %collective-permute-start.16 = (bf16[64,1024]{1,0:T(8,128)(2,1)S(1)}, bf16[64,1024]{1,0:T(8,128)(2,1)S(1)}, u32[]{:S(2)}, u32[]{:S(2)}) collective-permute-start(bf16[64,1024]{1,0:T(8,128)(2,1)S(1)} %get-tuple-element.98), channel_id=1, source_target_pairs={{0,1},{1,0},{2,3},{3,2},{4,5},{5,4},{6,7},{7,6},{8,9},{9,8},{10,11... | collective-permute-start | bytes 393224 | tf_op jit(solution)/shard_map/ppermute | solution.py:536
  58.8 6.3 %collective-permute-start.15 = (bf16[64,1024]{1,0:T(8,128)(2,1)S(1)}, bf16[64,1024]{1,0:T(8,128)(2,1)S(1)}, u32[]{:S(2)}, u32[]{:S(2)}) collective-permute-start(bf16[64,1024]{1,0:T(8,128)(2,1)S(1)} %get-tuple-element.99), channel_id=1, source_target_pairs={{0,1},{1,0},{2,3},{3,2},{4,5},{5,4},{6,7},{7,6},{8,9},{9,8},{10,11... | collective-permute-start | bytes 393224 | tf_op jit(solution)/shard_map/ppermute | solution.py:536
  59.2 5.9 %collective-permute-start.14 = (bf16[64,1024]{1,0:T(8,128)(2,1)S(1)}, bf16[64,1024]{1,0:T(8,128)(2,1)S(1)}, u32[]{:S(2)}, u32[]{:S(2)}) collective-permute-start(bf16[64,1024]{1,0:T(8,128)(2,1)S(1)} %get-tuple-element.100), channel_id=1, source_target_pairs={{0,1},{1,0},{2,3},{3,2},{4,5},{5,4},{6,7},{7,6},{8,9},{9,8},{10,11... | collective-permute-start | bytes 393224 | tf_op jit(solution)/shard_map/ppermute | solution.py:536
  60.4 4.7 %collective-permute-start.13 = (bf16[64,1024]{1,0:T(8,128)(2,1)S(1)}, bf16[64,1024]{1,0:T(8,128)(2,1)S(1)}, u32[]{:S(2)}, u32[]{:S(2)}) collective-permute-start(bf16[64,1024]{1,0:T(8,128)(2,1)S(1)} %get-tuple-element.101), channel_id=1, source_target_pairs={{0,1},{1,0},{2,3},{3,2},{4,5},{5,4},{6,7},{7,6},{8,9},{9,8},{10,11... | collective-permute-start | bytes 393224 | tf_op jit(solution)/shard_map/ppermute | solution.py:536

commit v6 on v5

--- a/solution.py
+++ b/solution.py
@@ -57,9 +57,16 @@
     return pl.ds(pl.multiple_of((lax.axis_index("tp") ^ which) * part + offset, size), size)
 
 
-def pair_place():
+def group_place():
     place = lax.axis_index("seq")
-    return place % 2 == 1, place // 2
+    return place % 4, place // 4
+
+
+def pick(index, values):
+    out = values[-1]
+    for i in reversed(range(len(values) - 1)):
+        out = jnp.where(index == i, values[i], out)
+    return out
 
 
 def prepare(lengths, forget, cols_h, rows_h, through):
@@ -144,31 +151,24 @@
     return total
 
 
-def project_last(piece, m, x, w, acc_in, out):
-    for cols in tiles(w.shape[2]):
-        out[:, cols] = (acc_in[m, :, cols] + products([piece], [x], w, m, cols)).astype(BF16)
-
-
-def project_key_value(piece, x, w, acc_in, rows_h, through, key, value, mine, message, states):
-    project_last(piece, 1, x, w, acc_in, key)
-    project_last(piece, 2, x, w, acc_in, value)
-    hand_out(lambda h: state_end(key, value, rows_h, h), states, mine, message)
-    message[mine.shape[0] * DH :, :] = through[...]
-
-
-def project_query(piece, x, w, acc_in, rows_h, grads, query, mine, message, states):
-    project_last(piece, 0, x, w, acc_in, query)
-    hand_out(lambda h: grad_start(query, grads, rows_h, h), states, mine, message)
-
-
-def hand_out(state_of, states, mine, message):
-    half = mine.shape[0]
-    for h in range(2 * half):
-        states[h] = state_of(h)
-    upper = jnp.where(pair_place()[0], half, 0)
-    for j in range(half):
-        mine[j] = states[upper + j]
-        message[j * DH : (j + 1) * DH, :] = states[half - upper + j].astype(BF16)
+def project_last(piece, x, w, acc_in, rows_h, own_through, grads, query, key, value, mine, to1, to2, to3, states):
+    for m, out in ((1, key), (2, value), (0, query)):
+        for cols in tiles(w.shape[2]):
+            out[:, cols] = (acc_in[m, :, cols] + products([piece], [x], w, m, cols)).astype(BF16)
+    own_states(query, key, value, grads, rows_h, states)
+    quarter = mine.shape[1]
+    place = group_place()[0]
+    for d, to in enumerate((mine, to1, to2, to3)):
+        for i in range(2):
+            for j in range(quarter):
+                state = states[i, (place ^ d) * quarter + j]
+                if d:
+                    first = (i * quarter + j) * DH
+                    to[first : first + DH, :] = state.astype(BF16)
+                else:
+                    to[i, j] = state
+        if d:
+            to[2 * quarter * DH :, :] = own_through[...]
 
 
 def columns(cols_h, h):
@@ -219,33 +219,30 @@
     gstack[2, :, at] = (gv[:, cols] * (1.0 / DH) + dot(key[:, cols], end, 1, 0) * tail).astype(BF16)
 
 
-def finish_out(query, cols_h, out, state_of, attn):
-    for h in range(query.shape[1] // DH):
-        cols = slice(h * DH, (h + 1) * DH)
-        lead = columns(cols_h, h)[1]
-        attn[:, cols] = (out[:, cols] + dot(query[:, cols], state_of(h), 1, 0) * lead) * (1.0 / DH)
-
-
 def finish_whole(query, key, value, grads, cols_h, out, gq, gk, gv, both, attn, gstack):
     for h in range(query.shape[1] // DH):
         cols = slice(h * DH, (h + 1) * DH)
         lead, tail = columns(cols_h, h)[1:]
         finish_grads(key, value, grads, gq, gk, gv, cols, lead, tail, both[0, h], both[1, h], gstack, cols)
-    finish_out(query, cols_h, out, lambda h: both[0, h], attn)
-
-
-def finish_half(kept, key, value, grads, cols_h, gq, gk, gv, states, gstack):
-    half = states.shape[1]
-    second = pair_place()[0] == kept
-    base = jnp.where(second, half * DH, 0)
-    for j in range(half):
-        cols = pl.ds(pl.multiple_of(base + j * DH, DH), DH)
-        lead, tail = [
-            jnp.where(second, b, a) for a, b in zip(columns(cols_h, j)[1:], columns(cols_h, half + j)[1:])
-        ]
+        attn[:, cols] = (out[:, cols] + dot(query[:, cols], both[0, h], 1, 0) * lead) * (1.0 / DH)
+
+
+def quarter_heads(d, quarter, cols_h):
+    member = group_place()[0] ^ d
+    for j in range(quarter):
+        lead, tail = [pick(member, [columns(cols_h, c * quarter + j)[i] for c in range(4)]) for i in (1, 2)]
+        yield j, pl.ds(pl.multiple_of((member * quarter + j) * DH, DH), DH), lead, tail
+
+
+def quarter_columns(d, w):
+    width = w.shape[2] // 4
+    return pl.ds(pl.multiple_of((group_place()[0] ^ d) * width, width), width)
+
+
+def finish_quarter(d, key, value, grads, cols_h, gq, gk, gv, states, stack):
+    for j, cols, lead, tail in quarter_heads(d, states.shape[1], cols_h):
         at = slice(j * DH, (j + 1) * DH)
-        finish_grads(key, value, grads, gq, gk, gv, cols, lead, tail, states[0, j], states[1, j], gstack, at)
-    return pl.ds(pl.multiple_of(base, half * DH), half * DH)
+        finish_grads(key, value, grads, gq, gk, gv, cols, lead, tail, states[0, j], states[1, j], stack, at)
 
 
 def back(which, stacks, w, out, offset=0, start=None):
@@ -253,34 +250,34 @@
     for cols in tiles(out.shape[1]):
         rows = rows_of(which, part, offset + cols.start, cols.stop - cols.start)
         total = None if start is None else start[:, slice(offset + cols.start, offset + cols.stop)]
-        for gstack, heads in stacks:
+        for d, stack in stacks:
             for m in range(3):
-                term = dot(gstack[m], w[m, rows, heads], 1, 1)
+                term = dot(stack[m], w[m, rows, quarter_columns(d, w)], 1, 1)
                 total = term if total is None else total + term
         out[:, cols] = total.astype(out.dtype)
 
 
-def half_columns(kept, w):
-    width = w.shape[2] // 2
-    return pl.ds(pl.multiple_of(jnp.where(pair_place()[0] == kept, width, 0), width), width)
-
-
-def back_kept(key, value, grads, cols_h, gq, gk, gv, kept, w, stack, start3, start2):
-    heads = finish_half(True, key, value, grads, cols_h, gq, gk, gv, kept, stack)
-    back(3, [(stack, heads)], w, start3)
-    back(2, [(stack, heads)], w, start2)
-
-
-def back_first(key, value, grads, cols_h, gq, gk, gv, passed, w, start3, stack, chunk3_a):
-    heads = finish_half(False, key, value, grads, cols_h, gq, gk, gv, passed, stack)
-    back(3, [(stack, heads)], w, chunk3_a, 0, start3)
+def back_own(key, value, grads, cols_h, gq, gk, gv, states, w, stack, out3, out2):
+    finish_quarter(0, key, value, grads, cols_h, gq, gk, gv, states, stack)
+    back(3, [(0, stack)], w, out3)
+    back(2, [(0, stack)], w, out2)
+
+
+def back_more(d, key, value, grads, cols_h, gq, gk, gv, states, w, start3, start2, stack, out3, out2):
+    finish_quarter(d, key, value, grads, cols_h, gq, gk, gv, states, stack)
+    back(3, [(d, stack)], w, out3, 0, start3)
+    back(2, [(d, stack)], w, out2, 0, start2)
+
+
+def back_first(key, value, grads, cols_h, gq, gk, gv, states, w, start3, stack, chunk3_a):
+    finish_quarter(3, key, value, grads, cols_h, gq, gk, gv, states, stack)
+    back(3, [(3, stack)], w, chunk3_a, 0, start3)
 
 
 def back_second(stack, w, start3, start2, chunk3_b, chunk2_a, chunk2_b):
-    stacks = [(stack, half_columns(False, w))]
-    back(3, stacks, w, chunk3_b, start3.shape[1] - chunk3_b.shape[1], start3)
-    back(2, stacks, w, chunk2_a, 0, start2)
-    back(2, stacks, w, chunk2_b, chunk2_a.shape[1], start2)
+    back(3, [(3, stack)], w, chunk3_b, start3.shape[1] - chunk3_b.shape[1], start3)
+    back(2, [(3, stack)], w, chunk2_a, 0, start2)
+    back(2, [(3, stack)], w, chunk2_b, chunk2_a.shape[1], start2)
 
 
 def hand_on(*refs):
@@ -301,17 +298,14 @@
         copy.wait()
 
 
-def back_rest(kept_stack, stack, w, query, cols_h, out, kept, passed, attn, chunk_other, chunk_own):
-    stacks = [(kept_stack, half_columns(True, w)), (stack, half_columns(False, w))]
+def back_rest(stack0, stack1, stack2, stack3, w, query, cols_h, out, states0, states1, states2, states3, *outs):
+    attn, chunk_other, chunk_own = outs
+    stacks = list(enumerate((stack0, stack1, stack2, stack3)))
     back(1, stacks, w, chunk_other)
     back(0, stacks, w, chunk_own)
-    half = kept.shape[1]
-    upper = pair_place()[0]
-
-    def state_of(h):
-        return jnp.where((h >= half) == upper, kept[0, h % half], passed[0, h % half])
-
-    finish_out(query, cols_h, out, state_of, attn)
+    for d, states in enumerate((states0, states1, states2, states3)):
+        for j, cols, lead, _ in quarter_heads(d, states.shape[1], cols_h):
+            attn[:, cols] = (out[:, cols] + dot(query[:, cols], states[0, j], 1, 0) * lead) * (1.0 / DH)
 
 
 def per_head(scale, matrix):
@@ -323,77 +317,58 @@
     return rows[:half].astype(F32) + rows[half:].astype(F32)
 
 
-def pair_kernel(own_through, my_state, my_grad, got_state, got_grad, to_far, to_middle, to_near, mate_through):
-    half = my_state.shape[0]
-    upper, z = pair_place()
-    own, mate = head_factors(own_through[...]), head_factors(got_state[half * DH :, :])
-    mate_through[...] = mate
-    low, high = jnp.where(upper, mate, own), jnp.where(upper, own, mate)
-    ends = jnp.concatenate(split(own * mate), axis=0)
-    for to in (to_near, to_middle, to_far):
-        to[half * DH :, :] = ends
-    for j in range(half):
-        rows = slice(j * DH, (j + 1) * DH)
-        theirs, theirs_grad = got_state[rows, :].astype(F32), got_grad[rows, :].astype(F32)
-        low_j, high_j = half_factor(upper, low, j), half_factor(upper, high, j)
-        mine, mine_grad = my_state[j], my_grad[j]
-        state = jnp.where(upper, mine + high_j * theirs, theirs + high_j * mine).astype(BF16)
-        grad = jnp.where(upper, theirs_grad + low_j * mine_grad, mine_grad + low_j * theirs_grad).astype(BF16)
-        to_near[rows, :] = jnp.where(z % 2 == 0, state, grad)
-        to_middle[rows, :] = jnp.where(z == 1, state, grad)
-        to_far[rows, :] = jnp.where(z < 2, state, grad)
-
-
-def half_factor(upper, factors, j):
-    half = factors.shape[0] // 2
-    return jnp.where(upper, factors[half + j : half + j + 1], factors[j : j + 1])
-
-
-def spread_kernel(own_through, mate_through, my_state, my_grad, got_state, got_grad, far, middle, near, kept, passed):
-    half = my_state.shape[0]
-    upper, z = pair_place()
-    own, mate = head_factors(own_through[...]), mate_through[...]
-    low, high = jnp.where(upper, mate, own), jnp.where(upper, own, mate)
-    inner = (z == 1) | (z == 2)
-    step = head_factors(jnp.where(inner, middle[half * DH :, :], near[half * DH :, :]))
-    for j in range(half):
-        rows = slice(j * DH, (j + 1) * DH)
-        close = near[rows, :].astype(F32)
-        beyond = jnp.where(inner, middle[rows, :], near[rows, :]).astype(F32)
-        beyond = beyond + half_factor(upper, step, j) * far[rows, :].astype(F32)
-        state = jnp.where(z == 0, 0.0, jnp.where(z == 1, close, beyond))
-        grad = jnp.where(z == 3, 0.0, jnp.where(z == 2, close, beyond))
-        low_state = jnp.where(upper, got_state[rows, :].astype(F32), my_state[j])
-        high_grad = jnp.where(upper, my_grad[j], got_grad[rows, :].astype(F32))
-        high_in = (low_state + half_factor(upper, low, j) * state).astype(BF16)
-        low_in = (high_grad + half_factor(upper, high, j) * grad).astype(BF16)
-        state, grad = state.astype(BF16), grad.astype(BF16)
-        kept[0, j], passed[0, j] = jnp.where(upper, high_in, state), jnp.where(upper, state, high_in)
-        kept[1, j], passed[1, j] = jnp.where(upper, grad, low_in), jnp.where(upper, low_in, grad)
-
-
-MATE = [(i, i ^ 1) for i in range(8)]
-NEAR = [(i, i ^ 2) for i in range(8)]
-MIDDLE = [(2, 4), (4, 2), (3, 5), (5, 3)]
-FAR = [(i, i ^ 4) for i in range(8)]
-
-
-def states_direct(own_through, my_state, my_grad, got_state, got_grad, inside):
-    half = my_state.shape[0]
-    to = ((half * DH + own_through.shape[0], DH), BF16)
-    known = [my_state, my_grad, got_state, got_grad]
-    to_far, to_middle, to_near, mate_through = call(
-        pair_kernel, "pair", [to, to, to, ((2 * half, DH), F32)], [own_through] + known
-    )
-    from_far = lax.ppermute(to_far, "seq", FAR)
-    from_middle = lax.ppermute(to_middle, "seq", MIDDLE)
-    from_near = lax.ppermute(to_near, "seq", NEAR)
-    inside, mate_through = lax.optimization_barrier((inside, mate_through))
-    both = ((2, half, DH, DH), BF16)
-    kept, passed = call(
-        spread_kernel, "spread", [both, both], [own_through, mate_through] + known + [from_far, from_middle, from_near]
-    )
-    return kept, lax.ppermute(passed, "seq", MATE), inside
+def join_kernel(own_through, mine, got1, got2, got3, to_group, inner, factors):
+    quarter = mine.shape[1]
+    place, group = group_place()
+    gots = (got1, got2, got3)
+    through = [own_through] + [got.at[2 * quarter * DH :, :] for got in gots]
+    through = [head_factors(rows[...]) for rows in through]
+    ones = jnp.ones((1, DH), F32)
+    for j in range(quarter):
+        step = [pick(place, [t[c * quarter + j : c * quarter + j + 1] for c in range(4)]) for t in through]
+        step = [pick(place, [step[k ^ p] for p in range(4)]) for k in range(4)]
+        totals = []
+        for i in range(2):
+            first = (i * quarter + j) * DH
+            own = [mine[i, j]] + [got[first : first + DH, :].astype(F32) for got in gots]
+            own = [pick(place, [own[k ^ p] for p in range(4)]) for k in range(4)]
+            order = (0, 1, 2, 3) if i == 0 else (3, 2, 1, 0)
+            state, factor = jnp.zeros((DH, DH), F32), ones
+            for k in order:
+                inner[i, k, j], factors[i, k, j] = state, factor
+                state, factor = own[k] + step[k] * state, step[k] * factor
+            totals.append(state)
+        to_group[j * DH : (j + 1) * DH, :] = jnp.where(group == 0, totals[0], totals[1]).astype(BF16)
+
+
+def spread_kernel(inner, factors, other, *outs):
+    quarter = inner.shape[2]
+    place, group = group_place()
+    for j in range(quarter):
+        arrived = other[j * DH : (j + 1) * DH, :].astype(F32)
+        for d, out in enumerate(outs):
+            for i in range(2):
+                factor = jnp.where(group == 1 - i, factors[i, place ^ d, j], 0.0)
+                out[i, j] = (inner[i, place ^ d, j] + factor * arrived).astype(BF16)
+
+
+def member(d):
+    return [(i, i ^ d) for i in range(8)]
+
+
+def states_direct(own_through, mine, messages, inside):
+    quarter = mine.shape[1]
+    got = [lax.ppermute(message, "seq", member(d)) for d, message in zip((1, 2, 3), messages)]
+    inside, mine = lax.optimization_barrier((inside, mine))
+    to_group, inner, factors = call(
+        join_kernel,
+        "join",
+        [((quarter * DH, DH), BF16), ((2, 4, quarter, DH, DH), F32), ((2, 4, quarter, 1, DH), F32)],
+        [own_through, mine] + got,
+    )
+    other = lax.ppermute(to_group, "seq", member(4))
+    states = call(spread_kernel, "spread", [(mine.shape, BF16)] * 4, [inner, factors, other])
+    return [states[0]] + [lax.ppermute(states[d], "seq", member(d)) for d in (1, 2, 3)], inside
 
 
 def states_gathered(own, through):
@@ -424,7 +399,7 @@
     heads = width // DH
     tps = lax.axis_size("tp")
     seqs = lax.axis_size("seq")
-    by_hand = tps == 4 and seqs == 8 and heads % 8 == 0
+    by_hand = tps == 4 and seqs == 8 and heads % 4 == 0
     decays = [((length, 3 * heads + 1), F32), ((3 * heads, length), F32), ((2 * heads, DH), BF16)]
     rows_shape = ((length, width), BF16)
     sum_shape = ((length, width), F32)
@@ -448,7 +423,7 @@
         grad_terms = jnp.einsum("mtc,mdc->td", gstack, w_qkv, preferred_element_type=F32)
         return attn, lax.psum_scatter(grad_terms, "tp", scatter_dimension=1, tiled=True)
 
-    half = heads // 2
+    quarter = heads // 4
     core = [(i, i ^ 1) for i in range(4)]
     chip = [(i, i ^ 2) for i in range(4)]
     step_flops = 2 * 3 * length * part * width
@@ -478,60 +453,59 @@
     across_beside = lax.ppermute(across, "tp", core)
     acc = project("project_across", acc, ((2, 0), across))
     last = (3, 0)
-    states_scratch = [pltpu.VMEM((heads, DH, DH), F32)]
-    mine_shape = ((half, DH, DH), F32)
-    key, value, my_state, message = call(
-        functools.partial(project_key_value, last),
-        "project_key_value",
-        [rows_shape, rows_shape, mine_shape, ((half * DH + through.shape[0], DH), BF16)],
-        [across_beside, w_vm, acc, rows_h, through],
-        scratch=states_scratch,
-    )
-    got_state = lax.ppermute(message, "seq", MATE)
-    acc, my_state = lax.optimization_barrier((acc, my_state))
-    query, my_grad, message = call(
-        functools.partial(project_query, last),
-        "project_query",
-        [rows_shape, mine_shape, ((half * DH, DH), BF16)],
-        [across_beside, w_vm, acc, rows_h, out_grad],
-        scratch=states_scratch,
-    )
-    got_grad = lax.ppermute(message, "seq", MATE)
+    message_shape = ((2 * quarter * DH + through.shape[0], DH), BF16)
+    query, key, value, mine, *messages = call(
+        functools.partial(project_last, last),
+        "project_last",
+        [rows_shape] * 3 + [((2, quarter, DH, DH), F32)] + [message_shape] * 3,
+        [across_beside, w_vm, acc, rows_h, through, out_grad],
+        scratch=[pltpu.VMEM((2, heads, DH, DH), F32)],
+    )
     inside = call(
         intra, "intra", [sum_shape] * 4, [query, key, value, out_grad, cols_h, rows_h], flops=intra_flops
     )
-    kept, passed, inside = states_direct(through, my_state, my_grad, got_state, got_grad, inside)
+    states, inside = states_direct(through, mine, messages, inside)
 
     part_a = part // 2
     part_b = part - part_a
-    stack_shape = ((3, length, width // 2), BF16)
+    stack_shape = ((3, length, width // 4), BF16)
     chunk_shape = ((length, part), F32)
     common = [key, value, out_grad, cols_h] + list(inside[1:])
-    kept_stack, start3, start2 = call(
-        back_kept, "back_kept", [stack_shape, chunk_shape, chunk_shape], common + [kept, w_vm]
-    )
-    stack, chunk3_a = call(
-        back_first, "back_first", [stack_shape, ((length, part_a), BF16)], common + [passed, w_vm, start3]
+    stack0, start3, start2 = call(
+        back_own, "back_own", [stack_shape, chunk_shape, chunk_shape], common + [states[0], w_vm]
+    )
+    stacks = [stack0]
+    for d in (1, 2):
+        stack, start3, start2 = call(
+            functools.partial(back_more, d),
+            f"back_{d}",
+            [stack_shape, chunk_shape, chunk_shape],
+            common + [states[d], w_vm, start3, start2],
+            aliases={9: 1, 10: 2},
+        )
+        stacks.append(stack)
+    stack3, chunk3_a = call(
+        back_first, "back_first", [stack_shape, ((length, part_a), BF16)], common + [states[3], w_vm, start3]
     )
     beside_a = lax.ppermute(chunk3_a, "tp", core)
     chunk3_b, chunk_a, chunk_b = call(
         back_second,
         "back_second",
         [((length, part_b), BF16), ((length, part_a), F32), ((length, part_b), F32)],
-        [stack, w_vm, start3, start2],
+        [stack3, w_vm, start3, start2],
     )
     beside_b = lax.ppermute(chunk3_b, "tp", core)
     chunk_a = (chunk_a + beside_a.astype(F32)).astype(BF16)
     chunk_a, chunk_b = lax.optimization_barrier((chunk_a, chunk_b))
     across_a = lax.ppermute(chunk_a, "tp", chip)
     chunk_b = (chunk_b + beside_b.astype(F32)).astype(BF16)
-    chunk_b, stack = lax.optimization_barrier((chunk_b, stack))
+    chunk_b, stack3 = lax.optimization_barrier((chunk_b, stack3))
     across_b = lax.ppermute(chunk_b, "tp", chip)
     attn, chunk_other, chunk_own = call(
         back_rest,
         "back_rest",
         [sum_shape, ((length, part), BF16), chunk_shape],
-        [kept_stack, stack, w_vm, query, cols_h, inside[0], kept, passed],
+        stacks + [stack3, w_vm, query, cols_h, inside[0]] + states,
     )
     beside = [lax.ppermute(c, "tp", core) for c in jnp.split(chunk_other, 4)]
     across = [across_a]

time: 66.5 us -> 63.6 us (0.956)
  waiting for transfers between devices: 18.3 us -> 14.8 us
  Pallas kernels: 28.6 us -> 29.7 us
    ppermute x6 -> x7, waiting for transfers between devices: 10.5 us -> 6.82 us  [the longest x3 2.94 us: states_direct(): lax.ppermute(message, 'seq', member(d))]
    pallas_call x15 -> x16, Pallas kernels: 28.6 us -> 29.7 us  [call(): pl.pallas_call(kernel, name=name, out_shape=[out_space(shape, dtype) for...]
    ppermute x6 -> x7, starting transfers between devices: 10.3 us -> 9.93 us  [the longest x3 3.55 us: states_direct(): lax.ppermute(message, 'seq', member(d))]
  transfers between devices with their start and end apart: 17 -> 18, of which waited for: 8 -> 9; matrix products, arithmetic and copies ran while one was open for 2% -> 2% of each run, Pallas kernels for 37% -> 39%
where the time goes in v6:
time: 63.6 us; the launch traced here: 63.4 us
  Pallas kernels  29.7 us (47%)
  starting transfers between devices  16.8 us (26%)
  waiting for transfers between devices  14.8 us (23%)
  local copies, waits for them, and re-layouts  1.01 us (2%)
  between operations  0.97 us (2%)
    pallas_call x16, Pallas kernels, call(): pl.pallas_call(kernel, name=name, out_shape=[out_space(shape, dtype) for...  29.7 us
    ppermute x1, waiting for transfers between devices, local(): across_b = lax.ppermute(chunk_b, 'tp', chip)  4.81 us
    ppermute x3, starting transfers between devices, states_direct(): lax.ppermute(message, 'seq', member(d))  3.55 us
    ppermute x3, starting transfers between devices, states_direct(): lax.ppermute(states[d], 'seq', member(d))  3.55 us
    ppermute x1, starting transfers between devices, local(): across = lax.ppermute(tokens, 'tp', chip)  3.03 us
    ppermute x3, waiting for transfers between devices, states_direct(): lax.ppermute(message, 'seq', member(d))  2.94 us
    ppermute x1, starting transfers between devices, states_direct(): other = lax.ppermute(to_group, 'seq', member(4))  2.82 us
    ppermute x1, waiting for transfers between devices, states_direct(): other = lax.ppermute(to_group, 'seq', member(4))  2.65 us
  transfers between devices with their start and end apart: 18, of which 9 were waited for; matrix products, arithmetic and copies ran while one was open for 2% of the time, Pallas kernels for 39%

profile of v6, /device:TPU:0, one launch (start us, length us, event | category | flops | bytes accessed | tf_op | source)
XLA Modules:
  0.0 63.4 jit_solution(3898177468453417871)
XLA Ops:
  0.6 3.0 %collective-permute-start = (bf16[256,1024]{1,0:T(8,128)(2,1)}, bf16[256,1024]{1,0:T(8,128)(2,1)S(1)}, u32[]{:S(2)}, u32[]{:S(2)}) collective-permute-start(bf16[256,1024]{1,0:T(8,128)(2,1)} %tokens.1), channel_id=1, source_target_pairs={{0,2},{1,3},{2,0},{3,1},{4,6},{5,7},{6,4},{7,5},{8,10},{9,11},{10,... | collective-permute-start | bytes 1572872 | tf_op jit(solution)/shard_map/ppermute | solution.py:430
  3.7 0.0 collective-permute-start.1
  3.7 8.4 %load_and_project.1 = (bf16[3,4096,1024]{2,1,0:T(8,128)(2,1)S(1)}, f32[3,256,1024]{2,1,0:T(8,128)S(1)}, f32[256,25]{1,0:T(8,128)S(1)}, f32[24,256]{1,0:T(8,128)S(1)}, bf16[16,128]{1,0:T(8,128)(2,1)S(1)}) custom-call(s32[16]{0:T(128)} %lengths.1, f32[8,256]{1,0:T(8,128)} %bitcast.1, bf16[256,1024]{1,0:T(8,128)(2,1)} %tokens.1, bf16[3,4096,1024]{2,1,0:T(8,128)(2,1)} %w.1), custom_call_target="tpu_custom_call" | custom-call | flops 12884901888 | tf_op jit(solution)/shard_map/load_and_project/pallas_call | solution.py:37
  12.1 1.8 %project_beside.1.refs_2_ = f32[3,256,1024]{2,1,0:T(8,128)S(1)} custom-call(bf16[256,1024]{1,0:T(8,128)(2,1)S(1)} %collective-permute-done.1.refs_0_, bf16[3,4096,1024]{2,1,0:T(8,128)(2,1)S(1)} %get-tuple-element.55.refs_1_.w, f32[3,256,1024]{2,1,0:T(8,128)S(1)} %get-tuple-element.56.refs_2_), custom_call_target="tpu_custom_call" | custom-call | tf_op jit(solution)/shard_map/project_beside/pallas_call | solution.py:37
  13.9 0.0 copy-start
  13.9 1.9 %collective-permute-done.refs_0_ = bf16[256,1024]{1,0:T(8,128)(2,1)S(1)} collective-permute-done((bf16[256,1024]{1,0:T(8,128)(2,1)}, bf16[256,1024]{1,0:T(8,128)(2,1)S(1)}, u32[]{:S(2)}, u32[]{:S(2)}) %collective-permute-start) | collective-permute-done | bytes 524320 | tf_op jit(solution)/shard_map/ppermute | solution.py:430
  15.8 1.8 %project_across.1.acc_in = f32[3,256,1024]{2,1,0:T(8,128)S(1)} custom-call(bf16[256,1024]{1,0:T(8,128)(2,1)S(1)} %collective-permute-done.refs_0_, bf16[3,4096,1024]{2,1,0:T(8,128)(2,1)S(1)} %get-tuple-element.55.refs_1_.w, f32[3,256,1024]{2,1,0:T(8,128)S(1)} %project_beside.1.refs_2_), custom_call_target="tpu_custom_call" | custom-call | tf_op jit(solution)/shard_map/project_across/pallas_call | solution.py:37
  17.6 0.1 collective-permute-done.2.x
  17.7 2.5 %project_last.1 = (bf16[256,1024]{1,0:T(8,128)(2,1)S(1)}, bf16[256,1024]{1,0:T(8,128)(2,1)S(1)}, bf16[256,1024]{1,0:T(8,128)(2,1)S(1)}, f32[2,2,128,128]{3,2,1,0...) custom-call(bf16[256,1024]{1,0:T(8,128)(2,1)S(1)} %collective-permute-done.2, ...), custom_call_target="tpu_custom_call" | custom-call | tf_op jit(solution)/shard_map/project_last/pallas_call | solution.py:37
  20.2 1.8 %collective-permute-start.3 = (bf16[528,128]{1,0:T(8,128)(2,1)S(1)}, bf16[528,128]{1,0:T(8,128)(2,1)S(1)}, u32[]{:S(2)}, u32[]{:S(2)}) collective-permute-start(bf16[528,128]{1,0:T(8,128)(2,1)S(1)} %get-tuple-element.74), channel_id=1, source_target_pairs={{0,4},{4,0},{8,12},{12,8},{16,20},{20,16},{24,28},{28,24},{1,5},{5... | collective-permute-start | bytes 405512 | tf_op jit(solution)/shard_map/ppermute | solution.py:361
  22.0 1.6 %collective-permute-start.4 = (bf16[528,128]{1,0:T(8,128)(2,1)S(1)}, bf16[528,128]{1,0:T(8,128)(2,1)S(1)}, u32[]{:S(2)}, u32[]{:S(2)}) collective-permute-start(bf16[528,128]{1,0:T(8,128)(2,1)S(1)} %get-tuple-element.75), channel_id=1, source_target_pairs={{0,8},{4,12},{8,0},{12,4},{16,24},{20,28},{24,16},{28,20},{1,9},{5... | collective-permute-start | bytes 405512 | tf_op jit(solution)/shard_map/ppermute | solution.py:361
  23.6 0.2 collective-permute-start.5
  23.8 3.6 %intra.1 = (f32[256,1024]{1,0:T(8,128)S(1)}, f32[256,1024]{1,0:T(8,128)S(1)}, f32[256,1024]{1,0:T(8,128)S(1)}, f32[256,1024]{1,0:T(8,128)S(1)}) custom-call(bf16[256,1024]{1,0:T(8,128)(2,1)S(1)} %get-tuple-element.64.query, bf16[256,1024]{1,0:T(8,128)(2,1)S(1)} %get-tuple-element.61.key, bf16[256,1024]{1,0:T(8,128)(2,1)S(1)} %get-tuple-element.62.value, ...), custom_call_target="tpu_custom_call" | custom-call | flops 1073741824 | tf_op jit(solution)/shard_map/intra/pallas_call | solution.py:37
  27.4 0.0 collective-permute-done.3.got1
  27.4 1.0 %collective-permute-done.4.got2 = bf16[528,128]{1,0:T(8,128)(2,1)S(1)} collective-permute-done((bf16[528,128]{1,0:T(8,128)(2,1)S(1)}, bf16[528,128]{1,0:T(8,128)(2,1)S(1)}, u32[]{:S(2)}, u32[]{:S(2)}) %collective-permute-start.4) | collective-permute-done | bytes 135200 | tf_op jit(solution)/shard_map/ppermute | solution.py:361
  28.4 1.9 %collective-permute-done.5.got3 = bf16[528,128]{1,0:T(8,128)(2,1)S(1)} collective-permute-done((bf16[528,128]{1,0:T(8,128)(2,1)S(1)}, bf16[528,128]{1,0:T(8,128)(2,1)S(1)}, u32[]{:S(2)}, u32[]{:S(2)}) %collective-permute-start.5) | collective-permute-done | bytes 135200 | tf_op jit(solution)/shard_map/ppermute | solution.py:361
  30.4 0.3 join.1
  30.6 2.8 %collective-permute-start.6 = (bf16[256,128]{1,0:T(8,128)(2,1)S(1)}, bf16[256,128]{1,0:T(8,128)(2,1)S(1)}, u32[]{:S(2)}, u32[]{:S(2)}) collective-permute-start(bf16[256,128]{1,0:T(8,128)(2,1)S(1)} %get-tuple-element.79), channel_id=1, source_target_pairs={{0,16},{4,20},{8,24},{12,28},{16,0},{20,4},{24,8},{28,12},{1,17},{... | collective-permute-start | bytes 196616 | tf_op jit(solution)/shard_map/ppermute | solution.py:369
  33.4 2.6 %collective-permute-done.6.other = bf16[256,128]{1,0:T(8,128)(2,1)S(1)} collective-permute-done((bf16[256,128]{1,0:T(8,128)(2,1)S(1)}, bf16[256,128]{1,0:T(8,128)(2,1)S(1)}, u32[]{:S(2)}, u32[]{:S(2)}) %collective-permute-start.6) | collective-permute-done | bytes 65568 | tf_op jit(solution)/shard_map/ppermute | solution.py:369
  36.1 0.1 spread.1
  36.2 1.6 %collective-permute-start.7 = (bf16[2,2,128,128]{3,2,1,0:T(8,128)(2,1)S(1)}, bf16[2,2,128,128]{3,2,1,0:T(8,128)(2,1)S(1)}, u32[]{:S(2)}, u32[]{:S(2)}) collective-permute-start(bf16[2,2,128,128]{3,2,1,0:T(8,128)(2,1)S(1)} %get-tuple-element.82), channel_id=1, source_target_pairs={{0,4},{4,0},{8,12},{12,8},{16,20},{20,16},{24,28},{28,24},{1,5},{5... | collective-permute-start | bytes 393224 | tf_op jit(solution)/shard_map/ppermute | solution.py:371
  37.7 1.5 %collective-permute-start.8 = (bf16[2,2,128,128]{3,2,1,0:T(8,128)(2,1)S(1)}, bf16[2,2,128,128]{3,2,1,0:T(8,128)(2,1)S(1)}, u32[]{:S(2)}, u32[]{:S(2)}) collective-permute-start(bf16[2,2,128,128]{3,2,1,0:T(8,128)(2,1)S(1)} %get-tuple-element.86), channel_id=1, source_target_pairs={{0,8},{4,12},{8,0},{12,4},{16,24},{20,28},{24,16},{28,20},{1,9},{5... | collective-permute-start | bytes 393224 | tf_op jit(solution)/shard_map/ppermute | solution.py:371
  39.3 0.5 collective-permute-start.9
  39.7 1.7 %back_own.1 = (bf16[3,256,256]{2,1,0:T(8,128)(2,1)S(1)}, f32[256,1024]{1,0:T(8,128)S(1)}, f32[256,1024]{1,0:T(8,128)S(1)}) custom-call(bf16[256,1024]{1,0:T(8,128)(2,1)S(1)} %get-tuple-element.61.key, bf16[256,1024]{1,0:T(8,128)(2,1)S(1)} %get-tuple-element.62.value, bf16[256,1024]{1,0:T(8,128)(2,1)S(1)} %copy-done, f32[256,25]{1,0:T(8,128)S(1)} %get-tuple-element.63.cols_h, ...), custom_call_target="tpu_custom_call" | custom-call | tf_op jit(solution)/shard_map/back_own/pallas_call | solution.py:37
  41.4 1.2 %collective-permute-done.7.states.states1 = bf16[2,2,128,128]{3,2,1,0:T(8,128)(2,1)S(1)} collective-permute-done((bf16[2,2,128,128]{3,2,1,0:T(8,128)(2,1)S(1)}, bf16[2,2,128,128]{3,2,1,0:T(8,128)(2,1)S(1)}, u32[]{:S(2)}, u32[]{:S(2)}) %collective-permute-start.7) | collective-permute-done | bytes 131104 | tf_op jit(solution)/shard_map/ppermute | solution.py:371
  42.6 1.5 %back_1.1 = (bf16[3,256,256]{2,1,0:T(8,128)(2,1)S(1)}, f32[256,1024]{1,0:T(8,128)S(1)}, f32[256,1024]{1,0:T(8,128)S(1)}) custom-call(bf16[256,1024]{1,0:T(8,128)(2,1)S(1)} %get-tuple-element.61.key, bf16[256,1024]{1,0:T(8,128)(2,1)S(1)} %get-tuple-element.62.value, bf16[256,1024]{1,0:T(8,128)(2,1)S(1)} %copy-done, ...), custom_call_target="tpu_custom_call", output_to_operand_aliasing={{1}: (9, {}), {2}: (10, {})} | custom-call | tf_op jit(solution)/shard_map/back_1/pallas_call | solution.py:37
  44.2 1.5 %back_2.1 = (bf16[3,256,256]{2,1,0:T(8,128)(2,1)S(1)}, f32[256,1024]{1,0:T(8,128)S(1)}, f32[256,1024]{1,0:T(8,128)S(1)}) custom-call(bf16[256,1024]{1,0:T(8,128)(2,1)S(1)} %get-tuple-element.61.key, bf16[256,1024]{1,0:T(8,128)(2,1)S(1)} %get-tuple-element.62.value, bf16[256,1024]{1,0:T(8,128)(2,1)S(1)} %copy-done, ...), custom_call_target="tpu_custom_call", output_to_operand_aliasing={{1}: (9, {}), {2}: (10, {})} | custom-call | tf_op jit(solution)/shard_map/back_2/pallas_call | solution.py:37
  45.7 0.0 collective-permute-done.9.states.states3
  45.7 0.8 %back_first.1 = (bf16[3,256,256]{2,1,0:T(8,128)(2,1)S(1)}, bf16[256,512]{1,0:T(8,128)(2,1)S(1)}) custom-call(bf16[256,1024]{1,0:T(8,128)(2,1)S(1)} %get-tuple-element.61.key, bf16[256,1024]{1,0:T(8,128)(2,1)S(1)} %get-tuple-element.62.value, bf16[256,1024]{1,0:T(8,128)(2,1)S(1)} %copy-done, f32[256,25]{1,0:T(8,128)S(1)} %get-tuple-element.63.cols_h, ...), custom_call_target="tpu_custom_call" | custom-call | tf_op jit(solution)/shard_map/back_first/pallas_call | solution.py:37
  46.5 0.1 collective-permute-start.10
  46.6 0.9 %back_second.1 = (bf16[256,512]{1,0:T(8,128)(2,1)S(1)}, f32[256,512]{1,0:T(8,128)S(1)}, f32[256,512]{1,0:T(8,128)S(1)}) custom-call(bf16[3,256,256]{2,1,0:T(8,128)(2,1)S(1)} %get-tuple-element.99.stack.stack3, bf16[3,4096,1024]{2,1,0:T(8,128)(2,1)S(1)} %get-tuple-element.55.refs_1_.w, f32[256,1024]{1,0:T(8,128)S(1)} %get-tuple-element.91.start3, ...), custom_call_target="tpu_custom_call" | custom-call | tf_op jit(solution)/shard_map/back_second/pallas_call | solution.py:37
  47.5 0.5 collective-permute-start.11
  48.0 0.1 collective-permute-done.10
  48.1 0.1 add_convert_fusion.1
  48.2 1.6 %collective-permute-start.12 = (bf16[256,512]{1,0:T(8,128)(2,1)S(1)}, bf16[256,512]{1,0:T(8,128)(2,1)S(1)}, u32[]{:S(2)}, u32[]{:S(2)}) collective-permute-start(bf16[256,512]{1,0:T(8,128)(2,1)S(1)} %add_convert_fusion.1), channel_id=1, source_target_pairs={{0,2},{1,3},{2,0},{3,1},{4,6},{5,7},{6,4},{7,5},{8,10},{9,11},{10,... | collective-permute-start | bytes 786440 | tf_op jit(solution)/shard_map/ppermute | solution.py:500
  49.8 0.1 add_convert_fusion
  49.8 1.0 %collective-permute-start.13 = (bf16[256,512]{1,0:T(8,128)(2,1)S(1)}, bf16[256,512]{1,0:T(8,128)(2,1)S(1)}, u32[]{:S(2)}, u32[]{:S(2)}) collective-permute-start(bf16[256,512]{1,0:T(8,128)(2,1)S(1)} %add_convert_fusion), channel_id=1, source_target_pairs={{0,2},{1,3},{2,0},{3,1},{4,6},{5,7},{6,4},{7,5},{8,10},{9,11},{10,... | collective-permute-start | bytes 786440 | tf_op jit(solution)/shard_map/ppermute | solution.py:503
  50.8 3.8 %back_rest.1 = (f32[256,1024]{1,0:T(8,128)S(1)}, bf16[256,1024]{1,0:T(8,128)(2,1)S(1)}, f32[256,1024]{1,0:T(8,128)S(1)}) custom-call(bf16[3,256,256]{2,1,0:T(8,128)(2,1)S(1)} %get-tuple-element.81.stack0, bf16[3,256,256]{2,1,0:T(8,128)(2,1)S(1)} %get-tuple-element.85.stack1, bf16[3,256,256]{2,1,0:T(8,128)(2,1)S(1)} %get-tuple-element.89.stack2, ...), custom_call_target="tpu_custom_call" | custom-call | tf_op jit(solution)/shard_map/back_rest/pallas_call | solution.py:37
  54.6 1.0 %copy.21 = f32[256,1024]{1,0:T(8,128)} copy(f32[256,1024]{1,0:T(8,128)S(1)} %get-tuple-element.112) | data formatting | bytes 2097152
  55.7 0.1 collective-permute-start.17
  55.8 0.4 collective-permute-start.16
  56.2 0.1 collective-permute-start.15
  56.3 1.1 %collective-permute-done.12.refs_0_ = bf16[256,512]{1,0:T(8,128)(2,1)S(1)} collective-permute-done((bf16[256,512]{1,0:T(8,128)(2,1)S(1)}, bf16[256,512]{1,0:T(8,128)(2,1)S(1)}, u32[]{:S(2)}, u32[]{:S(2)}) %collective-permute-start.12) | collective-permute-done | bytes 262176 | tf_op jit(solution)/shard_map/ppermute | solution.py:500
  57.4 4.8 %collective-permute-done.13.refs_1_ = bf16[256,512]{1,0:T(8,128)(2,1)S(1)} collective-permute-done((bf16[256,512]{1,0:T(8,128)(2,1)S(1)}, bf16[256,512]{1,0:T(8,128)(2,1)S(1)}, u32[]{:S(2)}, u32[]{:S(2)}) %collective-permute-start.13) | collective-permute-done | bytes 262176 | tf_op jit(solution)/shard_map/ppermute | solution.py:503
  62.2 0.0 collective-permute-done.17.refs_3_
  62.2 0.0 collective-permute-done.16.refs_2_
  62.2 0.0 collective-permute-done.15.refs_1_
  62.2 1.0 %last_sum.1 = f32[256,1024]{1,0:T(8,128)} custom-call(f32[256,1024]{1,0:T(8,128)S(1)} %get-tuple-element.102.own, bf16[256,512]{1,0:T(8,128)(2,1)S(1)} %get-tuple-element.105.across_a, bf16[256,512]{1,0:T(8,128)(2,1)S(1)} %get-tuple-element.106.across_b, bf16[64,1024]{1,0:T(8,128)(2,1)S(1)} %collective-permute-done.14.refs_0_, ...), custom_call_target="tpu_custom_call" | custom-call | tf_op jit(solution)/shard_map/last_sum/pallas_call | solution.py:37
  (10 shorter events, 0.1 us)
Async XLA Ops:
  0.6 15.2 %collective-permute-start = (bf16[256,1024]{1,0:T(8,128)(2,1)}, bf16[256,1024]{1,0:T(8,128)(2,1)S(1)}, u32[]{:S(2)}, u32[]{:S(2)}) collective-permute-start(bf16[256,1024]{1,0:T(8,128)(2,1)} %tokens.1), channel_id=1, source_target_pairs={{0,2},{1,3},{2,0},{3,1},{4,6},{5,7},{6,4},{7,5},{8,10},{9,11},{10,... | collective-permute-start | bytes 1572872 | tf_op jit(solution)/shard_map/ppermute | solution.py:430
  3.7 8.4 %collective-permute-start.1 = (bf16[256,1024]{1,0:T(8,128)(2,1)}, bf16[256,1024]{1,0:T(8,128)(2,1)S(1)}, u32[]{:S(2)}, u32[]{:S(2)}) collective-permute-start(bf16[256,1024]{1,0:T(8,128)(2,1)} %tokens.1), channel_id=1, source_target_pairs={{0,1},{1,0},{2,3},{3,2},{4,5},{5,4},{6,7},{7,6},{8,9},{9,8},{10,11... | collective-permute-start | bytes 1572872 | tf_op jit(solution)/shard_map/ppermute | solution.py:431
  13.9 3.8 %copy-start = (bf16[256,1024]{1,0:T(8,128)(2,1)S(1)}, bf16[256,1024]{1,0:T(8,128)(2,1)}, u32[]{:S(2)}) copy-start(bf16[256,1024]{1,0:T(8,128)(2,1)} %grads.11) | copy-start | bytes 1572868
  15.8 1.9 %collective-permute-start.2 = (bf16[256,1024]{1,0:T(8,128)(2,1)S(1)}, bf16[256,1024]{1,0:T(8,128)(2,1)S(1)}, u32[]{:S(2)}, u32[]{:S(2)}) collective-permute-start(bf16[256,1024]{1,0:T(8,128)(2,1)S(1)} %collective-permute-done.refs_0_), channel_id=1, source_target_pairs={{0,1},{1,0},{2,3},{3,2},{4,5},{5,4},{6,7},{7,6},{8,9},{9,8},{10,11... | collective-permute-start | bytes 1572872 | tf_op jit(solution)/shard_map/ppermute | solution.py:453
  20.2 7.2 %collective-permute-start.3 = (bf16[528,128]{1,0:T(8,128)(2,1)S(1)}, bf16[528,128]{1,0:T(8,128)(2,1)S(1)}, u32[]{:S(2)}, u32[]{:S(2)}) collective-permute-start(bf16[528,128]{1,0:T(8,128)(2,1)S(1)} %get-tuple-element.74), channel_id=1, source_target_pairs={{0,4},{4,0},{8,12},{12,8},{16,20},{20,16},{24,28},{28,24},{1,5},{5... | collective-permute-start | bytes 405512 | tf_op jit(solution)/shard_map/ppermute | solution.py:361
  22.0 6.4 %collective-permute-start.4 = (bf16[528,128]{1,0:T(8,128)(2,1)S(1)}, bf16[528,128]{1,0:T(8,128)(2,1)S(1)}, u32[]{:S(2)}, u32[]{:S(2)}) collective-permute-start(bf16[528,128]{1,0:T(8,128)(2,1)S(1)} %get-tuple-element.75), channel_id=1, source_target_pairs={{0,8},{4,12},{8,0},{12,4},{16,24},{20,28},{24,16},{28,20},{1,9},{5... | collective-permute-start | bytes 405512 | tf_op jit(solution)/shard_map/ppermute | solution.py:361
  23.6 6.8 %collective-permute-start.5 = (bf16[528,128]{1,0:T(8,128)(2,1)S(1)}, bf16[528,128]{1,0:T(8,128)(2,1)S(1)}, u32[]{:S(2)}, u32[]{:S(2)}) collective-permute-start(bf16[528,128]{1,0:T(8,128)(2,1)S(1)} %get-tuple-element.76), channel_id=1, source_target_pairs={{0,12},{4,8},{8,4},{12,0},{16,28},{20,24},{24,20},{28,16},{1,13},{... | collective-permute-start | bytes 405512 | tf_op jit(solution)/shard_map/ppermute | solution.py:361
  30.6 5.5 %collective-permute-start.6 = (bf16[256,128]{1,0:T(8,128)(2,1)S(1)}, bf16[256,128]{1,0:T(8,128)(2,1)S(1)}, u32[]{:S(2)}, u32[]{:S(2)}) collective-permute-start(bf16[256,128]{1,0:T(8,128)(2,1)S(1)} %get-tuple-element.79), channel_id=1, source_target_pairs={{0,16},{4,20},{8,24},{12,28},{16,0},{20,4},{24,8},{28,12},{1,17},{... | collective-permute-start | bytes 196616 | tf_op jit(solution)/shard_map/ppermute | solution.py:369
  36.2 6.4 %collective-permute-start.7 = (bf16[2,2,128,128]{3,2,1,0:T(8,128)(2,1)S(1)}, bf16[2,2,128,128]{3,2,1,0:T(8,128)(2,1)S(1)}, u32[]{:S(2)}, u32[]{:S(2)}) collective-permute-start(bf16[2,2,128,128]{3,2,1,0:T(8,128)(2,1)S(1)} %get-tuple-element.82), channel_id=1, source_target_pairs={{0,4},{4,0},{8,12},{12,8},{16,20},{20,16},{24,28},{28,24},{1,5},{5... | collective-permute-start | bytes 393224 | tf_op jit(solution)/shard_map/ppermute | solution.py:371
  37.7 6.4 %collective-permute-start.8 = (bf16[2,2,128,128]{3,2,1,0:T(8,128)(2,1)S(1)}, bf16[2,2,128,128]{3,2,1,0:T(8,128)(2,1)S(1)}, u32[]{:S(2)}, u32[]{:S(2)}) collective-permute-start(bf16[2,2,128,128]{3,2,1,0:T(8,128)(2,1)S(1)} %get-tuple-element.86), channel_id=1, source_target_pairs={{0,8},{4,12},{8,0},{12,4},{16,24},{20,28},{24,16},{28,20},{1,9},{5... | collective-permute-start | bytes 393224 | tf_op jit(solution)/shard_map/ppermute | solution.py:371
  39.3 6.4 %collective-permute-start.9 = (bf16[2,2,128,128]{3,2,1,0:T(8,128)(2,1)S(1)}, bf16[2,2,128,128]{3,2,1,0:T(8,128)(2,1)S(1)}, u32[]{:S(2)}, u32[]{:S(2)}) collective-permute-start(bf16[2,2,128,128]{3,2,1,0:T(8,128)(2,1)S(1)} %get-tuple-element.90), channel_id=1, source_target_pairs={{0,12},{4,8},{8,4},{12,0},{16,28},{20,24},{24,20},{28,16},{1,13},{... | collective-permute-start | bytes 393224 | tf_op jit(solution)/shard_map/ppermute | solution.py:371
  46.5 1.6 %collective-permute-start.10 = (bf16[256,512]{1,0:T(8,128)(2,1)S(1)}, bf16[256,512]{1,0:T(8,128)(2,1)S(1)}, u32[]{:S(2)}, u32[]{:S(2)}) collective-permute-start(bf16[256,512]{1,0:T(8,128)(2,1)S(1)} %get-tuple-element.95), channel_id=1, source_target_pairs={{0,1},{1,0},{2,3},{3,2},{4,5},{5,4},{6,7},{7,6},{8,9},{9,8},{10,11... | collective-permute-start | bytes 786440 | tf_op jit(solution)/shard_map/ppermute | solution.py:490
  47.5 2.3 %collective-permute-start.11 = (bf16[256,512]{1,0:T(8,128)(2,1)S(1)}, bf16[256,512]{1,0:T(8,128)(2,1)S(1)}, u32[]{:S(2)}, u32[]{:S(2)}) collective-permute-start(bf16[256,512]{1,0:T(8,128)(2,1)S(1)} %get-tuple-element.98), channel_id=1, source_target_pairs={{0,1},{1,0},{2,3},{3,2},{4,5},{5,4},{6,7},{7,6},{8,9},{9,8},{10,11... | collective-permute-start | bytes 786440 | tf_op jit(solution)/shard_map/ppermute | solution.py:497
  48.2 9.2 %collective-permute-start.12 = (bf16[256,512]{1,0:T(8,128)(2,1)S(1)}, bf16[256,512]{1,0:T(8,128)(2,1)S(1)}, u32[]{:S(2)}, u32[]{:S(2)}) collective-permute-start(bf16[256,512]{1,0:T(8,128)(2,1)S(1)} %add_convert_fusion.1), channel_id=1, source_target_pairs={{0,2},{1,3},{2,0},{3,1},{4,6},{5,7},{6,4},{7,5},{8,10},{9,11},{10,... | collective-permute-start | bytes 786440 | tf_op jit(solution)/shard_map/ppermute | solution.py:500
  49.8 12.4 %collective-permute-start.13 = (bf16[256,512]{1,0:T(8,128)(2,1)S(1)}, bf16[256,512]{1,0:T(8,128)(2,1)S(1)}, u32[]{:S(2)}, u32[]{:S(2)}) collective-permute-start(bf16[256,512]{1,0:T(8,128)(2,1)S(1)} %add_convert_fusion), channel_id=1, source_target_pairs={{0,2},{1,3},{2,0},{3,1},{4,6},{5,7},{6,4},{7,5},{8,10},{9,11},{10,... | collective-permute-start | bytes 786440 | tf_op jit(solution)/shard_map/ppermute | solution.py:503
  55.7 6.6 %collective-permute-start.17 = (bf16[64,1024]{1,0:T(8,128)(2,1)S(1)}, bf16[64,1024]{1,0:T(8,128)(2,1)S(1)}, u32[]{:S(2)}, u32[]{:S(2)}) collective-permute-start(bf16[64,1024]{1,0:T(8,128)(2,1)S(1)} %get-tuple-element.108), channel_id=1, source_target_pairs={{0,1},{1,0},{2,3},{3,2},{4,5},{5,4},{6,7},{7,6},{8,9},{9,8},{10,11... | collective-permute-start | bytes 393224 | tf_op jit(solution)/shard_map/ppermute | solution.py:510
  55.8 6.4 %collective-permute-start.16 = (bf16[64,1024]{1,0:T(8,128)(2,1)S(1)}, bf16[64,1024]{1,0:T(8,128)(2,1)S(1)}, u32[]{:S(2)}, u32[]{:S(2)}) collective-permute-start(bf16[64,1024]{1,0:T(8,128)(2,1)S(1)} %get-tuple-element.109), channel_id=1, source_target_pairs={{0,1},{1,0},{2,3},{3,2},{4,5},{5,4},{6,7},{7,6},{8,9},{9,8},{10,11... | collective-permute-start | bytes 393224 | tf_op jit(solution)/shard_map/ppermute | solution.py:510
  56.2 6.0 %collective-permute-start.15 = (bf16[64,1024]{1,0:T(8,128)(2,1)S(1)}, bf16[64,1024]{1,0:T(8,128)(2,1)S(1)}, u32[]{:S(2)}, u32[]{:S(2)}) collective-permute-start(bf16[64,1024]{1,0:T(8,128)(2,1)S(1)} %get-tuple-element.110), channel_id=1, source_target_pairs={{0,1},{1,0},{2,3},{3,2},{4,5},{5,4},{6,7},{7,6},{8,9},{9,8},{10,11... | collective-permute-start | bytes 393224 | tf_op jit(solution)/shard_map/ppermute | solution.py:510
  57.4 4.8 %collective-permute-start.14 = (bf16[64,1024]{1,0:T(8,128)(2,1)S(1)}, bf16[64,1024]{1,0:T(8,128)(2,1)S(1)}, u32[]{:S(2)}, u32[]{:S(2)}) collective-permute-start(bf16[64,1024]{1,0:T(8,128)(2,1)S(1)} %get-tuple-element.111), channel_id=1, source_target_pairs={{0,1},{1,0},{2,3},{3,2},{4,5},{5,4},{6,7},{7,6},{8,9},{9,8},{10,11... | collective-permute-start | bytes 393224 | tf_op jit(solution)/shard_map/ppermute | solution.py:510

commit v7 on v6

--- a/solution.py
+++ b/solution.py
@@ -27,8 +27,9 @@
     return dot(high, b, ca, cb) + dot(low, b, ca, cb)
 
 
-def call(kernel, name, outs, args, spaces=None, flops=0, limit=4, aliases=None, scratch=(), out_space=pltpu.VMEM):
+def call(kernel, name, outs, args, spaces=None, flops=0, limit=4, aliases=None, scratch=(), out_spaces=None):
     spaces = spaces or "v" * len(args)
+    out_spaces = out_spaces or "v" * len(outs)
     kinds = {"v": pltpu.VMEM, "s": pltpu.SMEM, "h": pltpu.HBM}
     placed = [
         a if s == "s" else pltpu.with_memory_space_constraint(a, kinds[s])
@@ -37,9 +38,9 @@
     return pl.pallas_call(
         kernel,
         name=name,
-        out_shape=[out_space(shape, dtype) for shape, dtype in outs],
+        out_shape=[kinds[s](shape, dtype) for s, (shape, dtype) in zip(out_spaces, outs)],
         in_specs=[pl.BlockSpec(memory_space=kinds[s]) for s in spaces],
-        out_specs=[pl.BlockSpec(memory_space=out_space)] * len(outs),
+        out_specs=[pl.BlockSpec(memory_space=kinds[s]) for s in out_spaces],
         input_output_aliases=aliases or {},
         scratch_shapes=scratch,
         compiler_params=pltpu.CompilerParams(vmem_limit_bytes=limit * MIB),
@@ -263,10 +264,10 @@
     back(2, [(0, stack)], w, out2)
 
 
-def back_more(d, key, value, grads, cols_h, gq, gk, gv, states, w, start3, start2, stack, out3, out2):
-    finish_quarter(d, key, value, grads, cols_h, gq, gk, gv, states, stack)
-    back(3, [(d, stack)], w, out3, 0, start3)
-    back(2, [(d, stack)], w, out2, 0, start2)
+def back_sides(key, value, grads, cols_h, gq, gk, gv, states1, states2, w, start3, stack1, stack2, out3):
+    finish_quarter(1, key, value, grads, cols_h, gq, gk, gv, states1, stack1)
+    finish_quarter(2, key, value, grads, cols_h, gq, gk, gv, states2, stack2)
+    back(3, [(1, stack1), (2, stack2)], w, out3, 0, start3)
 
 
 def back_first(key, value, grads, cols_h, gq, gk, gv, states, w, start3, stack, chunk3_a):
@@ -274,38 +275,50 @@
     back(3, [(3, stack)], w, chunk3_a, 0, start3)
 
 
-def back_second(stack, w, start3, start2, chunk3_b, chunk2_a, chunk2_b):
-    back(3, [(3, stack)], w, chunk3_b, start3.shape[1] - chunk3_b.shape[1], start3)
-    back(2, [(3, stack)], w, chunk2_a, 0, start2)
-    back(2, [(3, stack)], w, chunk2_b, chunk2_a.shape[1], start2)
+def back_second(stack1, stack2, stack3, w, start3, start2, chunk3_b, chunk2_a):
+    back(3, [(3, stack3)], w, chunk3_b, start3.shape[1] - chunk3_b.shape[1], start3)
+    back(2, [(1, stack1), (2, stack2), (3, stack3)], w, chunk2_a, 0, start2)
+
+
+def back_third(stack1, stack2, stack3, w, start2, chunk2_b):
+    back(2, [(1, stack1), (2, stack2), (3, stack3)], w, chunk2_b, start2.shape[1] - chunk2_b.shape[1], start2)
 
 
 def hand_on(*refs):
     pass
 
 
-def last_sum(own, across_a, across_b, *refs):
+def last_sum(own, across_b, *refs):
     besides, (out, total, sems) = refs[:-3], refs[-3:]
-    size, middle = besides[0].shape[0], across_a.shape[1]
+    size, middle = besides[0].shape[0], own.shape[1] - across_b.shape[1]
     copies = []
     for i, beside in enumerate(besides):
         rows = slice(i * size, (i + 1) * size)
-        for cols, across in ((slice(0, middle), across_a), (slice(middle, own.shape[1]), across_b)):
-            total[rows, cols] = (own[rows, cols] + beside[:, cols].astype(F32)) + across[rows, :].astype(F32)
+        total[rows, :middle] = own[rows, :middle] + beside[:, :middle].astype(F32)
+        right = own[rows, middle:] + beside[:, middle:].astype(F32)
+        total[rows, middle:] = right + across_b[rows, :].astype(F32)
         copies.append(pltpu.make_async_copy(total.at[rows, :], out.at[rows, :], sems.at[i]))
         copies[-1].start()
     for copy in copies:
         copy.wait()
 
 
-def back_rest(stack0, stack1, stack2, stack3, w, query, cols_h, out, states0, states1, states2, states3, *outs):
-    attn, chunk_other, chunk_own = outs
-    stacks = list(enumerate((stack0, stack1, stack2, stack3)))
-    back(1, stacks, w, chunk_other)
-    back(0, stacks, w, chunk_own)
+def back_mine(stack0, stack1, stack2, stack3, w, query, cols_h, out, states0, states1, states2, states3, *refs):
+    attn, chunk_own, attn_vm, sem = refs
     for d, states in enumerate((states0, states1, states2, states3)):
         for j, cols, lead, _ in quarter_heads(d, states.shape[1], cols_h):
-            attn[:, cols] = (out[:, cols] + dot(query[:, cols], states[0, j], 1, 0) * lead) * (1.0 / DH)
+            attn_vm[:, cols] = (out[:, cols] + dot(query[:, cols], states[0, j], 1, 0) * lead) * (1.0 / DH)
+    copy = pltpu.make_async_copy(attn_vm, attn, sem)
+    copy.start()
+    back(0, list(enumerate((stack0, stack1, stack2, stack3))), w, chunk_own)
+    copy.wait()
+
+
+def back_other(stack0, stack1, stack2, stack3, w, across_a, own_in, chunk_other, own):
+    back(1, list(enumerate((stack0, stack1, stack2, stack3))), w, chunk_other)
+    middle = across_a.shape[1]
+    own[:, :middle] = own_in[:, :middle] + across_a[...].astype(F32)
+    own[:, middle:] = own_in[:, middle:]
 
 
 def per_head(scale, matrix):
@@ -474,57 +487,55 @@
     stack0, start3, start2 = call(
         back_own, "back_own", [stack_shape, chunk_shape, chunk_shape], common + [states[0], w_vm]
     )
-    stacks = [stack0]
-    for d in (1, 2):
-        stack, start3, start2 = call(
-            functools.partial(back_more, d),
-            f"back_{d}",
-            [stack_shape, chunk_shape, chunk_shape],
-            common + [states[d], w_vm, start3, start2],
-            aliases={9: 1, 10: 2},
-        )
-        stacks.append(stack)
+    stack1, stack2, start3 = call(
+        back_sides,
+        "back_sides",
+        [stack_shape, stack_shape, chunk_shape],
+        common + [states[1], states[2], w_vm, start3],
+        aliases={10: 2},
+    )
     stack3, chunk3_a = call(
         back_first, "back_first", [stack_shape, ((length, part_a), BF16)], common + [states[3], w_vm, start3]
     )
     beside_a = lax.ppermute(chunk3_a, "tp", core)
-    chunk3_b, chunk_a, chunk_b = call(
-        back_second,
-        "back_second",
-        [((length, part_b), BF16), ((length, part_a), F32), ((length, part_b), F32)],
-        [stack3, w_vm, start3, start2],
+    late = [stack1, stack2, stack3, w_vm]
+    chunk3_b, chunk_a = call(
+        back_second, "back_second", [((length, part_b), BF16), ((length, part_a), F32)], late + [start3, start2]
     )
     beside_b = lax.ppermute(chunk3_b, "tp", core)
     chunk_a = (chunk_a + beside_a.astype(F32)).astype(BF16)
-    chunk_a, chunk_b = lax.optimization_barrier((chunk_a, chunk_b))
+    chunk_a, start2 = lax.optimization_barrier((chunk_a, start2))
     across_a = lax.ppermute(chunk_a, "tp", chip)
+    (chunk_b,) = call(back_third, "back_third", [((length, part_b), F32)], late + [start2])
     chunk_b = (chunk_b + beside_b.astype(F32)).astype(BF16)
-    chunk_b, stack3 = lax.optimization_barrier((chunk_b, stack3))
+    chunk_b, stack0 = lax.optimization_barrier((chunk_b, stack0))
     across_b = lax.ppermute(chunk_b, "tp", chip)
-    attn, chunk_other, chunk_own = call(
-        back_rest,
-        "back_rest",
-        [sum_shape, ((length, part), BF16), chunk_shape],
-        stacks + [stack3, w_vm, query, cols_h, inside[0]] + states,
+    attn, chunk_own = call(
+        back_mine,
+        "back_mine",
+        [sum_shape, chunk_shape],
+        [stack0] + late + [query, cols_h, inside[0]] + states,
+        out_spaces="hv",
+        scratch=[pltpu.VMEM(sum_shape[0], F32), pltpu.SemaphoreType.DMA],
+    )
+    chunk_other, chunk_own = call(
+        back_other,
+        "back_other",
+        [((length, part), BF16), chunk_shape],
+        [stack0] + late + [across_a, chunk_own],
+        flops=step_flops,
+        aliases={6: 1},
     )
     beside = [lax.ppermute(c, "tp", core) for c in jnp.split(chunk_other, 4)]
-    across = [across_a]
-    for more in ([], [across_b]):
-        across = list(across) + more
-        across = call(
-            hand_on,
-            "hand_on",
-            [(a.shape, BF16) for a in across],
-            across,
-            flops=8 * step_flops if more else 0,
-            aliases={i: i for i in range(len(across))},
-        )
+    (across_b,) = call(
+        hand_on, "hand_on", [(across_b.shape, BF16)], [across_b], flops=8 * step_flops, aliases={0: 0}
+    )
     (input_grad,) = call(
         last_sum,
         "last_sum",
         [chunk_shape],
-        [chunk_own] + list(across) + beside,
-        out_space=pltpu.HBM,
+        [chunk_own, across_b] + beside,
+        out_spaces="h",
         scratch=[pltpu.VMEM(chunk_shape[0], F32), pltpu.SemaphoreType.DMA((len(beside),))],
     )
     return attn, input_grad

time: 63.6 us -> 63 us (level)
  Pallas kernels: 29.7 us -> 30.9 us
  local copies, waits for them, and re-layouts: 1.01 us -> 0.04 us
  waiting for transfers between devices: 14.8 us -> 14 us
    ppermute x1, waiting for transfers between devices: 4.81 us -> 1.61 us  [local(): across_b = lax.ppermute(chunk_b, 'tp', chip)]
    ppermute x1, waiting for transfers between devices: 1.09 us -> 2.93 us  [local(): across_a = lax.ppermute(chunk_a, 'tp', chip)]
    pallas_call x16, Pallas kernels: 29.7 us -> 30.9 us  [call(): pl.pallas_call(kernel, name=name, out_shape=[kinds[s](shape, dtype) for s...]
    unnamed x3 -> x2, local copies, waits for them, and re-layouts: 0.98 us -> 0.01 us
  transfers between devices with their start and end apart: 18 -> 18, of which waited for: 9 -> 10; matrix products, arithmetic and copies ran while one was open for 2% -> 0% of each run, Pallas kernels for 39% -> 42%
where the time goes in v7:
time: 63 us; the launch traced here: 62.9 us
  Pallas kernels  30.9 us (49%)
  starting transfers between devices  16.8 us (27%)
  waiting for transfers between devices  14 us (22%)
  between operations  0.99 us (2%)
    pallas_call x16, Pallas kernels, call(): pl.pallas_call(kernel, name=name, out_shape=[kinds[s](shape, dtype) for s...  30.9 us
    ppermute x3, starting transfers between devices, states_direct(): lax.ppermute(message, 'seq', member(d))  3.55 us
    ppermute x3, starting transfers between devices, states_direct(): lax.ppermute(states[d], 'seq', member(d))  3.55 us
    ppermute x1, starting transfers between devices, local(): across = lax.ppermute(tokens, 'tp', chip)  3.03 us
    ppermute x3, waiting for transfers between devices, states_direct(): lax.ppermute(message, 'seq', member(d))  2.94 us
    ppermute x1, waiting for transfers between devices, local(): across_a = lax.ppermute(chunk_a, 'tp', chip)  2.93 us
    ppermute x1, starting transfers between devices, states_direct(): other = lax.ppermute(to_group, 'seq', member(4))  2.82 us
    ppermute x1, waiting for transfers between devices, states_direct(): other = lax.ppermute(to_group, 'seq', member(4))  2.65 us
  transfers between devices with their start and end apart: 18, of which 10 were waited for; matrix products, arithmetic and copies ran while one was open for 0% of the time, Pallas kernels for 42%

profile of v7, /device:TPU:0, one launch (start us, length us, event | category | flops | bytes accessed | tf_op | source)
XLA Modules:
  0.0 62.9 jit_solution(6632735618089453179)
XLA Ops:
  0.6 3.0 %collective-permute-start = (bf16[256,1024]{1,0:T(8,128)(2,1)}, bf16[256,1024]{1,0:T(8,128)(2,1)S(1)}, u32[]{:S(2)}, u32[]{:S(2)}) collective-permute-start(bf16[256,1024]{1,0:T(8,128)(2,1)} %tokens.1), channel_id=1, source_target_pairs={{0,2},{1,3},{2,0},{3,1},{4,6},{5,7},{6,4},{7,5},{8,10},{9,11},{10,... | collective-permute-start | bytes 1572872 | tf_op jit(solution)/shard_map/ppermute | solution.py:443
  3.7 0.0 collective-permute-start.1
  3.7 8.4 %load_and_project.1 = (bf16[3,4096,1024]{2,1,0:T(8,128)(2,1)S(1)}, f32[3,256,1024]{2,1,0:T(8,128)S(1)}, f32[256,25]{1,0:T(8,128)S(1)}, f32[24,256]{1,0:T(8,128)S(1)}, bf16[16,128]{1,0:T(8,128)(2,1)S(1)}) custom-call(s32[16]{0:T(128)} %lengths.1, f32[8,256]{1,0:T(8,128)} %bitcast.1, bf16[256,1024]{1,0:T(8,128)(2,1)} %tokens.1, bf16[3,4096,1024]{2,1,0:T(8,128)(2,1)} %w.1), custom_call_target="tpu_custom_call" | custom-call | flops 12884901888 | tf_op jit(solution)/shard_map/load_and_project/pallas_call | solution.py:38
  12.1 1.8 %project_beside.1.refs_2_ = f32[3,256,1024]{2,1,0:T(8,128)S(1)} custom-call(bf16[256,1024]{1,0:T(8,128)(2,1)S(1)} %collective-permute-done.1.refs_0_, bf16[3,4096,1024]{2,1,0:T(8,128)(2,1)S(1)} %get-tuple-element.50.refs_1_.w, f32[3,256,1024]{2,1,0:T(8,128)S(1)} %get-tuple-element.51.refs_2_), custom_call_target="tpu_custom_call" | custom-call | tf_op jit(solution)/shard_map/project_beside/pallas_call | solution.py:38
  13.9 0.0 copy-start
  13.9 1.9 %collective-permute-done.refs_0_ = bf16[256,1024]{1,0:T(8,128)(2,1)S(1)} collective-permute-done((bf16[256,1024]{1,0:T(8,128)(2,1)}, bf16[256,1024]{1,0:T(8,128)(2,1)S(1)}, u32[]{:S(2)}, u32[]{:S(2)}) %collective-permute-start) | collective-permute-done | bytes 524320 | tf_op jit(solution)/shard_map/ppermute | solution.py:443
  15.8 1.8 %project_across.1.acc_in = f32[3,256,1024]{2,1,0:T(8,128)S(1)} custom-call(bf16[256,1024]{1,0:T(8,128)(2,1)S(1)} %collective-permute-done.refs_0_, bf16[3,4096,1024]{2,1,0:T(8,128)(2,1)S(1)} %get-tuple-element.50.refs_1_.w, f32[3,256,1024]{2,1,0:T(8,128)S(1)} %project_beside.1.refs_2_), custom_call_target="tpu_custom_call" | custom-call | tf_op jit(solution)/shard_map/project_across/pallas_call | solution.py:38
  17.6 0.1 collective-permute-done.2.x
  17.7 2.5 %project_last.1 = (bf16[256,1024]{1,0:T(8,128)(2,1)S(1)}, bf16[256,1024]{1,0:T(8,128)(2,1)S(1)}, bf16[256,1024]{1,0:T(8,128)(2,1)S(1)}, f32[2,2,128,128]{3,2,1,0...) custom-call(bf16[256,1024]{1,0:T(8,128)(2,1)S(1)} %collective-permute-done.2, ...), custom_call_target="tpu_custom_call" | custom-call | tf_op jit(solution)/shard_map/project_last/pallas_call | solution.py:38
  20.2 1.8 %collective-permute-start.3 = (bf16[528,128]{1,0:T(8,128)(2,1)S(1)}, bf16[528,128]{1,0:T(8,128)(2,1)S(1)}, u32[]{:S(2)}, u32[]{:S(2)}) collective-permute-start(bf16[528,128]{1,0:T(8,128)(2,1)S(1)} %get-tuple-element.69), channel_id=1, source_target_pairs={{0,4},{4,0},{8,12},{12,8},{16,20},{20,16},{24,28},{28,24},{1,5},{5... | collective-permute-start | bytes 405512 | tf_op jit(solution)/shard_map/ppermute | solution.py:374
  22.0 1.6 %collective-permute-start.4 = (bf16[528,128]{1,0:T(8,128)(2,1)S(1)}, bf16[528,128]{1,0:T(8,128)(2,1)S(1)}, u32[]{:S(2)}, u32[]{:S(2)}) collective-permute-start(bf16[528,128]{1,0:T(8,128)(2,1)S(1)} %get-tuple-element.70), channel_id=1, source_target_pairs={{0,8},{4,12},{8,0},{12,4},{16,24},{20,28},{24,16},{28,20},{1,9},{5... | collective-permute-start | bytes 405512 | tf_op jit(solution)/shard_map/ppermute | solution.py:374
  23.6 0.2 collective-permute-start.5
  23.8 3.6 %intra.1 = (f32[256,1024]{1,0:T(8,128)S(1)}, f32[256,1024]{1,0:T(8,128)S(1)}, f32[256,1024]{1,0:T(8,128)S(1)}, f32[256,1024]{1,0:T(8,128)S(1)}) custom-call(bf16[256,1024]{1,0:T(8,128)(2,1)S(1)} %get-tuple-element.59.query, bf16[256,1024]{1,0:T(8,128)(2,1)S(1)} %get-tuple-element.56.key, bf16[256,1024]{1,0:T(8,128)(2,1)S(1)} %get-tuple-element.57.value, ...), custom_call_target="tpu_custom_call" | custom-call | flops 1073741824 | tf_op jit(solution)/shard_map/intra/pallas_call | solution.py:38
  27.4 0.0 collective-permute-done.3.got1
  27.4 1.0 %collective-permute-done.4.got2 = bf16[528,128]{1,0:T(8,128)(2,1)S(1)} collective-permute-done((bf16[528,128]{1,0:T(8,128)(2,1)S(1)}, bf16[528,128]{1,0:T(8,128)(2,1)S(1)}, u32[]{:S(2)}, u32[]{:S(2)}) %collective-permute-start.4) | collective-permute-done | bytes 135200 | tf_op jit(solution)/shard_map/ppermute | solution.py:374
  28.4 1.9 %collective-permute-done.5.got3 = bf16[528,128]{1,0:T(8,128)(2,1)S(1)} collective-permute-done((bf16[528,128]{1,0:T(8,128)(2,1)S(1)}, bf16[528,128]{1,0:T(8,128)(2,1)S(1)}, u32[]{:S(2)}, u32[]{:S(2)}) %collective-permute-start.5) | collective-permute-done | bytes 135200 | tf_op jit(solution)/shard_map/ppermute | solution.py:374
  30.3 0.3 join.1
  30.6 2.8 %collective-permute-start.6 = (bf16[256,128]{1,0:T(8,128)(2,1)S(1)}, bf16[256,128]{1,0:T(8,128)(2,1)S(1)}, u32[]{:S(2)}, u32[]{:S(2)}) collective-permute-start(bf16[256,128]{1,0:T(8,128)(2,1)S(1)} %get-tuple-element.74), channel_id=1, source_target_pairs={{0,16},{4,20},{8,24},{12,28},{16,0},{20,4},{24,8},{28,12},{1,17},{... | collective-permute-start | bytes 196616 | tf_op jit(solution)/shard_map/ppermute | solution.py:382
  33.4 2.6 %collective-permute-done.6.other = bf16[256,128]{1,0:T(8,128)(2,1)S(1)} collective-permute-done((bf16[256,128]{1,0:T(8,128)(2,1)S(1)}, bf16[256,128]{1,0:T(8,128)(2,1)S(1)}, u32[]{:S(2)}, u32[]{:S(2)}) %collective-permute-start.6) | collective-permute-done | bytes 65568 | tf_op jit(solution)/shard_map/ppermute | solution.py:382
  36.1 0.1 spread.1
  36.2 1.6 %collective-permute-start.7 = (bf16[2,2,128,128]{3,2,1,0:T(8,128)(2,1)S(1)}, bf16[2,2,128,128]{3,2,1,0:T(8,128)(2,1)S(1)}, u32[]{:S(2)}, u32[]{:S(2)}) collective-permute-start(bf16[2,2,128,128]{3,2,1,0:T(8,128)(2,1)S(1)} %get-tuple-element.75), channel_id=1, source_target_pairs={{0,4},{4,0},{8,12},{12,8},{16,20},{20,16},{24,28},{28,24},{1,5},{5... | collective-permute-start | bytes 393224 | tf_op jit(solution)/shard_map/ppermute | solution.py:384
  37.7 1.5 %collective-permute-start.8 = (bf16[2,2,128,128]{3,2,1,0:T(8,128)(2,1)S(1)}, bf16[2,2,128,128]{3,2,1,0:T(8,128)(2,1)S(1)}, u32[]{:S(2)}, u32[]{:S(2)}) collective-permute-start(bf16[2,2,128,128]{3,2,1,0:T(8,128)(2,1)S(1)} %get-tuple-element.76), channel_id=1, source_target_pairs={{0,8},{4,12},{8,0},{12,4},{16,24},{20,28},{24,16},{28,20},{1,9},{5... | collective-permute-start | bytes 393224 | tf_op jit(solution)/shard_map/ppermute | solution.py:384
  39.2 0.5 collective-permute-start.9
  39.7 1.6 %back_own.1 = (bf16[3,256,256]{2,1,0:T(8,128)(2,1)S(1)}, f32[256,1024]{1,0:T(8,128)S(1)}, f32[256,1024]{1,0:T(8,128)S(1)}) custom-call(bf16[256,1024]{1,0:T(8,128)(2,1)S(1)} %get-tuple-element.56.key, bf16[256,1024]{1,0:T(8,128)(2,1)S(1)} %get-tuple-element.57.value, bf16[256,1024]{1,0:T(8,128)(2,1)S(1)} %copy-done, f32[256,25]{1,0:T(8,128)S(1)} %get-tuple-element.58.cols_h, ...), custom_call_target="tpu_custom_call" | custom-call | tf_op jit(solution)/shard_map/back_own/pallas_call | solution.py:38
  41.4 1.2 %collective-permute-done.7.states1 = bf16[2,2,128,128]{3,2,1,0:T(8,128)(2,1)S(1)} collective-permute-done((bf16[2,2,128,128]{3,2,1,0:T(8,128)(2,1)S(1)}, bf16[2,2,128,128]{3,2,1,0:T(8,128)(2,1)S(1)}, u32[]{:S(2)}, u32[]{:S(2)}) %collective-permute-start.7) | collective-permute-done | bytes 131104 | tf_op jit(solution)/shard_map/ppermute | solution.py:384
  42.6 0.1 collective-permute-done.8.states2
  42.7 1.9 %back_sides.1 = (bf16[3,256,256]{2,1,0:T(8,128)(2,1)S(1)}, bf16[3,256,256]{2,1,0:T(8,128)(2,1)S(1)}, f32[256,1024]{1,0:T(8,128)S(1)}) custom-call(bf16[256,1024]{1,0:T(8,128)(2,1)S(1)} %get-tuple-element.56.key, bf16[256,1024]{1,0:T(8,128)(2,1)S(1)} %get-tuple-element.57.value, bf16[256,1024]{1,0:T(8,128)(2,1)S(1)} %copy-done, ...), custom_call_target="tpu_custom_call", output_to_operand_aliasing={{2}: (10, {})} | custom-call | tf_op jit(solution)/shard_map/back_sides/pallas_call | solution.py:38
  44.6 0.5 collective-permute-done.9.states.states3
  45.1 0.8 %back_first.1 = (bf16[3,256,256]{2,1,0:T(8,128)(2,1)S(1)}, bf16[256,512]{1,0:T(8,128)(2,1)S(1)}) custom-call(bf16[256,1024]{1,0:T(8,128)(2,1)S(1)} %get-tuple-element.56.key, bf16[256,1024]{1,0:T(8,128)(2,1)S(1)} %get-tuple-element.57.value, bf16[256,1024]{1,0:T(8,128)(2,1)S(1)} %copy-done, f32[256,25]{1,0:T(8,128)S(1)} %get-tuple-element.58.cols_h, ...), custom_call_target="tpu_custom_call" | custom-call | tf_op jit(solution)/shard_map/back_first/pallas_call | solution.py:38
  45.9 0.1 collective-permute-start.10
  46.0 1.0 %back_second.1 = (bf16[256,512]{1,0:T(8,128)(2,1)S(1)}, f32[256,512]{1,0:T(8,128)S(1)}) custom-call(bf16[3,256,256]{2,1,0:T(8,128)(2,1)S(1)} %get-tuple-element.79.stack1, bf16[3,256,256]{2,1,0:T(8,128)(2,1)S(1)} %get-tuple-element.80.stack2, bf16[3,256,256]{2,1,0:T(8,128)(2,1)S(1)} %get-tuple-element.83.stack3, ...), custom_call_target="tpu_custom_call" | custom-call | tf_op jit(solution)/shard_map/back_second/pallas_call | solution.py:38
  47.1 0.5 collective-permute-start.11
  47.6 0.0 collective-permute-done.10
  47.6 0.1 add_convert_fusion.1
  47.7 1.6 %collective-permute-start.12 = (bf16[256,512]{1,0:T(8,128)(2,1)S(1)}, bf16[256,512]{1,0:T(8,128)(2,1)S(1)}, u32[]{:S(2)}, u32[]{:S(2)}) collective-permute-start(bf16[256,512]{1,0:T(8,128)(2,1)S(1)} %add_convert_fusion.1), channel_id=1, source_target_pairs={{0,2},{1,3},{2,0},{3,1},{4,6},{5,7},{6,4},{7,5},{8,10},{9,11},{10,... | collective-permute-start | bytes 786440 | tf_op jit(solution)/shard_map/ppermute | solution.py:508
  49.3 0.8 %back_third.1 = f32[256,512]{1,0:T(8,128)S(1)} custom-call(bf16[3,256,256]{2,1,0:T(8,128)(2,1)S(1)} %get-tuple-element.79.stack1, bf16[3,256,256]{2,1,0:T(8,128)(2,1)S(1)} %get-tuple-element.80.stack2, bf16[3,256,256]{2,1,0:T(8,128)(2,1)S(1)} %get-tuple-element.83.stack3, bf16[3,4096,1024]{2,1,0:T(8,128)(2,1)S(1)} %get-tuple-element.50.refs_1_.w, ...), custom_call_target="tpu_custom_call" | custom-call | tf_op jit(solution)/shard_map/back_third/pallas_call | solution.py:38
  50.1 0.1 add_convert_fusion
  50.2 0.6 collective-permute-start.13
  50.7 3.2 %back_mine.1 = (f32[256,1024]{1,0:T(8,128)}, f32[256,1024]{1,0:T(8,128)S(1)}) custom-call(bf16[3,256,256]{2,1,0:T(8,128)(2,1)S(1)} %get-tuple-element.90.stack0, bf16[3,256,256]{2,1,0:T(8,128)(2,1)S(1)} %get-tuple-element.79.stack1, bf16[3,256,256]{2,1,0:T(8,128)(2,1)S(1)} %get-tuple-element.80.stack2, bf16[3,256,256]{2,1,0:T(8,128)(2,1)S(1)} %get-tuple-element.83.stack3, ...), custom_call_target="tpu_custom_call" | custom-call | tf_op jit(solution)/shard_map/back_mine/pallas_call | solution.py:38
  54.0 2.9 %collective-permute-done.12.across_a = bf16[256,512]{1,0:T(8,128)(2,1)S(1)} collective-permute-done((bf16[256,512]{1,0:T(8,128)(2,1)S(1)}, bf16[256,512]{1,0:T(8,128)(2,1)S(1)}, u32[]{:S(2)}, u32[]{:S(2)}) %collective-permute-start.12) | collective-permute-done | bytes 262176 | tf_op jit(solution)/shard_map/ppermute | solution.py:508
  56.9 2.0 %back_other.1 = (bf16[256,1024]{1,0:T(8,128)(2,1)S(1)}, f32[256,1024]{1,0:T(8,128)S(1)}) custom-call(bf16[3,256,256]{2,1,0:T(8,128)(2,1)S(1)} %get-tuple-element.90.stack0, bf16[3,256,256]{2,1,0:T(8,128)(2,1)S(1)} %get-tuple-element.79.stack1, bf16[3,256,256]{2,1,0:T(8,128)(2,1)S(1)} %get-tuple-element.80.stack2, ...), custom_call_target="tpu_custom_call", output_to_operand_aliasing={{1}: (6, {})} | custom-call | flops 1610612736 | tf_op jit(solution)/shard_map/back_other/pallas_call | solution.py:38
  58.9 0.1 collective-permute-start.17
  59.0 0.5 collective-permute-start.16
  59.5 0.1 collective-permute-start.15
  59.6 0.4 collective-permute-start.14
  60.0 1.6 %collective-permute-done.13.refs_0_ = bf16[256,512]{1,0:T(8,128)(2,1)S(1)} collective-permute-done((bf16[256,512]{1,0:T(8,128)(2,1)S(1)}, bf16[256,512]{1,0:T(8,128)(2,1)S(1)}, u32[]{:S(2)}, u32[]{:S(2)}) %collective-permute-start.13) | collective-permute-done | bytes 262176 | tf_op jit(solution)/shard_map/ppermute | solution.py:512
  61.6 0.0 collective-permute-done.17.refs_3_
  61.7 1.0 %last_sum.1 = f32[256,1024]{1,0:T(8,128)} custom-call(f32[256,1024]{1,0:T(8,128)S(1)} %get-tuple-element.95.own, bf16[256,512]{1,0:T(8,128)(2,1)S(1)} %hand_on.1.across_b, bf16[64,1024]{1,0:T(8,128)(2,1)S(1)} %collective-permute-done.14.refs_0_, bf16[64,1024]{1,0:T(8,128)(2,1)S(1)} %collective-permute-done.15.refs_1_, ...), custom_call_target="tpu_custom_call" | custom-call | tf_op jit(solution)/shard_map/last_sum/pallas_call | solution.py:38
  (9 shorter events, 0.1 us)
Async XLA Ops:
  0.6 15.2 %collective-permute-start = (bf16[256,1024]{1,0:T(8,128)(2,1)}, bf16[256,1024]{1,0:T(8,128)(2,1)S(1)}, u32[]{:S(2)}, u32[]{:S(2)}) collective-permute-start(bf16[256,1024]{1,0:T(8,128)(2,1)} %tokens.1), channel_id=1, source_target_pairs={{0,2},{1,3},{2,0},{3,1},{4,6},{5,7},{6,4},{7,5},{8,10},{9,11},{10,... | collective-permute-start | bytes 1572872 | tf_op jit(solution)/shard_map/ppermute | solution.py:443
  3.7 8.4 %collective-permute-start.1 = (bf16[256,1024]{1,0:T(8,128)(2,1)}, bf16[256,1024]{1,0:T(8,128)(2,1)S(1)}, u32[]{:S(2)}, u32[]{:S(2)}) collective-permute-start(bf16[256,1024]{1,0:T(8,128)(2,1)} %tokens.1), channel_id=1, source_target_pairs={{0,1},{1,0},{2,3},{3,2},{4,5},{5,4},{6,7},{7,6},{8,9},{9,8},{10,11... | collective-permute-start | bytes 1572872 | tf_op jit(solution)/shard_map/ppermute | solution.py:444
  13.9 3.8 %copy-start = (bf16[256,1024]{1,0:T(8,128)(2,1)S(1)}, bf16[256,1024]{1,0:T(8,128)(2,1)}, u32[]{:S(2)}) copy-start(bf16[256,1024]{1,0:T(8,128)(2,1)} %grads.9) | copy-start | bytes 1572868
  15.8 1.9 %collective-permute-start.2 = (bf16[256,1024]{1,0:T(8,128)(2,1)S(1)}, bf16[256,1024]{1,0:T(8,128)(2,1)S(1)}, u32[]{:S(2)}, u32[]{:S(2)}) collective-permute-start(bf16[256,1024]{1,0:T(8,128)(2,1)S(1)} %collective-permute-done.refs_0_), channel_id=1, source_target_pairs={{0,1},{1,0},{2,3},{3,2},{4,5},{5,4},{6,7},{7,6},{8,9},{9,8},{10,11... | collective-permute-start | bytes 1572872 | tf_op jit(solution)/shard_map/ppermute | solution.py:466
  20.2 7.2 %collective-permute-start.3 = (bf16[528,128]{1,0:T(8,128)(2,1)S(1)}, bf16[528,128]{1,0:T(8,128)(2,1)S(1)}, u32[]{:S(2)}, u32[]{:S(2)}) collective-permute-start(bf16[528,128]{1,0:T(8,128)(2,1)S(1)} %get-tuple-element.69), channel_id=1, source_target_pairs={{0,4},{4,0},{8,12},{12,8},{16,20},{20,16},{24,28},{28,24},{1,5},{5... | collective-permute-start | bytes 405512 | tf_op jit(solution)/shard_map/ppermute | solution.py:374
  22.0 6.4 %collective-permute-start.4 = (bf16[528,128]{1,0:T(8,128)(2,1)S(1)}, bf16[528,128]{1,0:T(8,128)(2,1)S(1)}, u32[]{:S(2)}, u32[]{:S(2)}) collective-permute-start(bf16[528,128]{1,0:T(8,128)(2,1)S(1)} %get-tuple-element.70), channel_id=1, source_target_pairs={{0,8},{4,12},{8,0},{12,4},{16,24},{20,28},{24,16},{28,20},{1,9},{5... | collective-permute-start | bytes 405512 | tf_op jit(solution)/shard_map/ppermute | solution.py:374
  23.6 6.8 %collective-permute-start.5 = (bf16[528,128]{1,0:T(8,128)(2,1)S(1)}, bf16[528,128]{1,0:T(8,128)(2,1)S(1)}, u32[]{:S(2)}, u32[]{:S(2)}) collective-permute-start(bf16[528,128]{1,0:T(8,128)(2,1)S(1)} %get-tuple-element.71), channel_id=1, source_target_pairs={{0,12},{4,8},{8,4},{12,0},{16,28},{20,24},{24,20},{28,16},{1,13},{... | collective-permute-start | bytes 405512 | tf_op jit(solution)/shard_map/ppermute | solution.py:374
  30.6 5.5 %collective-permute-start.6 = (bf16[256,128]{1,0:T(8,128)(2,1)S(1)}, bf16[256,128]{1,0:T(8,128)(2,1)S(1)}, u32[]{:S(2)}, u32[]{:S(2)}) collective-permute-start(bf16[256,128]{1,0:T(8,128)(2,1)S(1)} %get-tuple-element.74), channel_id=1, source_target_pairs={{0,16},{4,20},{8,24},{12,28},{16,0},{20,4},{24,8},{28,12},{1,17},{... | collective-permute-start | bytes 196616 | tf_op jit(solution)/shard_map/ppermute | solution.py:382
  36.2 6.4 %collective-permute-start.7 = (bf16[2,2,128,128]{3,2,1,0:T(8,128)(2,1)S(1)}, bf16[2,2,128,128]{3,2,1,0:T(8,128)(2,1)S(1)}, u32[]{:S(2)}, u32[]{:S(2)}) collective-permute-start(bf16[2,2,128,128]{3,2,1,0:T(8,128)(2,1)S(1)} %get-tuple-element.75), channel_id=1, source_target_pairs={{0,4},{4,0},{8,12},{12,8},{16,20},{20,16},{24,28},{28,24},{1,5},{5... | collective-permute-start | bytes 393224 | tf_op jit(solution)/shard_map/ppermute | solution.py:384
  37.7 5.0 %collective-permute-start.8 = (bf16[2,2,128,128]{3,2,1,0:T(8,128)(2,1)S(1)}, bf16[2,2,128,128]{3,2,1,0:T(8,128)(2,1)S(1)}, u32[]{:S(2)}, u32[]{:S(2)}) collective-permute-start(bf16[2,2,128,128]{3,2,1,0:T(8,128)(2,1)S(1)} %get-tuple-element.76), channel_id=1, source_target_pairs={{0,8},{4,12},{8,0},{12,4},{16,24},{20,28},{24,16},{28,20},{1,9},{5... | collective-permute-start | bytes 393224 | tf_op jit(solution)/shard_map/ppermute | solution.py:384
  39.2 5.9 %collective-permute-start.9 = (bf16[2,2,128,128]{3,2,1,0:T(8,128)(2,1)S(1)}, bf16[2,2,128,128]{3,2,1,0:T(8,128)(2,1)S(1)}, u32[]{:S(2)}, u32[]{:S(2)}) collective-permute-start(bf16[2,2,128,128]{3,2,1,0:T(8,128)(2,1)S(1)} %get-tuple-element.81), channel_id=1, source_target_pairs={{0,12},{4,8},{8,4},{12,0},{16,28},{20,24},{24,20},{28,16},{1,13},{... | collective-permute-start | bytes 393224 | tf_op jit(solution)/shard_map/ppermute | solution.py:384
  45.9 1.7 %collective-permute-start.10 = (bf16[256,512]{1,0:T(8,128)(2,1)S(1)}, bf16[256,512]{1,0:T(8,128)(2,1)S(1)}, u32[]{:S(2)}, u32[]{:S(2)}) collective-permute-start(bf16[256,512]{1,0:T(8,128)(2,1)S(1)} %get-tuple-element.86), channel_id=1, source_target_pairs={{0,1},{1,0},{2,3},{3,2},{4,5},{5,4},{6,7},{7,6},{8,9},{9,8},{10,11... | collective-permute-start | bytes 786440 | tf_op jit(solution)/shard_map/ppermute | solution.py:500
  47.1 3.0 %collective-permute-start.11 = (bf16[256,512]{1,0:T(8,128)(2,1)S(1)}, bf16[256,512]{1,0:T(8,128)(2,1)S(1)}, u32[]{:S(2)}, u32[]{:S(2)}) collective-permute-start(bf16[256,512]{1,0:T(8,128)(2,1)S(1)} %get-tuple-element.88), channel_id=1, source_target_pairs={{0,1},{1,0},{2,3},{3,2},{4,5},{5,4},{6,7},{7,6},{8,9},{9,8},{10,11... | collective-permute-start | bytes 786440 | tf_op jit(solution)/shard_map/ppermute | solution.py:505
  47.7 9.2 %collective-permute-start.12 = (bf16[256,512]{1,0:T(8,128)(2,1)S(1)}, bf16[256,512]{1,0:T(8,128)(2,1)S(1)}, u32[]{:S(2)}, u32[]{:S(2)}) collective-permute-start(bf16[256,512]{1,0:T(8,128)(2,1)S(1)} %add_convert_fusion.1), channel_id=1, source_target_pairs={{0,2},{1,3},{2,0},{3,1},{4,6},{5,7},{6,4},{7,5},{8,10},{9,11},{10,... | collective-permute-start | bytes 786440 | tf_op jit(solution)/shard_map/ppermute | solution.py:508
  50.2 11.5 %collective-permute-start.13 = (bf16[256,512]{1,0:T(8,128)(2,1)S(1)}, bf16[256,512]{1,0:T(8,128)(2,1)S(1)}, u32[]{:S(2)}, u32[]{:S(2)}) collective-permute-start(bf16[256,512]{1,0:T(8,128)(2,1)S(1)} %add_convert_fusion), channel_id=1, source_target_pairs={{0,2},{1,3},{2,0},{3,1},{4,6},{5,7},{6,4},{7,5},{8,10},{9,11},{10,... | collective-permute-start | bytes 786440 | tf_op jit(solution)/shard_map/ppermute | solution.py:512
  58.9 2.7 %collective-permute-start.17 = (bf16[64,1024]{1,0:T(8,128)(2,1)S(1)}, bf16[64,1024]{1,0:T(8,128)(2,1)S(1)}, u32[]{:S(2)}, u32[]{:S(2)}) collective-permute-start(bf16[64,1024]{1,0:T(8,128)(2,1)S(1)} %get-tuple-element.98), channel_id=1, source_target_pairs={{0,1},{1,0},{2,3},{3,2},{4,5},{5,4},{6,7},{7,6},{8,9},{9,8},{10,11... | collective-permute-start | bytes 393224 | tf_op jit(solution)/shard_map/ppermute | solution.py:529
  59.0 2.6 %collective-permute-start.16 = (bf16[64,1024]{1,0:T(8,128)(2,1)S(1)}, bf16[64,1024]{1,0:T(8,128)(2,1)S(1)}, u32[]{:S(2)}, u32[]{:S(2)}) collective-permute-start(bf16[64,1024]{1,0:T(8,128)(2,1)S(1)} %get-tuple-element.99), channel_id=1, source_target_pairs={{0,1},{1,0},{2,3},{3,2},{4,5},{5,4},{6,7},{7,6},{8,9},{9,8},{10,11... | collective-permute-start | bytes 393224 | tf_op jit(solution)/shard_map/ppermute | solution.py:529
  59.5 2.1 %collective-permute-start.15 = (bf16[64,1024]{1,0:T(8,128)(2,1)S(1)}, bf16[64,1024]{1,0:T(8,128)(2,1)S(1)}, u32[]{:S(2)}, u32[]{:S(2)}) collective-permute-start(bf16[64,1024]{1,0:T(8,128)(2,1)S(1)} %get-tuple-element.100), channel_id=1, source_target_pairs={{0,1},{1,0},{2,3},{3,2},{4,5},{5,4},{6,7},{7,6},{8,9},{9,8},{10,11... | collective-permute-start | bytes 393224 | tf_op jit(solution)/shard_map/ppermute | solution.py:529
  59.6 2.1 %collective-permute-start.14 = (bf16[64,1024]{1,0:T(8,128)(2,1)S(1)}, bf16[64,1024]{1,0:T(8,128)(2,1)S(1)}, u32[]{:S(2)}, u32[]{:S(2)}) collective-permute-start(bf16[64,1024]{1,0:T(8,128)(2,1)S(1)} %get-tuple-element.101), channel_id=1, source_target_pairs={{0,1},{1,0},{2,3},{3,2},{4,5},{5,4},{6,7},{7,6},{8,9},{9,8},{10,11... | collective-permute-start | bytes 393224 | tf_op jit(solution)/shard_map/ppermute | solution.py:529

commit v8 on v7

--- a/solution.py
+++ b/solution.py
@@ -61,6 +61,11 @@
 def group_place():
     place = lax.axis_index("seq")
     return place % 4, place // 4
+
+
+def order_of(turn):
+    odd = lax.axis_index("tp") % 2
+    return (0, 1 + odd, 2 - odd, 3)[turn]
 
 
 def pick(index, values):
@@ -162,7 +167,7 @@
     for d, to in enumerate((mine, to1, to2, to3)):
         for i in range(2):
             for j in range(quarter):
-                state = states[i, (place ^ d) * quarter + j]
+                state = states[i, (place ^ order_of(d)) * quarter + j]
                 if d:
                     first = (i * quarter + j) * DH
                     to[first : first + DH, :] = state.astype(BF16)
@@ -229,7 +234,7 @@
 
 
 def quarter_heads(d, quarter, cols_h):
-    member = group_place()[0] ^ d
+    member = group_place()[0] ^ order_of(d)
     for j in range(quarter):
         lead, tail = [pick(member, [columns(cols_h, c * quarter + j)[i] for c in range(4)]) for i in (1, 2)]
         yield j, pl.ds(pl.multiple_of((member * quarter + j) * DH, DH), DH), lead, tail
@@ -237,7 +242,7 @@
 
 def quarter_columns(d, w):
     width = w.shape[2] // 4
-    return pl.ds(pl.multiple_of((group_place()[0] ^ d) * width, width), width)
+    return pl.ds(pl.multiple_of((group_place()[0] ^ order_of(d)) * width, width), width)
 
 
 def finish_quarter(d, key, value, grads, cols_h, gq, gk, gv, states, stack):
@@ -333,9 +338,13 @@
 def join_kernel(own_through, mine, got1, got2, got3, to_group, inner, factors):
     quarter = mine.shape[1]
     place, group = group_place()
-    gots = (got1, got2, got3)
-    through = [own_through] + [got.at[2 * quarter * DH :, :] for got in gots]
-    through = [head_factors(rows[...]) for rows in through]
+    odd = order_of(1) == 2
+
+    def by_member(first, rows):
+        one, two, three = [got[rows, :] for got in (got1, got2, got3)]
+        return [first, jnp.where(odd, two, one), jnp.where(odd, one, two), three]
+
+    through = [head_factors(rows) for rows in by_member(own_through[...], slice(2 * quarter * DH, got1.shape[0]))]
     ones = jnp.ones((1, DH), F32)
     for j in range(quarter):
         step = [pick(place, [t[c * quarter + j : c * quarter + j + 1] for c in range(4)]) for t in through]
@@ -343,7 +352,7 @@
         totals = []
         for i in range(2):
             first = (i * quarter + j) * DH
-            own = [mine[i, j]] + [got[first : first + DH, :].astype(F32) for got in gots]
+            own = [a.astype(F32) for a in by_member(mine[i, j], slice(first, first + DH))]
             own = [pick(place, [own[k ^ p] for p in range(4)]) for k in range(4)]
             order = (0, 1, 2, 3) if i == 0 else (3, 2, 1, 0)
             state, factor = jnp.zeros((DH, DH), F32), ones
@@ -359,19 +368,30 @@
     place, group = group_place()
     for j in range(quarter):
         arrived = other[j * DH : (j + 1) * DH, :].astype(F32)
-        for d, out in enumerate(outs):
+        for turn, out in enumerate(outs):
+            k = place ^ order_of(turn)
             for i in range(2):
-                factor = jnp.where(group == 1 - i, factors[i, place ^ d, j], 0.0)
-                out[i, j] = (inner[i, place ^ d, j] + factor * arrived).astype(BF16)
-
-
-def member(d):
-    return [(i, i ^ d) for i in range(8)]
+                factor = jnp.where(group == 1 - i, factors[i, k, j], 0.0)
+                out[i, j] = (inner[i, k, j] + factor * arrived).astype(BF16)
+
+
+def to_other_group(a):
+    return lax.ppermute(a, "seq", [(i, i ^ 4) for i in range(8)])
+
+
+def to_member(a, turn):
+    seqs, tps = lax.axis_size("seq"), lax.axis_size("tp")
+    pairs = []
+    for i in range(seqs):
+        for t in range(tps):
+            partner = i ^ (0, 1 + t % 2, 2 - t % 2, 3)[turn]
+            pairs.append((i * tps + t, partner * tps + t))
+    return lax.ppermute(a, ("seq", "tp"), pairs)
 
 
 def states_direct(own_through, mine, messages, inside):
     quarter = mine.shape[1]
-    got = [lax.ppermute(message, "seq", member(d)) for d, message in zip((1, 2, 3), messages)]
+    got = [to_member(message, turn) for turn, message in zip((1, 2, 3), messages)]
     inside, mine = lax.optimization_barrier((inside, mine))
     to_group, inner, factors = call(
         join_kernel,
@@ -379,9 +399,9 @@
         [((quarter * DH, DH), BF16), ((2, 4, quarter, DH, DH), F32), ((2, 4, quarter, 1, DH), F32)],
         [own_through, mine] + got,
     )
-    other = lax.ppermute(to_group, "seq", member(4))
+    other = to_other_group(to_group)
     states = call(spread_kernel, "spread", [(mine.shape, BF16)] * 4, [inner, factors, other])
-    return [states[0]] + [lax.ppermute(states[d], "seq", member(d)) for d in (1, 2, 3)], inside
+    return [states[0]] + [to_member(states[turn], turn) for turn in (1, 2, 3)], inside
 
 
 def states_gathered(own, through):

time: 63 us -> 62.1 us (0.986)
  waiting for transfers between devices: 14 us -> 13.2 us
    ppermute x7, waiting for transfers between devices: 7.45 us -> 6.68 us  [the longest x6 4.1 us: to_member(): return lax.ppermute(a, ('seq', 'tp'), pairs)]
  transfers between devices with their start and end apart: 18 -> 18, of which waited for: 10 -> 9; matrix products, arithmetic and copies ran while one was open for 0% -> 0% of each run, Pallas kernels for 42% -> 42%
where the time goes in v8:
time: 62.1 us; the launch traced here: 61.9 us
  Pallas kernels  30.9 us (50%)
  starting transfers between devices  16.7 us (27%)
  waiting for transfers between devices  13.2 us (21%)
  between operations  0.99 us (2%)
    pallas_call x16, Pallas kernels, call(): pl.pallas_call(kernel, name=name, out_shape=[kinds[s](shape, dtype) for s...  30.9 us
    ppermute x6, starting transfers between devices, to_member(): return lax.ppermute(a, ('seq', 'tp'), pairs)  7.11 us
    ppermute x6, waiting for transfers between devices, to_member(): return lax.ppermute(a, ('seq', 'tp'), pairs)  4.1 us
    ppermute x1, starting transfers between devices, local(): across = lax.ppermute(tokens, 'tp', chip)  3.03 us
    ppermute x1, waiting for transfers between devices, local(): across_a = lax.ppermute(chunk_a, 'tp', chip)  2.92 us
    ppermute x1, starting transfers between devices, to_other_group(): return lax.ppermute(a, 'seq', [(i, i ^ 4) for i in range(8)])  2.65 us
    ppermute x1, waiting for transfers between devices, to_other_group(): return lax.ppermute(a, 'seq', [(i, i ^ 4) for i in range(8)])  2.57 us
    ppermute x1, waiting for transfers between devices, local(): across = lax.ppermute(tokens, 'tp', chip)  1.88 us
  transfers between devices with their start and end apart: 18, of which 9 were waited for; matrix products, arithmetic and copies ran while one was open for 0% of the time, Pallas kernels for 42%

profile of v8, /device:TPU:0, one launch (start us, length us, event | category | flops | bytes accessed | tf_op | source)
XLA Modules:
  0.0 61.9 jit_solution(4360381982190282826)
XLA Ops:
  0.6 3.0 %collective-permute-start = (bf16[256,1024]{1,0:T(8,128)(2,1)}, bf16[256,1024]{1,0:T(8,128)(2,1)S(1)}, u32[]{:S(2)}, u32[]{:S(2)}) collective-permute-start(bf16[256,1024]{1,0:T(8,128)(2,1)} %tokens.1), channel_id=1, source_target_pairs={{0,2},{1,3},{2,0},{3,1},{4,6},{5,7},{6,4},{7,5},{8,10},{9,11},{10,... | collective-permute-start | bytes 1572872 | tf_op jit(solution)/shard_map/ppermute | solution.py:463
  3.7 0.0 collective-permute-start.1
  3.7 8.4 %load_and_project.1 = (bf16[3,4096,1024]{2,1,0:T(8,128)(2,1)S(1)}, f32[3,256,1024]{2,1,0:T(8,128)S(1)}, f32[256,25]{1,0:T(8,128)S(1)}, f32[24,256]{1,0:T(8,128)S(1)}, bf16[16,128]{1,0:T(8,128)(2,1)S(1)}) custom-call(s32[16]{0:T(128)} %lengths.1, f32[8,256]{1,0:T(8,128)} %bitcast.1, bf16[256,1024]{1,0:T(8,128)(2,1)} %tokens.1, bf16[3,4096,1024]{2,1,0:T(8,128)(2,1)} %w.1), custom_call_target="tpu_custom_call" | custom-call | flops 12884901888 | tf_op jit(solution)/shard_map/load_and_project/pallas_call | solution.py:38
  12.1 0.0 collective-permute-done.1.refs_0_
  12.1 1.8 %project_beside.1.refs_2_ = f32[3,256,1024]{2,1,0:T(8,128)S(1)} custom-call(bf16[256,1024]{1,0:T(8,128)(2,1)S(1)} %collective-permute-done.1.refs_0_, bf16[3,4096,1024]{2,1,0:T(8,128)(2,1)S(1)} %get-tuple-element.50.refs_1_.w, f32[3,256,1024]{2,1,0:T(8,128)S(1)} %get-tuple-element.51.refs_2_), custom_call_target="tpu_custom_call" | custom-call | tf_op jit(solution)/shard_map/project_beside/pallas_call | solution.py:38
  13.9 0.0 copy-start
  13.9 1.9 %collective-permute-done.refs_0_ = bf16[256,1024]{1,0:T(8,128)(2,1)S(1)} collective-permute-done((bf16[256,1024]{1,0:T(8,128)(2,1)}, bf16[256,1024]{1,0:T(8,128)(2,1)S(1)}, u32[]{:S(2)}, u32[]{:S(2)}) %collective-permute-start) | collective-permute-done | bytes 524320 | tf_op jit(solution)/shard_map/ppermute | solution.py:463
  15.8 0.0 collective-permute-start.2
  15.8 1.8 %project_across.1.acc_in = f32[3,256,1024]{2,1,0:T(8,128)S(1)} custom-call(bf16[256,1024]{1,0:T(8,128)(2,1)S(1)} %collective-permute-done.refs_0_, bf16[3,4096,1024]{2,1,0:T(8,128)(2,1)S(1)} %get-tuple-element.50.refs_1_.w, f32[3,256,1024]{2,1,0:T(8,128)S(1)} %project_beside.1.refs_2_), custom_call_target="tpu_custom_call" | custom-call | tf_op jit(solution)/shard_map/project_across/pallas_call | solution.py:38
  17.6 0.1 collective-permute-done.2.x
  17.7 2.5 %project_last.1 = (bf16[256,1024]{1,0:T(8,128)(2,1)S(1)}, bf16[256,1024]{1,0:T(8,128)(2,1)S(1)}, bf16[256,1024]{1,0:T(8,128)(2,1)S(1)}, f32[2,2,128,128]{3,2,1,0...) custom-call(bf16[256,1024]{1,0:T(8,128)(2,1)S(1)} %collective-permute-done.2, ...), custom_call_target="tpu_custom_call" | custom-call | tf_op jit(solution)/shard_map/project_last/pallas_call | solution.py:38
  20.2 1.8 %collective-permute-start.3 = (bf16[528,128]{1,0:T(8,128)(2,1)S(1)}, bf16[528,128]{1,0:T(8,128)(2,1)S(1)}, u32[]{:S(2)}, u32[]{:S(2)}) collective-permute-start(bf16[528,128]{1,0:T(8,128)(2,1)S(1)} %get-tuple-element.69), channel_id=1, source_target_pairs={{0,4},{1,9},{2,6},{3,11},{4,0},{5,13},{6,2},{7,15},{8,12},{9,1},{1... | collective-permute-start | bytes 405512 | tf_op jit(solution)/shard_map/ppermute | solution.py:389
  22.0 1.6 %collective-permute-start.4 = (bf16[528,128]{1,0:T(8,128)(2,1)S(1)}, bf16[528,128]{1,0:T(8,128)(2,1)S(1)}, u32[]{:S(2)}, u32[]{:S(2)}) collective-permute-start(bf16[528,128]{1,0:T(8,128)(2,1)S(1)} %get-tuple-element.70), channel_id=1, source_target_pairs={{0,8},{1,5},{2,10},{3,7},{4,12},{5,1},{6,14},{7,3},{8,0},{9,13},{1... | collective-permute-start | bytes 405512 | tf_op jit(solution)/shard_map/ppermute | solution.py:389
  23.6 0.2 collective-permute-start.5
  23.8 3.6 %intra.1 = (f32[256,1024]{1,0:T(8,128)S(1)}, f32[256,1024]{1,0:T(8,128)S(1)}, f32[256,1024]{1,0:T(8,128)S(1)}, f32[256,1024]{1,0:T(8,128)S(1)}) custom-call(bf16[256,1024]{1,0:T(8,128)(2,1)S(1)} %get-tuple-element.59.query, bf16[256,1024]{1,0:T(8,128)(2,1)S(1)} %get-tuple-element.56.key, bf16[256,1024]{1,0:T(8,128)(2,1)S(1)} %get-tuple-element.57.value, ...), custom_call_target="tpu_custom_call" | custom-call | flops 1073741824 | tf_op jit(solution)/shard_map/intra/pallas_call | solution.py:38
  27.4 0.7 %collective-permute-done.4.got2 = bf16[528,128]{1,0:T(8,128)(2,1)S(1)} collective-permute-done((bf16[528,128]{1,0:T(8,128)(2,1)S(1)}, bf16[528,128]{1,0:T(8,128)(2,1)S(1)}, u32[]{:S(2)}, u32[]{:S(2)}) %collective-permute-start.4) | collective-permute-done | bytes 135200 | tf_op jit(solution)/shard_map/ppermute | solution.py:389
  28.1 2.2 %collective-permute-done.5.got3 = bf16[528,128]{1,0:T(8,128)(2,1)S(1)} collective-permute-done((bf16[528,128]{1,0:T(8,128)(2,1)S(1)}, bf16[528,128]{1,0:T(8,128)(2,1)S(1)}, u32[]{:S(2)}, u32[]{:S(2)}) %collective-permute-start.5) | collective-permute-done | bytes 135200 | tf_op jit(solution)/shard_map/ppermute | solution.py:389
  30.2 0.3 join.1
  30.5 2.7 %collective-permute-start.6 = (bf16[256,128]{1,0:T(8,128)(2,1)S(1)}, bf16[256,128]{1,0:T(8,128)(2,1)S(1)}, u32[]{:S(2)}, u32[]{:S(2)}) collective-permute-start(bf16[256,128]{1,0:T(8,128)(2,1)S(1)} %get-tuple-element.74), channel_id=1, source_target_pairs={{0,16},{4,20},{8,24},{12,28},{16,0},{20,4},{24,8},{28,12},{1,17},{... | collective-permute-start | bytes 196616 | tf_op jit(solution)/shard_map/ppermute | solution.py:379
  33.2 2.6 %collective-permute-done.6.other = bf16[256,128]{1,0:T(8,128)(2,1)S(1)} collective-permute-done((bf16[256,128]{1,0:T(8,128)(2,1)S(1)}, bf16[256,128]{1,0:T(8,128)(2,1)S(1)}, u32[]{:S(2)}, u32[]{:S(2)}) %collective-permute-start.6) | collective-permute-done | bytes 65568 | tf_op jit(solution)/shard_map/ppermute | solution.py:379
  35.7 0.1 spread.1
  35.8 1.2 %collective-permute-start.7 = (bf16[2,2,128,128]{3,2,1,0:T(8,128)(2,1)S(1)}, bf16[2,2,128,128]{3,2,1,0:T(8,128)(2,1)S(1)}, u32[]{:S(2)}, u32[]{:S(2)}) collective-permute-start(bf16[2,2,128,128]{3,2,1,0:T(8,128)(2,1)S(1)} %get-tuple-element.75), channel_id=1, source_target_pairs={{0,4},{1,9},{2,6},{3,11},{4,0},{5,13},{6,2},{7,15},{8,12},{9,1},{1... | collective-permute-start | bytes 393224 | tf_op jit(solution)/shard_map/ppermute | solution.py:389
  37.0 1.3 %collective-permute-start.8 = (bf16[2,2,128,128]{3,2,1,0:T(8,128)(2,1)S(1)}, bf16[2,2,128,128]{3,2,1,0:T(8,128)(2,1)S(1)}, u32[]{:S(2)}, u32[]{:S(2)}) collective-permute-start(bf16[2,2,128,128]{3,2,1,0:T(8,128)(2,1)S(1)} %get-tuple-element.76), channel_id=1, source_target_pairs={{0,8},{1,5},{2,10},{3,7},{4,12},{5,1},{6,14},{7,3},{8,0},{9,13},{1... | collective-permute-start | bytes 393224 | tf_op jit(solution)/shard_map/ppermute | solution.py:389
  38.3 1.1 %collective-permute-start.9 = (bf16[2,2,128,128]{3,2,1,0:T(8,128)(2,1)S(1)}, bf16[2,2,128,128]{3,2,1,0:T(8,128)(2,1)S(1)}, u32[]{:S(2)}, u32[]{:S(2)}) collective-permute-start(bf16[2,2,128,128]{3,2,1,0:T(8,128)(2,1)S(1)} %get-tuple-element.81), channel_id=1, source_target_pairs={{0,12},{1,13},{2,14},{3,15},{4,8},{5,9},{6,10},{7,11},{8,4},{9,5},... | collective-permute-start | bytes 393224 | tf_op jit(solution)/shard_map/ppermute | solution.py:389
  39.4 1.6 %back_own.1 = (bf16[3,256,256]{2,1,0:T(8,128)(2,1)S(1)}, f32[256,1024]{1,0:T(8,128)S(1)}, f32[256,1024]{1,0:T(8,128)S(1)}) custom-call(bf16[256,1024]{1,0:T(8,128)(2,1)S(1)} %get-tuple-element.56.key, bf16[256,1024]{1,0:T(8,128)(2,1)S(1)} %get-tuple-element.57.value, bf16[256,1024]{1,0:T(8,128)(2,1)S(1)} %copy-done, f32[256,25]{1,0:T(8,128)S(1)} %get-tuple-element.58.cols_h, ...), custom_call_target="tpu_custom_call" | custom-call | tf_op jit(solution)/shard_map/back_own/pallas_call | solution.py:38
  41.0 1.1 %collective-permute-done.7.states1 = bf16[2,2,128,128]{3,2,1,0:T(8,128)(2,1)S(1)} collective-permute-done((bf16[2,2,128,128]{3,2,1,0:T(8,128)(2,1)S(1)}, bf16[2,2,128,128]{3,2,1,0:T(8,128)(2,1)S(1)}, u32[]{:S(2)}, u32[]{:S(2)}) %collective-permute-start.7) | collective-permute-done | bytes 131104 | tf_op jit(solution)/shard_map/ppermute | solution.py:389
  42.1 0.0 collective-permute-done.8.states2
  42.1 1.9 %back_sides.1 = (bf16[3,256,256]{2,1,0:T(8,128)(2,1)S(1)}, bf16[3,256,256]{2,1,0:T(8,128)(2,1)S(1)}, f32[256,1024]{1,0:T(8,128)S(1)}) custom-call(bf16[256,1024]{1,0:T(8,128)(2,1)S(1)} %get-tuple-element.56.key, bf16[256,1024]{1,0:T(8,128)(2,1)S(1)} %get-tuple-element.57.value, bf16[256,1024]{1,0:T(8,128)(2,1)S(1)} %copy-done, ...), custom_call_target="tpu_custom_call", output_to_operand_aliasing={{2}: (10, {})} | custom-call | tf_op jit(solution)/shard_map/back_sides/pallas_call | solution.py:38
  44.0 0.2 collective-permute-done.9.states.states3
  44.2 0.8 %back_first.1 = (bf16[3,256,256]{2,1,0:T(8,128)(2,1)S(1)}, bf16[256,512]{1,0:T(8,128)(2,1)S(1)}) custom-call(bf16[256,1024]{1,0:T(8,128)(2,1)S(1)} %get-tuple-element.56.key, bf16[256,1024]{1,0:T(8,128)(2,1)S(1)} %get-tuple-element.57.value, bf16[256,1024]{1,0:T(8,128)(2,1)S(1)} %copy-done, f32[256,25]{1,0:T(8,128)S(1)} %get-tuple-element.58.cols_h, ...), custom_call_target="tpu_custom_call" | custom-call | tf_op jit(solution)/shard_map/back_first/pallas_call | solution.py:38
  45.0 0.1 collective-permute-start.10
  45.1 1.0 %back_second.1 = (bf16[256,512]{1,0:T(8,128)(2,1)S(1)}, f32[256,512]{1,0:T(8,128)S(1)}) custom-call(bf16[3,256,256]{2,1,0:T(8,128)(2,1)S(1)} %get-tuple-element.79.stack1, bf16[3,256,256]{2,1,0:T(8,128)(2,1)S(1)} %get-tuple-element.80.stack2, bf16[3,256,256]{2,1,0:T(8,128)(2,1)S(1)} %get-tuple-element.83.stack3, ...), custom_call_target="tpu_custom_call" | custom-call | tf_op jit(solution)/shard_map/back_second/pallas_call | solution.py:38
  46.1 0.5 collective-permute-start.11
  46.7 0.0 collective-permute-done.10
  46.7 0.1 add_convert_fusion.1
  46.7 1.6 %collective-permute-start.12 = (bf16[256,512]{1,0:T(8,128)(2,1)S(1)}, bf16[256,512]{1,0:T(8,128)(2,1)S(1)}, u32[]{:S(2)}, u32[]{:S(2)}) collective-permute-start(bf16[256,512]{1,0:T(8,128)(2,1)S(1)} %add_convert_fusion.1), channel_id=1, source_target_pairs={{0,2},{1,3},{2,0},{3,1},{4,6},{5,7},{6,4},{7,5},{8,10},{9,11},{10,... | collective-permute-start | bytes 786440 | tf_op jit(solution)/shard_map/ppermute | solution.py:528
  48.3 0.8 %back_third.1 = f32[256,512]{1,0:T(8,128)S(1)} custom-call(bf16[3,256,256]{2,1,0:T(8,128)(2,1)S(1)} %get-tuple-element.79.stack1, bf16[3,256,256]{2,1,0:T(8,128)(2,1)S(1)} %get-tuple-element.80.stack2, bf16[3,256,256]{2,1,0:T(8,128)(2,1)S(1)} %get-tuple-element.83.stack3, bf16[3,4096,1024]{2,1,0:T(8,128)(2,1)S(1)} %get-tuple-element.50.refs_1_.w, ...), custom_call_target="tpu_custom_call" | custom-call | tf_op jit(solution)/shard_map/back_third/pallas_call | solution.py:38
  49.1 0.1 add_convert_fusion
  49.2 0.6 collective-permute-start.13
  49.8 3.2 %back_mine.1 = (f32[256,1024]{1,0:T(8,128)}, f32[256,1024]{1,0:T(8,128)S(1)}) custom-call(bf16[3,256,256]{2,1,0:T(8,128)(2,1)S(1)} %get-tuple-element.90.stack0, bf16[3,256,256]{2,1,0:T(8,128)(2,1)S(1)} %get-tuple-element.79.stack1, bf16[3,256,256]{2,1,0:T(8,128)(2,1)S(1)} %get-tuple-element.80.stack2, bf16[3,256,256]{2,1,0:T(8,128)(2,1)S(1)} %get-tuple-element.83.stack3, ...), custom_call_target="tpu_custom_call" | custom-call | tf_op jit(solution)/shard_map/back_mine/pallas_call | solution.py:38
  53.1 2.9 %collective-permute-done.12.across_a = bf16[256,512]{1,0:T(8,128)(2,1)S(1)} collective-permute-done((bf16[256,512]{1,0:T(8,128)(2,1)S(1)}, bf16[256,512]{1,0:T(8,128)(2,1)S(1)}, u32[]{:S(2)}, u32[]{:S(2)}) %collective-permute-start.12) | collective-permute-done | bytes 262176 | tf_op jit(solution)/shard_map/ppermute | solution.py:528
  56.0 2.0 %back_other.1 = (bf16[256,1024]{1,0:T(8,128)(2,1)S(1)}, f32[256,1024]{1,0:T(8,128)S(1)}) custom-call(bf16[3,256,256]{2,1,0:T(8,128)(2,1)S(1)} %get-tuple-element.90.stack0, bf16[3,256,256]{2,1,0:T(8,128)(2,1)S(1)} %get-tuple-element.79.stack1, bf16[3,256,256]{2,1,0:T(8,128)(2,1)S(1)} %get-tuple-element.80.stack2, ...), custom_call_target="tpu_custom_call", output_to_operand_aliasing={{1}: (6, {})} | custom-call | flops 1610612736 | tf_op jit(solution)/shard_map/back_other/pallas_call | solution.py:38
  58.0 0.1 collective-permute-start.17
  58.1 0.5 collective-permute-start.16
  58.6 0.1 collective-permute-start.15
  58.7 0.4 collective-permute-start.14
  59.1 1.6 %collective-permute-done.13.refs_0_ = bf16[256,512]{1,0:T(8,128)(2,1)S(1)} collective-permute-done((bf16[256,512]{1,0:T(8,128)(2,1)S(1)}, bf16[256,512]{1,0:T(8,128)(2,1)S(1)}, u32[]{:S(2)}, u32[]{:S(2)}) %collective-permute-start.13) | collective-permute-done | bytes 262176 | tf_op jit(solution)/shard_map/ppermute | solution.py:532
  60.7 1.0 %last_sum.1 = f32[256,1024]{1,0:T(8,128)} custom-call(f32[256,1024]{1,0:T(8,128)S(1)} %get-tuple-element.95.own, bf16[256,512]{1,0:T(8,128)(2,1)S(1)} %hand_on.1.across_b, bf16[64,1024]{1,0:T(8,128)(2,1)S(1)} %collective-permute-done.14.refs_0_, bf16[64,1024]{1,0:T(8,128)(2,1)S(1)} %collective-permute-done.15.refs_1_, ...), custom_call_target="tpu_custom_call" | custom-call | tf_op jit(solution)/shard_map/last_sum/pallas_call | solution.py:38
  (9 shorter events, 0.1 us)
Async XLA Ops:
  0.6 15.2 %collective-permute-start = (bf16[256,1024]{1,0:T(8,128)(2,1)}, bf16[256,1024]{1,0:T(8,128)(2,1)S(1)}, u32[]{:S(2)}, u32[]{:S(2)}) collective-permute-start(bf16[256,1024]{1,0:T(8,128)(2,1)} %tokens.1), channel_id=1, source_target_pairs={{0,2},{1,3},{2,0},{3,1},{4,6},{5,7},{6,4},{7,5},{8,10},{9,11},{10,... | collective-permute-start | bytes 1572872 | tf_op jit(solution)/shard_map/ppermute | solution.py:463
  3.7 8.4 %collective-permute-start.1 = (bf16[256,1024]{1,0:T(8,128)(2,1)}, bf16[256,1024]{1,0:T(8,128)(2,1)S(1)}, u32[]{:S(2)}, u32[]{:S(2)}) collective-permute-start(bf16[256,1024]{1,0:T(8,128)(2,1)} %tokens.1), channel_id=1, source_target_pairs={{0,1},{1,0},{2,3},{3,2},{4,5},{5,4},{6,7},{7,6},{8,9},{9,8},{10,11... | collective-permute-start | bytes 1572872 | tf_op jit(solution)/shard_map/ppermute | solution.py:464
  13.9 3.8 %copy-start = (bf16[256,1024]{1,0:T(8,128)(2,1)S(1)}, bf16[256,1024]{1,0:T(8,128)(2,1)}, u32[]{:S(2)}) copy-start(bf16[256,1024]{1,0:T(8,128)(2,1)} %grads.9) | copy-start | bytes 1572868
  15.8 1.9 %collective-permute-start.2 = (bf16[256,1024]{1,0:T(8,128)(2,1)S(1)}, bf16[256,1024]{1,0:T(8,128)(2,1)S(1)}, u32[]{:S(2)}, u32[]{:S(2)}) collective-permute-start(bf16[256,1024]{1,0:T(8,128)(2,1)S(1)} %collective-permute-done.refs_0_), channel_id=1, source_target_pairs={{0,1},{1,0},{2,3},{3,2},{4,5},{5,4},{6,7},{7,6},{8,9},{9,8},{10,11... | collective-permute-start | bytes 1572872 | tf_op jit(solution)/shard_map/ppermute | solution.py:486
  20.2 7.2 %collective-permute-start.3 = (bf16[528,128]{1,0:T(8,128)(2,1)S(1)}, bf16[528,128]{1,0:T(8,128)(2,1)S(1)}, u32[]{:S(2)}, u32[]{:S(2)}) collective-permute-start(bf16[528,128]{1,0:T(8,128)(2,1)S(1)} %get-tuple-element.69), channel_id=1, source_target_pairs={{0,4},{1,9},{2,6},{3,11},{4,0},{5,13},{6,2},{7,15},{8,12},{9,1},{1... | collective-permute-start | bytes 405512 | tf_op jit(solution)/shard_map/ppermute | solution.py:389
  22.0 6.1 %collective-permute-start.4 = (bf16[528,128]{1,0:T(8,128)(2,1)S(1)}, bf16[528,128]{1,0:T(8,128)(2,1)S(1)}, u32[]{:S(2)}, u32[]{:S(2)}) collective-permute-start(bf16[528,128]{1,0:T(8,128)(2,1)S(1)} %get-tuple-element.70), channel_id=1, source_target_pairs={{0,8},{1,5},{2,10},{3,7},{4,12},{5,1},{6,14},{7,3},{8,0},{9,13},{1... | collective-permute-start | bytes 405512 | tf_op jit(solution)/shard_map/ppermute | solution.py:389
  23.6 6.7 %collective-permute-start.5 = (bf16[528,128]{1,0:T(8,128)(2,1)S(1)}, bf16[528,128]{1,0:T(8,128)(2,1)S(1)}, u32[]{:S(2)}, u32[]{:S(2)}) collective-permute-start(bf16[528,128]{1,0:T(8,128)(2,1)S(1)} %get-tuple-element.71), channel_id=1, source_target_pairs={{0,12},{1,13},{2,14},{3,15},{4,8},{5,9},{6,10},{7,11},{8,4},{9,5},... | collective-permute-start | bytes 405512 | tf_op jit(solution)/shard_map/ppermute | solution.py:389
  30.5 5.2 %collective-permute-start.6 = (bf16[256,128]{1,0:T(8,128)(2,1)S(1)}, bf16[256,128]{1,0:T(8,128)(2,1)S(1)}, u32[]{:S(2)}, u32[]{:S(2)}) collective-permute-start(bf16[256,128]{1,0:T(8,128)(2,1)S(1)} %get-tuple-element.74), channel_id=1, source_target_pairs={{0,16},{4,20},{8,24},{12,28},{16,0},{20,4},{24,8},{28,12},{1,17},{... | collective-permute-start | bytes 196616 | tf_op jit(solution)/shard_map/ppermute | solution.py:379
  35.8 6.2 %collective-permute-start.7 = (bf16[2,2,128,128]{3,2,1,0:T(8,128)(2,1)S(1)}, bf16[2,2,128,128]{3,2,1,0:T(8,128)(2,1)S(1)}, u32[]{:S(2)}, u32[]{:S(2)}) collective-permute-start(bf16[2,2,128,128]{3,2,1,0:T(8,128)(2,1)S(1)} %get-tuple-element.75), channel_id=1, source_target_pairs={{0,4},{1,9},{2,6},{3,11},{4,0},{5,13},{6,2},{7,15},{8,12},{9,1},{1... | collective-permute-start | bytes 393224 | tf_op jit(solution)/shard_map/ppermute | solution.py:389
  37.0 5.1 %collective-permute-start.8 = (bf16[2,2,128,128]{3,2,1,0:T(8,128)(2,1)S(1)}, bf16[2,2,128,128]{3,2,1,0:T(8,128)(2,1)S(1)}, u32[]{:S(2)}, u32[]{:S(2)}) collective-permute-start(bf16[2,2,128,128]{3,2,1,0:T(8,128)(2,1)S(1)} %get-tuple-element.76), channel_id=1, source_target_pairs={{0,8},{1,5},{2,10},{3,7},{4,12},{5,1},{6,14},{7,3},{8,0},{9,13},{1... | collective-permute-start | bytes 393224 | tf_op jit(solution)/shard_map/ppermute | solution.py:389
  38.3 5.9 %collective-permute-start.9 = (bf16[2,2,128,128]{3,2,1,0:T(8,128)(2,1)S(1)}, bf16[2,2,128,128]{3,2,1,0:T(8,128)(2,1)S(1)}, u32[]{:S(2)}, u32[]{:S(2)}) collective-permute-start(bf16[2,2,128,128]{3,2,1,0:T(8,128)(2,1)S(1)} %get-tuple-element.81), channel_id=1, source_target_pairs={{0,12},{1,13},{2,14},{3,15},{4,8},{5,9},{6,10},{7,11},{8,4},{9,5},... | collective-permute-start | bytes 393224 | tf_op jit(solution)/shard_map/ppermute | solution.py:389
  45.0 1.7 %collective-permute-start.10 = (bf16[256,512]{1,0:T(8,128)(2,1)S(1)}, bf16[256,512]{1,0:T(8,128)(2,1)S(1)}, u32[]{:S(2)}, u32[]{:S(2)}) collective-permute-start(bf16[256,512]{1,0:T(8,128)(2,1)S(1)} %get-tuple-element.86), channel_id=1, source_target_pairs={{0,1},{1,0},{2,3},{3,2},{4,5},{5,4},{6,7},{7,6},{8,9},{9,8},{10,11... | collective-permute-start | bytes 786440 | tf_op jit(solution)/shard_map/ppermute | solution.py:520
  46.1 3.0 %collective-permute-start.11 = (bf16[256,512]{1,0:T(8,128)(2,1)S(1)}, bf16[256,512]{1,0:T(8,128)(2,1)S(1)}, u32[]{:S(2)}, u32[]{:S(2)}) collective-permute-start(bf16[256,512]{1,0:T(8,128)(2,1)S(1)} %get-tuple-element.88), channel_id=1, source_target_pairs={{0,1},{1,0},{2,3},{3,2},{4,5},{5,4},{6,7},{7,6},{8,9},{9,8},{10,11... | collective-permute-start | bytes 786440 | tf_op jit(solution)/shard_map/ppermute | solution.py:525
  46.7 9.2 %collective-permute-start.12 = (bf16[256,512]{1,0:T(8,128)(2,1)S(1)}, bf16[256,512]{1,0:T(8,128)(2,1)S(1)}, u32[]{:S(2)}, u32[]{:S(2)}) collective-permute-start(bf16[256,512]{1,0:T(8,128)(2,1)S(1)} %add_convert_fusion.1), channel_id=1, source_target_pairs={{0,2},{1,3},{2,0},{3,1},{4,6},{5,7},{6,4},{7,5},{8,10},{9,11},{10,... | collective-permute-start | bytes 786440 | tf_op jit(solution)/shard_map/ppermute | solution.py:528
  49.2 11.5 %collective-permute-start.13 = (bf16[256,512]{1,0:T(8,128)(2,1)S(1)}, bf16[256,512]{1,0:T(8,128)(2,1)S(1)}, u32[]{:S(2)}, u32[]{:S(2)}) collective-permute-start(bf16[256,512]{1,0:T(8,128)(2,1)S(1)} %add_convert_fusion), channel_id=1, source_target_pairs={{0,2},{1,3},{2,0},{3,1},{4,6},{5,7},{6,4},{7,5},{8,10},{9,11},{10,... | collective-permute-start | bytes 786440 | tf_op jit(solution)/shard_map/ppermute | solution.py:532
  58.0 2.7 %collective-permute-start.17 = (bf16[64,1024]{1,0:T(8,128)(2,1)S(1)}, bf16[64,1024]{1,0:T(8,128)(2,1)S(1)}, u32[]{:S(2)}, u32[]{:S(2)}) collective-permute-start(bf16[64,1024]{1,0:T(8,128)(2,1)S(1)} %get-tuple-element.98), channel_id=1, source_target_pairs={{0,1},{1,0},{2,3},{3,2},{4,5},{5,4},{6,7},{7,6},{8,9},{9,8},{10,11... | collective-permute-start | bytes 393224 | tf_op jit(solution)/shard_map/ppermute | solution.py:549
  58.1 2.6 %collective-permute-start.16 = (bf16[64,1024]{1,0:T(8,128)(2,1)S(1)}, bf16[64,1024]{1,0:T(8,128)(2,1)S(1)}, u32[]{:S(2)}, u32[]{:S(2)}) collective-permute-start(bf16[64,1024]{1,0:T(8,128)(2,1)S(1)} %get-tuple-element.99), channel_id=1, source_target_pairs={{0,1},{1,0},{2,3},{3,2},{4,5},{5,4},{6,7},{7,6},{8,9},{9,8},{10,11... | collective-permute-start | bytes 393224 | tf_op jit(solution)/shard_map/ppermute | solution.py:549
  58.6 2.1 %collective-permute-start.15 = (bf16[64,1024]{1,0:T(8,128)(2,1)S(1)}, bf16[64,1024]{1,0:T(8,128)(2,1)S(1)}, u32[]{:S(2)}, u32[]{:S(2)}) collective-permute-start(bf16[64,1024]{1,0:T(8,128)(2,1)S(1)} %get-tuple-element.100), channel_id=1, source_target_pairs={{0,1},{1,0},{2,3},{3,2},{4,5},{5,4},{6,7},{7,6},{8,9},{9,8},{10,11... | collective-permute-start | bytes 393224 | tf_op jit(solution)/shard_map/ppermute | solution.py:549
  58.7 2.1 %collective-permute-start.14 = (bf16[64,1024]{1,0:T(8,128)(2,1)S(1)}, bf16[64,1024]{1,0:T(8,128)(2,1)S(1)}, u32[]{:S(2)}, u32[]{:S(2)}) collective-permute-start(bf16[64,1024]{1,0:T(8,128)(2,1)S(1)} %get-tuple-element.101), channel_id=1, source_target_pairs={{0,1},{1,0},{2,3},{3,2},{4,5},{5,4},{6,7},{7,6},{8,9},{9,8},{10,11... | collective-permute-start | bytes 393224 | tf_op jit(solution)/shard_map/ppermute | solution.py:549

commit v9 on v8

--- a/solution.py
+++ b/solution.py
@@ -20,11 +20,6 @@
 def split(a):
     high = a.astype(BF16)
     return high, (a - high.astype(F32)).astype(BF16)
-
-
-def dot_split(a, b, ca, cb):
-    high, low = split(a)
-    return dot(high, b, ca, cb) + dot(low, b, ca, cb)
 
 
 def call(kernel, name, outs, args, spaces=None, flops=0, limit=4, aliases=None, scratch=(), out_spaces=None):
@@ -185,14 +180,14 @@
 def state_end(key, value, rows_h, h):
     cols = slice(h * DH, (h + 1) * DH)
     heads = rows_h.shape[0] // 3
-    return dot_split(key[:, cols].T.astype(F32) * rows_h[2 * heads + h : 2 * heads + h + 1, :], value[:, cols], 1, 0)
+    return dot((key[:, cols].T.astype(F32) * rows_h[2 * heads + h : 2 * heads + h + 1, :]).astype(BF16), value[:, cols], 1, 0)
 
 
 def grad_start(query, grads, rows_h, h):
     cols = slice(h * DH, (h + 1) * DH)
     heads = rows_h.shape[0] // 3
     weight = rows_h[heads + h : heads + h + 1, :] * (1.0 / DH)
-    return dot_split(query[:, cols].T.astype(F32) * weight, grads[:, cols], 1, 0)
+    return dot((query[:, cols].T.astype(F32) * weight).astype(BF16), grads[:, cols], 1, 0)
 
 
 def own_states(query, key, value, grads, rows_h, states):
@@ -253,14 +248,14 @@
 
 def back(which, stacks, w, out, offset=0, start=None):
     part = w.shape[1] // 4
-    for cols in tiles(out.shape[1]):
-        rows = rows_of(which, part, offset + cols.start, cols.stop - cols.start)
-        total = None if start is None else start[:, slice(offset + cols.start, offset + cols.stop)]
-        for d, stack in stacks:
-            for m in range(3):
-                term = dot(stack[m], w[m, rows, quarter_columns(d, w)], 1, 1)
-                total = term if total is None else total + term
-        out[:, cols] = total.astype(out.dtype)
+    size = out.shape[1]
+    rows = rows_of(which, part, offset, size)
+    total = None if start is None else start[:, offset : offset + size]
+    for d, stack in stacks:
+        for m in range(3):
+            term = dot(stack[m], w[m, rows, quarter_columns(d, w)], 1, 1)
+            total = term if total is None else total + term
+    out[...] = total.astype(out.dtype)
 
 
 def back_own(key, value, grads, cols_h, gq, gk, gv, states, w, stack, out3, out2):

time: 62.1 us -> 61.9 us (level)
  no operation moved by 1% of the time
where the time goes in v9:
time: 61.9 us; the launch traced here: 61.7 us
  Pallas kernels  30.4 us (49%)
  starting transfers between devices  16.7 us (27%)
  waiting for transfers between devices  13.4 us (22%)
  between operations  0.99 us (2%)
    pallas_call x16, Pallas kernels, call(): pl.pallas_call(kernel, name=name, out_shape=[kinds[s](shape, dtype) for s...  30.4 us
    ppermute x6, starting transfers between devices, to_member(): return lax.ppermute(a, ('seq', 'tp'), pairs)  7.11 us
    ppermute x6, waiting for transfers between devices, to_member(): return lax.ppermute(a, ('seq', 'tp'), pairs)  4.35 us
    ppermute x1, starting transfers between devices, local(): across = lax.ppermute(tokens, 'tp', chip)  3.03 us
    ppermute x1, waiting for transfers between devices, local(): across_a = lax.ppermute(chunk_a, 'tp', chip)  2.91 us
    ppermute x1, starting transfers between devices, to_other_group(): return lax.ppermute(a, 'seq', [(i, i ^ 4) for i in range(8)])  2.65 us
    ppermute x1, waiting for transfers between devices, to_other_group(): return lax.ppermute(a, 'seq', [(i, i ^ 4) for i in range(8)])  2.58 us
    ppermute x1, waiting for transfers between devices, local(): across = lax.ppermute(tokens, 'tp', chip)  1.88 us
  transfers between devices with their start and end apart: 18, of which 9 were waited for; matrix products, arithmetic and copies ran while one was open for 0% of the time, Pallas kernels for 42%

profile of v9, /device:TPU:0, one launch (start us, length us, event | category | flops | bytes accessed | tf_op | source)
XLA Modules:
  0.0 61.7 jit_solution(8752733441912569306)
XLA Ops:
  0.6 3.0 %collective-permute-start = (bf16[256,1024]{1,0:T(8,128)(2,1)}, bf16[256,1024]{1,0:T(8,128)(2,1)S(1)}, u32[]{:S(2)}, u32[]{:S(2)}) collective-permute-start(bf16[256,1024]{1,0:T(8,128)(2,1)} %tokens.1), channel_id=1, source_target_pairs={{0,2},{1,3},{2,0},{3,1},{4,6},{5,7},{6,4},{7,5},{8,10},{9,11},{10,... | collective-permute-start | bytes 1572872 | tf_op jit(solution)/shard_map/ppermute | solution.py:458
  3.7 0.0 collective-permute-start.1
  3.7 8.4 %load_and_project.1 = (bf16[3,4096,1024]{2,1,0:T(8,128)(2,1)S(1)}, f32[3,256,1024]{2,1,0:T(8,128)S(1)}, f32[256,25]{1,0:T(8,128)S(1)}, f32[24,256]{1,0:T(8,128)S(1)}, bf16[16,128]{1,0:T(8,128)(2,1)S(1)}) custom-call(s32[16]{0:T(128)} %lengths.1, f32[8,256]{1,0:T(8,128)} %bitcast.1, bf16[256,1024]{1,0:T(8,128)(2,1)} %tokens.1, bf16[3,4096,1024]{2,1,0:T(8,128)(2,1)} %w.1), custom_call_target="tpu_custom_call" | custom-call | flops 12884901888 | tf_op jit(solution)/shard_map/load_and_project/pallas_call | solution.py:33
  12.1 1.8 %project_beside.1.refs_2_ = f32[3,256,1024]{2,1,0:T(8,128)S(1)} custom-call(bf16[256,1024]{1,0:T(8,128)(2,1)S(1)} %collective-permute-done.1.refs_0_, bf16[3,4096,1024]{2,1,0:T(8,128)(2,1)S(1)} %get-tuple-element.50.refs_1_.w, f32[3,256,1024]{2,1,0:T(8,128)S(1)} %get-tuple-element.51.refs_2_), custom_call_target="tpu_custom_call" | custom-call | tf_op jit(solution)/shard_map/project_beside/pallas_call | solution.py:33
  13.9 0.0 copy-start
  13.9 1.9 %collective-permute-done.refs_0_ = bf16[256,1024]{1,0:T(8,128)(2,1)S(1)} collective-permute-done((bf16[256,1024]{1,0:T(8,128)(2,1)}, bf16[256,1024]{1,0:T(8,128)(2,1)S(1)}, u32[]{:S(2)}, u32[]{:S(2)}) %collective-permute-start) | collective-permute-done | bytes 524320 | tf_op jit(solution)/shard_map/ppermute | solution.py:458
  15.8 1.8 %project_across.1.acc_in = f32[3,256,1024]{2,1,0:T(8,128)S(1)} custom-call(bf16[256,1024]{1,0:T(8,128)(2,1)S(1)} %collective-permute-done.refs_0_, bf16[3,4096,1024]{2,1,0:T(8,128)(2,1)S(1)} %get-tuple-element.50.refs_1_.w, f32[3,256,1024]{2,1,0:T(8,128)S(1)} %project_beside.1.refs_2_), custom_call_target="tpu_custom_call" | custom-call | tf_op jit(solution)/shard_map/project_across/pallas_call | solution.py:33
  17.6 0.1 collective-permute-done.2.x
  17.7 2.3 %project_last.1 = (bf16[256,1024]{1,0:T(8,128)(2,1)S(1)}, bf16[256,1024]{1,0:T(8,128)(2,1)S(1)}, bf16[256,1024]{1,0:T(8,128)(2,1)S(1)}, f32[2,2,128,128]{3,2,1,0...) custom-call(bf16[256,1024]{1,0:T(8,128)(2,1)S(1)} %collective-permute-done.2, ...), custom_call_target="tpu_custom_call" | custom-call | tf_op jit(solution)/shard_map/project_last/pallas_call | solution.py:33
  20.0 1.8 %collective-permute-start.3 = (bf16[528,128]{1,0:T(8,128)(2,1)S(1)}, bf16[528,128]{1,0:T(8,128)(2,1)S(1)}, u32[]{:S(2)}, u32[]{:S(2)}) collective-permute-start(bf16[528,128]{1,0:T(8,128)(2,1)S(1)} %get-tuple-element.69), channel_id=1, source_target_pairs={{0,4},{1,9},{2,6},{3,11},{4,0},{5,13},{6,2},{7,15},{8,12},{9,1},{1... | collective-permute-start | bytes 405512 | tf_op jit(solution)/shard_map/ppermute | solution.py:384
  21.8 1.6 %collective-permute-start.4 = (bf16[528,128]{1,0:T(8,128)(2,1)S(1)}, bf16[528,128]{1,0:T(8,128)(2,1)S(1)}, u32[]{:S(2)}, u32[]{:S(2)}) collective-permute-start(bf16[528,128]{1,0:T(8,128)(2,1)S(1)} %get-tuple-element.70), channel_id=1, source_target_pairs={{0,8},{1,5},{2,10},{3,7},{4,12},{5,1},{6,14},{7,3},{8,0},{9,13},{1... | collective-permute-start | bytes 405512 | tf_op jit(solution)/shard_map/ppermute | solution.py:384
  23.4 0.2 collective-permute-start.5
  23.6 3.6 %intra.1 = (f32[256,1024]{1,0:T(8,128)S(1)}, f32[256,1024]{1,0:T(8,128)S(1)}, f32[256,1024]{1,0:T(8,128)S(1)}, f32[256,1024]{1,0:T(8,128)S(1)}) custom-call(bf16[256,1024]{1,0:T(8,128)(2,1)S(1)} %get-tuple-element.59.query, bf16[256,1024]{1,0:T(8,128)(2,1)S(1)} %get-tuple-element.56.key, bf16[256,1024]{1,0:T(8,128)(2,1)S(1)} %get-tuple-element.57.value, ...), custom_call_target="tpu_custom_call" | custom-call | flops 1073741824 | tf_op jit(solution)/shard_map/intra/pallas_call | solution.py:33
  27.2 0.0 collective-permute-done.3.got1
  27.2 0.7 %collective-permute-done.4.got2 = bf16[528,128]{1,0:T(8,128)(2,1)S(1)} collective-permute-done((bf16[528,128]{1,0:T(8,128)(2,1)S(1)}, bf16[528,128]{1,0:T(8,128)(2,1)S(1)}, u32[]{:S(2)}, u32[]{:S(2)}) %collective-permute-start.4) | collective-permute-done | bytes 135200 | tf_op jit(solution)/shard_map/ppermute | solution.py:384
  27.9 2.2 %collective-permute-done.5.got3 = bf16[528,128]{1,0:T(8,128)(2,1)S(1)} collective-permute-done((bf16[528,128]{1,0:T(8,128)(2,1)S(1)}, bf16[528,128]{1,0:T(8,128)(2,1)S(1)}, u32[]{:S(2)}, u32[]{:S(2)}) %collective-permute-start.5) | collective-permute-done | bytes 135200 | tf_op jit(solution)/shard_map/ppermute | solution.py:384
  30.0 0.3 join.1
  30.3 2.7 %collective-permute-start.6 = (bf16[256,128]{1,0:T(8,128)(2,1)S(1)}, bf16[256,128]{1,0:T(8,128)(2,1)S(1)}, u32[]{:S(2)}, u32[]{:S(2)}) collective-permute-start(bf16[256,128]{1,0:T(8,128)(2,1)S(1)} %get-tuple-element.74), channel_id=1, source_target_pairs={{0,16},{4,20},{8,24},{12,28},{16,0},{20,4},{24,8},{28,12},{1,17},{... | collective-permute-start | bytes 196616 | tf_op jit(solution)/shard_map/ppermute | solution.py:374
  33.0 2.6 %collective-permute-done.6.other = bf16[256,128]{1,0:T(8,128)(2,1)S(1)} collective-permute-done((bf16[256,128]{1,0:T(8,128)(2,1)S(1)}, bf16[256,128]{1,0:T(8,128)(2,1)S(1)}, u32[]{:S(2)}, u32[]{:S(2)}) %collective-permute-start.6) | collective-permute-done | bytes 65568 | tf_op jit(solution)/shard_map/ppermute | solution.py:374
  35.5 0.1 spread.1
  35.6 1.2 %collective-permute-start.7 = (bf16[2,2,128,128]{3,2,1,0:T(8,128)(2,1)S(1)}, bf16[2,2,128,128]{3,2,1,0:T(8,128)(2,1)S(1)}, u32[]{:S(2)}, u32[]{:S(2)}) collective-permute-start(bf16[2,2,128,128]{3,2,1,0:T(8,128)(2,1)S(1)} %get-tuple-element.75), channel_id=1, source_target_pairs={{0,4},{1,9},{2,6},{3,11},{4,0},{5,13},{6,2},{7,15},{8,12},{9,1},{1... | collective-permute-start | bytes 393224 | tf_op jit(solution)/shard_map/ppermute | solution.py:384
  36.8 1.3 %collective-permute-start.8 = (bf16[2,2,128,128]{3,2,1,0:T(8,128)(2,1)S(1)}, bf16[2,2,128,128]{3,2,1,0:T(8,128)(2,1)S(1)}, u32[]{:S(2)}, u32[]{:S(2)}) collective-permute-start(bf16[2,2,128,128]{3,2,1,0:T(8,128)(2,1)S(1)} %get-tuple-element.76), channel_id=1, source_target_pairs={{0,8},{1,5},{2,10},{3,7},{4,12},{5,1},{6,14},{7,3},{8,0},{9,13},{1... | collective-permute-start | bytes 393224 | tf_op jit(solution)/shard_map/ppermute | solution.py:384
  38.1 1.1 %collective-permute-start.9 = (bf16[2,2,128,128]{3,2,1,0:T(8,128)(2,1)S(1)}, bf16[2,2,128,128]{3,2,1,0:T(8,128)(2,1)S(1)}, u32[]{:S(2)}, u32[]{:S(2)}) collective-permute-start(bf16[2,2,128,128]{3,2,1,0:T(8,128)(2,1)S(1)} %get-tuple-element.81), channel_id=1, source_target_pairs={{0,12},{1,13},{2,14},{3,15},{4,8},{5,9},{6,10},{7,11},{8,4},{9,5},... | collective-permute-start | bytes 393224 | tf_op jit(solution)/shard_map/ppermute | solution.py:384
  39.2 1.6 %back_own.1 = (bf16[3,256,256]{2,1,0:T(8,128)(2,1)S(1)}, f32[256,1024]{1,0:T(8,128)S(1)}, f32[256,1024]{1,0:T(8,128)S(1)}) custom-call(bf16[256,1024]{1,0:T(8,128)(2,1)S(1)} %get-tuple-element.56.key, bf16[256,1024]{1,0:T(8,128)(2,1)S(1)} %get-tuple-element.57.value, bf16[256,1024]{1,0:T(8,128)(2,1)S(1)} %copy-done, f32[256,25]{1,0:T(8,128)S(1)} %get-tuple-element.58.cols_h, ...), custom_call_target="tpu_custom_call" | custom-call | tf_op jit(solution)/shard_map/back_own/pallas_call | solution.py:33
  40.8 1.1 %collective-permute-done.7.states1 = bf16[2,2,128,128]{3,2,1,0:T(8,128)(2,1)S(1)} collective-permute-done((bf16[2,2,128,128]{3,2,1,0:T(8,128)(2,1)S(1)}, bf16[2,2,128,128]{3,2,1,0:T(8,128)(2,1)S(1)}, u32[]{:S(2)}, u32[]{:S(2)}) %collective-permute-start.7) | collective-permute-done | bytes 131104 | tf_op jit(solution)/shard_map/ppermute | solution.py:384
  41.9 0.0 collective-permute-done.8.states2
  41.9 1.6 %back_sides.1 = (bf16[3,256,256]{2,1,0:T(8,128)(2,1)S(1)}, bf16[3,256,256]{2,1,0:T(8,128)(2,1)S(1)}, f32[256,1024]{1,0:T(8,128)S(1)}) custom-call(bf16[256,1024]{1,0:T(8,128)(2,1)S(1)} %get-tuple-element.56.key, bf16[256,1024]{1,0:T(8,128)(2,1)S(1)} %get-tuple-element.57.value, bf16[256,1024]{1,0:T(8,128)(2,1)S(1)} %copy-done, ...), custom_call_target="tpu_custom_call", output_to_operand_aliasing={{2}: (10, {})} | custom-call | tf_op jit(solution)/shard_map/back_sides/pallas_call | solution.py:33
  43.5 0.4 collective-permute-done.9.states.states3
  44.0 0.8 %back_first.1 = (bf16[3,256,256]{2,1,0:T(8,128)(2,1)S(1)}, bf16[256,512]{1,0:T(8,128)(2,1)S(1)}) custom-call(bf16[256,1024]{1,0:T(8,128)(2,1)S(1)} %get-tuple-element.56.key, bf16[256,1024]{1,0:T(8,128)(2,1)S(1)} %get-tuple-element.57.value, bf16[256,1024]{1,0:T(8,128)(2,1)S(1)} %copy-done, f32[256,25]{1,0:T(8,128)S(1)} %get-tuple-element.58.cols_h, ...), custom_call_target="tpu_custom_call" | custom-call | tf_op jit(solution)/shard_map/back_first/pallas_call | solution.py:33
  44.8 0.1 collective-permute-start.10
  44.9 1.0 %back_second.1 = (bf16[256,512]{1,0:T(8,128)(2,1)S(1)}, f32[256,512]{1,0:T(8,128)S(1)}) custom-call(bf16[3,256,256]{2,1,0:T(8,128)(2,1)S(1)} %get-tuple-element.79.stack1, bf16[3,256,256]{2,1,0:T(8,128)(2,1)S(1)} %get-tuple-element.80.stack2, bf16[3,256,256]{2,1,0:T(8,128)(2,1)S(1)} %get-tuple-element.83.stack3, ...), custom_call_target="tpu_custom_call" | custom-call | tf_op jit(solution)/shard_map/back_second/pallas_call | solution.py:33
  45.9 0.6 collective-permute-start.11
  46.5 0.1 add_convert_fusion.1
  46.5 1.6 %collective-permute-start.12 = (bf16[256,512]{1,0:T(8,128)(2,1)S(1)}, bf16[256,512]{1,0:T(8,128)(2,1)S(1)}, u32[]{:S(2)}, u32[]{:S(2)}) collective-permute-start(bf16[256,512]{1,0:T(8,128)(2,1)S(1)} %add_convert_fusion.1), channel_id=1, source_target_pairs={{0,2},{1,3},{2,0},{3,1},{4,6},{5,7},{6,4},{7,5},{8,10},{9,11},{10,... | collective-permute-start | bytes 786440 | tf_op jit(solution)/shard_map/ppermute | solution.py:523
  48.1 0.8 %back_third.1 = f32[256,512]{1,0:T(8,128)S(1)} custom-call(bf16[3,256,256]{2,1,0:T(8,128)(2,1)S(1)} %get-tuple-element.79.stack1, bf16[3,256,256]{2,1,0:T(8,128)(2,1)S(1)} %get-tuple-element.80.stack2, bf16[3,256,256]{2,1,0:T(8,128)(2,1)S(1)} %get-tuple-element.83.stack3, bf16[3,4096,1024]{2,1,0:T(8,128)(2,1)S(1)} %get-tuple-element.50.refs_1_.w, ...), custom_call_target="tpu_custom_call" | custom-call | tf_op jit(solution)/shard_map/back_third/pallas_call | solution.py:33
  48.9 0.1 add_convert_fusion
  49.0 0.6 collective-permute-start.13
  49.6 3.2 %back_mine.1 = (f32[256,1024]{1,0:T(8,128)}, f32[256,1024]{1,0:T(8,128)S(1)}) custom-call(bf16[3,256,256]{2,1,0:T(8,128)(2,1)S(1)} %get-tuple-element.90.stack0, bf16[3,256,256]{2,1,0:T(8,128)(2,1)S(1)} %get-tuple-element.79.stack1, bf16[3,256,256]{2,1,0:T(8,128)(2,1)S(1)} %get-tuple-element.80.stack2, bf16[3,256,256]{2,1,0:T(8,128)(2,1)S(1)} %get-tuple-element.83.stack3, ...), custom_call_target="tpu_custom_call" | custom-call | tf_op jit(solution)/shard_map/back_mine/pallas_call | solution.py:33
  52.9 2.9 %collective-permute-done.12.across_a = bf16[256,512]{1,0:T(8,128)(2,1)S(1)} collective-permute-done((bf16[256,512]{1,0:T(8,128)(2,1)S(1)}, bf16[256,512]{1,0:T(8,128)(2,1)S(1)}, u32[]{:S(2)}, u32[]{:S(2)}) %collective-permute-start.12) | collective-permute-done | bytes 262176 | tf_op jit(solution)/shard_map/ppermute | solution.py:523
  55.8 2.0 %back_other.1 = (bf16[256,1024]{1,0:T(8,128)(2,1)S(1)}, f32[256,1024]{1,0:T(8,128)S(1)}) custom-call(bf16[3,256,256]{2,1,0:T(8,128)(2,1)S(1)} %get-tuple-element.90.stack0, bf16[3,256,256]{2,1,0:T(8,128)(2,1)S(1)} %get-tuple-element.79.stack1, bf16[3,256,256]{2,1,0:T(8,128)(2,1)S(1)} %get-tuple-element.80.stack2, ...), custom_call_target="tpu_custom_call", output_to_operand_aliasing={{1}: (6, {})} | custom-call | flops 1610612736 | tf_op jit(solution)/shard_map/back_other/pallas_call | solution.py:33
  57.8 0.1 collective-permute-start.17
  57.9 0.5 collective-permute-start.16
  58.4 0.1 collective-permute-start.15
  58.5 0.4 collective-permute-start.14
  58.9 1.6 %collective-permute-done.13.refs_0_ = bf16[256,512]{1,0:T(8,128)(2,1)S(1)} collective-permute-done((bf16[256,512]{1,0:T(8,128)(2,1)S(1)}, bf16[256,512]{1,0:T(8,128)(2,1)S(1)}, u32[]{:S(2)}, u32[]{:S(2)}) %collective-permute-start.13) | collective-permute-done | bytes 262176 | tf_op jit(solution)/shard_map/ppermute | solution.py:527
  60.5 0.0 collective-permute-done.15.refs_1_
  60.5 0.0 collective-permute-done.14.refs_0_
  60.5 1.0 %last_sum.1 = f32[256,1024]{1,0:T(8,128)} custom-call(f32[256,1024]{1,0:T(8,128)S(1)} %get-tuple-element.95.own, bf16[256,512]{1,0:T(8,128)(2,1)S(1)} %hand_on.1.across_b, bf16[64,1024]{1,0:T(8,128)(2,1)S(1)} %collective-permute-done.14.refs_0_, bf16[64,1024]{1,0:T(8,128)(2,1)S(1)} %collective-permute-done.15.refs_1_, ...), custom_call_target="tpu_custom_call" | custom-call | tf_op jit(solution)/shard_map/last_sum/pallas_call | solution.py:33
  (9 shorter events, 0.1 us)
Async XLA Ops:
  0.6 15.2 %collective-permute-start = (bf16[256,1024]{1,0:T(8,128)(2,1)}, bf16[256,1024]{1,0:T(8,128)(2,1)S(1)}, u32[]{:S(2)}, u32[]{:S(2)}) collective-permute-start(bf16[256,1024]{1,0:T(8,128)(2,1)} %tokens.1), channel_id=1, source_target_pairs={{0,2},{1,3},{2,0},{3,1},{4,6},{5,7},{6,4},{7,5},{8,10},{9,11},{10,... | collective-permute-start | bytes 1572872 | tf_op jit(solution)/shard_map/ppermute | solution.py:458
  3.7 8.4 %collective-permute-start.1 = (bf16[256,1024]{1,0:T(8,128)(2,1)}, bf16[256,1024]{1,0:T(8,128)(2,1)S(1)}, u32[]{:S(2)}, u32[]{:S(2)}) collective-permute-start(bf16[256,1024]{1,0:T(8,128)(2,1)} %tokens.1), channel_id=1, source_target_pairs={{0,1},{1,0},{2,3},{3,2},{4,5},{5,4},{6,7},{7,6},{8,9},{9,8},{10,11... | collective-permute-start | bytes 1572872 | tf_op jit(solution)/shard_map/ppermute | solution.py:459
  13.9 3.8 %copy-start = (bf16[256,1024]{1,0:T(8,128)(2,1)S(1)}, bf16[256,1024]{1,0:T(8,128)(2,1)}, u32[]{:S(2)}) copy-start(bf16[256,1024]{1,0:T(8,128)(2,1)} %grads.9) | copy-start | bytes 1572868
  15.8 1.9 %collective-permute-start.2 = (bf16[256,1024]{1,0:T(8,128)(2,1)S(1)}, bf16[256,1024]{1,0:T(8,128)(2,1)S(1)}, u32[]{:S(2)}, u32[]{:S(2)}) collective-permute-start(bf16[256,1024]{1,0:T(8,128)(2,1)S(1)} %collective-permute-done.refs_0_), channel_id=1, source_target_pairs={{0,1},{1,0},{2,3},{3,2},{4,5},{5,4},{6,7},{7,6},{8,9},{9,8},{10,11... | collective-permute-start | bytes 1572872 | tf_op jit(solution)/shard_map/ppermute | solution.py:481
  20.0 7.2 %collective-permute-start.3 = (bf16[528,128]{1,0:T(8,128)(2,1)S(1)}, bf16[528,128]{1,0:T(8,128)(2,1)S(1)}, u32[]{:S(2)}, u32[]{:S(2)}) collective-permute-start(bf16[528,128]{1,0:T(8,128)(2,1)S(1)} %get-tuple-element.69), channel_id=1, source_target_pairs={{0,4},{1,9},{2,6},{3,11},{4,0},{5,13},{6,2},{7,15},{8,12},{9,1},{1... | collective-permute-start | bytes 405512 | tf_op jit(solution)/shard_map/ppermute | solution.py:384
  21.8 6.1 %collective-permute-start.4 = (bf16[528,128]{1,0:T(8,128)(2,1)S(1)}, bf16[528,128]{1,0:T(8,128)(2,1)S(1)}, u32[]{:S(2)}, u32[]{:S(2)}) collective-permute-start(bf16[528,128]{1,0:T(8,128)(2,1)S(1)} %get-tuple-element.70), channel_id=1, source_target_pairs={{0,8},{1,5},{2,10},{3,7},{4,12},{5,1},{6,14},{7,3},{8,0},{9,13},{1... | collective-permute-start | bytes 405512 | tf_op jit(solution)/shard_map/ppermute | solution.py:384
  23.4 6.7 %collective-permute-start.5 = (bf16[528,128]{1,0:T(8,128)(2,1)S(1)}, bf16[528,128]{1,0:T(8,128)(2,1)S(1)}, u32[]{:S(2)}, u32[]{:S(2)}) collective-permute-start(bf16[528,128]{1,0:T(8,128)(2,1)S(1)} %get-tuple-element.71), channel_id=1, source_target_pairs={{0,12},{1,13},{2,14},{3,15},{4,8},{5,9},{6,10},{7,11},{8,4},{9,5},... | collective-permute-start | bytes 405512 | tf_op jit(solution)/shard_map/ppermute | solution.py:384
  30.3 5.2 %collective-permute-start.6 = (bf16[256,128]{1,0:T(8,128)(2,1)S(1)}, bf16[256,128]{1,0:T(8,128)(2,1)S(1)}, u32[]{:S(2)}, u32[]{:S(2)}) collective-permute-start(bf16[256,128]{1,0:T(8,128)(2,1)S(1)} %get-tuple-element.74), channel_id=1, source_target_pairs={{0,16},{4,20},{8,24},{12,28},{16,0},{20,4},{24,8},{28,12},{1,17},{... | collective-permute-start | bytes 196616 | tf_op jit(solution)/shard_map/ppermute | solution.py:374
  35.6 6.2 %collective-permute-start.7 = (bf16[2,2,128,128]{3,2,1,0:T(8,128)(2,1)S(1)}, bf16[2,2,128,128]{3,2,1,0:T(8,128)(2,1)S(1)}, u32[]{:S(2)}, u32[]{:S(2)}) collective-permute-start(bf16[2,2,128,128]{3,2,1,0:T(8,128)(2,1)S(1)} %get-tuple-element.75), channel_id=1, source_target_pairs={{0,4},{1,9},{2,6},{3,11},{4,0},{5,13},{6,2},{7,15},{8,12},{9,1},{1... | collective-permute-start | bytes 393224 | tf_op jit(solution)/shard_map/ppermute | solution.py:384
  36.8 5.1 %collective-permute-start.8 = (bf16[2,2,128,128]{3,2,1,0:T(8,128)(2,1)S(1)}, bf16[2,2,128,128]{3,2,1,0:T(8,128)(2,1)S(1)}, u32[]{:S(2)}, u32[]{:S(2)}) collective-permute-start(bf16[2,2,128,128]{3,2,1,0:T(8,128)(2,1)S(1)} %get-tuple-element.76), channel_id=1, source_target_pairs={{0,8},{1,5},{2,10},{3,7},{4,12},{5,1},{6,14},{7,3},{8,0},{9,13},{1... | collective-permute-start | bytes 393224 | tf_op jit(solution)/shard_map/ppermute | solution.py:384
  38.1 5.9 %collective-permute-start.9 = (bf16[2,2,128,128]{3,2,1,0:T(8,128)(2,1)S(1)}, bf16[2,2,128,128]{3,2,1,0:T(8,128)(2,1)S(1)}, u32[]{:S(2)}, u32[]{:S(2)}) collective-permute-start(bf16[2,2,128,128]{3,2,1,0:T(8,128)(2,1)S(1)} %get-tuple-element.81), channel_id=1, source_target_pairs={{0,12},{1,13},{2,14},{3,15},{4,8},{5,9},{6,10},{7,11},{8,4},{9,5},... | collective-permute-start | bytes 393224 | tf_op jit(solution)/shard_map/ppermute | solution.py:384
  44.8 1.7 %collective-permute-start.10 = (bf16[256,512]{1,0:T(8,128)(2,1)S(1)}, bf16[256,512]{1,0:T(8,128)(2,1)S(1)}, u32[]{:S(2)}, u32[]{:S(2)}) collective-permute-start(bf16[256,512]{1,0:T(8,128)(2,1)S(1)} %get-tuple-element.86), channel_id=1, source_target_pairs={{0,1},{1,0},{2,3},{3,2},{4,5},{5,4},{6,7},{7,6},{8,9},{9,8},{10,11... | collective-permute-start | bytes 786440 | tf_op jit(solution)/shard_map/ppermute | solution.py:515
  45.9 3.0 %collective-permute-start.11 = (bf16[256,512]{1,0:T(8,128)(2,1)S(1)}, bf16[256,512]{1,0:T(8,128)(2,1)S(1)}, u32[]{:S(2)}, u32[]{:S(2)}) collective-permute-start(bf16[256,512]{1,0:T(8,128)(2,1)S(1)} %get-tuple-element.88), channel_id=1, source_target_pairs={{0,1},{1,0},{2,3},{3,2},{4,5},{5,4},{6,7},{7,6},{8,9},{9,8},{10,11... | collective-permute-start | bytes 786440 | tf_op jit(solution)/shard_map/ppermute | solution.py:520
  46.5 9.2 %collective-permute-start.12 = (bf16[256,512]{1,0:T(8,128)(2,1)S(1)}, bf16[256,512]{1,0:T(8,128)(2,1)S(1)}, u32[]{:S(2)}, u32[]{:S(2)}) collective-permute-start(bf16[256,512]{1,0:T(8,128)(2,1)S(1)} %add_convert_fusion.1), channel_id=1, source_target_pairs={{0,2},{1,3},{2,0},{3,1},{4,6},{5,7},{6,4},{7,5},{8,10},{9,11},{10,... | collective-permute-start | bytes 786440 | tf_op jit(solution)/shard_map/ppermute | solution.py:523
  49.0 11.5 %collective-permute-start.13 = (bf16[256,512]{1,0:T(8,128)(2,1)S(1)}, bf16[256,512]{1,0:T(8,128)(2,1)S(1)}, u32[]{:S(2)}, u32[]{:S(2)}) collective-permute-start(bf16[256,512]{1,0:T(8,128)(2,1)S(1)} %add_convert_fusion), channel_id=1, source_target_pairs={{0,2},{1,3},{2,0},{3,1},{4,6},{5,7},{6,4},{7,5},{8,10},{9,11},{10,... | collective-permute-start | bytes 786440 | tf_op jit(solution)/shard_map/ppermute | solution.py:527
  57.8 2.7 %collective-permute-start.17 = (bf16[64,1024]{1,0:T(8,128)(2,1)S(1)}, bf16[64,1024]{1,0:T(8,128)(2,1)S(1)}, u32[]{:S(2)}, u32[]{:S(2)}) collective-permute-start(bf16[64,1024]{1,0:T(8,128)(2,1)S(1)} %get-tuple-element.98), channel_id=1, source_target_pairs={{0,1},{1,0},{2,3},{3,2},{4,5},{5,4},{6,7},{7,6},{8,9},{9,8},{10,11... | collective-permute-start | bytes 393224 | tf_op jit(solution)/shard_map/ppermute | solution.py:544
  57.9 2.6 %collective-permute-start.16 = (bf16[64,1024]{1,0:T(8,128)(2,1)S(1)}, bf16[64,1024]{1,0:T(8,128)(2,1)S(1)}, u32[]{:S(2)}, u32[]{:S(2)}) collective-permute-start(bf16[64,1024]{1,0:T(8,128)(2,1)S(1)} %get-tuple-element.99), channel_id=1, source_target_pairs={{0,1},{1,0},{2,3},{3,2},{4,5},{5,4},{6,7},{7,6},{8,9},{9,8},{10,11... | collective-permute-start | bytes 393224 | tf_op jit(solution)/shard_map/ppermute | solution.py:544
  58.4 2.1 %collective-permute-start.15 = (bf16[64,1024]{1,0:T(8,128)(2,1)S(1)}, bf16[64,1024]{1,0:T(8,128)(2,1)S(1)}, u32[]{:S(2)}, u32[]{:S(2)}) collective-permute-start(bf16[64,1024]{1,0:T(8,128)(2,1)S(1)} %get-tuple-element.100), channel_id=1, source_target_pairs={{0,1},{1,0},{2,3},{3,2},{4,5},{5,4},{6,7},{7,6},{8,9},{9,8},{10,11... | collective-permute-start | bytes 393224 | tf_op jit(solution)/shard_map/ppermute | solution.py:544
  58.5 2.0 %collective-permute-start.14 = (bf16[64,1024]{1,0:T(8,128)(2,1)S(1)}, bf16[64,1024]{1,0:T(8,128)(2,1)S(1)}, u32[]{:S(2)}, u32[]{:S(2)}) collective-permute-start(bf16[64,1024]{1,0:T(8,128)(2,1)S(1)} %get-tuple-element.101), channel_id=1, source_target_pairs={{0,1},{1,0},{2,3},{3,2},{4,5},{5,4},{6,7},{7,6},{8,9},{9,8},{10,11... | collective-permute-start | bytes 393224 | tf_op jit(solution)/shard_map/ppermute | solution.py:544

commit v10 on v9

--- a/solution.py
+++ b/solution.py
@@ -20,6 +20,11 @@
 def split(a):
     high = a.astype(BF16)
     return high, (a - high.astype(F32)).astype(BF16)
+
+
+def dot_split(a, b, ca, cb):
+    high, low = split(a)
+    return dot(high, b, ca, cb) + dot(low, b, ca, cb)
 
 
 def call(kernel, name, outs, args, spaces=None, flops=0, limit=4, aliases=None, scratch=(), out_spaces=None):
@@ -180,14 +185,14 @@
 def state_end(key, value, rows_h, h):
     cols = slice(h * DH, (h + 1) * DH)
     heads = rows_h.shape[0] // 3
-    return dot((key[:, cols].T.astype(F32) * rows_h[2 * heads + h : 2 * heads + h + 1, :]).astype(BF16), value[:, cols], 1, 0)
+    return dot_split(key[:, cols].T.astype(F32) * rows_h[2 * heads + h : 2 * heads + h + 1, :], value[:, cols], 1, 0)
 
 
 def grad_start(query, grads, rows_h, h):
     cols = slice(h * DH, (h + 1) * DH)
     heads = rows_h.shape[0] // 3
     weight = rows_h[heads + h : heads + h + 1, :] * (1.0 / DH)
-    return dot((query[:, cols].T.astype(F32) * weight).astype(BF16), grads[:, cols], 1, 0)
+    return dot_split(query[:, cols].T.astype(F32) * weight, grads[:, cols], 1, 0)
 
 
 def own_states(query, key, value, grads, rows_h, states):

time: 61.9 us -> 62.1 us (level)
  no operation moved by 1% of the time
where the time goes in v10:
time: 62.1 us; the launch traced here: 61.9 us
  Pallas kernels  30.6 us (49%)
  starting transfers between devices  16.7 us (27%)
  waiting for transfers between devices  13.4 us (22%)
  between operations  0.99 us (2%)
    pallas_call x16, Pallas kernels, call(): pl.pallas_call(kernel, name=name, out_shape=[kinds[s](shape, dtype) for s...  30.6 us
    ppermute x6, starting transfers between devices, to_member(): return lax.ppermute(a, ('seq', 'tp'), pairs)  7.11 us
    ppermute x6, waiting for transfers between devices, to_member(): return lax.ppermute(a, ('seq', 'tp'), pairs)  4.35 us
    ppermute x1, starting transfers between devices, local(): across = lax.ppermute(tokens, 'tp', chip)  3.03 us
    ppermute x1, waiting for transfers between devices, local(): across_a = lax.ppermute(chunk_a, 'tp', chip)  2.91 us
    ppermute x1, starting transfers between devices, to_other_group(): return lax.ppermute(a, 'seq', [(i, i ^ 4) for i in range(8)])  2.65 us
    ppermute x1, waiting for transfers between devices, to_other_group(): return lax.ppermute(a, 'seq', [(i, i ^ 4) for i in range(8)])  2.57 us
    ppermute x1, waiting for transfers between devices, local(): across = lax.ppermute(tokens, 'tp', chip)  1.88 us
  transfers between devices with their start and end apart: 18, of which 9 were waited for; matrix products, arithmetic and copies ran while one was open for 0% of the time, Pallas kernels for 42%

profile of v10, /device:TPU:0, one launch (start us, length us, event | category | flops | bytes accessed | tf_op | source)
XLA Modules:
  0.0 61.9 jit_solution(12182187083895982602)
XLA Ops:
  0.6 3.0 %collective-permute-start = (bf16[256,1024]{1,0:T(8,128)(2,1)}, bf16[256,1024]{1,0:T(8,128)(2,1)S(1)}, u32[]{:S(2)}, u32[]{:S(2)}) collective-permute-start(bf16[256,1024]{1,0:T(8,128)(2,1)} %tokens.1), channel_id=1, source_target_pairs={{0,2},{1,3},{2,0},{3,1},{4,6},{5,7},{6,4},{7,5},{8,10},{9,11},{10,... | collective-permute-start | bytes 1572872 | tf_op jit(solution)/shard_map/ppermute | solution.py:463
  3.7 0.0 collective-permute-start.1
  3.7 8.4 %load_and_project.1 = (bf16[3,4096,1024]{2,1,0:T(8,128)(2,1)S(1)}, f32[3,256,1024]{2,1,0:T(8,128)S(1)}, f32[256,25]{1,0:T(8,128)S(1)}, f32[24,256]{1,0:T(8,128)S(1)}, bf16[16,128]{1,0:T(8,128)(2,1)S(1)}) custom-call(s32[16]{0:T(128)} %lengths.1, f32[8,256]{1,0:T(8,128)} %bitcast.1, bf16[256,1024]{1,0:T(8,128)(2,1)} %tokens.1, bf16[3,4096,1024]{2,1,0:T(8,128)(2,1)} %w.1), custom_call_target="tpu_custom_call" | custom-call | flops 12884901888 | tf_op jit(solution)/shard_map/load_and_project/pallas_call | solution.py:38
  12.1 1.8 %project_beside.1.refs_2_ = f32[3,256,1024]{2,1,0:T(8,128)S(1)} custom-call(bf16[256,1024]{1,0:T(8,128)(2,1)S(1)} %collective-permute-done.1.refs_0_, bf16[3,4096,1024]{2,1,0:T(8,128)(2,1)S(1)} %get-tuple-element.50.refs_1_.w, f32[3,256,1024]{2,1,0:T(8,128)S(1)} %get-tuple-element.51.refs_2_), custom_call_target="tpu_custom_call" | custom-call | tf_op jit(solution)/shard_map/project_beside/pallas_call | solution.py:38
  13.9 0.0 copy-start
  13.9 1.9 %collective-permute-done.refs_0_ = bf16[256,1024]{1,0:T(8,128)(2,1)S(1)} collective-permute-done((bf16[256,1024]{1,0:T(8,128)(2,1)}, bf16[256,1024]{1,0:T(8,128)(2,1)S(1)}, u32[]{:S(2)}, u32[]{:S(2)}) %collective-permute-start) | collective-permute-done | bytes 524320 | tf_op jit(solution)/shard_map/ppermute | solution.py:463
  15.8 1.8 %project_across.1.acc_in = f32[3,256,1024]{2,1,0:T(8,128)S(1)} custom-call(bf16[256,1024]{1,0:T(8,128)(2,1)S(1)} %collective-permute-done.refs_0_, bf16[3,4096,1024]{2,1,0:T(8,128)(2,1)S(1)} %get-tuple-element.50.refs_1_.w, f32[3,256,1024]{2,1,0:T(8,128)S(1)} %project_beside.1.refs_2_), custom_call_target="tpu_custom_call" | custom-call | tf_op jit(solution)/shard_map/project_across/pallas_call | solution.py:38
  17.6 0.1 collective-permute-done.2.x
  17.7 2.5 %project_last.1 = (bf16[256,1024]{1,0:T(8,128)(2,1)S(1)}, bf16[256,1024]{1,0:T(8,128)(2,1)S(1)}, bf16[256,1024]{1,0:T(8,128)(2,1)S(1)}, f32[2,2,128,128]{3,2,1,0...) custom-call(bf16[256,1024]{1,0:T(8,128)(2,1)S(1)} %collective-permute-done.2, ...), custom_call_target="tpu_custom_call" | custom-call | tf_op jit(solution)/shard_map/project_last/pallas_call | solution.py:38
  20.2 1.8 %collective-permute-start.3 = (bf16[528,128]{1,0:T(8,128)(2,1)S(1)}, bf16[528,128]{1,0:T(8,128)(2,1)S(1)}, u32[]{:S(2)}, u32[]{:S(2)}) collective-permute-start(bf16[528,128]{1,0:T(8,128)(2,1)S(1)} %get-tuple-element.69), channel_id=1, source_target_pairs={{0,4},{1,9},{2,6},{3,11},{4,0},{5,13},{6,2},{7,15},{8,12},{9,1},{1... | collective-permute-start | bytes 405512 | tf_op jit(solution)/shard_map/ppermute | solution.py:389
  22.0 1.6 %collective-permute-start.4 = (bf16[528,128]{1,0:T(8,128)(2,1)S(1)}, bf16[528,128]{1,0:T(8,128)(2,1)S(1)}, u32[]{:S(2)}, u32[]{:S(2)}) collective-permute-start(bf16[528,128]{1,0:T(8,128)(2,1)S(1)} %get-tuple-element.70), channel_id=1, source_target_pairs={{0,8},{1,5},{2,10},{3,7},{4,12},{5,1},{6,14},{7,3},{8,0},{9,13},{1... | collective-permute-start | bytes 405512 | tf_op jit(solution)/shard_map/ppermute | solution.py:389
  23.6 0.2 collective-permute-start.5
  23.8 3.6 %intra.1 = (f32[256,1024]{1,0:T(8,128)S(1)}, f32[256,1024]{1,0:T(8,128)S(1)}, f32[256,1024]{1,0:T(8,128)S(1)}, f32[256,1024]{1,0:T(8,128)S(1)}) custom-call(bf16[256,1024]{1,0:T(8,128)(2,1)S(1)} %get-tuple-element.59.query, bf16[256,1024]{1,0:T(8,128)(2,1)S(1)} %get-tuple-element.56.key, bf16[256,1024]{1,0:T(8,128)(2,1)S(1)} %get-tuple-element.57.value, ...), custom_call_target="tpu_custom_call" | custom-call | flops 1073741824 | tf_op jit(solution)/shard_map/intra/pallas_call | solution.py:38
  27.4 0.0 collective-permute-done.3.got1
  27.4 0.7 %collective-permute-done.4.got2 = bf16[528,128]{1,0:T(8,128)(2,1)S(1)} collective-permute-done((bf16[528,128]{1,0:T(8,128)(2,1)S(1)}, bf16[528,128]{1,0:T(8,128)(2,1)S(1)}, u32[]{:S(2)}, u32[]{:S(2)}) %collective-permute-start.4) | collective-permute-done | bytes 135200 | tf_op jit(solution)/shard_map/ppermute | solution.py:389
  28.1 2.2 %collective-permute-done.5.got3 = bf16[528,128]{1,0:T(8,128)(2,1)S(1)} collective-permute-done((bf16[528,128]{1,0:T(8,128)(2,1)S(1)}, bf16[528,128]{1,0:T(8,128)(2,1)S(1)}, u32[]{:S(2)}, u32[]{:S(2)}) %collective-permute-start.5) | collective-permute-done | bytes 135200 | tf_op jit(solution)/shard_map/ppermute | solution.py:389
  30.2 0.3 join.1
  30.5 2.7 %collective-permute-start.6 = (bf16[256,128]{1,0:T(8,128)(2,1)S(1)}, bf16[256,128]{1,0:T(8,128)(2,1)S(1)}, u32[]{:S(2)}, u32[]{:S(2)}) collective-permute-start(bf16[256,128]{1,0:T(8,128)(2,1)S(1)} %get-tuple-element.74), channel_id=1, source_target_pairs={{0,16},{4,20},{8,24},{12,28},{16,0},{20,4},{24,8},{28,12},{1,17},{... | collective-permute-start | bytes 196616 | tf_op jit(solution)/shard_map/ppermute | solution.py:379
  33.2 2.6 %collective-permute-done.6.other = bf16[256,128]{1,0:T(8,128)(2,1)S(1)} collective-permute-done((bf16[256,128]{1,0:T(8,128)(2,1)S(1)}, bf16[256,128]{1,0:T(8,128)(2,1)S(1)}, u32[]{:S(2)}, u32[]{:S(2)}) %collective-permute-start.6) | collective-permute-done | bytes 65568 | tf_op jit(solution)/shard_map/ppermute | solution.py:379
  35.7 0.1 spread.1
  35.8 1.2 %collective-permute-start.7 = (bf16[2,2,128,128]{3,2,1,0:T(8,128)(2,1)S(1)}, bf16[2,2,128,128]{3,2,1,0:T(8,128)(2,1)S(1)}, u32[]{:S(2)}, u32[]{:S(2)}) collective-permute-start(bf16[2,2,128,128]{3,2,1,0:T(8,128)(2,1)S(1)} %get-tuple-element.75), channel_id=1, source_target_pairs={{0,4},{1,9},{2,6},{3,11},{4,0},{5,13},{6,2},{7,15},{8,12},{9,1},{1... | collective-permute-start | bytes 393224 | tf_op jit(solution)/shard_map/ppermute | solution.py:389
  37.0 1.3 %collective-permute-start.8 = (bf16[2,2,128,128]{3,2,1,0:T(8,128)(2,1)S(1)}, bf16[2,2,128,128]{3,2,1,0:T(8,128)(2,1)S(1)}, u32[]{:S(2)}, u32[]{:S(2)}) collective-permute-start(bf16[2,2,128,128]{3,2,1,0:T(8,128)(2,1)S(1)} %get-tuple-element.76), channel_id=1, source_target_pairs={{0,8},{1,5},{2,10},{3,7},{4,12},{5,1},{6,14},{7,3},{8,0},{9,13},{1... | collective-permute-start | bytes 393224 | tf_op jit(solution)/shard_map/ppermute | solution.py:389
  38.3 1.1 %collective-permute-start.9 = (bf16[2,2,128,128]{3,2,1,0:T(8,128)(2,1)S(1)}, bf16[2,2,128,128]{3,2,1,0:T(8,128)(2,1)S(1)}, u32[]{:S(2)}, u32[]{:S(2)}) collective-permute-start(bf16[2,2,128,128]{3,2,1,0:T(8,128)(2,1)S(1)} %get-tuple-element.81), channel_id=1, source_target_pairs={{0,12},{1,13},{2,14},{3,15},{4,8},{5,9},{6,10},{7,11},{8,4},{9,5},... | collective-permute-start | bytes 393224 | tf_op jit(solution)/shard_map/ppermute | solution.py:389
  39.4 1.6 %back_own.1 = (bf16[3,256,256]{2,1,0:T(8,128)(2,1)S(1)}, f32[256,1024]{1,0:T(8,128)S(1)}, f32[256,1024]{1,0:T(8,128)S(1)}) custom-call(bf16[256,1024]{1,0:T(8,128)(2,1)S(1)} %get-tuple-element.56.key, bf16[256,1024]{1,0:T(8,128)(2,1)S(1)} %get-tuple-element.57.value, bf16[256,1024]{1,0:T(8,128)(2,1)S(1)} %copy-done, f32[256,25]{1,0:T(8,128)S(1)} %get-tuple-element.58.cols_h, ...), custom_call_target="tpu_custom_call" | custom-call | tf_op jit(solution)/shard_map/back_own/pallas_call | solution.py:38
  41.0 1.1 %collective-permute-done.7.states1 = bf16[2,2,128,128]{3,2,1,0:T(8,128)(2,1)S(1)} collective-permute-done((bf16[2,2,128,128]{3,2,1,0:T(8,128)(2,1)S(1)}, bf16[2,2,128,128]{3,2,1,0:T(8,128)(2,1)S(1)}, u32[]{:S(2)}, u32[]{:S(2)}) %collective-permute-start.7) | collective-permute-done | bytes 131104 | tf_op jit(solution)/shard_map/ppermute | solution.py:389
  42.1 1.6 %back_sides.1 = (bf16[3,256,256]{2,1,0:T(8,128)(2,1)S(1)}, bf16[3,256,256]{2,1,0:T(8,128)(2,1)S(1)}, f32[256,1024]{1,0:T(8,128)S(1)}) custom-call(bf16[256,1024]{1,0:T(8,128)(2,1)S(1)} %get-tuple-element.56.key, bf16[256,1024]{1,0:T(8,128)(2,1)S(1)} %get-tuple-element.57.value, bf16[256,1024]{1,0:T(8,128)(2,1)S(1)} %copy-done, ...), custom_call_target="tpu_custom_call", output_to_operand_aliasing={{2}: (10, {})} | custom-call | tf_op jit(solution)/shard_map/back_sides/pallas_call | solution.py:38
  43.8 0.4 collective-permute-done.9.states.states3
  44.2 0.8 %back_first.1 = (bf16[3,256,256]{2,1,0:T(8,128)(2,1)S(1)}, bf16[256,512]{1,0:T(8,128)(2,1)S(1)}) custom-call(bf16[256,1024]{1,0:T(8,128)(2,1)S(1)} %get-tuple-element.56.key, bf16[256,1024]{1,0:T(8,128)(2,1)S(1)} %get-tuple-element.57.value, bf16[256,1024]{1,0:T(8,128)(2,1)S(1)} %copy-done, f32[256,25]{1,0:T(8,128)S(1)} %get-tuple-element.58.cols_h, ...), custom_call_target="tpu_custom_call" | custom-call | tf_op jit(solution)/shard_map/back_first/pallas_call | solution.py:38
  45.0 0.1 collective-permute-start.10
  45.1 1.0 %back_second.1 = (bf16[256,512]{1,0:T(8,128)(2,1)S(1)}, f32[256,512]{1,0:T(8,128)S(1)}) custom-call(bf16[3,256,256]{2,1,0:T(8,128)(2,1)S(1)} %get-tuple-element.79.stack1, bf16[3,256,256]{2,1,0:T(8,128)(2,1)S(1)} %get-tuple-element.80.stack2, bf16[3,256,256]{2,1,0:T(8,128)(2,1)S(1)} %get-tuple-element.83.stack3, ...), custom_call_target="tpu_custom_call" | custom-call | tf_op jit(solution)/shard_map/back_second/pallas_call | solution.py:38
  46.1 0.5 collective-permute-start.11
  46.7 0.0 collective-permute-done.10
  46.7 0.1 add_convert_fusion.1
  46.7 1.6 %collective-permute-start.12 = (bf16[256,512]{1,0:T(8,128)(2,1)S(1)}, bf16[256,512]{1,0:T(8,128)(2,1)S(1)}, u32[]{:S(2)}, u32[]{:S(2)}) collective-permute-start(bf16[256,512]{1,0:T(8,128)(2,1)S(1)} %add_convert_fusion.1), channel_id=1, source_target_pairs={{0,2},{1,3},{2,0},{3,1},{4,6},{5,7},{6,4},{7,5},{8,10},{9,11},{10,... | collective-permute-start | bytes 786440 | tf_op jit(solution)/shard_map/ppermute | solution.py:528
  48.3 0.8 %back_third.1 = f32[256,512]{1,0:T(8,128)S(1)} custom-call(bf16[3,256,256]{2,1,0:T(8,128)(2,1)S(1)} %get-tuple-element.79.stack1, bf16[3,256,256]{2,1,0:T(8,128)(2,1)S(1)} %get-tuple-element.80.stack2, bf16[3,256,256]{2,1,0:T(8,128)(2,1)S(1)} %get-tuple-element.83.stack3, bf16[3,4096,1024]{2,1,0:T(8,128)(2,1)S(1)} %get-tuple-element.50.refs_1_.w, ...), custom_call_target="tpu_custom_call" | custom-call | tf_op jit(solution)/shard_map/back_third/pallas_call | solution.py:38
  49.1 0.0 collective-permute-done.11
  49.1 0.1 add_convert_fusion
  49.2 0.6 collective-permute-start.13
  49.8 3.2 %back_mine.1 = (f32[256,1024]{1,0:T(8,128)}, f32[256,1024]{1,0:T(8,128)S(1)}) custom-call(bf16[3,256,256]{2,1,0:T(8,128)(2,1)S(1)} %get-tuple-element.90.stack0, bf16[3,256,256]{2,1,0:T(8,128)(2,1)S(1)} %get-tuple-element.79.stack1, bf16[3,256,256]{2,1,0:T(8,128)(2,1)S(1)} %get-tuple-element.80.stack2, bf16[3,256,256]{2,1,0:T(8,128)(2,1)S(1)} %get-tuple-element.83.stack3, ...), custom_call_target="tpu_custom_call" | custom-call | tf_op jit(solution)/shard_map/back_mine/pallas_call | solution.py:38
  53.1 2.9 %collective-permute-done.12.across_a = bf16[256,512]{1,0:T(8,128)(2,1)S(1)} collective-permute-done((bf16[256,512]{1,0:T(8,128)(2,1)S(1)}, bf16[256,512]{1,0:T(8,128)(2,1)S(1)}, u32[]{:S(2)}, u32[]{:S(2)}) %collective-permute-start.12) | collective-permute-done | bytes 262176 | tf_op jit(solution)/shard_map/ppermute | solution.py:528
  56.0 2.0 %back_other.1 = (bf16[256,1024]{1,0:T(8,128)(2,1)S(1)}, f32[256,1024]{1,0:T(8,128)S(1)}) custom-call(bf16[3,256,256]{2,1,0:T(8,128)(2,1)S(1)} %get-tuple-element.90.stack0, bf16[3,256,256]{2,1,0:T(8,128)(2,1)S(1)} %get-tuple-element.79.stack1, bf16[3,256,256]{2,1,0:T(8,128)(2,1)S(1)} %get-tuple-element.80.stack2, ...), custom_call_target="tpu_custom_call", output_to_operand_aliasing={{1}: (6, {})} | custom-call | flops 1610612736 | tf_op jit(solution)/shard_map/back_other/pallas_call | solution.py:38
  58.0 0.1 collective-permute-start.17
  58.1 0.5 collective-permute-start.16
  58.6 0.1 collective-permute-start.15
  58.7 0.4 collective-permute-start.14
  59.1 1.6 %collective-permute-done.13.refs_0_ = bf16[256,512]{1,0:T(8,128)(2,1)S(1)} collective-permute-done((bf16[256,512]{1,0:T(8,128)(2,1)S(1)}, bf16[256,512]{1,0:T(8,128)(2,1)S(1)}, u32[]{:S(2)}, u32[]{:S(2)}) %collective-permute-start.13) | collective-permute-done | bytes 262176 | tf_op jit(solution)/shard_map/ppermute | solution.py:532
  60.7 0.0 collective-permute-done.17.refs_3_
  60.7 1.0 %last_sum.1 = f32[256,1024]{1,0:T(8,128)} custom-call(f32[256,1024]{1,0:T(8,128)S(1)} %get-tuple-element.95.own, bf16[256,512]{1,0:T(8,128)(2,1)S(1)} %hand_on.1.across_b, bf16[64,1024]{1,0:T(8,128)(2,1)S(1)} %collective-permute-done.14.refs_0_, bf16[64,1024]{1,0:T(8,128)(2,1)S(1)} %collective-permute-done.15.refs_1_, ...), custom_call_target="tpu_custom_call" | custom-call | tf_op jit(solution)/shard_map/last_sum/pallas_call | solution.py:38
  (9 shorter events, 0.1 us)
Async XLA Ops:
  0.6 15.2 %collective-permute-start = (bf16[256,1024]{1,0:T(8,128)(2,1)}, bf16[256,1024]{1,0:T(8,128)(2,1)S(1)}, u32[]{:S(2)}, u32[]{:S(2)}) collective-permute-start(bf16[256,1024]{1,0:T(8,128)(2,1)} %tokens.1), channel_id=1, source_target_pairs={{0,2},{1,3},{2,0},{3,1},{4,6},{5,7},{6,4},{7,5},{8,10},{9,11},{10,... | collective-permute-start | bytes 1572872 | tf_op jit(solution)/shard_map/ppermute | solution.py:463
  3.7 8.4 %collective-permute-start.1 = (bf16[256,1024]{1,0:T(8,128)(2,1)}, bf16[256,1024]{1,0:T(8,128)(2,1)S(1)}, u32[]{:S(2)}, u32[]{:S(2)}) collective-permute-start(bf16[256,1024]{1,0:T(8,128)(2,1)} %tokens.1), channel_id=1, source_target_pairs={{0,1},{1,0},{2,3},{3,2},{4,5},{5,4},{6,7},{7,6},{8,9},{9,8},{10,11... | collective-permute-start | bytes 1572872 | tf_op jit(solution)/shard_map/ppermute | solution.py:464
  13.9 3.8 %copy-start = (bf16[256,1024]{1,0:T(8,128)(2,1)S(1)}, bf16[256,1024]{1,0:T(8,128)(2,1)}, u32[]{:S(2)}) copy-start(bf16[256,1024]{1,0:T(8,128)(2,1)} %grads.9) | copy-start | bytes 1572868
  15.8 1.9 %collective-permute-start.2 = (bf16[256,1024]{1,0:T(8,128)(2,1)S(1)}, bf16[256,1024]{1,0:T(8,128)(2,1)S(1)}, u32[]{:S(2)}, u32[]{:S(2)}) collective-permute-start(bf16[256,1024]{1,0:T(8,128)(2,1)S(1)} %collective-permute-done.refs_0_), channel_id=1, source_target_pairs={{0,1},{1,0},{2,3},{3,2},{4,5},{5,4},{6,7},{7,6},{8,9},{9,8},{10,11... | collective-permute-start | bytes 1572872 | tf_op jit(solution)/shard_map/ppermute | solution.py:486
  20.2 7.2 %collective-permute-start.3 = (bf16[528,128]{1,0:T(8,128)(2,1)S(1)}, bf16[528,128]{1,0:T(8,128)(2,1)S(1)}, u32[]{:S(2)}, u32[]{:S(2)}) collective-permute-start(bf16[528,128]{1,0:T(8,128)(2,1)S(1)} %get-tuple-element.69), channel_id=1, source_target_pairs={{0,4},{1,9},{2,6},{3,11},{4,0},{5,13},{6,2},{7,15},{8,12},{9,1},{1... | collective-permute-start | bytes 405512 | tf_op jit(solution)/shard_map/ppermute | solution.py:389
  22.0 6.1 %collective-permute-start.4 = (bf16[528,128]{1,0:T(8,128)(2,1)S(1)}, bf16[528,128]{1,0:T(8,128)(2,1)S(1)}, u32[]{:S(2)}, u32[]{:S(2)}) collective-permute-start(bf16[528,128]{1,0:T(8,128)(2,1)S(1)} %get-tuple-element.70), channel_id=1, source_target_pairs={{0,8},{1,5},{2,10},{3,7},{4,12},{5,1},{6,14},{7,3},{8,0},{9,13},{1... | collective-permute-start | bytes 405512 | tf_op jit(solution)/shard_map/ppermute | solution.py:389
  23.6 6.7 %collective-permute-start.5 = (bf16[528,128]{1,0:T(8,128)(2,1)S(1)}, bf16[528,128]{1,0:T(8,128)(2,1)S(1)}, u32[]{:S(2)}, u32[]{:S(2)}) collective-permute-start(bf16[528,128]{1,0:T(8,128)(2,1)S(1)} %get-tuple-element.71), channel_id=1, source_target_pairs={{0,12},{1,13},{2,14},{3,15},{4,8},{5,9},{6,10},{7,11},{8,4},{9,5},... | collective-permute-start | bytes 405512 | tf_op jit(solution)/shard_map/ppermute | solution.py:389
  30.5 5.2 %collective-permute-start.6 = (bf16[256,128]{1,0:T(8,128)(2,1)S(1)}, bf16[256,128]{1,0:T(8,128)(2,1)S(1)}, u32[]{:S(2)}, u32[]{:S(2)}) collective-permute-start(bf16[256,128]{1,0:T(8,128)(2,1)S(1)} %get-tuple-element.74), channel_id=1, source_target_pairs={{0,16},{4,20},{8,24},{12,28},{16,0},{20,4},{24,8},{28,12},{1,17},{... | collective-permute-start | bytes 196616 | tf_op jit(solution)/shard_map/ppermute | solution.py:379
  35.8 6.2 %collective-permute-start.7 = (bf16[2,2,128,128]{3,2,1,0:T(8,128)(2,1)S(1)}, bf16[2,2,128,128]{3,2,1,0:T(8,128)(2,1)S(1)}, u32[]{:S(2)}, u32[]{:S(2)}) collective-permute-start(bf16[2,2,128,128]{3,2,1,0:T(8,128)(2,1)S(1)} %get-tuple-element.75), channel_id=1, source_target_pairs={{0,4},{1,9},{2,6},{3,11},{4,0},{5,13},{6,2},{7,15},{8,12},{9,1},{1... | collective-permute-start | bytes 393224 | tf_op jit(solution)/shard_map/ppermute | solution.py:389
  37.0 5.1 %collective-permute-start.8 = (bf16[2,2,128,128]{3,2,1,0:T(8,128)(2,1)S(1)}, bf16[2,2,128,128]{3,2,1,0:T(8,128)(2,1)S(1)}, u32[]{:S(2)}, u32[]{:S(2)}) collective-permute-start(bf16[2,2,128,128]{3,2,1,0:T(8,128)(2,1)S(1)} %get-tuple-element.76), channel_id=1, source_target_pairs={{0,8},{1,5},{2,10},{3,7},{4,12},{5,1},{6,14},{7,3},{8,0},{9,13},{1... | collective-permute-start | bytes 393224 | tf_op jit(solution)/shard_map/ppermute | solution.py:389
  38.3 5.9 %collective-permute-start.9 = (bf16[2,2,128,128]{3,2,1,0:T(8,128)(2,1)S(1)}, bf16[2,2,128,128]{3,2,1,0:T(8,128)(2,1)S(1)}, u32[]{:S(2)}, u32[]{:S(2)}) collective-permute-start(bf16[2,2,128,128]{3,2,1,0:T(8,128)(2,1)S(1)} %get-tuple-element.81), channel_id=1, source_target_pairs={{0,12},{1,13},{2,14},{3,15},{4,8},{5,9},{6,10},{7,11},{8,4},{9,5},... | collective-permute-start | bytes 393224 | tf_op jit(solution)/shard_map/ppermute | solution.py:389
  45.0 1.7 %collective-permute-start.10 = (bf16[256,512]{1,0:T(8,128)(2,1)S(1)}, bf16[256,512]{1,0:T(8,128)(2,1)S(1)}, u32[]{:S(2)}, u32[]{:S(2)}) collective-permute-start(bf16[256,512]{1,0:T(8,128)(2,1)S(1)} %get-tuple-element.86), channel_id=1, source_target_pairs={{0,1},{1,0},{2,3},{3,2},{4,5},{5,4},{6,7},{7,6},{8,9},{9,8},{10,11... | collective-permute-start | bytes 786440 | tf_op jit(solution)/shard_map/ppermute | solution.py:520
  46.1 3.0 %collective-permute-start.11 = (bf16[256,512]{1,0:T(8,128)(2,1)S(1)}, bf16[256,512]{1,0:T(8,128)(2,1)S(1)}, u32[]{:S(2)}, u32[]{:S(2)}) collective-permute-start(bf16[256,512]{1,0:T(8,128)(2,1)S(1)} %get-tuple-element.88), channel_id=1, source_target_pairs={{0,1},{1,0},{2,3},{3,2},{4,5},{5,4},{6,7},{7,6},{8,9},{9,8},{10,11... | collective-permute-start | bytes 786440 | tf_op jit(solution)/shard_map/ppermute | solution.py:525
  46.7 9.2 %collective-permute-start.12 = (bf16[256,512]{1,0:T(8,128)(2,1)S(1)}, bf16[256,512]{1,0:T(8,128)(2,1)S(1)}, u32[]{:S(2)}, u32[]{:S(2)}) collective-permute-start(bf16[256,512]{1,0:T(8,128)(2,1)S(1)} %add_convert_fusion.1), channel_id=1, source_target_pairs={{0,2},{1,3},{2,0},{3,1},{4,6},{5,7},{6,4},{7,5},{8,10},{9,11},{10,... | collective-permute-start | bytes 786440 | tf_op jit(solution)/shard_map/ppermute | solution.py:528
  49.2 11.5 %collective-permute-start.13 = (bf16[256,512]{1,0:T(8,128)(2,1)S(1)}, bf16[256,512]{1,0:T(8,128)(2,1)S(1)}, u32[]{:S(2)}, u32[]{:S(2)}) collective-permute-start(bf16[256,512]{1,0:T(8,128)(2,1)S(1)} %add_convert_fusion), channel_id=1, source_target_pairs={{0,2},{1,3},{2,0},{3,1},{4,6},{5,7},{6,4},{7,5},{8,10},{9,11},{10,... | collective-permute-start | bytes 786440 | tf_op jit(solution)/shard_map/ppermute | solution.py:532
  58.0 2.7 %collective-permute-start.17 = (bf16[64,1024]{1,0:T(8,128)(2,1)S(1)}, bf16[64,1024]{1,0:T(8,128)(2,1)S(1)}, u32[]{:S(2)}, u32[]{:S(2)}) collective-permute-start(bf16[64,1024]{1,0:T(8,128)(2,1)S(1)} %get-tuple-element.98), channel_id=1, source_target_pairs={{0,1},{1,0},{2,3},{3,2},{4,5},{5,4},{6,7},{7,6},{8,9},{9,8},{10,11... | collective-permute-start | bytes 393224 | tf_op jit(solution)/shard_map/ppermute | solution.py:549
  58.1 2.6 %collective-permute-start.16 = (bf16[64,1024]{1,0:T(8,128)(2,1)S(1)}, bf16[64,1024]{1,0:T(8,128)(2,1)S(1)}, u32[]{:S(2)}, u32[]{:S(2)}) collective-permute-start(bf16[64,1024]{1,0:T(8,128)(2,1)S(1)} %get-tuple-element.99), channel_id=1, source_target_pairs={{0,1},{1,0},{2,3},{3,2},{4,5},{5,4},{6,7},{7,6},{8,9},{9,8},{10,11... | collective-permute-start | bytes 393224 | tf_op jit(solution)/shard_map/ppermute | solution.py:549
  58.6 2.1 %collective-permute-start.15 = (bf16[64,1024]{1,0:T(8,128)(2,1)S(1)}, bf16[64,1024]{1,0:T(8,128)(2,1)S(1)}, u32[]{:S(2)}, u32[]{:S(2)}) collective-permute-start(bf16[64,1024]{1,0:T(8,128)(2,1)S(1)} %get-tuple-element.100), channel_id=1, source_target_pairs={{0,1},{1,0},{2,3},{3,2},{4,5},{5,4},{6,7},{7,6},{8,9},{9,8},{10,11... | collective-permute-start | bytes 393224 | tf_op jit(solution)/shard_map/ppermute | solution.py:549
  58.7 2.0 %collective-permute-start.14 = (bf16[64,1024]{1,0:T(8,128)(2,1)S(1)}, bf16[64,1024]{1,0:T(8,128)(2,1)S(1)}, u32[]{:S(2)}, u32[]{:S(2)}) collective-permute-start(bf16[64,1024]{1,0:T(8,128)(2,1)S(1)} %get-tuple-element.101), channel_id=1, source_target_pairs={{0,1},{1,0},{2,3},{3,2},{4,5},{5,4},{6,7},{7,6},{8,9},{9,8},{10,11... | collective-permute-start | bytes 393224 | tf_op jit(solution)/shard_map/ppermute | solution.py:549
